TPU v7x, 32 devices: a whole 2x2x4 slice. The times are simulated.
32 devices in a mesh: band: 2 (over x), ingest: 16 (over z, y, core).
Axes of the slice: x: 2, y: 2, z: 4, core: 2. Of those that a mesh axis runs over, the one named last changes fastest.
Arguments:
- voltages: int32 [1024, 2, 2, 45056], P(('band', 'ingest')), parts along dimension 0, may hold values from -127 to 127
- taps: float32 [4, 4096], replicated, may hold values from -3 to 3
- station_gain: float32 [512], P('ingest'), may hold values from 0.5 to 2
- station_order: int32 [512], replicated, may hold values from 0 to 511, each once
Outputs:
- visibilities: bfloat16 [64, 36, 2, 128, 128], P(('band', 'ingest')), parts along dimension 0
There are 2 independent parts, one for each index of `band`. A program takes and returns all parts, laid end to end along the dimension named above; an argument that names none is the same for every part. Nothing has to cross between parts.
Inputs may be any that keep to these rules, and one draw needn't show every extreme that they name: `station_order`: a permutation of the stations.
All inputs are finite; a program needn't handle non-finite values.
Results may differ from a plain program's by a relative error of at most 0.0052.
Values may be sent and summed in bfloat16 or wider, within the bound.
No kernel may reach another device: no remote copies, remote signals or barrier semaphores. Data moves between devices by JAX's collectives and lax.ppermute only.
A program may use at most 128 MiB of HBM per device.

v0:
```python
import functools
import math

import jax
import jax.numpy as jnp
import ml_dtypes
import numpy as np
from jax import lax
from jax.experimental import pallas as pl
from jax.experimental.pallas import tpu as pltpu
from jax.sharding import PartitionSpec as P

STATIONS = 512
NCHAN = 4096
BLOCK = 64
TAPS = 4
SPECTRA = 8
AVG = 32
OUT_DEV = 2
LANES = 128
CHUNKS = ((0, 4), (4, 4))
GROUP = 4
ROWS = 16
BF16 = jnp.bfloat16
F32 = jnp.float32
NT = (((1,), (1,)), ((), ()))


def split(values):
    high = values.astype(ml_dtypes.bfloat16)
    low = (values - high.astype(np.float64)).astype(ml_dtypes.bfloat16)
    return high, low


def tables(all_out):
    blocks = NCHAN // LANES
    angle = 2.0 * math.pi * (np.outer(np.arange(AVG), np.arange(blocks)) % blocks) / blocks
    cos, sin = np.cos(angle), np.sin(angle)
    stage = np.zeros((2, AVG, blocks, 2))
    stage[0, :, :, 0], stage[0, :, :, 1] = cos, sin
    stage[1, :, :, 0], stage[1, :, :, 1] = -sin, cos
    stage = stage.reshape(2 * AVG, 2 * blocks)
    stage = np.kron(np.eye(GROUP), stage)
    angle = 2.0 * math.pi * np.outer(np.arange(AVG), np.arange(LANES)) / NCHAN
    turn = np.stack([np.cos(angle), -np.sin(angle)]).astype(np.float32)
    first = (NCHAN - all_out * AVG) // 2
    bins = first // AVG + np.arange(all_out)
    angle = 2.0 * math.pi * (np.outer(bins, np.arange(LANES)) % LANES) / LANES
    cos, sin = np.cos(angle), np.sin(angle)
    last = np.zeros((all_out, 2, 2, LANES))
    last[:, 0, 0], last[:, 0, 1] = cos, sin
    last[:, 1, 0], last[:, 1, 1] = -sin, cos
    last = last.reshape(2 * all_out, 2 * LANES)
    return np.concatenate(split(stage)), turn, np.concatenate(split(last))


def halves(values):
    high = values.astype(BF16)
    return high, (values - high.astype(F32)).astype(BF16)


def spectra_kernel(count, gain_ref, *refs):
    frames = refs[: count + TAPS - 1]
    taps_ref, stage_ref, turn_ref, last_ref, out_ref, high_ref, low_ref, zhigh_ref, zlow_ref, held_ref = refs[count + TAPS - 1 :]
    outer, inner = pl.program_id(0), pl.program_id(1)
    wide = 2 * AVG
    for u in range(GROUP):
        for r in range(0, wide, 16):
            rows = slice(r, r + 16)
            coeffs = [taps_ref[j, rows, :] for j in range(TAPS)]
            samples = [ref[u, 0, rows, :].astype(F32) for ref in frames]
            for m in range(count):
                value = coeffs[0] * samples[m]
                for j in range(1, TAPS):
                    value = value + coeffs[j] * samples[m + j]
                high, low = halves(value)
                place = (slice(u * wide + r, u * wide + r + 16), slice(m * LANES, (m + 1) * LANES))
                high_ref[place] = high
                low_ref[place] = low
    size = GROUP * wide
    for start in range(0, count, 2):
        lanes = slice(start * LANES, (start + 2) * LANES)
        both = jnp.dot(stage_ref[...], high_ref[:, lanes], preferred_element_type=F32)
        rest = jnp.dot(stage_ref[:size, :], low_ref[:, lanes], preferred_element_type=F32)
        section = both[:size] + (both[size:] + rest)
        for u in range(GROUP):
            for m in range(start, start + 2):
                at = slice((m - start) * LANES, (m - start + 1) * LANES)
                real = section[u * wide : u * wide + AVG, at]
                imag = section[u * wide + AVG : (u + 1) * wide, at]
                turn_real, turn_imag = turn_ref[0], turn_ref[1]
                row = slice((u * count + m) * AVG, (u * count + m + 1) * AVG)
                high, low = halves(real * turn_real - imag * turn_imag)
                zhigh_ref[row, :LANES] = high
                zlow_ref[row, :LANES] = low
                high, low = halves(real * turn_imag + imag * turn_real)
                zhigh_ref[row, LANES:] = high
                zlow_ref[row, LANES:] = low
    outs = last_ref.shape[0] // 2
    width = count * AVG
    for pair in range(GROUP // 2):
        rows = slice(pair * 2 * width, (pair + 1) * 2 * width)
        both = lax.dot_general(last_ref[...], zhigh_ref[rows, :], NT, preferred_element_type=F32)
        rest = lax.dot_general(last_ref[:outs, :], zlow_ref[rows, :], NT, preferred_element_type=F32)
        found = both[:outs] + (both[outs:] + rest)
        for p in range(2):
            factor = gain_ref[(outer * ROWS + inner * GROUP + pair * 2) // 2] * (1.0 / (64.0 * math.sqrt(NCHAN)))
            at = pl.multiple_of((inner * GROUP + pair * 2 + p) * outs, outs)
            held_ref[pl.ds(at, outs), :] = found[:, p * width : (p + 1) * width] * factor

    @pl.when(inner == ROWS // GROUP - 1)
    def _():
        for row in range(outs):
            out_ref[row] = held_ref[pl.ds(row, ROWS, stride=outs), :].astype(BF16)


def spectra(voltages, taps, station_gain, consts, start, count):
    streams = voltages.shape[0]
    stage, turn, last = consts
    outs = last.shape[0] // 2
    steps = ROWS // GROUP
    wide = 2 * AVG
    width = count * AVG
    frame_spec = [
        pl.BlockSpec((GROUP, 1, wide, LANES), functools.partial(lambda j, a, b: (a * steps + b, j, 0, 0), start + j))
        for j in range(count + TAPS - 1)
    ]
    whole = lambda shape: pl.BlockSpec(shape, lambda a, b: (0,) * len(shape))
    return pl.pallas_call(
        functools.partial(spectra_kernel, count),
        out_shape=jax.ShapeDtypeStruct((outs, streams, width), BF16),
        grid=(streams // ROWS, steps),
        in_specs=[pl.BlockSpec(memory_space=pltpu.SMEM)]
        + frame_spec
        + [whole(taps.shape), whole(stage.shape), whole(turn.shape), whole(last.shape)],
        out_specs=pl.BlockSpec((outs, ROWS, width), lambda a, b: (0, a, 0)),
        scratch_shapes=[
            pltpu.VMEM((GROUP * wide, count * LANES), BF16),
            pltpu.VMEM((GROUP * wide, count * LANES), BF16),
            pltpu.VMEM((GROUP * width, 2 * LANES), BF16),
            pltpu.VMEM((GROUP * width, 2 * LANES), BF16),
            pltpu.VMEM((ROWS * outs, width), F32),
        ],
        compiler_params=pltpu.CompilerParams(vmem_limit_bytes=40 * 2**20),
        cost_estimate=pl.CostEstimate(
            flops=streams * count * 12_000_000,
            bytes_accessed=streams * (count + TAPS - 1) * wide * LANES * 4,
            transcendentals=0,
        ),
        name="spectra",
    )(station_gain, *([voltages] * (count + TAPS - 1)), taps, stage, turn, last)


def tiles_kernel(pick_ref, *refs):
    count = len(CHUNKS)
    parts, (out_ref, held_ref) = refs[:count], refs[count:]
    rows = 2 * STATIONS
    pieces = [part[:, ri].reshape(rows, part.shape[-1]) for ri in range(2) for part in parts]
    total = jnp.zeros((8, LANES), F32)
    for piece in pieces:
        wide = piece.astype(F32)
        total = total + jnp.sum((wide * wide).reshape(rows // 8, 8, LANES), axis=0)
    power = jnp.sum(total) / (STATIONS * 2 * SPECTRA * AVG)
    scale = 1.0 / jnp.full((1, LANES), SPECTRA * AVG * power, F32)
    data = jnp.concatenate(pieces, axis=1)
    half = data.shape[1] // 2
    side = 2 * BLOCK
    tile = 0
    for b in range(STATIONS // BLOCK):
        own = slice(b * side, (b + 1) * side)
        held_ref[own, :] = jnp.dot(pick_ref[own, :], data, preferred_element_type=F32).astype(BF16)
        mine = held_ref[own, :]
        left = jnp.concatenate([mine, jnp.concatenate([mine[:, half:], -mine[:, :half]], axis=1)], axis=0)
        for c in range(b + 1):
            product = lax.dot_general(left, held_ref[c * side : (c + 1) * side, :], NT, preferred_element_type=F32)
            scaled = (product * scale).astype(BF16)
            out_ref[0, tile, 0] = scaled[:side]
            out_ref[0, tile, 1] = scaled[side:]
            tile += 1


def tiles(pick, parts):
    devices, _, own, width = parts[0].shape
    blocks = STATIONS // BLOCK
    pairs = blocks * (blocks + 1) // 2
    side = 2 * BLOCK
    part_spec = pl.BlockSpec((devices, 2, own, width), lambda o: (0, o, 0, 0))
    return pl.pallas_call(
        tiles_kernel,
        out_shape=jax.ShapeDtypeStruct((OUT_DEV, pairs, 2, side, side), BF16),
        grid=(OUT_DEV,),
        in_specs=[pl.BlockSpec(pick.shape, lambda o: (0, 0))] + [part_spec] * len(parts),
        out_specs=pl.BlockSpec((1, pairs, 2, side, side), lambda o: (o, 0, 0, 0, 0)),
        scratch_shapes=[pltpu.VMEM((2 * STATIONS, 2 * SPECTRA * AVG), BF16)],
        compiler_params=pltpu.CompilerParams(vmem_limit_bytes=40 * 2**20),
        cost_estimate=pl.CostEstimate(flops=4_500_000_000, bytes_accessed=9_000_000, transcendentals=0),
        name="tiles",
    )(pick, *parts)


def body(voltages, taps, station_gain, station_order):
    devices = lax.axis_size("ingest")
    streams = 2 * voltages.shape[0]
    blocks = NCHAN // LANES
    all_out = OUT_DEV * devices
    consts = tables(all_out)
    frames = SPECTRA + TAPS - 1
    samples = voltages.reshape(streams, 2, frames * blocks, LANES).transpose(0, 2, 1, 3)
    samples = samples.reshape(streams, frames, 2 * blocks, LANES)
    coeffs = jnp.repeat(taps.reshape(TAPS, blocks, LANES), 2, axis=1)
    parts = []
    for start, count in CHUNKS:
        packed = spectra(samples, coeffs, station_gain, consts, start, count)
        packed = packed.reshape(devices, 2 * OUT_DEV, streams, count * AVG)
        parts.append(lax.all_to_all(packed, "ingest", split_axis=0, concat_axis=0, tiled=True))
    wanted = (2 * station_order[:, None] + jnp.arange(2, dtype=jnp.int32)).reshape(-1, 1)
    pick = (wanted == jnp.arange(2 * STATIONS, dtype=jnp.int32)).astype(BF16)
    return tiles(pick, parts)


def solution(mesh):
    return jax.shard_map(
        body,
        mesh=mesh,
        in_specs=(P(("band", "ingest"), None, None, None), P(), P("ingest"), P()),
        out_specs=P(("band", "ingest"), None, None, None, None),
        check_vma=False,
    )
```

profile of v0, /device:TPU:11, one launch (start us, length us, event | category | flops | bytes accessed | tf_op | source)
XLA Modules:
  0.0 98.2 jit_solution(6728299320378948293)
XLA Ops:
  0.0 0.8 copy.12
  0.9 0.0 copy-start
  0.9 0.9 copy-done
  1.8 0.0 copy-start.2
  1.9 0.8 copy-done.2
  2.7 0.0 copy-start.4
  2.7 0.8 copy-done.4
  3.4 0.7 copy-done.6
  4.1 20.8 %spectra.3 = bf16[64,64,128]{2,1,0:T(8,128)(2,1)} custom-call(f32[32]{0:T(128)S(1)} %copy-done.6, s32[64,11,64,128]{3,2,1,0:T(8,128)} %bitcast.14, s32[64,11,64,128]{3,2,1,0:T(8,128)} %bitcast.15, s32[64,11,64,128]{3,2,1,0:T(8,128)} %bitcast.16, s32[64,11,64,128]{3,2,1,0:T(8,128)} %bitcast.17, s32[64,11,64,128]{3,2,1,0:T(8,128)} %bitcast.18, ...), custom_call_target="tpu_custom_call" | custom-call | flops 3072000000 | bytes 14680064 | tf_op jit(solution)/shard_map/spectra/pallas_call | solution.py:129
  24.9 6.6 %all-to-all-start.1 = ((bf16[16,4,64,128]{3,2,1,0:T(8,128)(2,1)}), bf16[16,4,64,128]{3,2,1,0:T(8,128)(2,1)S(1)}, u32[]{:S(2)}, u32[]{:S(2)}) async-start(bf16[16,4,64,128]{3,2,1,0:T(8,128)(2,1)} %bitcast.7), calls=%async_computation.1 | async-start | bytes 2097152 | tf_op jit(solution)/shard_map/all_to_all | solution.py:215
  31.5 0.0 copy-done.1
  31.5 0.0 copy-done.3
  31.5 0.0 copy-done.5
  31.5 0.0 copy-done.7
  31.5 0.0 copy-start.8
  31.5 20.7 %spectra.2 = bf16[64,64,128]{2,1,0:T(8,128)(2,1)} custom-call(f32[32]{0:T(128)S(1)} %copy-done.7, s32[64,11,64,128]{3,2,1,0:T(8,128)} %bitcast.21, s32[64,11,64,128]{3,2,1,0:T(8,128)} %bitcast.22, s32[64,11,64,128]{3,2,1,0:T(8,128)} %bitcast.23, s32[64,11,64,128]{3,2,1,0:T(8,128)} %bitcast.24, s32[64,11,64,128]{3,2,1,0:T(8,128)} %bitcast.25, ...), custom_call_target="tpu_custom_call" | custom-call | flops 3072000000 | bytes 14680064 | tf_op jit(solution)/shard_map/spectra/pallas_call | solution.py:129
  52.2 4.1 %all-to-all-done.1.refs_1_ = bf16[16,4,64,128]{3,2,1,0:T(8,128)(2,1)S(1)} async-done(((bf16[16,4,64,128]{3,2,1,0:T(8,128)(2,1)}), bf16[16,4,64,128]{3,2,1,0:T(8,128)(2,1)S(1)}, u32[]{:S(2)}, u32[]{:S(2)}) %all-to-all-start.1) | async-done | bytes 1048608 | tf_op jit(solution)/shard_map/all_to_all | solution.py:215
  56.3 5.0 %all-to-all-start = ((bf16[16,4,64,128]{3,2,1,0:T(8,128)(2,1)}), bf16[16,4,64,128]{3,2,1,0:T(8,128)(2,1)}, u32[]{:S(2)}, u32[]{:S(2)}) async-start(bf16[16,4,64,128]{3,2,1,0:T(8,128)(2,1)} %bitcast.4), calls=%async_computation | async-start | bytes 2097152 | tf_op jit(solution)/shard_map/all_to_all | solution.py:215
  61.3 0.0 copy-done.8
  61.3 0.1 iota_add_fusion
  61.5 0.2 add.23
  61.6 0.4 fusion.pick_ref
  62.0 24.2 %all-to-all-done.refs_0_ = bf16[16,4,64,128]{3,2,1,0:T(8,128)(2,1)} async-done(((bf16[16,4,64,128]{3,2,1,0:T(8,128)(2,1)}), bf16[16,4,64,128]{3,2,1,0:T(8,128)(2,1)}, u32[]{:S(2)}, u32[]{:S(2)}) %all-to-all-start) | async-done | bytes 1048608 | tf_op jit(solution)/shard_map/all_to_all | solution.py:215
  86.3 12.0 %tiles.1 = bf16[2,36,2,128,128]{4,3,2,1,0:T(8,128)(2,1)} custom-call(bf16[1024,1024]{1,0:T(8,128)(2,1)S(1)} %fusion.pick_ref, bf16[16,4,64,128]{3,2,1,0:T(8,128)(2,1)} %all-to-all-done.refs_0_, bf16[16,4,64,128]{3,2,1,0:T(8,128)(2,1)S(1)} %all-to-all-done.1.refs_1_), custom_call_target="tpu_custom_call" | custom-call | flops 4499999744 | bytes 9000000 | tf_op jit(solution)/shard_map/tiles/pallas_call | solution.py:188
  (7 shorter events, 0.1 us)
Async XLA Ops:
  0.9 1.0 copy-start
  1.8 0.8 copy-start.2
  2.7 0.8 copy-start.4
  3.4 0.7 copy-start.6
  4.1 27.4 %copy-start.1 = (bf16[512,256]{1,0:T(8,128)(2,1)S(1)}, bf16[512,256]{1,0:T(8,128)(2,1)}, u32[]{:S(2)}) copy-start(bf16[512,256]{1,0:T(8,128)(2,1)} %constant.8.clone.refs_8_) | copy-start | bytes 786436
  4.1 27.4 %copy-start.3 = (bf16[128,256]{1,0:T(8,128)(2,1)S(1)}, bf16[128,256]{1,0:T(8,128)(2,1)}, u32[]{:S(2)}) copy-start(bf16[128,256]{1,0:T(8,128)(2,1)} %constant.10.clone.refs_10_) | copy-start | bytes 196612
  4.1 27.4 %copy-start.5 = (f32[2,32,128]{2,1,0:T(8,128)S(1)}, f32[2,32,128]{2,1,0:T(8,128)}, u32[]{:S(2)}) copy-start(f32[2,32,128]{2,1,0:T(8,128)} %constant.9.clone.refs_9_) | copy-start | bytes 98308
  4.1 27.4 %copy-start.7 = (f32[32]{0:T(128)S(1)}, f32[32]{0:T(128)}, u32[]{:S(2)}) copy-start(f32[32]{0:T(128)} %gain_ref.3) | copy-start | bytes 388
  24.9 31.5 %all-to-all-start.1 = ((bf16[16,4,64,128]{3,2,1,0:T(8,128)(2,1)}), bf16[16,4,64,128]{3,2,1,0:T(8,128)(2,1)S(1)}, u32[]{:S(2)}, u32[]{:S(2)}) async-start(bf16[16,4,64,128]{3,2,1,0:T(8,128)(2,1)} %bitcast.7), calls=%async_computation.1 | async-start | bytes 2097152 | tf_op jit(solution)/shard_map/all_to_all | solution.py:215
  31.5 29.8 %copy-start.8 = (s32[512]{0:T(512)S(1)}, s32[512]{0:T(512)}, u32[]{:S(2)}) copy-start(s32[512]{0:T(512)} %param.10) | copy-start | bytes 6148
  56.3 29.9 %all-to-all-start = ((bf16[16,4,64,128]{3,2,1,0:T(8,128)(2,1)}), bf16[16,4,64,128]{3,2,1,0:T(8,128)(2,1)}, u32[]{:S(2)}, u32[]{:S(2)}) async-start(bf16[16,4,64,128]{3,2,1,0:T(8,128)(2,1)} %bitcast.4), calls=%async_computation | async-start | bytes 2097152 | tf_op jit(solution)/shard_map/all_to_all | solution.py:215
where the time goes:
time: 99.2 us; the launch traced here: 98.2 us
  Pallas kernels  53.4 us (54%)
  waiting for transfers between devices  28.3 us (29%)
  starting transfers between devices  11.6 us (12%)
  local copies, waits for them, and re-layouts  4.27 us (4%)
    pallas_call x2, Pallas kernels, spectra(): pl.pallas_call(functools.partial(spectra_kernel, count), out_shape=jax.Sh...  41.4 us
    all_to_all x2, waiting for transfers between devices, body(): lax.all_to_all(packed, 'ingest', split_axis=0, concat_axis=0, tiled=True)  28.3 us
    pallas_call x1, Pallas kernels, tiles(): pl.pallas_call(tiles_kernel, out_shape=jax.ShapeDtypeStruct((OUT_DEV, pai...  12 us
    all_to_all x2, starting transfers between devices, body(): lax.all_to_all(packed, 'ingest', split_axis=0, concat_axis=0, tiled=True)  11.6 us
    unnamed x19, local copies, waits for them, and re-layouts  4.06 us
  transfers between devices with their start and end apart: 2, of which 2 were waited for; matrix products, arithmetic and copies ran while one was open for 1% of the time, Pallas kernels for 21%

commit v1 on v0

v1 whole, which is shorter than its diff:
```python
import functools
import math

import jax
import jax.numpy as jnp
import ml_dtypes
import numpy as np
from jax import lax
from jax.experimental import pallas as pl
from jax.experimental.pallas import tpu as pltpu
from jax.sharding import PartitionSpec as P

STATIONS = 512
NCHAN = 4096
BLOCK = 64
TAPS = 4
SPECTRA = 8
AVG = 32
OUT_DEV = 2
LANES = 128
CHUNKS = ((0, 4), (4, 4))
GROUP = 4
ROWS = 16
BF16 = jnp.bfloat16
F32 = jnp.float32
NT = (((1,), (1,)), ((), ()))


def split(values):
    high = values.astype(ml_dtypes.bfloat16)
    low = (values - high.astype(np.float64)).astype(ml_dtypes.bfloat16)
    return high, low


def tables(all_out):
    blocks = NCHAN // LANES
    angle = 2.0 * math.pi * (np.outer(np.arange(AVG), np.arange(blocks)) % blocks) / blocks
    cos, sin = np.cos(angle), np.sin(angle)
    stage = np.zeros((2, AVG, blocks, 2))
    stage[0, :, :, 0], stage[0, :, :, 1] = cos, sin
    stage[1, :, :, 0], stage[1, :, :, 1] = -sin, cos
    stage = stage.reshape(2 * AVG, 2 * blocks)
    stage = np.kron(np.eye(GROUP), stage)
    angle = 2.0 * math.pi * np.outer(np.arange(AVG), np.arange(LANES)) / NCHAN
    turn = np.stack([np.cos(angle), -np.sin(angle)]).astype(np.float32)
    first = (NCHAN - all_out * AVG) // 2
    bins = first // AVG + np.arange(all_out)
    angle = 2.0 * math.pi * (np.outer(bins, np.arange(LANES)) % LANES) / LANES
    cos, sin = np.cos(angle), np.sin(angle)
    last = np.zeros((all_out, 2, 2, LANES))
    last[:, 0, 0], last[:, 0, 1] = cos, sin
    last[:, 1, 0], last[:, 1, 1] = -sin, cos
    last = last.reshape(2 * all_out, 2 * LANES)
    return np.concatenate(split(stage)), turn, np.concatenate(split(last))


def halves(values):
    high = values.astype(BF16)
    return high, (values - high.astype(F32)).astype(BF16)


def spectra_kernel(count, gain_ref, *refs):
    frames = refs[: count + TAPS - 1]
    taps_ref, stage_ref, turn_ref, last_ref, out_ref, coeff_ref, high_ref, low_ref, zhigh_ref, zlow_ref, held_ref = refs[count + TAPS - 1 :]
    step = pl.program_id(0)
    wide = 2 * AVG
    size = GROUP * wide
    outs = last_ref.shape[0] // 2
    width = count * AVG

    @pl.when(step == 0)
    def _():
        for j in range(TAPS):
            rows = taps_ref[pl.ds(j, AVG, stride=TAPS), :]
            for ri in range(2):
                coeff_ref[j, pl.ds(ri, AVG, stride=2), :] = rows

    def filter_group(g):
        for u in range(GROUP):
            for r in range(0, wide, 16):
                rows = slice(r, r + 16)
                coeffs = [coeff_ref[j, rows, :] for j in range(TAPS)]
                samples = [ref[g * GROUP + u, 0, rows, :].astype(F32) for ref in frames]
                for m in range(count):
                    value = coeffs[0] * samples[m]
                    for j in range(1, TAPS):
                        value = value + coeffs[j] * samples[m + j]
                    high, low = halves(value)
                    place = (g, slice(u * wide + r, u * wide + r + 16), slice(m * LANES, (m + 1) * LANES))
                    high_ref[place] = high
                    low_ref[place] = low

    def first_group(g):
        for start in range(0, count, 2):
            lanes = slice(start * LANES, (start + 2) * LANES)
            both = jnp.dot(stage_ref[...], high_ref[g, :, lanes], preferred_element_type=F32)
            rest = jnp.dot(stage_ref[:size, :], low_ref[g, :, lanes], preferred_element_type=F32)
            section = both[:size] + (both[size:] + rest)
            for u in range(GROUP):
                for m in range(start, start + 2):
                    at = slice((m - start) * LANES, (m - start + 1) * LANES)
                    real = section[u * wide : u * wide + AVG, at]
                    imag = section[u * wide + AVG : (u + 1) * wide, at]
                    turn_real, turn_imag = turn_ref[0], turn_ref[1]
                    row = slice((u * count + m) * AVG, (u * count + m + 1) * AVG)
                    high, low = halves(real * turn_real - imag * turn_imag)
                    zhigh_ref[g, row, :LANES] = high
                    zlow_ref[g, row, :LANES] = low
                    high, low = halves(real * turn_imag + imag * turn_real)
                    zhigh_ref[g, row, LANES:] = high
                    zlow_ref[g, row, LANES:] = low

    def last_group(g):
        for pair in range(GROUP // 2):
            rows = slice(pair * 2 * width, (pair + 1) * 2 * width)
            both = lax.dot_general(last_ref[...], zhigh_ref[g, rows, :], NT, preferred_element_type=F32)
            rest = lax.dot_general(last_ref[:outs, :], zlow_ref[g, rows, :], NT, preferred_element_type=F32)
            found = both[:outs] + (both[outs:] + rest)
            stream = g * GROUP + pair * 2
            factor = gain_ref[(step * ROWS + stream) // 2] * (1.0 / (64.0 * math.sqrt(NCHAN)))
            for p in range(2):
                held_ref[(stream + p) * outs : (stream + p + 1) * outs, :] = found[:, p * width : (p + 1) * width] * factor

    groups = ROWS // GROUP
    for g in range(groups + 2):
        if g < groups:
            filter_group(g)
        if 1 <= g <= groups:
            first_group(g - 1)
        if g >= 2:
            last_group(g - 2)
    for row in range(outs):
        out_ref[row] = held_ref[pl.ds(row, ROWS, stride=outs), :].astype(BF16)


def spectra(voltages, taps, station_gain, consts, start, count):
    streams = voltages.shape[0]
    stage, turn, last = consts
    outs = last.shape[0] // 2
    groups = ROWS // GROUP
    wide = 2 * AVG
    width = count * AVG
    frame_spec = [
        pl.BlockSpec((ROWS, 1, wide, LANES), functools.partial(lambda j, a: (a, j, 0, 0), start + j))
        for j in range(count + TAPS - 1)
    ]
    whole = lambda shape: pl.BlockSpec(shape, lambda a: (0,) * len(shape))
    return pl.pallas_call(
        functools.partial(spectra_kernel, count),
        out_shape=jax.ShapeDtypeStruct((outs, streams, width), BF16),
        grid=(streams // ROWS,),
        in_specs=[pl.BlockSpec(memory_space=pltpu.SMEM)]
        + frame_spec
        + [whole(taps.shape), whole(stage.shape), whole(turn.shape), whole(last.shape)],
        out_specs=pl.BlockSpec((outs, ROWS, width), lambda a: (0, a, 0)),
        scratch_shapes=[
            pltpu.VMEM((TAPS, wide, LANES), F32),
            pltpu.VMEM((groups, GROUP * wide, count * LANES), BF16),
            pltpu.VMEM((groups, GROUP * wide, count * LANES), BF16),
            pltpu.VMEM((groups, GROUP * width, 2 * LANES), BF16),
            pltpu.VMEM((groups, GROUP * width, 2 * LANES), BF16),
            pltpu.VMEM((ROWS * outs, width), F32),
        ],
        compiler_params=pltpu.CompilerParams(vmem_limit_bytes=60_000_000),
        cost_estimate=pl.CostEstimate(
            flops=streams * count * 12_000_000,
            bytes_accessed=streams * (count + TAPS - 1) * wide * LANES * 4,
            transcendentals=0,
        ),
        name="spectra",
    )(station_gain, *([voltages] * (count + TAPS - 1)), taps, stage, turn, last)


def squares(pieces):
    total = jnp.zeros((8, LANES), F32)
    for piece in pieces:
        values = piece.astype(F32)
        total = total + jnp.sum((values * values).reshape(-1, 8, LANES), axis=0)
    return total


def arrange_kernel(pick_ref, part_ref, out_ref, power_ref):
    rows = 2 * STATIONS
    pieces = [part_ref[:, ri].reshape(rows, LANES) for ri in range(2)]
    power_ref[0] = squares(pieces)
    data = jnp.concatenate(pieces, axis=1)
    for r in range(0, rows, 2 * LANES):
        own = slice(r, r + 2 * LANES)
        out_ref[0, own, :] = jnp.dot(pick_ref[own, :], data, preferred_element_type=F32).astype(BF16)


def arrange(pick, part):
    devices, _, own, width = part.shape
    rows = 2 * STATIONS
    return pl.pallas_call(
        arrange_kernel,
        out_shape=(
            jax.ShapeDtypeStruct((OUT_DEV, rows, 2 * width), BF16),
            jax.ShapeDtypeStruct((OUT_DEV, 8, LANES), F32),
        ),
        grid=(OUT_DEV,),
        in_specs=[
            pl.BlockSpec(pick.shape, lambda o: (0, 0)),
            pl.BlockSpec((devices, 2, own, width), lambda o: (0, o, 0, 0)),
        ],
        out_specs=(
            pl.BlockSpec((1, rows, 2 * width), lambda o: (o, 0, 0)),
            pl.BlockSpec((1, 8, LANES), lambda o: (o, 0, 0)),
        ),
        compiler_params=pltpu.CompilerParams(vmem_limit_bytes=40 * 2**20),
        cost_estimate=pl.CostEstimate(flops=1_100_000_000, bytes_accessed=4_000_000, transcendentals=0),
        name="arrange",
    )(pick, part)


def turned(values):
    return jnp.concatenate([values[:, LANES:], -values[:, :LANES]], axis=1)


def tiles_kernel(pick_ref, part_ref, early_ref, power_ref, out_ref, left_ref, right_ref):
    rows = 2 * STATIONS
    side = 2 * BLOCK
    blocks = STATIONS // BLOCK
    pieces = [part_ref[:, ri].reshape(rows, LANES) for ri in range(2)]
    power = jnp.sum(squares(pieces) + power_ref[0]) / (STATIONS * 2 * SPECTRA * AVG)
    scale = 1.0 / jnp.full((1, LANES), SPECTRA * AVG * power, F32)
    data = jnp.concatenate(pieces, axis=1)
    half = data.shape[1]
    for r in range(0, rows, 2 * side):
        found = jnp.dot(pick_ref[r : r + 2 * side, :], data, preferred_element_type=F32).astype(BF16)
        early = early_ref[0, r : r + 2 * side, :]
        right_ref[r : r + 2 * side, :half] = early
        right_ref[r : r + 2 * side, half:] = found
        for p in range(2):
            own = slice(p * side, (p + 1) * side)
            at = 2 * r + p * 2 * side
            left_ref[at : at + side, :half] = early[own]
            left_ref[at : at + side, half:] = found[own]
            left_ref[at + side : at + 2 * side, :half] = turned(early[own])
            left_ref[at + side : at + 2 * side, half:] = turned(found[own])
    for c in range(0, blocks, 2):
        right = right_ref[c * side : (c + 2) * side, :]
        for b in range(c, blocks):
            left = left_ref[b * 2 * side : (b + 1) * 2 * side, :]
            product = lax.dot_general(left, right, NT, preferred_element_type=F32)
            for p in range(2):
                if c + p <= b:
                    tile = b * (b + 1) // 2 + c + p
                    scaled = (product[:, p * side : (p + 1) * side] * scale).astype(BF16)
                    out_ref[0, tile, 0] = scaled[:side]
                    out_ref[0, tile, 1] = scaled[side:]


def tiles(pick, part, early, power):
    devices, _, own, width = part.shape
    blocks = STATIONS // BLOCK
    pairs = blocks * (blocks + 1) // 2
    side = 2 * BLOCK
    rows = 2 * STATIONS
    return pl.pallas_call(
        tiles_kernel,
        out_shape=jax.ShapeDtypeStruct((OUT_DEV, pairs, 2, side, side), BF16),
        grid=(OUT_DEV,),
        in_specs=[
            pl.BlockSpec(pick.shape, lambda o: (0, 0)),
            pl.BlockSpec((devices, 2, own, width), lambda o: (0, o, 0, 0)),
            pl.BlockSpec((1, rows, 2 * width), lambda o: (o, 0, 0)),
            pl.BlockSpec((1, 8, LANES), lambda o: (o, 0, 0)),
        ],
        out_specs=pl.BlockSpec((1, pairs, 2, side, side), lambda o: (o, 0, 0, 0, 0)),
        scratch_shapes=[
            pltpu.VMEM((2 * rows, 4 * width), BF16),
            pltpu.VMEM((rows, 4 * width), BF16),
        ],
        compiler_params=pltpu.CompilerParams(vmem_limit_bytes=40 * 2**20),
        cost_estimate=pl.CostEstimate(flops=4_500_000_000, bytes_accessed=9_000_000, transcendentals=0),
        name="tiles",
    )(pick, part, early, power)


def body(voltages, taps, station_gain, station_order):
    devices = lax.axis_size("ingest")
    streams = 2 * voltages.shape[0]
    blocks = NCHAN // LANES
    all_out = OUT_DEV * devices
    consts = tables(all_out)
    frames = SPECTRA + TAPS - 1
    samples = voltages.reshape(streams, 2, frames * blocks, LANES).transpose(0, 2, 1, 3)
    samples = samples.reshape(streams, frames, 2 * blocks, LANES)
    coeffs = taps.reshape(TAPS, blocks, LANES).transpose(1, 0, 2).reshape(TAPS * blocks, LANES)
    parts = []
    for start, count in CHUNKS:
        packed = spectra(samples, coeffs, station_gain, consts, start, count)
        packed = packed.reshape(devices, 2 * OUT_DEV, streams, count * AVG)
        parts.append(lax.all_to_all(packed, "ingest", split_axis=0, concat_axis=0, tiled=True))
    wanted = (2 * station_order[:, None] + jnp.arange(2, dtype=jnp.int32)).reshape(-1, 1)
    pick = (wanted == jnp.arange(2 * STATIONS, dtype=jnp.int32)).astype(BF16)
    early, power = arrange(pick, parts[0])
    return tiles(pick, parts[1], early, power)


def solution(mesh):
    return jax.shard_map(
        body,
        mesh=mesh,
        in_specs=(P(("band", "ingest"), None, None, None), P(), P("ingest"), P()),
        out_specs=P(("band", "ingest"), None, None, None, None),
        check_vma=False,
    )
```

time: 99.2 us -> 83.4 us (0.84)
  Pallas kernels: 53.4 us -> 35.9 us
  waiting for transfers between devices: 28.3 us -> 32.6 us
  local copies, waits for them, and re-layouts: 4.27 us -> 2.42 us
    pallas_call x2, Pallas kernels: 41.4 us -> 27.7 us  [spectra(): pl.pallas_call(functools.partial(spectra_kernel, count), out_shape=jax.Sh...]
    pallas_call x1, Pallas kernels: 12 us -> 6.64 us  [tiles(): pl.pallas_call(tiles_kernel, out_shape=jax.ShapeDtypeStruct((OUT_DEV, pai...]
    all_to_all x2, waiting for transfers between devices: 28.3 us -> 32.6 us  [body(): lax.all_to_all(packed, 'ingest', split_axis=0, concat_axis=0, tiled=True)]
    unnamed x19 -> x6, local copies, waits for them, and re-layouts: 4.06 us -> 2.25 us
    pallas_call x0 -> x1, Pallas kernels: none -> 1.57 us  [arrange(): pl.pallas_call(arrange_kernel, out_shape=(jax.ShapeDtypeStruct((OUT_DEV,...]
  transfers between devices with their start and end apart: 2 -> 2, of which waited for: 2 -> 2; matrix products, arithmetic and copies ran while one was open for 1% -> 1% of each run, Pallas kernels for 21% -> 19%
where the time goes in v1:
time: 83.4 us; the launch traced here: 83.1 us
  Pallas kernels  35.9 us (43%)
  waiting for transfers between devices  32.6 us (39%)
  starting transfers between devices  11.6 us (14%)
  local copies, waits for them, and re-layouts  2.42 us (3%)
    all_to_all x2, waiting for transfers between devices, body(): lax.all_to_all(packed, 'ingest', split_axis=0, concat_axis=0, tiled=True)  32.6 us
    pallas_call x2, Pallas kernels, spectra(): pl.pallas_call(functools.partial(spectra_kernel, count), out_shape=jax.Sh...  27.7 us
    all_to_all x2, starting transfers between devices, body(): lax.all_to_all(packed, 'ingest', split_axis=0, concat_axis=0, tiled=True)  11.6 us
    pallas_call x1, Pallas kernels, tiles(): pl.pallas_call(tiles_kernel, out_shape=jax.ShapeDtypeStruct((OUT_DEV, pai...  6.64 us
    unnamed x6, local copies, waits for them, and re-layouts  2.25 us
  transfers between devices with their start and end apart: 2, of which 2 were waited for; matrix products, arithmetic and copies ran while one was open for 1% of the time, Pallas kernels for 19%

profile of v1, /device:TPU:11, one launch (start us, length us, event | category | flops | bytes accessed | tf_op | source)
XLA Modules:
  0.0 83.1 jit_solution(891548339015777708)
XLA Ops:
  0.0 13.8 %spectra.3 = bf16[64,64,128]{2,1,0:T(8,128)(2,1)} custom-call(f32[32]{0:T(128)} %gain_ref.3, s32[64,11,64,128]{3,2,1,0:T(8,128)} %bitcast.12, s32[64,11,64,128]{3,2,1,0:T(8,128)} %bitcast.13, s32[64,11,64,128]{3,2,1,0:T(8,128)} %bitcast.14, s32[64,11,64,128]{3,2,1,0:T(8,128)} %bitcast.15, s32[64,11,64,128]{3,2,1,0:T(8,128)} %bitcast.16, ...), custom_call_target="tpu_custom_call" | custom-call | flops 3072000000 | bytes 14680064 | tf_op jit(solution)/shard_map/spectra/pallas_call | solution.py:148
  13.8 6.6 %all-to-all-start.1 = ((bf16[16,4,64,128]{3,2,1,0:T(8,128)(2,1)}), bf16[16,4,64,128]{3,2,1,0:T(8,128)(2,1)S(1)}, u32[]{:S(2)}, u32[]{:S(2)}) async-start(bf16[16,4,64,128]{3,2,1,0:T(8,128)(2,1)} %bitcast.27), calls=%async_computation.1 | async-start | bytes 2097152 | tf_op jit(solution)/shard_map/all_to_all | solution.py:295
  20.4 0.0 copy-start.2
  20.4 13.9 %spectra.2 = bf16[64,64,128]{2,1,0:T(8,128)(2,1)} custom-call(f32[32]{0:T(128)} %gain_ref.3, s32[64,11,64,128]{3,2,1,0:T(8,128)} %bitcast.19, s32[64,11,64,128]{3,2,1,0:T(8,128)} %bitcast.20, s32[64,11,64,128]{3,2,1,0:T(8,128)} %bitcast.21, s32[64,11,64,128]{3,2,1,0:T(8,128)} %bitcast.22, s32[64,11,64,128]{3,2,1,0:T(8,128)} %bitcast.23, ...), custom_call_target="tpu_custom_call" | custom-call | flops 3072000000 | bytes 14680064 | tf_op jit(solution)/shard_map/spectra/pallas_call | solution.py:148
  34.3 11.0 %all-to-all-done.1.part_ref = bf16[16,4,64,128]{3,2,1,0:T(8,128)(2,1)S(1)} async-done(((bf16[16,4,64,128]{3,2,1,0:T(8,128)(2,1)}), bf16[16,4,64,128]{3,2,1,0:T(8,128)(2,1)S(1)}, u32[]{:S(2)}, u32[]{:S(2)}) %all-to-all-start.1) | async-done | bytes 1048608 | tf_op jit(solution)/shard_map/all_to_all | solution.py:295
  45.3 5.0 %all-to-all-start = ((bf16[16,4,64,128]{3,2,1,0:T(8,128)(2,1)}), bf16[16,4,64,128]{3,2,1,0:T(8,128)(2,1)}, u32[]{:S(2)}, u32[]{:S(2)}) async-start(bf16[16,4,64,128]{3,2,1,0:T(8,128)(2,1)} %bitcast.26), calls=%async_computation | async-start | bytes 2097152 | tf_op jit(solution)/shard_map/all_to_all | solution.py:295
  50.3 0.0 copy-done.2
  50.3 0.1 iota_add_fusion
  50.4 0.2 add.23
  50.6 0.4 fusion.pick_ref
  51.0 1.6 %arrange.1 = (bf16[2,1024,256]{2,1,0:T(8,128)(2,1)S(1)}, f32[2,8,128]{2,1,0:T(8,128)S(1)}) custom-call(bf16[1024,1024]{1,0:T(8,128)(2,1)S(1)} %fusion.pick_ref, bf16[16,4,64,128]{3,2,1,0:T(8,128)(2,1)S(1)} %all-to-all-done.1.part_ref), custom_call_target="tpu_custom_call" | custom-call | flops 1100000000 | bytes 4000000 | tf_op jit(solution)/shard_map/arrange/pallas_call | solution.py:195
  52.6 0.0 copy-start
  52.6 1.0 %copy-done = bf16[2,1024,256]{2,1,0:T(8,128)(2,1)} copy-done((bf16[2,1024,256]{2,1,0:T(8,128)(2,1)}, bf16[2,1024,256]{2,1,0:T(8,128)(2,1)S(1)}, u32[]{:S(2)}) %copy-start) | copy-done | bytes 1048600
  53.6 21.6 %all-to-all-done.part_ref = bf16[16,4,64,128]{3,2,1,0:T(8,128)(2,1)} async-done(((bf16[16,4,64,128]{3,2,1,0:T(8,128)(2,1)}), bf16[16,4,64,128]{3,2,1,0:T(8,128)(2,1)}, u32[]{:S(2)}, u32[]{:S(2)}) %all-to-all-start) | async-done | bytes 1048608 | tf_op jit(solution)/shard_map/all_to_all | solution.py:295
  75.2 0.0 copy-start.1
  75.2 1.2 %copy-done.1 = bf16[2,1024,256]{2,1,0:T(8,128)(2,1)S(1)} copy-done((bf16[2,1024,256]{2,1,0:T(8,128)(2,1)S(1)}, bf16[2,1024,256]{2,1,0:T(8,128)(2,1)}, u32[]{:S(2)}) %copy-start.1) | copy-done | bytes 1048600
  76.4 6.6 %tiles.1 = bf16[2,36,2,128,128]{4,3,2,1,0:T(8,128)(2,1)} custom-call(bf16[1024,1024]{1,0:T(8,128)(2,1)S(1)} %fusion.pick_ref, bf16[16,4,64,128]{3,2,1,0:T(8,128)(2,1)} %all-to-all-done.part_ref, bf16[2,1024,256]{2,1,0:T(8,128)(2,1)S(1)} %copy-done.1, f32[2,8,128]{2,1,0:T(8,128)S(1)} %get-tuple-element.8.power_ref), custom_call_target="tpu_custom_call" | custom-call | flops 4499999744 | bytes 9000000 | tf_op jit(solution)/shard_map/tiles/pallas_call | solution.py:260
  (1 shorter events, 0.0 us)
Async XLA Ops:
  13.8 31.5 %all-to-all-start.1 = ((bf16[16,4,64,128]{3,2,1,0:T(8,128)(2,1)}), bf16[16,4,64,128]{3,2,1,0:T(8,128)(2,1)S(1)}, u32[]{:S(2)}, u32[]{:S(2)}) async-start(bf16[16,4,64,128]{3,2,1,0:T(8,128)(2,1)} %bitcast.27), calls=%async_computation.1 | async-start | bytes 2097152 | tf_op jit(solution)/shard_map/all_to_all | solution.py:295
  20.4 29.8 %copy-start.2 = (s32[512]{0:T(512)S(1)}, s32[512]{0:T(512)}, u32[]{:S(2)}) copy-start(s32[512]{0:T(512)} %param.10) | copy-start | bytes 6148
  45.3 29.9 %all-to-all-start = ((bf16[16,4,64,128]{3,2,1,0:T(8,128)(2,1)}), bf16[16,4,64,128]{3,2,1,0:T(8,128)(2,1)}, u32[]{:S(2)}, u32[]{:S(2)}) async-start(bf16[16,4,64,128]{3,2,1,0:T(8,128)(2,1)} %bitcast.26), calls=%async_computation | async-start | bytes 2097152 | tf_op jit(solution)/shard_map/all_to_all | solution.py:295
  52.6 1.0 %copy-start = (bf16[2,1024,256]{2,1,0:T(8,128)(2,1)}, bf16[2,1024,256]{2,1,0:T(8,128)(2,1)S(1)}, u32[]{:S(2)}) copy-start(bf16[2,1024,256]{2,1,0:T(8,128)(2,1)S(1)} %get-tuple-element.7.early_ref) | copy-start | bytes 3145732
  75.2 1.2 %copy-start.1 = (bf16[2,1024,256]{2,1,0:T(8,128)(2,1)S(1)}, bf16[2,1024,256]{2,1,0:T(8,128)(2,1)}, u32[]{:S(2)}) copy-start(bf16[2,1024,256]{2,1,0:T(8,128)(2,1)} %copy-done) | copy-start | bytes 3145732

commit v2 on v1

--- a/solution.py
+++ b/solution.py
@@ -59,9 +59,11 @@
     return high, (values - high.astype(F32)).astype(BF16)
 
 
-def spectra_kernel(count, gain_ref, *refs):
-    frames = refs[: count + TAPS - 1]
-    taps_ref, stage_ref, turn_ref, last_ref, out_ref, coeff_ref, high_ref, low_ref, zhigh_ref, zlow_ref, held_ref = refs[count + TAPS - 1 :]
+def spectra_kernel(count, partners, gain_ref, *refs):
+    frames, refs = refs[: count + TAPS - 1], refs[count + TAPS - 1 :]
+    (taps_ref, stage_ref, turn_ref, last_ref), refs = refs[:4], refs[4:]
+    out_refs = refs[: max(partners, 1)]
+    coeff_ref, high_ref, low_ref, zhigh_ref, zlow_ref, held_ref = refs[len(out_refs) :]
     step = pl.program_id(0)
     wide = 2 * AVG
     size = GROUP * wide
@@ -129,11 +131,19 @@
             first_group(g - 1)
         if g >= 2:
             last_group(g - 2)
-    for row in range(outs):
-        out_ref[row] = held_ref[pl.ds(row, ROWS, stride=outs), :].astype(BF16)
-
-
-def spectra(voltages, taps, station_gain, consts, start, count):
+    if partners:
+        me = lax.axis_index("ingest")
+        each = outs // partners
+        for k in range(partners):
+            target = jnp.bitwise_xor(me, k) * each
+            for q in range(each):
+                out_refs[k][q] = held_ref[pl.ds(target + q, ROWS, stride=outs), :].astype(BF16)
+    else:
+        for row in range(outs):
+            out_refs[0][row] = held_ref[pl.ds(row, ROWS, stride=outs), :].astype(BF16)
+
+
+def spectra(voltages, taps, station_gain, consts, start, count, partners=0):
     streams = voltages.shape[0]
     stage, turn, last = consts
     outs = last.shape[0] // 2
@@ -145,14 +155,15 @@
         for j in range(count + TAPS - 1)
     ]
     whole = lambda shape: pl.BlockSpec(shape, lambda a: (0,) * len(shape))
+    pieces = max(partners, 1)
     return pl.pallas_call(
-        functools.partial(spectra_kernel, count),
-        out_shape=jax.ShapeDtypeStruct((outs, streams, width), BF16),
+        functools.partial(spectra_kernel, count, partners),
+        out_shape=[jax.ShapeDtypeStruct((outs // pieces, streams, width), BF16)] * pieces,
         grid=(streams // ROWS,),
         in_specs=[pl.BlockSpec(memory_space=pltpu.SMEM)]
         + frame_spec
         + [whole(taps.shape), whole(stage.shape), whole(turn.shape), whole(last.shape)],
-        out_specs=pl.BlockSpec((outs, ROWS, width), lambda a: (0, a, 0)),
+        out_specs=[pl.BlockSpec((outs // pieces, ROWS, width), lambda a: (0, a, 0))] * pieces,
         scratch_shapes=[
             pltpu.VMEM((TAPS, wide, LANES), F32),
             pltpu.VMEM((groups, GROUP * wide, count * LANES), BF16),
@@ -179,9 +190,10 @@
     return total
 
 
-def arrange_kernel(pick_ref, part_ref, out_ref, power_ref):
+def arrange_kernel(pick_ref, *refs):
+    part_refs, (out_ref, power_ref) = refs[:-2], refs[-2:]
     rows = 2 * STATIONS
-    pieces = [part_ref[:, ri].reshape(rows, LANES) for ri in range(2)]
+    pieces = [jnp.concatenate([part_ref[ri] for part_ref in part_refs], axis=0) for ri in range(2)]
     power_ref[0] = squares(pieces)
     data = jnp.concatenate(pieces, axis=1)
     for r in range(0, rows, 2 * LANES):
@@ -189,8 +201,8 @@
         out_ref[0, own, :] = jnp.dot(pick_ref[own, :], data, preferred_element_type=F32).astype(BF16)
 
 
-def arrange(pick, part):
-    devices, _, own, width = part.shape
+def arrange(pick, parts):
+    _, own, width = parts[0].shape
     rows = 2 * STATIONS
     return pl.pallas_call(
         arrange_kernel,
@@ -201,8 +213,8 @@
         grid=(OUT_DEV,),
         in_specs=[
             pl.BlockSpec(pick.shape, lambda o: (0, 0)),
-            pl.BlockSpec((devices, 2, own, width), lambda o: (0, o, 0, 0)),
-        ],
+        ]
+        + [pl.BlockSpec((2, own, width), lambda o: (o, 0, 0))] * len(parts),
         out_specs=(
             pl.BlockSpec((1, rows, 2 * width), lambda o: (o, 0, 0)),
             pl.BlockSpec((1, 8, LANES), lambda o: (o, 0, 0)),
@@ -210,7 +222,7 @@
         compiler_params=pltpu.CompilerParams(vmem_limit_bytes=40 * 2**20),
         cost_estimate=pl.CostEstimate(flops=1_100_000_000, bytes_accessed=4_000_000, transcendentals=0),
         name="arrange",
-    )(pick, part)
+    )(pick, *parts)
 
 
 def turned(values):
@@ -288,15 +300,20 @@
     samples = voltages.reshape(streams, 2, frames * blocks, LANES).transpose(0, 2, 1, 3)
     samples = samples.reshape(streams, frames, 2 * blocks, LANES)
     coeffs = taps.reshape(TAPS, blocks, LANES).transpose(1, 0, 2).reshape(TAPS * blocks, LANES)
-    parts = []
-    for start, count in CHUNKS:
-        packed = spectra(samples, coeffs, station_gain, consts, start, count)
-        packed = packed.reshape(devices, 2 * OUT_DEV, streams, count * AVG)
-        parts.append(lax.all_to_all(packed, "ingest", split_axis=0, concat_axis=0, tiled=True))
+    (start, count), (later, rest) = CHUNKS
+    sent = spectra(samples, coeffs, station_gain, consts, start, count, devices)
+    early = [sent[0]] + [
+        lax.ppermute(sent[k], "ingest", [(i, i ^ k) for i in range(devices)]) for k in range(1, devices)
+    ]
+    packed = spectra(samples, coeffs, station_gain, consts, later, rest)[0]
+    packed = packed.reshape(devices, 2 * OUT_DEV, streams, rest * AVG)
+    late = lax.all_to_all(packed, "ingest", split_axis=0, concat_axis=0, tiled=True)
     wanted = (2 * station_order[:, None] + jnp.arange(2, dtype=jnp.int32)).reshape(-1, 1)
-    pick = (wanted == jnp.arange(2 * STATIONS, dtype=jnp.int32)).astype(BF16)
-    early, power = arrange(pick, parts[0])
-    return tiles(pick, parts[1], early, power)
+    column = jnp.arange(2 * STATIONS, dtype=jnp.int32)
+    pick = (wanted == column).astype(BF16)
+    mixed = (wanted == jnp.bitwise_xor(column, lax.axis_index("ingest") * streams)).astype(BF16)
+    held, power = arrange(mixed, early)
+    return tiles(pick, late, held, power)
 
 
 def solution(mesh):

time: 83.4 us -> 80.4 us (0.964)
  waiting for transfers between devices: 32.6 us -> 12.8 us
  starting transfers between devices: 11.6 us -> 28.4 us
    all_to_all x2 -> x1, waiting for transfers between devices: 32.6 us -> 0.01 us  [body(): lax.all_to_all(packed, 'ingest', split_axis=0, concat_axis=0, tiled=True)]
    ppermute x0 -> x15, starting transfers between devices: none -> 21.8 us  [body(): lax.ppermute(sent[k], 'ingest', [(i, i ^ k) for i in range(devices)])]
    ppermute x0 -> x15, waiting for transfers between devices: none -> 12.8 us  [body(): lax.ppermute(sent[k], 'ingest', [(i, i ^ k) for i in range(devices)])]
    all_to_all x2 -> x1, starting transfers between devices: 11.6 us -> 6.62 us  [body(): lax.all_to_all(packed, 'ingest', split_axis=0, concat_axis=0, tiled=True)]
    pallas_call x1, Pallas kernels: 6.64 us -> 5.71 us  [tiles(): pl.pallas_call(tiles_kernel, out_shape=jax.ShapeDtypeStruct((OUT_DEV, pai...]
    unnamed x6 -> x8, local copies, waits for them, and re-layouts: 2.25 us -> 2.22 us
  transfers between devices with their start and end apart: 2 -> 16, of which waited for: 2 -> 8; matrix products, arithmetic and copies ran while one was open for 1% -> 1% of each run, Pallas kernels for 19% -> 20%
where the time goes in v2:
time: 80.4 us; the launch traced here: 80.2 us
  Pallas kernels  35.6 us (44%)
  starting transfers between devices  28.4 us (35%)
  waiting for transfers between devices  12.8 us (16%)
  local copies, waits for them, and re-layouts  2.39 us (3%)
  other arithmetic  0.88 us (1%)
    pallas_call x2, Pallas kernels, spectra(): pl.pallas_call(functools.partial(spectra_kernel, count, partners), out_sh...  28.5 us
    ppermute x15, starting transfers between devices, body(): lax.ppermute(sent[k], 'ingest', [(i, i ^ k) for i in range(devices)])  21.8 us
    ppermute x15, waiting for transfers between devices, body(): lax.ppermute(sent[k], 'ingest', [(i, i ^ k) for i in range(devices)])  12.8 us
    all_to_all x1, starting transfers between devices, body(): lax.all_to_all(packed, 'ingest', split_axis=0, concat_axis=0, tiled=True)  6.62 us
    pallas_call x1, Pallas kernels, tiles(): pl.pallas_call(tiles_kernel, out_shape=jax.ShapeDtypeStruct((OUT_DEV, pai...  5.71 us
    unnamed x8, local copies, waits for them, and re-layouts  2.22 us
  transfers between devices with their start and end apart: 16, of which 8 were waited for; matrix products, arithmetic and copies ran while one was open for 1% of the time, Pallas kernels for 20%

profile of v2, /device:TPU:11, one launch (start us, length us, event | category | flops | bytes accessed | tf_op | source)
XLA Modules:
  0.0 80.2 jit_solution(258020228530832062)
XLA Ops:
  0.0 13.8 %spectra.2 = bf16[64,64,128]{2,1,0:T(8,128)(2,1)} custom-call(f32[32]{0:T(128)} %gain_ref.3, s32[64,11,64,128]{3,2,1,0:T(8,128)} %bitcast.11, s32[64,11,64,128]{3,2,1,0:T(8,128)} %bitcast.12, s32[64,11,64,128]{3,2,1,0:T(8,128)} %bitcast.13, s32[64,11,64,128]{3,2,1,0:T(8,128)} %bitcast.14, s32[64,11,64,128]{3,2,1,0:T(8,128)} %bitcast.15, ...), custom_call_target="tpu_custom_call" | custom-call | flops 3072000000 | bytes 14680064 | tf_op jit(solution)/shard_map/spectra/pallas_call | solution.py:159
  13.8 6.6 %all-to-all-start = ((bf16[16,4,64,128]{3,2,1,0:T(8,128)(2,1)}), bf16[16,4,64,128]{3,2,1,0:T(8,128)(2,1)S(1)}, u32[]{:S(2)}, u32[]{:S(2)}) async-start(bf16[16,4,64,128]{3,2,1,0:T(8,128)(2,1)} %bitcast.25), calls=%async_computation | async-start | bytes 2097152 | tf_op jit(solution)/shard_map/all_to_all | solution.py:310
  20.4 14.7 %spectra.3 = (bf16[4,64,128]{2,1,0:T(8,128)(2,1)}, bf16[4,64,128]{2,1,0:T(8,128)(2,1)}, bf16[4,64,128]{2,1,0:T(8,128)(2,1)}, bf16[4,64,128]{2,1,0:T(8,128)(2,1)}...) custom-call(f32[32]{0:T(128)} %gain_ref.3, ...), custom_call_target="tpu_custom_call" | custom-call | flops 3072000000 | bytes 14680064 | tf_op jit(solution)/shard_map/spectra/pallas_call | solution.py:159
  35.5 1.2 %collective-permute-start.1 = (bf16[4,64,128]{2,1,0:T(8,128)(2,1)}, bf16[4,64,128]{2,1,0:T(8,128)(2,1)S(1)}, u32[]{:S(2)}, u32[]{:S(2)}) collective-permute-start(bf16[4,64,128]{2,1,0:T(8,128)(2,1)} %get-tuple-element.25), channel_id=1, source_target_pairs={{0,2},{1,3},{2,0},{3,1},{4,6},{5,7},{6,4},{7,5},{8,10},{9,11},{10,... | collective-permute-start | bytes 196616 | tf_op jit(solution)/shard_map/ppermute | solution.py:306
  36.7 0.6 collective-permute-start.2
  37.4 1.6 %collective-permute-start.4 = (bf16[4,64,128]{2,1,0:T(8,128)(2,1)}, bf16[4,64,128]{2,1,0:T(8,128)(2,1)S(1)}, u32[]{:S(2)}, u32[]{:S(2)}) collective-permute-start(bf16[4,64,128]{2,1,0:T(8,128)(2,1)} %get-tuple-element.28), channel_id=1, source_target_pairs={{0,5},{1,4},{2,7},{3,6},{4,1},{5,0},{6,3},{7,2},{8,13},{9,12},{10,... | collective-permute-start | bytes 196616 | tf_op jit(solution)/shard_map/ppermute | solution.py:306
  39.4 1.2 %collective-permute-start.5 = (bf16[4,64,128]{2,1,0:T(8,128)(2,1)}, bf16[4,64,128]{2,1,0:T(8,128)(2,1)S(1)}, u32[]{:S(2)}, u32[]{:S(2)}) collective-permute-start(bf16[4,64,128]{2,1,0:T(8,128)(2,1)} %get-tuple-element.29), channel_id=1, source_target_pairs={{0,6},{1,7},{2,4},{3,5},{4,2},{5,3},{6,0},{7,1},{8,14},{9,15},{10,... | collective-permute-start | bytes 196616 | tf_op jit(solution)/shard_map/ppermute | solution.py:306
  40.9 1.2 %collective-permute-start.6 = (bf16[4,64,128]{2,1,0:T(8,128)(2,1)}, bf16[4,64,128]{2,1,0:T(8,128)(2,1)S(1)}, u32[]{:S(2)}, u32[]{:S(2)}) collective-permute-start(bf16[4,64,128]{2,1,0:T(8,128)(2,1)} %get-tuple-element.30), channel_id=1, source_target_pairs={{0,7},{1,6},{2,5},{3,4},{4,3},{5,2},{6,1},{7,0},{8,15},{9,14},{10,... | collective-permute-start | bytes 196616 | tf_op jit(solution)/shard_map/ppermute | solution.py:306
  42.6 3.8 %collective-permute-start.7 = (bf16[4,64,128]{2,1,0:T(8,128)(2,1)}, bf16[4,64,128]{2,1,0:T(8,128)(2,1)S(1)}, u32[]{:S(2)}, u32[]{:S(2)}) collective-permute-start(bf16[4,64,128]{2,1,0:T(8,128)(2,1)} %get-tuple-element.31), channel_id=1, source_target_pairs={{0,8},{1,9},{2,10},{3,11},{4,12},{5,13},{6,14},{7,15},{8,0},{9,1},... | collective-permute-start | bytes 196616 | tf_op jit(solution)/shard_map/ppermute | solution.py:306
  46.4 0.9 %collective-permute-start.8 = (bf16[4,64,128]{2,1,0:T(8,128)(2,1)}, bf16[4,64,128]{2,1,0:T(8,128)(2,1)S(1)}, u32[]{:S(2)}, u32[]{:S(2)}) collective-permute-start(bf16[4,64,128]{2,1,0:T(8,128)(2,1)} %get-tuple-element.32), channel_id=1, source_target_pairs={{0,9},{1,8},{2,11},{3,10},{4,13},{5,12},{6,15},{7,14},{8,1},{9,0},... | collective-permute-start | bytes 196616 | tf_op jit(solution)/shard_map/ppermute | solution.py:306
  47.3 1.4 %collective-permute-start.9 = (bf16[4,64,128]{2,1,0:T(8,128)(2,1)}, bf16[4,64,128]{2,1,0:T(8,128)(2,1)S(1)}, u32[]{:S(2)}, u32[]{:S(2)}) collective-permute-start(bf16[4,64,128]{2,1,0:T(8,128)(2,1)} %get-tuple-element.33), channel_id=1, source_target_pairs={{0,10},{1,11},{2,8},{3,9},{4,14},{5,15},{6,12},{7,13},{8,2},{9,3},... | collective-permute-start | bytes 196616 | tf_op jit(solution)/shard_map/ppermute | solution.py:306
  48.7 2.3 %collective-permute-start.10 = (bf16[4,64,128]{2,1,0:T(8,128)(2,1)}, bf16[4,64,128]{2,1,0:T(8,128)(2,1)S(1)}, u32[]{:S(2)}, u32[]{:S(2)}) collective-permute-start(bf16[4,64,128]{2,1,0:T(8,128)(2,1)} %get-tuple-element.34), channel_id=1, source_target_pairs={{0,11},{1,10},{2,9},{3,8},{4,15},{5,14},{6,13},{7,12},{8,3},{9,2},... | collective-permute-start | bytes 196616 | tf_op jit(solution)/shard_map/ppermute | solution.py:306
  51.0 1.6 %collective-permute-start.12 = (bf16[4,64,128]{2,1,0:T(8,128)(2,1)}, bf16[4,64,128]{2,1,0:T(8,128)(2,1)S(1)}, u32[]{:S(2)}, u32[]{:S(2)}) collective-permute-start(bf16[4,64,128]{2,1,0:T(8,128)(2,1)} %get-tuple-element.36), channel_id=1, source_target_pairs={{0,13},{1,12},{2,15},{3,14},{4,9},{5,8},{6,11},{7,10},{8,5},{9,4},... | collective-permute-start | bytes 196616 | tf_op jit(solution)/shard_map/ppermute | solution.py:306
  52.6 4.8 %collective-permute-start.13 = (bf16[4,64,128]{2,1,0:T(8,128)(2,1)}, bf16[4,64,128]{2,1,0:T(8,128)(2,1)S(1)}, u32[]{:S(2)}, u32[]{:S(2)}) collective-permute-start(bf16[4,64,128]{2,1,0:T(8,128)(2,1)} %get-tuple-element.37), channel_id=1, source_target_pairs={{0,14},{1,15},{2,12},{3,13},{4,10},{5,11},{6,8},{7,9},{8,6},{9,7},... | collective-permute-start | bytes 196616 | tf_op jit(solution)/shard_map/ppermute | solution.py:306
  57.4 1.8 %collective-permute-done.9.refs_10_ = bf16[4,64,128]{2,1,0:T(8,128)(2,1)S(1)} collective-permute-done((bf16[4,64,128]{2,1,0:T(8,128)(2,1)}, bf16[4,64,128]{2,1,0:T(8,128)(2,1)S(1)}, u32[]{:S(2)}, u32[]{:S(2)}) %collective-permute-start.9) | collective-permute-done | bytes 65568 | tf_op jit(solution)/shard_map/ppermute | solution.py:306
  59.7 0.7 compare_convert_fusion
  60.6 2.1 %collective-permute-done.11.refs_12_ = bf16[4,64,128]{2,1,0:T(8,128)(2,1)S(1)} collective-permute-done((bf16[4,64,128]{2,1,0:T(8,128)(2,1)}, bf16[4,64,128]{2,1,0:T(8,128)(2,1)S(1)}, u32[]{:S(2)}, u32[]{:S(2)}) %collective-permute-start.11) | collective-permute-done | bytes 65568 | tf_op jit(solution)/shard_map/ppermute | solution.py:306
  62.6 3.1 %collective-permute-done.12.refs_13_ = bf16[4,64,128]{2,1,0:T(8,128)(2,1)S(1)} collective-permute-done((bf16[4,64,128]{2,1,0:T(8,128)(2,1)}, bf16[4,64,128]{2,1,0:T(8,128)(2,1)S(1)}, u32[]{:S(2)}, u32[]{:S(2)}) %collective-permute-start.12) | collective-permute-done | bytes 65568 | tf_op jit(solution)/shard_map/ppermute | solution.py:306
  65.8 3.6 %collective-permute-done.13.refs_14_ = bf16[4,64,128]{2,1,0:T(8,128)(2,1)S(1)} collective-permute-done((bf16[4,64,128]{2,1,0:T(8,128)(2,1)}, bf16[4,64,128]{2,1,0:T(8,128)(2,1)S(1)}, u32[]{:S(2)}, u32[]{:S(2)}) %collective-permute-start.13) | collective-permute-done | bytes 65568 | tf_op jit(solution)/shard_map/ppermute | solution.py:306
  69.4 1.4 %collective-permute-done.14.refs_15_ = bf16[4,64,128]{2,1,0:T(8,128)(2,1)S(1)} collective-permute-done((bf16[4,64,128]{2,1,0:T(8,128)(2,1)}, bf16[4,64,128]{2,1,0:T(8,128)(2,1)S(1)}, u32[]{:S(2)}, u32[]{:S(2)}) %collective-permute-start.14) | collective-permute-done | bytes 65568 | tf_op jit(solution)/shard_map/ppermute | solution.py:306
  70.8 1.5 %arrange.1 = (bf16[2,1024,256]{2,1,0:T(8,128)(2,1)S(1)}, f32[2,8,128]{2,1,0:T(8,128)S(1)}) custom-call(bf16[1024,1024]{1,0:T(8,128)(2,1)S(1)} %get-tuple-element.41.pick_ref, bf16[4,64,128]{2,1,0:T(8,128)(2,1)S(1)} %copy-done, bf16[4,64,128]{2,1,0:T(8,128)(2,1)S(1)} %collective-permute-done.refs_1_, bf16[4,64,128]{2,1,0:T(8,128)(2,1)S(1)} %collective-permute-done.1.refs_2_, ...), custom_call_target="tpu_custom_call" | custom-call | flops 1100000000 | bytes 4000000 | tf_op jit(solution)/shard_map/arrange/pallas_call | solution.py:207
  72.3 1.0 %copy-done.1 = bf16[2,1024,256]{2,1,0:T(8,128)(2,1)} copy-done((bf16[2,1024,256]{2,1,0:T(8,128)(2,1)}, bf16[2,1024,256]{2,1,0:T(8,128)(2,1)S(1)}, u32[]{:S(2)}) %copy-start.1) | copy-done | bytes 1048600
  73.3 1.2 %copy-done.2 = bf16[2,1024,256]{2,1,0:T(8,128)(2,1)S(1)} copy-done((bf16[2,1024,256]{2,1,0:T(8,128)(2,1)S(1)}, bf16[2,1024,256]{2,1,0:T(8,128)(2,1)}, u32[]{:S(2)}) %copy-start.2) | copy-done | bytes 1048600
  74.5 5.7 %tiles.1 = bf16[2,36,2,128,128]{4,3,2,1,0:T(8,128)(2,1)} custom-call(bf16[1024,1024]{1,0:T(8,128)(2,1)S(1)} %get-tuple-element.42.pick_ref, bf16[16,4,64,128]{3,2,1,0:T(8,128)(2,1)S(1)} %all-to-all-done.part_ref, bf16[2,1024,256]{2,1,0:T(8,128)(2,1)S(1)} %copy-done.2, f32[2,8,128]{2,1,0:T(8,128)S(1)} %get-tuple-element.40.power_ref), custom_call_target="tpu_custom_call" | custom-call | flops 4499999744 | bytes 9000000 | tf_op jit(solution)/shard_map/tiles/pallas_call | solution.py:272
  (25 shorter events, 2.2 us)
Async XLA Ops:
  13.8 59.5 %all-to-all-start = ((bf16[16,4,64,128]{3,2,1,0:T(8,128)(2,1)}), bf16[16,4,64,128]{3,2,1,0:T(8,128)(2,1)S(1)}, u32[]{:S(2)}, u32[]{:S(2)}) async-start(bf16[16,4,64,128]{3,2,1,0:T(8,128)(2,1)} %bitcast.25), calls=%async_computation | async-start | bytes 2097152 | tf_op jit(solution)/shard_map/all_to_all | solution.py:310
  20.4 18.6 %copy-start.3 = (s32[512]{0:T(512)S(1)}, s32[512]{0:T(512)}, u32[]{:S(2)}) copy-start(s32[512]{0:T(512)} %param.10) | copy-start | bytes 6148
  35.1 35.7 %copy-start = (bf16[4,64,128]{2,1,0:T(8,128)(2,1)S(1)}, bf16[4,64,128]{2,1,0:T(8,128)(2,1)}, u32[]{:S(2)}) copy-start(bf16[4,64,128]{2,1,0:T(8,128)(2,1)} %get-tuple-element.23.refs_0_) | copy-start | bytes 196612
  35.1 4.2 %collective-permute-start = (bf16[4,64,128]{2,1,0:T(8,128)(2,1)}, bf16[4,64,128]{2,1,0:T(8,128)(2,1)S(1)}, u32[]{:S(2)}, u32[]{:S(2)}) collective-permute-start(bf16[4,64,128]{2,1,0:T(8,128)(2,1)} %get-tuple-element.24), channel_id=1, source_target_pairs={{0,1},{1,0},{2,3},{3,2},{4,5},{5,4},{6,7},{7,6},{8,9},{9,8},{10,11... | collective-permute-start | bytes 196616 | tf_op jit(solution)/shard_map/ppermute | solution.py:306
  35.5 5.4 %collective-permute-start.1 = (bf16[4,64,128]{2,1,0:T(8,128)(2,1)}, bf16[4,64,128]{2,1,0:T(8,128)(2,1)S(1)}, u32[]{:S(2)}, u32[]{:S(2)}) collective-permute-start(bf16[4,64,128]{2,1,0:T(8,128)(2,1)} %get-tuple-element.25), channel_id=1, source_target_pairs={{0,2},{1,3},{2,0},{3,1},{4,6},{5,7},{6,4},{7,5},{8,10},{9,11},{10,... | collective-permute-start | bytes 196616 | tf_op jit(solution)/shard_map/ppermute | solution.py:306
  36.7 5.8 %collective-permute-start.2 = (bf16[4,64,128]{2,1,0:T(8,128)(2,1)}, bf16[4,64,128]{2,1,0:T(8,128)(2,1)S(1)}, u32[]{:S(2)}, u32[]{:S(2)}) collective-permute-start(bf16[4,64,128]{2,1,0:T(8,128)(2,1)} %get-tuple-element.26), channel_id=1, source_target_pairs={{0,3},{1,2},{2,1},{3,0},{4,7},{5,6},{6,5},{7,4},{8,11},{9,10},{10,... | collective-permute-start | bytes 196616 | tf_op jit(solution)/shard_map/ppermute | solution.py:306
  37.3 9.1 %collective-permute-start.3 = (bf16[4,64,128]{2,1,0:T(8,128)(2,1)}, bf16[4,64,128]{2,1,0:T(8,128)(2,1)S(1)}, u32[]{:S(2)}, u32[]{:S(2)}) collective-permute-start(bf16[4,64,128]{2,1,0:T(8,128)(2,1)} %get-tuple-element.27), channel_id=1, source_target_pairs={{0,4},{1,5},{2,6},{3,7},{4,0},{5,1},{6,2},{7,3},{8,12},{9,13},{10,... | collective-permute-start | bytes 196616 | tf_op jit(solution)/shard_map/ppermute | solution.py:306
  37.4 9.9 %collective-permute-start.4 = (bf16[4,64,128]{2,1,0:T(8,128)(2,1)}, bf16[4,64,128]{2,1,0:T(8,128)(2,1)S(1)}, u32[]{:S(2)}, u32[]{:S(2)}) collective-permute-start(bf16[4,64,128]{2,1,0:T(8,128)(2,1)} %get-tuple-element.28), channel_id=1, source_target_pairs={{0,5},{1,4},{2,7},{3,6},{4,1},{5,0},{6,3},{7,2},{8,13},{9,12},{10,... | collective-permute-start | bytes 196616 | tf_op jit(solution)/shard_map/ppermute | solution.py:306
  39.4 9.3 %collective-permute-start.5 = (bf16[4,64,128]{2,1,0:T(8,128)(2,1)}, bf16[4,64,128]{2,1,0:T(8,128)(2,1)S(1)}, u32[]{:S(2)}, u32[]{:S(2)}) collective-permute-start(bf16[4,64,128]{2,1,0:T(8,128)(2,1)} %get-tuple-element.29), channel_id=1, source_target_pairs={{0,6},{1,7},{2,4},{3,5},{4,2},{5,3},{6,0},{7,1},{8,14},{9,15},{10,... | collective-permute-start | bytes 196616 | tf_op jit(solution)/shard_map/ppermute | solution.py:306
  40.9 10.1 %collective-permute-start.6 = (bf16[4,64,128]{2,1,0:T(8,128)(2,1)}, bf16[4,64,128]{2,1,0:T(8,128)(2,1)S(1)}, u32[]{:S(2)}, u32[]{:S(2)}) collective-permute-start(bf16[4,64,128]{2,1,0:T(8,128)(2,1)} %get-tuple-element.30), channel_id=1, source_target_pairs={{0,7},{1,6},{2,5},{3,4},{4,3},{5,2},{6,1},{7,0},{8,15},{9,14},{10,... | collective-permute-start | bytes 196616 | tf_op jit(solution)/shard_map/ppermute | solution.py:306
  42.6 8.5 %collective-permute-start.7 = (bf16[4,64,128]{2,1,0:T(8,128)(2,1)}, bf16[4,64,128]{2,1,0:T(8,128)(2,1)S(1)}, u32[]{:S(2)}, u32[]{:S(2)}) collective-permute-start(bf16[4,64,128]{2,1,0:T(8,128)(2,1)} %get-tuple-element.31), channel_id=1, source_target_pairs={{0,8},{1,9},{2,10},{3,11},{4,12},{5,13},{6,14},{7,15},{8,0},{9,1},... | collective-permute-start | bytes 196616 | tf_op jit(solution)/shard_map/ppermute | solution.py:306
  46.4 6.2 %collective-permute-start.8 = (bf16[4,64,128]{2,1,0:T(8,128)(2,1)}, bf16[4,64,128]{2,1,0:T(8,128)(2,1)S(1)}, u32[]{:S(2)}, u32[]{:S(2)}) collective-permute-start(bf16[4,64,128]{2,1,0:T(8,128)(2,1)} %get-tuple-element.32), channel_id=1, source_target_pairs={{0,9},{1,8},{2,11},{3,10},{4,13},{5,12},{6,15},{7,14},{8,1},{9,0},... | collective-permute-start | bytes 196616 | tf_op jit(solution)/shard_map/ppermute | solution.py:306
  47.3 11.9 %collective-permute-start.9 = (bf16[4,64,128]{2,1,0:T(8,128)(2,1)}, bf16[4,64,128]{2,1,0:T(8,128)(2,1)S(1)}, u32[]{:S(2)}, u32[]{:S(2)}) collective-permute-start(bf16[4,64,128]{2,1,0:T(8,128)(2,1)} %get-tuple-element.33), channel_id=1, source_target_pairs={{0,10},{1,11},{2,8},{3,9},{4,14},{5,15},{6,12},{7,13},{8,2},{9,3},... | collective-permute-start | bytes 196616 | tf_op jit(solution)/shard_map/ppermute | solution.py:306
  48.7 11.9 %collective-permute-start.10 = (bf16[4,64,128]{2,1,0:T(8,128)(2,1)}, bf16[4,64,128]{2,1,0:T(8,128)(2,1)S(1)}, u32[]{:S(2)}, u32[]{:S(2)}) collective-permute-start(bf16[4,64,128]{2,1,0:T(8,128)(2,1)} %get-tuple-element.34), channel_id=1, source_target_pairs={{0,11},{1,10},{2,9},{3,8},{4,15},{5,14},{6,13},{7,12},{8,3},{9,2},... | collective-permute-start | bytes 196616 | tf_op jit(solution)/shard_map/ppermute | solution.py:306
  51.0 11.6 %collective-permute-start.11 = (bf16[4,64,128]{2,1,0:T(8,128)(2,1)}, bf16[4,64,128]{2,1,0:T(8,128)(2,1)S(1)}, u32[]{:S(2)}, u32[]{:S(2)}) collective-permute-start(bf16[4,64,128]{2,1,0:T(8,128)(2,1)} %get-tuple-element.35), channel_id=1, source_target_pairs={{0,12},{1,13},{2,14},{3,15},{4,8},{5,9},{6,10},{7,11},{8,4},{9,5},... | collective-permute-start | bytes 196616 | tf_op jit(solution)/shard_map/ppermute | solution.py:306
  51.0 14.8 %collective-permute-start.12 = (bf16[4,64,128]{2,1,0:T(8,128)(2,1)}, bf16[4,64,128]{2,1,0:T(8,128)(2,1)S(1)}, u32[]{:S(2)}, u32[]{:S(2)}) collective-permute-start(bf16[4,64,128]{2,1,0:T(8,128)(2,1)} %get-tuple-element.36), channel_id=1, source_target_pairs={{0,13},{1,12},{2,15},{3,14},{4,9},{5,8},{6,11},{7,10},{8,5},{9,4},... | collective-permute-start | bytes 196616 | tf_op jit(solution)/shard_map/ppermute | solution.py:306
  52.6 16.8 %collective-permute-start.13 = (bf16[4,64,128]{2,1,0:T(8,128)(2,1)}, bf16[4,64,128]{2,1,0:T(8,128)(2,1)S(1)}, u32[]{:S(2)}, u32[]{:S(2)}) collective-permute-start(bf16[4,64,128]{2,1,0:T(8,128)(2,1)} %get-tuple-element.37), channel_id=1, source_target_pairs={{0,14},{1,15},{2,12},{3,13},{4,10},{5,11},{6,8},{7,9},{8,6},{9,7},... | collective-permute-start | bytes 196616 | tf_op jit(solution)/shard_map/ppermute | solution.py:306
  59.1 11.6 %collective-permute-start.14 = (bf16[4,64,128]{2,1,0:T(8,128)(2,1)}, bf16[4,64,128]{2,1,0:T(8,128)(2,1)S(1)}, u32[]{:S(2)}, u32[]{:S(2)}) collective-permute-start(bf16[4,64,128]{2,1,0:T(8,128)(2,1)} %get-tuple-element.38), channel_id=1, source_target_pairs={{0,15},{1,14},{2,13},{3,12},{4,11},{5,10},{6,9},{7,8},{8,7},{9,6},... | collective-permute-start | bytes 196616 | tf_op jit(solution)/shard_map/ppermute | solution.py:306
  72.3 1.0 %copy-start.1 = (bf16[2,1024,256]{2,1,0:T(8,128)(2,1)}, bf16[2,1024,256]{2,1,0:T(8,128)(2,1)S(1)}, u32[]{:S(2)}) copy-start(bf16[2,1024,256]{2,1,0:T(8,128)(2,1)S(1)} %get-tuple-element.39.early_ref) | copy-start | bytes 3145732
  73.3 1.2 %copy-start.2 = (bf16[2,1024,256]{2,1,0:T(8,128)(2,1)S(1)}, bf16[2,1024,256]{2,1,0:T(8,128)(2,1)}, u32[]{:S(2)}) copy-start(bf16[2,1024,256]{2,1,0:T(8,128)(2,1)} %copy-done.1) | copy-start | bytes 3145732

commit v3 on v2

--- a/solution.py
+++ b/solution.py
@@ -20,6 +20,8 @@
 LANES = 128
 CHUNKS = ((0, 4), (4, 4))
 GROUP = 4
+FIRST_SENT = 5
+WINDOW = 5
 ROWS = 16
 BF16 = jnp.bfloat16
 F32 = jnp.float32
@@ -219,7 +221,7 @@
             pl.BlockSpec((1, rows, 2 * width), lambda o: (o, 0, 0)),
             pl.BlockSpec((1, 8, LANES), lambda o: (o, 0, 0)),
         ),
-        compiler_params=pltpu.CompilerParams(vmem_limit_bytes=40 * 2**20),
+        compiler_params=pltpu.CompilerParams(vmem_limit_bytes=16 * 2**20),
         cost_estimate=pl.CostEstimate(flops=1_100_000_000, bytes_accessed=4_000_000, transcendentals=0),
         name="arrange",
     )(pick, *parts)
@@ -229,11 +231,12 @@
     return jnp.concatenate([values[:, LANES:], -values[:, :LANES]], axis=1)
 
 
-def tiles_kernel(pick_ref, part_ref, early_ref, power_ref, out_ref, left_ref, right_ref):
+def tiles_kernel(pick_ref, early_ref, power_ref, *refs):
+    part_refs, (out_ref, left_ref, right_ref) = refs[:-3], refs[-3:]
     rows = 2 * STATIONS
     side = 2 * BLOCK
     blocks = STATIONS // BLOCK
-    pieces = [part_ref[:, ri].reshape(rows, LANES) for ri in range(2)]
+    pieces = [jnp.concatenate([part_ref[ri] for part_ref in part_refs], axis=0) for ri in range(2)]
     power = jnp.sum(squares(pieces) + power_ref[0]) / (STATIONS * 2 * SPECTRA * AVG)
     scale = 1.0 / jnp.full((1, LANES), SPECTRA * AVG * power, F32)
     data = jnp.concatenate(pieces, axis=1)
@@ -263,8 +266,8 @@
                     out_ref[0, tile, 1] = scaled[side:]
 
 
-def tiles(pick, part, early, power):
-    devices, _, own, width = part.shape
+def tiles(pick, parts, early, power):
+    _, own, width = parts[0].shape
     blocks = STATIONS // BLOCK
     pairs = blocks * (blocks + 1) // 2
     side = 2 * BLOCK
@@ -275,19 +278,29 @@
         grid=(OUT_DEV,),
         in_specs=[
             pl.BlockSpec(pick.shape, lambda o: (0, 0)),
-            pl.BlockSpec((devices, 2, own, width), lambda o: (0, o, 0, 0)),
             pl.BlockSpec((1, rows, 2 * width), lambda o: (o, 0, 0)),
             pl.BlockSpec((1, 8, LANES), lambda o: (o, 0, 0)),
-        ],
+        ]
+        + [pl.BlockSpec((2, own, width), lambda o: (o, 0, 0))] * len(parts),
         out_specs=pl.BlockSpec((1, pairs, 2, side, side), lambda o: (o, 0, 0, 0, 0)),
         scratch_shapes=[
             pltpu.VMEM((2 * rows, 4 * width), BF16),
             pltpu.VMEM((rows, 4 * width), BF16),
         ],
-        compiler_params=pltpu.CompilerParams(vmem_limit_bytes=40 * 2**20),
+        compiler_params=pltpu.CompilerParams(vmem_limit_bytes=24 * 2**20),
         cost_estimate=pl.CostEstimate(flops=4_500_000_000, bytes_accessed=9_000_000, transcendentals=0),
         name="tiles",
-    )(pick, part, early, power)
+    )(pick, early, power, *parts)
+
+
+def sending_order(devices):
+    far = [(piece, k) for piece in range(2) for k in range(devices // 2, devices)]
+    near = [(piece, k) for piece in range(2) for k in range(1, devices // 2)]
+    order, far = far[:FIRST_SENT], far[FIRST_SENT:]
+    while far or near:
+        order += far[:1] + near[:1]
+        far, near = far[1:], near[1:]
+    return order
 
 
 def body(voltages, taps, station_gain, station_order):
@@ -300,20 +313,21 @@
     samples = voltages.reshape(streams, 2, frames * blocks, LANES).transpose(0, 2, 1, 3)
     samples = samples.reshape(streams, frames, 2 * blocks, LANES)
     coeffs = taps.reshape(TAPS, blocks, LANES).transpose(1, 0, 2).reshape(TAPS * blocks, LANES)
-    (start, count), (later, rest) = CHUNKS
-    sent = spectra(samples, coeffs, station_gain, consts, start, count, devices)
-    early = [sent[0]] + [
-        lax.ppermute(sent[k], "ingest", [(i, i ^ k) for i in range(devices)]) for k in range(1, devices)
-    ]
-    packed = spectra(samples, coeffs, station_gain, consts, later, rest)[0]
-    packed = packed.reshape(devices, 2 * OUT_DEV, streams, rest * AVG)
-    late = lax.all_to_all(packed, "ingest", split_axis=0, concat_axis=0, tiled=True)
+    sent = [spectra(samples, coeffs, station_gain, consts, start, count, devices) for start, count in CHUNKS]
+    held = [{0: pieces[0]} for pieces in sent]
+    order = sending_order(devices)
+    for place, (piece, k) in enumerate(order):
+        ready = sent[piece][k]
+        if place >= WINDOW:
+            before, past = order[place - WINDOW]
+            ready, held[before][past] = lax.optimization_barrier((ready, held[before][past]))
+        held[piece][k] = lax.ppermute(ready, "ingest", [(i, i ^ k) for i in range(devices)])
+    early, late = [[pieces[k] for k in range(devices)] for pieces in held]
     wanted = (2 * station_order[:, None] + jnp.arange(2, dtype=jnp.int32)).reshape(-1, 1)
-    column = jnp.arange(2 * STATIONS, dtype=jnp.int32)
+    column = jnp.bitwise_xor(jnp.arange(2 * STATIONS, dtype=jnp.int32), lax.axis_index("ingest") * streams)
     pick = (wanted == column).astype(BF16)
-    mixed = (wanted == jnp.bitwise_xor(column, lax.axis_index("ingest") * streams)).astype(BF16)
-    held, power = arrange(mixed, early)
-    return tiles(pick, late, held, power)
+    rows, power = arrange(pick, early)
+    return tiles(pick, late, rows, power)
 
 
 def solution(mesh):

time: 80.4 us -> 94.7 us (1.18)
  the two profiles are of different devices: /device:TPU:11 before, /device:TPU:0 now
where the time goes in v3:
time: 94.7 us; the launch traced here: 94.6 us
  starting transfers between devices  42.1 us (44%)
  Pallas kernels  36.4 us (38%)
  waiting for transfers between devices  15 us (16%)
    ppermute x30, starting transfers between devices, body(): lax.ppermute(ready, 'ingest', [(i, i ^ k) for i in range(devices)])  42.1 us
    pallas_call x2, Pallas kernels, spectra(): pl.pallas_call(functools.partial(spectra_kernel, count, partners), out_sh...  29.3 us
    ppermute x30, waiting for transfers between devices, body(): lax.ppermute(ready, 'ingest', [(i, i ^ k) for i in range(devices)])  15 us
    pallas_call x1, Pallas kernels, tiles(): pl.pallas_call(tiles_kernel, out_shape=jax.ShapeDtypeStruct((OUT_DEV, pai...  5.62 us
  transfers between devices with their start and end apart: 30, of which 7 were waited for; matrix products, arithmetic and copies ran while one was open for 1% of the time, Pallas kernels for 17%

profile of v3, /device:TPU:0, one launch (start us, length us, event | category | flops | bytes accessed | tf_op | source)
XLA Modules:
  0.0 94.6 jit_solution(1247080315202449663)
XLA Ops:
  0.0 14.6 %spectra.2 = (bf16[4,64,128]{2,1,0:T(8,128)(2,1)}, bf16[4,64,128]{2,1,0:T(8,128)(2,1)}, bf16[4,64,128]{2,1,0:T(8,128)(2,1)}, bf16[4,64,128]{2,1,0:T(8,128)(2,1)}...) custom-call(f32[32]{0:T(128)} %gain_ref.3, ...), custom_call_target="tpu_custom_call" | custom-call | flops 3072000000 | bytes 14680064 | tf_op jit(solution)/shard_map/spectra/pallas_call | solution.py:161
  14.6 3.5 %collective-permute-start = (bf16[4,64,128]{2,1,0:T(8,128)(2,1)}, bf16[4,64,128]{2,1,0:T(8,128)(2,1)S(1)}, u32[]{:S(2)}, u32[]{:S(2)}) collective-permute-start(bf16[4,64,128]{2,1,0:T(8,128)(2,1)} %get-tuple-element.92), channel_id=1, source_target_pairs={{0,9},{1,8},{2,11},{3,10},{4,13},{5,12},{6,15},{7,14},{8,1},{9,0},... | collective-permute-start | bytes 196616 | tf_op jit(solution)/shard_map/ppermute | solution.py:324
  18.1 1.6 %collective-permute-start.2 = (bf16[4,64,128]{2,1,0:T(8,128)(2,1)}, bf16[4,64,128]{2,1,0:T(8,128)(2,1)S(1)}, u32[]{:S(2)}, u32[]{:S(2)}) collective-permute-start(bf16[4,64,128]{2,1,0:T(8,128)(2,1)} %get-tuple-element.97), channel_id=1, source_target_pairs={{0,11},{1,10},{2,9},{3,8},{4,15},{5,14},{6,13},{7,12},{8,3},{9,2},... | collective-permute-start | bytes 196616 | tf_op jit(solution)/shard_map/ppermute | solution.py:324
  19.7 2.6 %collective-permute-start.4 = (bf16[4,64,128]{2,1,0:T(8,128)(2,1)}, bf16[4,64,128]{2,1,0:T(8,128)(2,1)S(1)}, u32[]{:S(2)}, u32[]{:S(2)}) collective-permute-start(bf16[4,64,128]{2,1,0:T(8,128)(2,1)} %get-tuple-element.103), channel_id=1, source_target_pairs={{0,8},{1,9},{2,10},{3,11},{4,12},{5,13},{6,14},{7,15},{8,0},{9,1},... | collective-permute-start | bytes 196616 | tf_op jit(solution)/shard_map/ppermute | solution.py:324
  22.4 3.9 %collective-permute-start.10 = (bf16[4,64,128]{2,1,0:T(8,128)(2,1)}, bf16[4,64,128]{2,1,0:T(8,128)(2,1)S(1)}, u32[]{:S(2)}, u32[]{:S(2)}) collective-permute-start(bf16[4,64,128]{2,1,0:T(8,128)(2,1)} %get-tuple-element.117), channel_id=1, source_target_pairs={{0,12},{1,13},{2,14},{3,15},{4,8},{5,9},{6,10},{7,11},{8,4},{9,5},... | collective-permute-start | bytes 196616 | tf_op jit(solution)/shard_map/ppermute | solution.py:324
  26.3 14.7 %spectra.3 = (bf16[4,64,128]{2,1,0:T(8,128)(2,1)}, bf16[4,64,128]{2,1,0:T(8,128)(2,1)}, bf16[4,64,128]{2,1,0:T(8,128)(2,1)}, bf16[4,64,128]{2,1,0:T(8,128)(2,1)}...) custom-call(f32[32]{0:T(128)} %gain_ref.3, ...), custom_call_target="tpu_custom_call" | custom-call | flops 3072000000 | bytes 14680064 | tf_op jit(solution)/shard_map/spectra/pallas_call | solution.py:161
  41.2 1.6 %collective-permute-start.3 = (bf16[4,64,128]{2,1,0:T(8,128)(2,1)S(1)}, bf16[4,64,128]{2,1,0:T(8,128)(2,1)S(1)}, u32[]{:S(2)}, u32[]{:S(2)}) collective-permute-start(bf16[4,64,128]{2,1,0:T(8,128)(2,1)S(1)} %copy-done.11), channel_id=1, source_target_pairs={{0,2},{1,3},{2,0},{3,1},{4,6},{5,7},{6,4},{7,5},{8,10},{9,11},{10,... | collective-permute-start | bytes 196616 | tf_op jit(solution)/shard_map/ppermute | solution.py:324
  42.8 3.5 %collective-permute-start.8 = (bf16[4,64,128]{2,1,0:T(8,128)(2,1)S(1)}, bf16[4,64,128]{2,1,0:T(8,128)(2,1)S(1)}, u32[]{:S(2)}, u32[]{:S(2)}) collective-permute-start(bf16[4,64,128]{2,1,0:T(8,128)(2,1)S(1)} %copy-done.9), channel_id=1, source_target_pairs={{0,14},{1,15},{2,12},{3,13},{4,10},{5,11},{6,8},{7,9},{8,6},{9,7},... | collective-permute-start | bytes 196616 | tf_op jit(solution)/shard_map/ppermute | solution.py:324
  47.3 2.8 %collective-permute-start.15 = (bf16[4,64,128]{2,1,0:T(8,128)(2,1)}, bf16[4,64,128]{2,1,0:T(8,128)(2,1)S(1)}, u32[]{:S(2)}, u32[]{:S(2)}) collective-permute-start(bf16[4,64,128]{2,1,0:T(8,128)(2,1)} %get-tuple-element.128), channel_id=1, source_target_pairs={{0,9},{1,8},{2,11},{3,10},{4,13},{5,12},{6,15},{7,14},{8,1},{9,0},... | collective-permute-start | bytes 196616 | tf_op jit(solution)/shard_map/ppermute | solution.py:324
  51.8 1.5 %collective-permute-done.11.refs_15_ = bf16[4,64,128]{2,1,0:T(8,128)(2,1)S(1)} collective-permute-done((bf16[4,64,128]{2,1,0:T(8,128)(2,1)S(1)}, bf16[4,64,128]{2,1,0:T(8,128)(2,1)S(1)}, u32[]{:S(2)}, u32[]{:S(2)}) %collective-permute-start.11) | collective-permute-done | bytes 65568 | tf_op jit(solution)/shard_map/ppermute | solution.py:324
  53.6 4.1 %collective-permute-done.13.refs_8_ = bf16[4,64,128]{2,1,0:T(8,128)(2,1)S(1)} collective-permute-done((bf16[4,64,128]{2,1,0:T(8,128)(2,1)}, bf16[4,64,128]{2,1,0:T(8,128)(2,1)S(1)}, u32[]{:S(2)}, u32[]{:S(2)}) %collective-permute-start.13) | collective-permute-done | bytes 65568 | tf_op jit(solution)/shard_map/ppermute | solution.py:324
  59.6 1.6 %collective-permute-start.17 = (bf16[4,64,128]{2,1,0:T(8,128)(2,1)}, bf16[4,64,128]{2,1,0:T(8,128)(2,1)S(1)}, u32[]{:S(2)}, u32[]{:S(2)}) collective-permute-start(bf16[4,64,128]{2,1,0:T(8,128)(2,1)} %get-tuple-element.144), channel_id=1, source_target_pairs={{0,10},{1,11},{2,8},{3,9},{4,14},{5,15},{6,12},{7,13},{8,2},{9,3},... | collective-permute-start | bytes 196616 | tf_op jit(solution)/shard_map/ppermute | solution.py:324
  61.2 2.8 %collective-permute-start.19 = (bf16[4,64,128]{2,1,0:T(8,128)(2,1)}, bf16[4,64,128]{2,1,0:T(8,128)(2,1)S(1)}, u32[]{:S(2)}, u32[]{:S(2)}) collective-permute-start(bf16[4,64,128]{2,1,0:T(8,128)(2,1)} %get-tuple-element.149), channel_id=1, source_target_pairs={{0,11},{1,10},{2,9},{3,8},{4,15},{5,14},{6,13},{7,12},{8,3},{9,2},... | collective-permute-start | bytes 196616 | tf_op jit(solution)/shard_map/ppermute | solution.py:324
  63.9 1.5 %collective-permute-start.21 = (bf16[4,64,128]{2,1,0:T(8,128)(2,1)}, bf16[4,64,128]{2,1,0:T(8,128)(2,1)S(1)}, u32[]{:S(2)}, u32[]{:S(2)}) collective-permute-start(bf16[4,64,128]{2,1,0:T(8,128)(2,1)} %get-tuple-element.154), channel_id=1, source_target_pairs={{0,12},{1,13},{2,14},{3,15},{4,8},{5,9},{6,10},{7,11},{8,4},{9,5},... | collective-permute-start | bytes 196616 | tf_op jit(solution)/shard_map/ppermute | solution.py:324
  66.7 1.8 %collective-permute-start.26 = (bf16[4,64,128]{2,1,0:T(8,128)(2,1)}, bf16[4,64,128]{2,1,0:T(8,128)(2,1)S(1)}, u32[]{:S(2)}, u32[]{:S(2)}) collective-permute-start(bf16[4,64,128]{2,1,0:T(8,128)(2,1)} %get-tuple-element.162), channel_id=1, source_target_pairs={{0,14},{1,15},{2,12},{3,13},{4,10},{5,11},{6,8},{7,9},{8,6},{9,7},... | collective-permute-start | bytes 196616 | tf_op jit(solution)/shard_map/ppermute | solution.py:324
  69.7 3.4 %collective-permute-done.19.refs_11_ = bf16[4,64,128]{2,1,0:T(8,128)(2,1)S(1)} collective-permute-done((bf16[4,64,128]{2,1,0:T(8,128)(2,1)}, bf16[4,64,128]{2,1,0:T(8,128)(2,1)S(1)}, u32[]{:S(2)}, u32[]{:S(2)}) %collective-permute-start.19) | collective-permute-done | bytes 65568 | tf_op jit(solution)/shard_map/ppermute | solution.py:324
  73.1 2.6 %collective-permute-start.20 = (bf16[4,64,128]{2,1,0:T(8,128)(2,1)}, bf16[4,64,128]{2,1,0:T(8,128)(2,1)S(1)}, u32[]{:S(2)}, u32[]{:S(2)}) collective-permute-start(bf16[4,64,128]{2,1,0:T(8,128)(2,1)} %get-tuple-element.150), channel_id=1, source_target_pairs={{0,2},{1,3},{2,0},{3,1},{4,6},{5,7},{6,4},{7,5},{8,10},{9,11},{10,... | collective-permute-start | bytes 196616 | tf_op jit(solution)/shard_map/ppermute | solution.py:324
  76.1 1.5 %collective-permute-start.24 = (bf16[4,64,128]{2,1,0:T(8,128)(2,1)}, bf16[4,64,128]{2,1,0:T(8,128)(2,1)S(1)}, u32[]{:S(2)}, u32[]{:S(2)}) collective-permute-start(bf16[4,64,128]{2,1,0:T(8,128)(2,1)} %get-tuple-element.159), channel_id=1, source_target_pairs={{0,4},{1,5},{2,6},{3,7},{4,0},{5,1},{6,2},{7,3},{8,12},{9,13},{10,... | collective-permute-start | bytes 196616 | tf_op jit(solution)/shard_map/ppermute | solution.py:324
  77.6 1.4 %collective-permute-start.27 = (bf16[4,64,128]{2,1,0:T(8,128)(2,1)}, bf16[4,64,128]{2,1,0:T(8,128)(2,1)S(1)}, u32[]{:S(2)}, u32[]{:S(2)}) collective-permute-start(bf16[4,64,128]{2,1,0:T(8,128)(2,1)} %get-tuple-element.163), channel_id=1, source_target_pairs={{0,6},{1,7},{2,4},{3,5},{4,2},{5,3},{6,0},{7,1},{8,14},{9,15},{10,... | collective-permute-start | bytes 196616 | tf_op jit(solution)/shard_map/ppermute | solution.py:324
  79.1 2.1 %collective-permute-start.29 = (bf16[4,64,128]{2,1,0:T(8,128)(2,1)}, bf16[4,64,128]{2,1,0:T(8,128)(2,1)S(1)}, u32[]{:S(2)}, u32[]{:S(2)}) collective-permute-start(bf16[4,64,128]{2,1,0:T(8,128)(2,1)} %get-tuple-element.172), channel_id=1, source_target_pairs={{0,15},{1,14},{2,13},{3,12},{4,11},{5,10},{6,9},{7,8},{8,7},{9,6},... | collective-permute-start | bytes 196616 | tf_op jit(solution)/shard_map/ppermute | solution.py:324
  81.2 2.3 %collective-permute-start.28 = (bf16[4,64,128]{2,1,0:T(8,128)(2,1)}, bf16[4,64,128]{2,1,0:T(8,128)(2,1)S(1)}, u32[]{:S(2)}, u32[]{:S(2)}) collective-permute-start(bf16[4,64,128]{2,1,0:T(8,128)(2,1)} %get-tuple-element.164), channel_id=1, source_target_pairs={{0,7},{1,6},{2,5},{3,4},{4,3},{5,2},{6,1},{7,0},{8,15},{9,14},{10,... | collective-permute-start | bytes 196616 | tf_op jit(solution)/shard_map/ppermute | solution.py:324
  83.4 1.5 %arrange.1 = (bf16[2,1024,256]{2,1,0:T(8,128)(2,1)S(1)}, f32[2,8,128]{2,1,0:T(8,128)S(1)}) custom-call(bf16[1024,1024]{1,0:T(8,128)(2,1)S(1)} %compare_convert_fusion.pick_ref, bf16[4,64,128]{2,1,0:T(8,128)(2,1)S(1)} %copy-done.1, bf16[4,64,128]{2,1,0:T(8,128)(2,1)S(1)} %collective-permute-done.1.refs_1_, ...), custom_call_target="tpu_custom_call" | custom-call | flops 1100000000 | bytes 4000000 | tf_op jit(solution)/shard_map/arrange/pallas_call | solution.py:209
  86.2 2.7 %collective-permute-done.28.refs_7_ = bf16[4,64,128]{2,1,0:T(8,128)(2,1)S(1)} collective-permute-done((bf16[4,64,128]{2,1,0:T(8,128)(2,1)}, bf16[4,64,128]{2,1,0:T(8,128)(2,1)S(1)}, u32[]{:S(2)}, u32[]{:S(2)}) %collective-permute-start.28) | collective-permute-done | bytes 65568 | tf_op jit(solution)/shard_map/ppermute | solution.py:324
  88.9 5.6 %tiles.1 = bf16[2,36,2,128,128]{4,3,2,1,0:T(8,128)(2,1)} custom-call(bf16[1024,1024]{1,0:T(8,128)(2,1)S(1)} %compare_convert_fusion.pick_ref, bf16[2,1024,256]{2,1,0:T(8,128)(2,1)S(1)} %get-tuple-element.139.early_ref, f32[2,8,128]{2,1,0:T(8,128)S(1)} %get-tuple-element.140.power_ref, bf16[4,64,128]{2,1,0:T(8,128)(2,1)S(1)} %copy-done, ...), custom_call_target="tpu_custom_call" | custom-call | flops 4499999744 | bytes 9000000 | tf_op jit(solution)/shard_map/tiles/pallas_call | solution.py:275
  (71 shorter events, 9.1 us)
Async XLA Ops:
  14.6 26.5 %collective-permute-start = (bf16[4,64,128]{2,1,0:T(8,128)(2,1)}, bf16[4,64,128]{2,1,0:T(8,128)(2,1)S(1)}, u32[]{:S(2)}, u32[]{:S(2)}) collective-permute-start(bf16[4,64,128]{2,1,0:T(8,128)(2,1)} %get-tuple-element.92), channel_id=1, source_target_pairs={{0,9},{1,8},{2,11},{3,10},{4,13},{5,12},{6,15},{7,14},{8,1},{9,0},... | collective-permute-start | bytes 196616 | tf_op jit(solution)/shard_map/ppermute | solution.py:324
  18.1 23.0 %collective-permute-start.2 = (bf16[4,64,128]{2,1,0:T(8,128)(2,1)}, bf16[4,64,128]{2,1,0:T(8,128)(2,1)S(1)}, u32[]{:S(2)}, u32[]{:S(2)}) collective-permute-start(bf16[4,64,128]{2,1,0:T(8,128)(2,1)} %get-tuple-element.97), channel_id=1, source_target_pairs={{0,11},{1,10},{2,9},{3,8},{4,15},{5,14},{6,13},{7,12},{8,3},{9,2},... | collective-permute-start | bytes 196616 | tf_op jit(solution)/shard_map/ppermute | solution.py:324
  19.7 23.1 %collective-permute-start.4 = (bf16[4,64,128]{2,1,0:T(8,128)(2,1)}, bf16[4,64,128]{2,1,0:T(8,128)(2,1)S(1)}, u32[]{:S(2)}, u32[]{:S(2)}) collective-permute-start(bf16[4,64,128]{2,1,0:T(8,128)(2,1)} %get-tuple-element.103), channel_id=1, source_target_pairs={{0,8},{1,9},{2,10},{3,11},{4,12},{5,13},{6,14},{7,15},{8,0},{9,1},... | collective-permute-start | bytes 196616 | tf_op jit(solution)/shard_map/ppermute | solution.py:324
  22.3 20.5 %collective-permute-start.7 = (bf16[4,64,128]{2,1,0:T(8,128)(2,1)}, bf16[4,64,128]{2,1,0:T(8,128)(2,1)S(1)}, u32[]{:S(2)}, u32[]{:S(2)}) collective-permute-start(bf16[4,64,128]{2,1,0:T(8,128)(2,1)} %get-tuple-element.110), channel_id=1, source_target_pairs={{0,10},{1,11},{2,8},{3,9},{4,14},{5,15},{6,12},{7,13},{8,2},{9,3},... | collective-permute-start | bytes 196616 | tf_op jit(solution)/shard_map/ppermute | solution.py:324
  22.4 23.9 %collective-permute-start.10 = (bf16[4,64,128]{2,1,0:T(8,128)(2,1)}, bf16[4,64,128]{2,1,0:T(8,128)(2,1)S(1)}, u32[]{:S(2)}, u32[]{:S(2)}) collective-permute-start(bf16[4,64,128]{2,1,0:T(8,128)(2,1)} %get-tuple-element.117), channel_id=1, source_target_pairs={{0,12},{1,13},{2,14},{3,15},{4,8},{5,9},{6,10},{7,11},{8,4},{9,5},... | collective-permute-start | bytes 196616 | tf_op jit(solution)/shard_map/ppermute | solution.py:324
  42.8 7.3 %collective-permute-start.5 = (bf16[4,64,128]{2,1,0:T(8,128)(2,1)S(1)}, bf16[4,64,128]{2,1,0:T(8,128)(2,1)S(1)}, u32[]{:S(2)}, u32[]{:S(2)}) collective-permute-start(bf16[4,64,128]{2,1,0:T(8,128)(2,1)S(1)} %copy-done.10), channel_id=1, source_target_pairs={{0,13},{1,12},{2,15},{3,14},{4,9},{5,8},{6,11},{7,10},{8,5},{9,4},... | collective-permute-start | bytes 196616 | tf_op jit(solution)/shard_map/ppermute | solution.py:324
  42.8 7.8 %collective-permute-start.8 = (bf16[4,64,128]{2,1,0:T(8,128)(2,1)S(1)}, bf16[4,64,128]{2,1,0:T(8,128)(2,1)S(1)}, u32[]{:S(2)}, u32[]{:S(2)}) collective-permute-start(bf16[4,64,128]{2,1,0:T(8,128)(2,1)S(1)} %copy-done.9), channel_id=1, source_target_pairs={{0,14},{1,15},{2,12},{3,13},{4,10},{5,11},{6,8},{7,9},{8,6},{9,7},... | collective-permute-start | bytes 196616 | tf_op jit(solution)/shard_map/ppermute | solution.py:324
  47.2 10.5 %collective-permute-start.13 = (bf16[4,64,128]{2,1,0:T(8,128)(2,1)}, bf16[4,64,128]{2,1,0:T(8,128)(2,1)S(1)}, u32[]{:S(2)}, u32[]{:S(2)}) collective-permute-start(bf16[4,64,128]{2,1,0:T(8,128)(2,1)} %get-tuple-element.123), channel_id=1, source_target_pairs={{0,8},{1,9},{2,10},{3,11},{4,12},{5,13},{6,14},{7,15},{8,0},{9,1},... | collective-permute-start | bytes 196616 | tf_op jit(solution)/shard_map/ppermute | solution.py:324
  47.3 11.4 %collective-permute-start.15 = (bf16[4,64,128]{2,1,0:T(8,128)(2,1)}, bf16[4,64,128]{2,1,0:T(8,128)(2,1)S(1)}, u32[]{:S(2)}, u32[]{:S(2)}) collective-permute-start(bf16[4,64,128]{2,1,0:T(8,128)(2,1)} %get-tuple-element.128), channel_id=1, source_target_pairs={{0,9},{1,8},{2,11},{3,10},{4,13},{5,12},{6,15},{7,14},{8,1},{9,0},... | collective-permute-start | bytes 196616 | tf_op jit(solution)/shard_map/ppermute | solution.py:324
  50.1 9.5 %collective-permute-start.6 = (bf16[4,64,128]{2,1,0:T(8,128)(2,1)S(1)}, bf16[4,64,128]{2,1,0:T(8,128)(2,1)S(1)}, u32[]{:S(2)}, u32[]{:S(2)}) collective-permute-start(bf16[4,64,128]{2,1,0:T(8,128)(2,1)S(1)} %copy-done.7), channel_id=1, source_target_pairs={{0,3},{1,2},{2,1},{3,0},{4,7},{5,6},{6,5},{7,4},{8,11},{9,10},{10,... | collective-permute-start | bytes 196616 | tf_op jit(solution)/shard_map/ppermute | solution.py:324
  50.6 10.5 %collective-permute-start.9 = (bf16[4,64,128]{2,1,0:T(8,128)(2,1)S(1)}, bf16[4,64,128]{2,1,0:T(8,128)(2,1)S(1)}, u32[]{:S(2)}, u32[]{:S(2)}) collective-permute-start(bf16[4,64,128]{2,1,0:T(8,128)(2,1)S(1)} %copy-done.6), channel_id=1, source_target_pairs={{0,4},{1,5},{2,6},{3,7},{4,0},{5,1},{6,2},{7,3},{8,12},{9,13},{10,... | collective-permute-start | bytes 196616 | tf_op jit(solution)/shard_map/ppermute | solution.py:324
  53.3 10.6 %collective-permute-start.12 = (bf16[4,64,128]{2,1,0:T(8,128)(2,1)S(1)}, bf16[4,64,128]{2,1,0:T(8,128)(2,1)S(1)}, u32[]{:S(2)}, u32[]{:S(2)}) collective-permute-start(bf16[4,64,128]{2,1,0:T(8,128)(2,1)S(1)} %copy-done.5), channel_id=1, source_target_pairs={{0,5},{1,4},{2,7},{3,6},{4,1},{5,0},{6,3},{7,2},{8,13},{9,12},{10,... | collective-permute-start | bytes 196616 | tf_op jit(solution)/shard_map/ppermute | solution.py:324
  57.7 7.7 %collective-permute-start.14 = (bf16[4,64,128]{2,1,0:T(8,128)(2,1)S(1)}, bf16[4,64,128]{2,1,0:T(8,128)(2,1)S(1)}, u32[]{:S(2)}, u32[]{:S(2)}) collective-permute-start(bf16[4,64,128]{2,1,0:T(8,128)(2,1)S(1)} %copy-done.4), channel_id=1, source_target_pairs={{0,6},{1,7},{2,4},{3,5},{4,2},{5,3},{6,0},{7,1},{8,14},{9,15},{10,... | collective-permute-start | bytes 196616 | tf_op jit(solution)/shard_map/ppermute | solution.py:324
  58.7 8.0 %collective-permute-start.16 = (bf16[4,64,128]{2,1,0:T(8,128)(2,1)S(1)}, bf16[4,64,128]{2,1,0:T(8,128)(2,1)S(1)}, u32[]{:S(2)}, u32[]{:S(2)}) collective-permute-start(bf16[4,64,128]{2,1,0:T(8,128)(2,1)S(1)} %copy-done.3), channel_id=1, source_target_pairs={{0,7},{1,6},{2,5},{3,4},{4,3},{5,2},{6,1},{7,0},{8,15},{9,14},{10,... | collective-permute-start | bytes 196616 | tf_op jit(solution)/shard_map/ppermute | solution.py:324
  59.6 10.0 %collective-permute-start.17 = (bf16[4,64,128]{2,1,0:T(8,128)(2,1)}, bf16[4,64,128]{2,1,0:T(8,128)(2,1)S(1)}, u32[]{:S(2)}, u32[]{:S(2)}) collective-permute-start(bf16[4,64,128]{2,1,0:T(8,128)(2,1)} %get-tuple-element.144), channel_id=1, source_target_pairs={{0,10},{1,11},{2,8},{3,9},{4,14},{5,15},{6,12},{7,13},{8,2},{9,3},... | collective-permute-start | bytes 196616 | tf_op jit(solution)/shard_map/ppermute | solution.py:324
  61.2 11.9 %collective-permute-start.19 = (bf16[4,64,128]{2,1,0:T(8,128)(2,1)}, bf16[4,64,128]{2,1,0:T(8,128)(2,1)S(1)}, u32[]{:S(2)}, u32[]{:S(2)}) collective-permute-start(bf16[4,64,128]{2,1,0:T(8,128)(2,1)} %get-tuple-element.149), channel_id=1, source_target_pairs={{0,11},{1,10},{2,9},{3,8},{4,15},{5,14},{6,13},{7,12},{8,3},{9,2},... | collective-permute-start | bytes 196616 | tf_op jit(solution)/shard_map/ppermute | solution.py:324
  63.9 11.8 %collective-permute-start.21 = (bf16[4,64,128]{2,1,0:T(8,128)(2,1)}, bf16[4,64,128]{2,1,0:T(8,128)(2,1)S(1)}, u32[]{:S(2)}, u32[]{:S(2)}) collective-permute-start(bf16[4,64,128]{2,1,0:T(8,128)(2,1)} %get-tuple-element.154), channel_id=1, source_target_pairs={{0,12},{1,13},{2,14},{3,15},{4,8},{5,9},{6,10},{7,11},{8,4},{9,5},... | collective-permute-start | bytes 196616 | tf_op jit(solution)/shard_map/ppermute | solution.py:324
  65.4 10.7 %collective-permute-start.23 = (bf16[4,64,128]{2,1,0:T(8,128)(2,1)}, bf16[4,64,128]{2,1,0:T(8,128)(2,1)S(1)}, u32[]{:S(2)}, u32[]{:S(2)}) collective-permute-start(bf16[4,64,128]{2,1,0:T(8,128)(2,1)} %get-tuple-element.158), channel_id=1, source_target_pairs={{0,13},{1,12},{2,15},{3,14},{4,9},{5,8},{6,11},{7,10},{8,5},{9,4},... | collective-permute-start | bytes 196616 | tf_op jit(solution)/shard_map/ppermute | solution.py:324
  66.7 11.0 %collective-permute-start.26 = (bf16[4,64,128]{2,1,0:T(8,128)(2,1)}, bf16[4,64,128]{2,1,0:T(8,128)(2,1)S(1)}, u32[]{:S(2)}, u32[]{:S(2)}) collective-permute-start(bf16[4,64,128]{2,1,0:T(8,128)(2,1)} %get-tuple-element.162), channel_id=1, source_target_pairs={{0,14},{1,15},{2,12},{3,13},{4,10},{5,11},{6,8},{7,9},{8,6},{9,7},... | collective-permute-start | bytes 196616 | tf_op jit(solution)/shard_map/ppermute | solution.py:324
  69.5 9.5 %collective-permute-start.18 = (bf16[4,64,128]{2,1,0:T(8,128)(2,1)}, bf16[4,64,128]{2,1,0:T(8,128)(2,1)S(1)}, u32[]{:S(2)}, u32[]{:S(2)}) collective-permute-start(bf16[4,64,128]{2,1,0:T(8,128)(2,1)} %get-tuple-element.145), channel_id=1, source_target_pairs={{0,1},{1,0},{2,3},{3,2},{4,5},{5,4},{6,7},{7,6},{8,9},{9,8},{10,11... | collective-permute-start | bytes 196616 | tf_op jit(solution)/shard_map/ppermute | solution.py:324
  73.1 8.1 %collective-permute-start.20 = (bf16[4,64,128]{2,1,0:T(8,128)(2,1)}, bf16[4,64,128]{2,1,0:T(8,128)(2,1)S(1)}, u32[]{:S(2)}, u32[]{:S(2)}) collective-permute-start(bf16[4,64,128]{2,1,0:T(8,128)(2,1)} %get-tuple-element.150), channel_id=1, source_target_pairs={{0,2},{1,3},{2,0},{3,1},{4,6},{5,7},{6,4},{7,5},{8,10},{9,11},{10,... | collective-permute-start | bytes 196616 | tf_op jit(solution)/shard_map/ppermute | solution.py:324
  76.1 8.8 %collective-permute-start.24 = (bf16[4,64,128]{2,1,0:T(8,128)(2,1)}, bf16[4,64,128]{2,1,0:T(8,128)(2,1)S(1)}, u32[]{:S(2)}, u32[]{:S(2)}) collective-permute-start(bf16[4,64,128]{2,1,0:T(8,128)(2,1)} %get-tuple-element.159), channel_id=1, source_target_pairs={{0,4},{1,5},{2,6},{3,7},{4,0},{5,1},{6,2},{7,3},{8,12},{9,13},{10,... | collective-permute-start | bytes 196616 | tf_op jit(solution)/shard_map/ppermute | solution.py:324
  77.6 7.3 %collective-permute-start.27 = (bf16[4,64,128]{2,1,0:T(8,128)(2,1)}, bf16[4,64,128]{2,1,0:T(8,128)(2,1)S(1)}, u32[]{:S(2)}, u32[]{:S(2)}) collective-permute-start(bf16[4,64,128]{2,1,0:T(8,128)(2,1)} %get-tuple-element.163), channel_id=1, source_target_pairs={{0,6},{1,7},{2,4},{3,5},{4,2},{5,3},{6,0},{7,1},{8,14},{9,15},{10,... | collective-permute-start | bytes 196616 | tf_op jit(solution)/shard_map/ppermute | solution.py:324
  81.2 7.8 %collective-permute-start.28 = (bf16[4,64,128]{2,1,0:T(8,128)(2,1)}, bf16[4,64,128]{2,1,0:T(8,128)(2,1)S(1)}, u32[]{:S(2)}, u32[]{:S(2)}) collective-permute-start(bf16[4,64,128]{2,1,0:T(8,128)(2,1)} %get-tuple-element.164), channel_id=1, source_target_pairs={{0,7},{1,6},{2,5},{3,4},{4,3},{5,2},{6,1},{7,0},{8,15},{9,14},{10,... | collective-permute-start | bytes 196616 | tf_op jit(solution)/shard_map/ppermute | solution.py:324
  (19 other events, 431.9 us)

commit v4 on v3

--- a/solution.py
+++ b/solution.py
@@ -20,7 +20,6 @@
 LANES = 128
 CHUNKS = ((0, 4), (4, 4))
 GROUP = 4
-FIRST_SENT = 5
 WINDOW = 5
 ROWS = 16
 BF16 = jnp.bfloat16
@@ -65,7 +64,9 @@
     frames, refs = refs[: count + TAPS - 1], refs[count + TAPS - 1 :]
     (taps_ref, stage_ref, turn_ref, last_ref), refs = refs[:4], refs[4:]
     out_refs = refs[: max(partners, 1)]
-    coeff_ref, high_ref, low_ref, zhigh_ref, zlow_ref, held_ref = refs[len(out_refs) :]
+    (coeff_ref, held_ref), refs = refs[len(out_refs) : len(out_refs) + 2], refs[len(out_refs) + 2 :]
+    groups = ROWS // GROUP
+    high_refs, low_refs, zhigh_refs, zlow_refs = [refs[i * groups : (i + 1) * groups] for i in range(4)]
     step = pl.program_id(0)
     wide = 2 * AVG
     size = GROUP * wide
@@ -79,60 +80,57 @@
             for ri in range(2):
                 coeff_ref[j, pl.ds(ri, AVG, stride=2), :] = rows
 
-    def filter_group(g):
+    def filter_rows(g, u, r):
+        rows = slice(r, r + 16)
+        coeffs = [coeff_ref[j, rows, :] for j in range(TAPS)]
+        samples = [ref[g * GROUP + u, 0, rows, :].astype(F32) for ref in frames]
+        for m in range(count):
+            value = coeffs[0] * samples[m]
+            for j in range(1, TAPS):
+                value = value + coeffs[j] * samples[m + j]
+            high, low = halves(value)
+            place = (slice(u * wide + r, u * wide + r + 16), slice(m * LANES, (m + 1) * LANES))
+            high_refs[g][place] = high
+            low_refs[g][place] = low
+
+    def first_part(g, start):
+        lanes = slice(start * LANES, (start + 2) * LANES)
+        both = jnp.dot(stage_ref[...], high_refs[g][:, lanes], preferred_element_type=F32)
+        rest = jnp.dot(stage_ref[:size, :], low_refs[g][:, lanes], preferred_element_type=F32)
+        section = both[:size] + (both[size:] + rest)
         for u in range(GROUP):
-            for r in range(0, wide, 16):
-                rows = slice(r, r + 16)
-                coeffs = [coeff_ref[j, rows, :] for j in range(TAPS)]
-                samples = [ref[g * GROUP + u, 0, rows, :].astype(F32) for ref in frames]
-                for m in range(count):
-                    value = coeffs[0] * samples[m]
-                    for j in range(1, TAPS):
-                        value = value + coeffs[j] * samples[m + j]
-                    high, low = halves(value)
-                    place = (g, slice(u * wide + r, u * wide + r + 16), slice(m * LANES, (m + 1) * LANES))
-                    high_ref[place] = high
-                    low_ref[place] = low
-
-    def first_group(g):
-        for start in range(0, count, 2):
-            lanes = slice(start * LANES, (start + 2) * LANES)
-            both = jnp.dot(stage_ref[...], high_ref[g, :, lanes], preferred_element_type=F32)
-            rest = jnp.dot(stage_ref[:size, :], low_ref[g, :, lanes], preferred_element_type=F32)
-            section = both[:size] + (both[size:] + rest)
-            for u in range(GROUP):
-                for m in range(start, start + 2):
-                    at = slice((m - start) * LANES, (m - start + 1) * LANES)
-                    real = section[u * wide : u * wide + AVG, at]
-                    imag = section[u * wide + AVG : (u + 1) * wide, at]
-                    turn_real, turn_imag = turn_ref[0], turn_ref[1]
-                    row = slice((u * count + m) * AVG, (u * count + m + 1) * AVG)
-                    high, low = halves(real * turn_real - imag * turn_imag)
-                    zhigh_ref[g, row, :LANES] = high
-                    zlow_ref[g, row, :LANES] = low
-                    high, low = halves(real * turn_imag + imag * turn_real)
-                    zhigh_ref[g, row, LANES:] = high
-                    zlow_ref[g, row, LANES:] = low
-
-    def last_group(g):
-        for pair in range(GROUP // 2):
-            rows = slice(pair * 2 * width, (pair + 1) * 2 * width)
-            both = lax.dot_general(last_ref[...], zhigh_ref[g, rows, :], NT, preferred_element_type=F32)
-            rest = lax.dot_general(last_ref[:outs, :], zlow_ref[g, rows, :], NT, preferred_element_type=F32)
-            found = both[:outs] + (both[outs:] + rest)
-            stream = g * GROUP + pair * 2
-            factor = gain_ref[(step * ROWS + stream) // 2] * (1.0 / (64.0 * math.sqrt(NCHAN)))
-            for p in range(2):
-                held_ref[(stream + p) * outs : (stream + p + 1) * outs, :] = found[:, p * width : (p + 1) * width] * factor
-
-    groups = ROWS // GROUP
+            for m in range(start, start + 2):
+                at = slice((m - start) * LANES, (m - start + 1) * LANES)
+                real = section[u * wide : u * wide + AVG, at]
+                imag = section[u * wide + AVG : (u + 1) * wide, at]
+                turn_real, turn_imag = turn_ref[0], turn_ref[1]
+                row = slice((u * count + m) * AVG, (u * count + m + 1) * AVG)
+                high, low = halves(real * turn_real - imag * turn_imag)
+                zhigh_refs[g][row, :LANES] = high
+                zlow_refs[g][row, :LANES] = low
+                high, low = halves(real * turn_imag + imag * turn_real)
+                zhigh_refs[g][row, LANES:] = high
+                zlow_refs[g][row, LANES:] = low
+
+    def last_part(g, pair):
+        rows = slice(pair * 2 * width, (pair + 1) * 2 * width)
+        both = lax.dot_general(last_ref[...], zhigh_refs[g][rows, :], NT, preferred_element_type=F32)
+        rest = lax.dot_general(last_ref[:outs, :], zlow_refs[g][rows, :], NT, preferred_element_type=F32)
+        found = both[:outs] + (both[outs:] + rest)
+        stream = g * GROUP + pair * 2
+        factor = gain_ref[(step * ROWS + stream) // 2] * (1.0 / (64.0 * math.sqrt(NCHAN)))
+        for p in range(2):
+            held_ref[(stream + p) * outs : (stream + p + 1) * outs, :] = found[:, p * width : (p + 1) * width] * factor
+
     for g in range(groups + 2):
-        if g < groups:
-            filter_group(g)
-        if 1 <= g <= groups:
-            first_group(g - 1)
-        if g >= 2:
-            last_group(g - 2)
+        filters = [(g, u, r) for u in range(GROUP) for r in range(0, wide, 16)] if g < groups else []
+        firsts = [(g - 1, start) for start in range(0, count, 2)] if 1 <= g <= groups else []
+        lasts = [(g - 2, pair) for pair in range(GROUP // 2)] if g >= 2 else []
+        while filters or firsts or lasts:
+            for work, jobs, most in ((first_part, firsts, 1), (filter_rows, filters, 4), (last_part, lasts, 1), (filter_rows, filters, 4)):
+                for job in jobs[:most]:
+                    work(*job)
+                del jobs[:most]
     if partners:
         me = lax.axis_index("ingest")
         each = outs // partners
@@ -168,12 +166,10 @@
         out_specs=[pl.BlockSpec((outs // pieces, ROWS, width), lambda a: (0, a, 0))] * pieces,
         scratch_shapes=[
             pltpu.VMEM((TAPS, wide, LANES), F32),
-            pltpu.VMEM((groups, GROUP * wide, count * LANES), BF16),
-            pltpu.VMEM((groups, GROUP * wide, count * LANES), BF16),
-            pltpu.VMEM((groups, GROUP * width, 2 * LANES), BF16),
-            pltpu.VMEM((groups, GROUP * width, 2 * LANES), BF16),
             pltpu.VMEM((ROWS * outs, width), F32),
-        ],
+        ]
+        + [pltpu.VMEM((GROUP * wide, count * LANES), BF16)] * (2 * groups)
+        + [pltpu.VMEM((GROUP * width, 2 * LANES), BF16)] * (2 * groups),
         compiler_params=pltpu.CompilerParams(vmem_limit_bytes=60_000_000),
         cost_estimate=pl.CostEstimate(
             flops=streams * count * 12_000_000,
@@ -192,10 +188,9 @@
     return total
 
 
-def arrange_kernel(pick_ref, *refs):
-    part_refs, (out_ref, power_ref) = refs[:-2], refs[-2:]
+def arrange_kernel(pick_ref, part_ref, out_ref, power_ref):
     rows = 2 * STATIONS
-    pieces = [jnp.concatenate([part_ref[ri] for part_ref in part_refs], axis=0) for ri in range(2)]
+    pieces = [part_ref[:, ri].reshape(rows, LANES) for ri in range(2)]
     power_ref[0] = squares(pieces)
     data = jnp.concatenate(pieces, axis=1)
     for r in range(0, rows, 2 * LANES):
@@ -203,8 +198,8 @@
         out_ref[0, own, :] = jnp.dot(pick_ref[own, :], data, preferred_element_type=F32).astype(BF16)
 
 
-def arrange(pick, parts):
-    _, own, width = parts[0].shape
+def arrange(pick, part):
+    devices, _, own, width = part.shape
     rows = 2 * STATIONS
     return pl.pallas_call(
         arrange_kernel,
@@ -215,8 +210,8 @@
         grid=(OUT_DEV,),
         in_specs=[
             pl.BlockSpec(pick.shape, lambda o: (0, 0)),
-        ]
-        + [pl.BlockSpec((2, own, width), lambda o: (o, 0, 0))] * len(parts),
+            pl.BlockSpec((devices, 2, own, width), lambda o: (0, o, 0, 0)),
+        ],
         out_specs=(
             pl.BlockSpec((1, rows, 2 * width), lambda o: (o, 0, 0)),
             pl.BlockSpec((1, 8, LANES), lambda o: (o, 0, 0)),
@@ -224,7 +219,7 @@
         compiler_params=pltpu.CompilerParams(vmem_limit_bytes=16 * 2**20),
         cost_estimate=pl.CostEstimate(flops=1_100_000_000, bytes_accessed=4_000_000, transcendentals=0),
         name="arrange",
-    )(pick, *parts)
+    )(pick, part)
 
 
 def turned(values):
@@ -294,9 +289,8 @@
 
 
 def sending_order(devices):
-    far = [(piece, k) for piece in range(2) for k in range(devices // 2, devices)]
-    near = [(piece, k) for piece in range(2) for k in range(1, devices // 2)]
-    order, far = far[:FIRST_SENT], far[FIRST_SENT:]
+    far, near = list(range(devices // 2, devices)), list(range(1, devices // 2))
+    order, far = far[:1], far[1:]
     while far or near:
         order += far[:1] + near[:1]
         far, near = far[1:], near[1:]
@@ -313,21 +307,26 @@
     samples = voltages.reshape(streams, 2, frames * blocks, LANES).transpose(0, 2, 1, 3)
     samples = samples.reshape(streams, frames, 2 * blocks, LANES)
     coeffs = taps.reshape(TAPS, blocks, LANES).transpose(1, 0, 2).reshape(TAPS * blocks, LANES)
-    sent = [spectra(samples, coeffs, station_gain, consts, start, count, devices) for start, count in CHUNKS]
-    held = [{0: pieces[0]} for pieces in sent]
+    (start, count), (later, rest) = CHUNKS
+    packed = spectra(samples, coeffs, station_gain, consts, start, count)[0]
+    packed = packed.reshape(devices, 2 * OUT_DEV, streams, count * AVG)
+    packed, station_gain = lax.optimization_barrier((packed, station_gain))
+    early = lax.all_to_all(packed, "ingest", split_axis=0, concat_axis=0, tiled=True)
+    sent = spectra(samples, coeffs, station_gain, consts, later, rest, devices)
+    late = {0: sent[0]}
     order = sending_order(devices)
-    for place, (piece, k) in enumerate(order):
-        ready = sent[piece][k]
+    for place, k in enumerate(order):
+        ready = sent[k]
         if place >= WINDOW:
-            before, past = order[place - WINDOW]
-            ready, held[before][past] = lax.optimization_barrier((ready, held[before][past]))
-        held[piece][k] = lax.ppermute(ready, "ingest", [(i, i ^ k) for i in range(devices)])
-    early, late = [[pieces[k] for k in range(devices)] for pieces in held]
+            past = order[place - WINDOW]
+            ready, late[past] = lax.optimization_barrier((ready, late[past]))
+        late[k] = lax.ppermute(ready, "ingest", [(i, i ^ k) for i in range(devices)])
     wanted = (2 * station_order[:, None] + jnp.arange(2, dtype=jnp.int32)).reshape(-1, 1)
-    column = jnp.bitwise_xor(jnp.arange(2 * STATIONS, dtype=jnp.int32), lax.axis_index("ingest") * streams)
+    column = jnp.arange(2 * STATIONS, dtype=jnp.int32)
     pick = (wanted == column).astype(BF16)
+    mixed = (wanted == jnp.bitwise_xor(column, lax.axis_index("ingest") * streams)).astype(BF16)
     rows, power = arrange(pick, early)
-    return tiles(pick, late, rows, power)
+    return tiles(mixed, [late[k] for k in range(devices)], rows, power)
 
 
 def solution(mesh):

time: 94.7 us -> 90 us (0.950)
  starting transfers between devices: 42.1 us -> 27.7 us
  local copies, waits for them, and re-layouts: 0.22 us -> 9.08 us
  other arithmetic: 0.54 us -> 2.2 us
  waiting for transfers between devices: 15 us -> 13.5 us
    ppermute x30 -> x15, starting transfers between devices: 42.1 us -> 20.3 us  [body(): lax.ppermute(ready, 'ingest', [(i, i ^ k) for i in range(devices)])]
    unnamed x26, local copies, waits for them, and re-layouts: 0.06 us -> 8.92 us
    all_to_all x0 -> x1, starting transfers between devices: none -> 7.41 us  [body(): lax.all_to_all(packed, 'ingest', split_axis=0, concat_axis=0, tiled=True)]
    convert_element_type x1, other arithmetic: 0.4 us -> 2.06 us  [body(): pick = (wanted == column).astype(BF16)]
    ppermute x30 -> x15, waiting for transfers between devices: 15 us -> 13.5 us  [body(): lax.ppermute(ready, 'ingest', [(i, i ^ k) for i in range(devices)])]
  transfers between devices with their start and end apart: 30 -> 16, of which waited for: 7 -> 4; matrix products, arithmetic and copies ran while one was open for 1% -> 3% of each run, Pallas kernels for 17% -> 18%
where the time goes in v4:
time: 90 us; the launch traced here: 89.4 us
  Pallas kernels  36.9 us (41%)
  starting transfers between devices  27.7 us (31%)
  waiting for transfers between devices  13.5 us (15%)
  local copies, waits for them, and re-layouts  9.08 us (10%)
  other arithmetic  2.2 us (2%)
    pallas_call x2, Pallas kernels, spectra(): pl.pallas_call(functools.partial(spectra_kernel, count, partners), out_sh...  28.9 us
    ppermute x15, starting transfers between devices, body(): lax.ppermute(ready, 'ingest', [(i, i ^ k) for i in range(devices)])  20.3 us
    ppermute x15, waiting for transfers between devices, body(): lax.ppermute(ready, 'ingest', [(i, i ^ k) for i in range(devices)])  13.5 us
    unnamed x26, local copies, waits for them, and re-layouts  8.92 us
    all_to_all x1, starting transfers between devices, body(): lax.all_to_all(packed, 'ingest', split_axis=0, concat_axis=0, tiled=True)  7.41 us
    pallas_call x1, Pallas kernels, tiles(): pl.pallas_call(tiles_kernel, out_shape=jax.ShapeDtypeStruct((OUT_DEV, pai...  6.43 us
    convert_element_type x1, other arithmetic, body(): pick = (wanted == column).astype(BF16)  2.06 us
  transfers between devices with their start and end apart: 16, of which 4 were waited for; matrix products, arithmetic and copies ran while one was open for 3% of the time, Pallas kernels for 18%

profile of v4, /device:TPU:0, one launch (start us, length us, event | category | flops | bytes accessed | tf_op | source)
XLA Modules:
  0.0 89.4 jit_solution(764517527492909221)
XLA Ops:
  0.0 14.2 %spectra.2 = bf16[64,64,128]{2,1,0:T(8,128)(2,1)} custom-call(f32[32]{0:T(128)} %gain_ref.2, s32[64,11,64,128]{3,2,1,0:T(8,128)} %bitcast.11, s32[64,11,64,128]{3,2,1,0:T(8,128)} %bitcast.12, s32[64,11,64,128]{3,2,1,0:T(8,128)} %bitcast.13, s32[64,11,64,128]{3,2,1,0:T(8,128)} %bitcast.14, s32[64,11,64,128]{3,2,1,0:T(8,128)} %bitcast.15, ...), custom_call_target="tpu_custom_call" | custom-call | flops 3072000000 | bytes 14680064 | tf_op jit(solution)/shard_map/spectra/pallas_call | solution.py:159
  14.2 7.4 %all-to-all-start = ((bf16[16,4,64,128]{3,2,1,0:T(8,128)(2,1)}), bf16[16,4,64,128]{3,2,1,0:T(8,128)(2,1)S(1)}, u32[]{:S(2)}, u32[]{:S(2)}) async-start(bf16[16,4,64,128]{3,2,1,0:T(8,128)(2,1)} %bitcast.25), calls=%async_computation | async-start | bytes 2097152 | tf_op jit(solution)/shard_map/all_to_all | solution.py:314
  21.6 14.7 %spectra.3 = (bf16[4,64,128]{2,1,0:T(8,128)(2,1)}, bf16[4,64,128]{2,1,0:T(8,128)(2,1)}, bf16[4,64,128]{2,1,0:T(8,128)(2,1)}, bf16[4,64,128]{2,1,0:T(8,128)(2,1)}...) custom-call(f32[32]{0:T(128)} %gain_ref.2, ...), custom_call_target="tpu_custom_call" | custom-call | flops 3072000000 | bytes 14680064 | tf_op jit(solution)/shard_map/spectra/pallas_call | solution.py:159
  36.8 1.7 %collective-permute-start.1 = (bf16[4,64,128]{2,1,0:T(8,128)(2,1)}, bf16[4,64,128]{2,1,0:T(8,128)(2,1)S(1)}, u32[]{:S(2)}, u32[]{:S(2)}) collective-permute-start(bf16[4,64,128]{2,1,0:T(8,128)(2,1)} %get-tuple-element.54), channel_id=1, source_target_pairs={{0,2},{1,3},{2,0},{3,1},{4,6},{5,7},{6,4},{7,5},{8,10},{9,11},{10,... | collective-permute-start | bytes 196616 | tf_op jit(solution)/shard_map/ppermute | solution.py:323
  38.5 2.0 %collective-permute-start.2 = (bf16[4,64,128]{2,1,0:T(8,128)(2,1)}, bf16[4,64,128]{2,1,0:T(8,128)(2,1)S(1)}, u32[]{:S(2)}, u32[]{:S(2)}) collective-permute-start(bf16[4,64,128]{2,1,0:T(8,128)(2,1)} %get-tuple-element.58), channel_id=1, source_target_pairs={{0,9},{1,8},{2,11},{3,10},{4,13},{5,12},{6,15},{7,14},{8,1},{9,0},... | collective-permute-start | bytes 196616 | tf_op jit(solution)/shard_map/ppermute | solution.py:323
  40.8 2.6 %collective-permute-start.6 = (bf16[4,64,128]{2,1,0:T(8,128)(2,1)}, bf16[4,64,128]{2,1,0:T(8,128)(2,1)S(1)}, u32[]{:S(2)}, u32[]{:S(2)}) collective-permute-start(bf16[4,64,128]{2,1,0:T(8,128)(2,1)} %get-tuple-element.68), channel_id=1, source_target_pairs={{0,8},{1,9},{2,10},{3,11},{4,12},{5,13},{6,14},{7,15},{8,0},{9,1},... | collective-permute-start | bytes 196616 | tf_op jit(solution)/shard_map/ppermute | solution.py:323
  43.8 1.5 %collective-permute-start.9 = (bf16[4,64,128]{2,1,0:T(8,128)(2,1)}, bf16[4,64,128]{2,1,0:T(8,128)(2,1)S(1)}, u32[]{:S(2)}, u32[]{:S(2)}) collective-permute-start(bf16[4,64,128]{2,1,0:T(8,128)(2,1)} %get-tuple-element.72), channel_id=1, source_target_pairs={{0,12},{1,13},{2,14},{3,15},{4,8},{5,9},{6,10},{7,11},{8,4},{9,5},... | collective-permute-start | bytes 196616 | tf_op jit(solution)/shard_map/ppermute | solution.py:323
  45.3 1.6 %collective-permute-start.11 = (bf16[4,64,128]{2,1,0:T(8,128)(2,1)}, bf16[4,64,128]{2,1,0:T(8,128)(2,1)S(1)}, u32[]{:S(2)}, u32[]{:S(2)}) collective-permute-start(bf16[4,64,128]{2,1,0:T(8,128)(2,1)} %get-tuple-element.75), channel_id=1, source_target_pairs={{0,13},{1,12},{2,15},{3,14},{4,9},{5,8},{6,11},{7,10},{8,5},{9,4},... | collective-permute-start | bytes 196616 | tf_op jit(solution)/shard_map/ppermute | solution.py:323
  46.9 9.2 %collective-permute-done.2.refs_9_ = bf16[4,64,128]{2,1,0:T(8,128)(2,1)S(1)} collective-permute-done((bf16[4,64,128]{2,1,0:T(8,128)(2,1)}, bf16[4,64,128]{2,1,0:T(8,128)(2,1)S(1)}, u32[]{:S(2)}, u32[]{:S(2)}) %collective-permute-start.2) | collective-permute-done | bytes 65568 | tf_op jit(solution)/shard_map/ppermute | solution.py:323
  56.1 2.2 %collective-permute-start.3 = (bf16[4,64,128]{2,1,0:T(8,128)(2,1)}, bf16[4,64,128]{2,1,0:T(8,128)(2,1)S(1)}, u32[]{:S(2)}, u32[]{:S(2)}) collective-permute-start(bf16[4,64,128]{2,1,0:T(8,128)(2,1)} %get-tuple-element.59), channel_id=1, source_target_pairs={{0,3},{1,2},{2,1},{3,0},{4,7},{5,6},{6,5},{7,4},{8,11},{9,10},{10,... | collective-permute-start | bytes 196616 | tf_op jit(solution)/shard_map/ppermute | solution.py:323
  58.3 1.1 %collective-permute-done.4.refs_10_ = bf16[4,64,128]{2,1,0:T(8,128)(2,1)S(1)} collective-permute-done((bf16[4,64,128]{2,1,0:T(8,128)(2,1)}, bf16[4,64,128]{2,1,0:T(8,128)(2,1)S(1)}, u32[]{:S(2)}, u32[]{:S(2)}) %collective-permute-start.4) | collective-permute-done | bytes 65568 | tf_op jit(solution)/shard_map/ppermute | solution.py:323
  59.9 2.1 %fusion = (bf16[1024,1024]{1,0:T(8,128)(2,1)}, bf16[1024,1024]{1,0:T(8,128)(2,1)S(1)}) fusion(s32[1024]{0:T(1024)S(1)} %add.23, s32[1024]{0:T(1024)S(1)} %iota_xor_fusion), kind=kLoop, calls=%fused_computation.1 | loop fusion | flops 4194304 | bytes 4202496 | tf_op jit(solution)/shard_map/convert_element_type | solution.py:326
  62.6 1.7 %collective-permute-start.10 = (bf16[4,64,128]{2,1,0:T(8,128)(2,1)}, bf16[4,64,128]{2,1,0:T(8,128)(2,1)}, u32[]{:S(2)}, u32[]{:S(2)}) collective-permute-start(bf16[4,64,128]{2,1,0:T(8,128)(2,1)} %get-tuple-element.73), channel_id=1, source_target_pairs={{0,6},{1,7},{2,4},{3,5},{4,2},{5,3},{6,0},{7,1},{8,14},{9,15},{10,... | collective-permute-start | bytes 196616 | tf_op jit(solution)/shard_map/ppermute | solution.py:323
  64.9 2.2 %collective-permute-start.12 = (bf16[4,64,128]{2,1,0:T(8,128)(2,1)}, bf16[4,64,128]{2,1,0:T(8,128)(2,1)}, u32[]{:S(2)}, u32[]{:S(2)}) collective-permute-start(bf16[4,64,128]{2,1,0:T(8,128)(2,1)} %get-tuple-element.76), channel_id=1, source_target_pairs={{0,7},{1,6},{2,5},{3,4},{4,3},{5,2},{6,1},{7,0},{8,15},{9,14},{10,... | collective-permute-start | bytes 196616 | tf_op jit(solution)/shard_map/ppermute | solution.py:323
  67.7 3.3 %collective-permute-start.13 = (bf16[4,64,128]{2,1,0:T(8,128)(2,1)}, bf16[4,64,128]{2,1,0:T(8,128)(2,1)}, u32[]{:S(2)}, u32[]{:S(2)}) collective-permute-start(bf16[4,64,128]{2,1,0:T(8,128)(2,1)} %get-tuple-element.83), channel_id=1, source_target_pairs={{0,14},{1,15},{2,12},{3,13},{4,10},{5,11},{6,8},{7,9},{8,6},{9,7},... | collective-permute-start | bytes 196616 | tf_op jit(solution)/shard_map/ppermute | solution.py:323
  73.0 1.6 %copy-done = bf16[1024,1024]{1,0:T(8,128)(2,1)S(1)} copy-done((bf16[1024,1024]{1,0:T(8,128)(2,1)S(1)}, bf16[1024,1024]{1,0:T(8,128)(2,1)}, u32[]{:S(2)}) %copy-start) | copy-done | bytes 2097176
  74.6 1.6 %arrange.1 = (bf16[2,1024,256]{2,1,0:T(8,128)(2,1)S(1)}, f32[2,8,128]{2,1,0:T(8,128)S(1)}) custom-call(bf16[1024,1024]{1,0:T(8,128)(2,1)S(1)} %copy-done, bf16[16,4,64,128]{3,2,1,0:T(8,128)(2,1)S(1)} %all-to-all-done.part_ref), custom_call_target="tpu_custom_call" | custom-call | flops 1100000000 | bytes 4000000 | tf_op jit(solution)/shard_map/arrange/pallas_call | solution.py:204
  76.2 2.6 %collective-permute-done.14.refs_15_ = bf16[4,64,128]{2,1,0:T(8,128)(2,1)} collective-permute-done((bf16[4,64,128]{2,1,0:T(8,128)(2,1)}, bf16[4,64,128]{2,1,0:T(8,128)(2,1)}, u32[]{:S(2)}, u32[]{:S(2)}) %collective-permute-start.14) | collective-permute-done | bytes 65568 | tf_op jit(solution)/shard_map/ppermute | solution.py:323
  78.8 0.8 copy-done.3
  79.6 0.8 copy-done.5
  80.5 0.8 copy-done.7
  81.3 0.8 copy-done.9
  82.2 0.8 copy-done.11
  83.0 6.4 %tiles.1 = bf16[2,36,2,128,128]{4,3,2,1,0:T(8,128)(2,1)} custom-call(bf16[1024,1024]{1,0:T(8,128)(2,1)S(1)} %get-tuple-element.86.pick_ref, bf16[2,1024,256]{2,1,0:T(8,128)(2,1)S(1)} %get-tuple-element.46.early_ref, f32[2,8,128]{2,1,0:T(8,128)S(1)} %get-tuple-element.47.power_ref, bf16[4,64,128]{2,1,0:T(8,128)(2,1)S(1)} %copy-done.1, ...), custom_call_target="tpu_custom_call" | custom-call | flops 4499999744 | bytes 9000000 | tf_op jit(solution)/shard_map/tiles/pallas_call | solution.py:270
  (43 shorter events, 5.5 us)
Async XLA Ops:
  14.2 58.8 %all-to-all-start = ((bf16[16,4,64,128]{3,2,1,0:T(8,128)(2,1)}), bf16[16,4,64,128]{3,2,1,0:T(8,128)(2,1)S(1)}, u32[]{:S(2)}, u32[]{:S(2)}) async-start(bf16[16,4,64,128]{3,2,1,0:T(8,128)(2,1)} %bitcast.25), calls=%async_computation | async-start | bytes 2097152 | tf_op jit(solution)/shard_map/all_to_all | solution.py:314
  21.6 21.8 %copy-start.12 = (s32[512]{0:T(512)S(1)}, s32[512]{0:T(512)}, u32[]{:S(2)}) copy-start(s32[512]{0:T(512)} %param.10) | copy-start | bytes 6148
  36.3 7.5 %collective-permute-start = (bf16[4,64,128]{2,1,0:T(8,128)(2,1)}, bf16[4,64,128]{2,1,0:T(8,128)(2,1)S(1)}, u32[]{:S(2)}, u32[]{:S(2)}) collective-permute-start(bf16[4,64,128]{2,1,0:T(8,128)(2,1)} %get-tuple-element.51), channel_id=1, source_target_pairs={{0,1},{1,0},{2,3},{3,2},{4,5},{5,4},{6,7},{7,6},{8,9},{9,8},{10,11... | collective-permute-start | bytes 196616 | tf_op jit(solution)/shard_map/ppermute | solution.py:323
  36.8 8.5 %collective-permute-start.1 = (bf16[4,64,128]{2,1,0:T(8,128)(2,1)}, bf16[4,64,128]{2,1,0:T(8,128)(2,1)S(1)}, u32[]{:S(2)}, u32[]{:S(2)}) collective-permute-start(bf16[4,64,128]{2,1,0:T(8,128)(2,1)} %get-tuple-element.54), channel_id=1, source_target_pairs={{0,2},{1,3},{2,0},{3,1},{4,6},{5,7},{6,4},{7,5},{8,10},{9,11},{10,... | collective-permute-start | bytes 196616 | tf_op jit(solution)/shard_map/ppermute | solution.py:323
  38.5 17.6 %collective-permute-start.2 = (bf16[4,64,128]{2,1,0:T(8,128)(2,1)}, bf16[4,64,128]{2,1,0:T(8,128)(2,1)S(1)}, u32[]{:S(2)}, u32[]{:S(2)}) collective-permute-start(bf16[4,64,128]{2,1,0:T(8,128)(2,1)} %get-tuple-element.58), channel_id=1, source_target_pairs={{0,9},{1,8},{2,11},{3,10},{4,13},{5,12},{6,15},{7,14},{8,1},{9,0},... | collective-permute-start | bytes 196616 | tf_op jit(solution)/shard_map/ppermute | solution.py:323
  40.5 18.9 %collective-permute-start.4 = (bf16[4,64,128]{2,1,0:T(8,128)(2,1)}, bf16[4,64,128]{2,1,0:T(8,128)(2,1)S(1)}, u32[]{:S(2)}, u32[]{:S(2)}) collective-permute-start(bf16[4,64,128]{2,1,0:T(8,128)(2,1)} %get-tuple-element.63), channel_id=1, source_target_pairs={{0,10},{1,11},{2,8},{3,9},{4,14},{5,15},{6,12},{7,13},{8,2},{9,3},... | collective-permute-start | bytes 196616 | tf_op jit(solution)/shard_map/ppermute | solution.py:323
  40.8 19.0 %collective-permute-start.6 = (bf16[4,64,128]{2,1,0:T(8,128)(2,1)}, bf16[4,64,128]{2,1,0:T(8,128)(2,1)S(1)}, u32[]{:S(2)}, u32[]{:S(2)}) collective-permute-start(bf16[4,64,128]{2,1,0:T(8,128)(2,1)} %get-tuple-element.68), channel_id=1, source_target_pairs={{0,8},{1,9},{2,10},{3,11},{4,12},{5,13},{6,14},{7,15},{8,0},{9,1},... | collective-permute-start | bytes 196616 | tf_op jit(solution)/shard_map/ppermute | solution.py:323
  43.8 35.1 %copy-start.1 = (bf16[4,64,128]{2,1,0:T(8,128)(2,1)S(1)}, bf16[4,64,128]{2,1,0:T(8,128)(2,1)}, u32[]{:S(2)}) copy-start(bf16[4,64,128]{2,1,0:T(8,128)(2,1)} %get-tuple-element.49.refs_0_) | copy-start | bytes 196612
  43.8 18.1 %collective-permute-start.9 = (bf16[4,64,128]{2,1,0:T(8,128)(2,1)}, bf16[4,64,128]{2,1,0:T(8,128)(2,1)S(1)}, u32[]{:S(2)}, u32[]{:S(2)}) collective-permute-start(bf16[4,64,128]{2,1,0:T(8,128)(2,1)} %get-tuple-element.72), channel_id=1, source_target_pairs={{0,12},{1,13},{2,14},{3,15},{4,8},{5,9},{6,10},{7,11},{8,4},{9,5},... | collective-permute-start | bytes 196616 | tf_op jit(solution)/shard_map/ppermute | solution.py:323
  45.3 18.9 %collective-permute-start.11 = (bf16[4,64,128]{2,1,0:T(8,128)(2,1)}, bf16[4,64,128]{2,1,0:T(8,128)(2,1)S(1)}, u32[]{:S(2)}, u32[]{:S(2)}) collective-permute-start(bf16[4,64,128]{2,1,0:T(8,128)(2,1)} %get-tuple-element.75), channel_id=1, source_target_pairs={{0,13},{1,12},{2,15},{3,14},{4,9},{5,8},{6,11},{7,10},{8,5},{9,4},... | collective-permute-start | bytes 196616 | tf_op jit(solution)/shard_map/ppermute | solution.py:323
  56.1 11.0 %collective-permute-start.3 = (bf16[4,64,128]{2,1,0:T(8,128)(2,1)}, bf16[4,64,128]{2,1,0:T(8,128)(2,1)S(1)}, u32[]{:S(2)}, u32[]{:S(2)}) collective-permute-start(bf16[4,64,128]{2,1,0:T(8,128)(2,1)} %get-tuple-element.59), channel_id=1, source_target_pairs={{0,3},{1,2},{2,1},{3,0},{4,7},{5,6},{6,5},{7,4},{8,11},{9,10},{10,... | collective-permute-start | bytes 196616 | tf_op jit(solution)/shard_map/ppermute | solution.py:323
  59.4 11.6 %collective-permute-start.5 = (bf16[4,64,128]{2,1,0:T(8,128)(2,1)}, bf16[4,64,128]{2,1,0:T(8,128)(2,1)S(1)}, u32[]{:S(2)}, u32[]{:S(2)}) collective-permute-start(bf16[4,64,128]{2,1,0:T(8,128)(2,1)} %get-tuple-element.64), channel_id=1, source_target_pairs={{0,4},{1,5},{2,6},{3,7},{4,0},{5,1},{6,2},{7,3},{8,12},{9,13},{10,... | collective-permute-start | bytes 196616 | tf_op jit(solution)/shard_map/ppermute | solution.py:323
  59.9 11.8 %collective-permute-start.7 = (bf16[4,64,128]{2,1,0:T(8,128)(2,1)}, bf16[4,64,128]{2,1,0:T(8,128)(2,1)S(1)}, u32[]{:S(2)}, u32[]{:S(2)}) collective-permute-start(bf16[4,64,128]{2,1,0:T(8,128)(2,1)} %get-tuple-element.69), channel_id=1, source_target_pairs={{0,11},{1,10},{2,9},{3,8},{4,15},{5,14},{6,13},{7,12},{8,3},{9,2},... | collective-permute-start | bytes 196616 | tf_op jit(solution)/shard_map/ppermute | solution.py:323
  62.6 13.6 %collective-permute-start.10 = (bf16[4,64,128]{2,1,0:T(8,128)(2,1)}, bf16[4,64,128]{2,1,0:T(8,128)(2,1)}, u32[]{:S(2)}, u32[]{:S(2)}) collective-permute-start(bf16[4,64,128]{2,1,0:T(8,128)(2,1)} %get-tuple-element.73), channel_id=1, source_target_pairs={{0,6},{1,7},{2,4},{3,5},{4,2},{5,3},{6,0},{7,1},{8,14},{9,15},{10,... | collective-permute-start | bytes 196616 | tf_op jit(solution)/shard_map/ppermute | solution.py:323
  64.9 11.3 %collective-permute-start.12 = (bf16[4,64,128]{2,1,0:T(8,128)(2,1)}, bf16[4,64,128]{2,1,0:T(8,128)(2,1)}, u32[]{:S(2)}, u32[]{:S(2)}) collective-permute-start(bf16[4,64,128]{2,1,0:T(8,128)(2,1)} %get-tuple-element.76), channel_id=1, source_target_pairs={{0,7},{1,6},{2,5},{3,4},{4,3},{5,2},{6,1},{7,0},{8,15},{9,14},{10,... | collective-permute-start | bytes 196616 | tf_op jit(solution)/shard_map/ppermute | solution.py:323
  67.7 8.5 %collective-permute-start.13 = (bf16[4,64,128]{2,1,0:T(8,128)(2,1)}, bf16[4,64,128]{2,1,0:T(8,128)(2,1)}, u32[]{:S(2)}, u32[]{:S(2)}) collective-permute-start(bf16[4,64,128]{2,1,0:T(8,128)(2,1)} %get-tuple-element.83), channel_id=1, source_target_pairs={{0,14},{1,15},{2,12},{3,13},{4,10},{5,11},{6,8},{7,9},{8,6},{9,7},... | collective-permute-start | bytes 196616 | tf_op jit(solution)/shard_map/ppermute | solution.py:323
  71.6 7.2 %collective-permute-start.14 = (bf16[4,64,128]{2,1,0:T(8,128)(2,1)}, bf16[4,64,128]{2,1,0:T(8,128)(2,1)}, u32[]{:S(2)}, u32[]{:S(2)}) collective-permute-start(bf16[4,64,128]{2,1,0:T(8,128)(2,1)} %get-tuple-element.84), channel_id=1, source_target_pairs={{0,15},{1,14},{2,13},{3,12},{4,11},{5,10},{6,9},{7,8},{8,7},{9,6},... | collective-permute-start | bytes 196616 | tf_op jit(solution)/shard_map/ppermute | solution.py:323
  72.2 6.6 %collective-permute-start.8 = (bf16[4,64,128]{2,1,0:T(8,128)(2,1)}, bf16[4,64,128]{2,1,0:T(8,128)(2,1)}, u32[]{:S(2)}, u32[]{:S(2)}) collective-permute-start(bf16[4,64,128]{2,1,0:T(8,128)(2,1)} %get-tuple-element.70), channel_id=1, source_target_pairs={{0,5},{1,4},{2,7},{3,6},{4,1},{5,0},{6,3},{7,2},{8,13},{9,12},{10,... | collective-permute-start | bytes 196616 | tf_op jit(solution)/shard_map/ppermute | solution.py:323
  73.0 1.6 %copy-start = (bf16[1024,1024]{1,0:T(8,128)(2,1)S(1)}, bf16[1024,1024]{1,0:T(8,128)(2,1)}, u32[]{:S(2)}) copy-start(bf16[1024,1024]{1,0:T(8,128)(2,1)} %get-tuple-element.85.pick_ref) | copy-start | bytes 6291460
  78.8 0.8 copy-start.3
  79.6 0.8 copy-start.5
  80.5 0.8 copy-start.7
  81.3 0.8 copy-start.9
  82.2 0.8 copy-start.11
  (5 other events, 3.1 us)

commit v5 on v4

v5 whole, which is shorter than its diff:
```python
import functools
import math

import jax
import jax.numpy as jnp
import ml_dtypes
import numpy as np
from jax import lax
from jax.experimental import pallas as pl
from jax.experimental.pallas import tpu as pltpu
from jax.sharding import PartitionSpec as P

STATIONS = 512
NCHAN = 4096
BLOCK = 64
TAPS = 4
SPECTRA = 8
FRAMES = SPECTRA + TAPS - 1
AVG = 32
OUT_DEV = 2
LANES = 128
WIDE = 2 * AVG
WIDTH = SPECTRA * AVG
GROUP = 4
STEP = 8
ROWS = 16
WINDOW = 5
VMEM_LIMIT = 60_000_000
BF16 = jnp.bfloat16
F32 = jnp.float32
NT = (((1,), (1,)), ((), ()))


def split(values):
    high = values.astype(ml_dtypes.bfloat16)
    low = (values - high.astype(np.float64)).astype(ml_dtypes.bfloat16)
    return high, low


def tables(all_out):
    blocks = NCHAN // LANES
    angle = 2.0 * math.pi * (np.outer(np.arange(AVG), np.arange(blocks)) % blocks) / blocks
    cos, sin = np.cos(angle), np.sin(angle)
    stage = np.zeros((2, AVG, blocks, 2))
    stage[0, :, :, 0], stage[0, :, :, 1] = cos, sin
    stage[1, :, :, 0], stage[1, :, :, 1] = -sin, cos
    stage = np.kron(np.eye(GROUP), stage.reshape(2 * AVG, 2 * blocks))
    angle = 2.0 * math.pi * np.outer(np.arange(AVG), np.arange(LANES)) / NCHAN
    turn = np.stack([np.cos(angle), -np.sin(angle)]).astype(np.float32)
    first = (NCHAN - all_out * AVG) // 2
    bins = first // AVG + np.arange(all_out)
    angle = 2.0 * math.pi * (np.outer(np.arange(LANES), bins) % LANES) / LANES
    cos, sin = np.cos(angle), np.sin(angle)
    last = np.zeros((2, LANES, all_out, 2))
    last[0, :, :, 0], last[0, :, :, 1] = cos, -sin
    last[1, :, :, 0], last[1, :, :, 1] = sin, cos
    beside = max(1, LANES // (2 * all_out))
    last = np.kron(np.eye(beside), last.reshape(2 * LANES, 2 * all_out))
    return np.concatenate(split(stage)), turn, np.concatenate(split(last), axis=1)


def halves(values):
    high = values.astype(BF16)
    return high, (values - high.astype(F32)).astype(BF16)


def spectra_kernel(first_stream, partners, outs, gain_ref, *refs):
    frames, refs = refs[:FRAMES], refs[FRAMES:]
    (taps_ref, stage_ref, turn_ref, last_ref), refs = refs[:4], refs[4:]
    out_refs, refs = refs[: max(partners, 1)], refs[max(partners, 1) :]
    (coeff_ref, held_ref), refs = refs[:2], refs[2:]
    groups = STEP // GROUP
    high_refs, low_refs, turned_refs = [refs[i * groups : (i + 1) * groups] for i in range(3)]
    outer, inner = pl.program_id(0), pl.program_id(1)
    size = GROUP * WIDE
    beside = last_ref.shape[0] // (2 * LANES)
    columns = beside * outs

    @pl.when((outer == 0) & (inner == 0))
    def _():
        for j in range(TAPS):
            rows = taps_ref[pl.ds(j, AVG, stride=TAPS), :]
            for ri in range(2):
                coeff_ref[j, pl.ds(ri, AVG, stride=2), :] = rows

    def filter_rows(g, u, r):
        rows = slice(r, r + 16)
        coeffs = [coeff_ref[j, rows, :] for j in range(TAPS)]
        samples = [ref[g * GROUP + u, 0, rows, :].astype(F32) for ref in frames]
        for m in range(SPECTRA):
            value = coeffs[0] * samples[m]
            for j in range(1, TAPS):
                value = value + coeffs[j] * samples[m + j]
            high, low = halves(value)
            place = (slice(u * WIDE + r, u * WIDE + r + 16), slice(m * LANES, (m + 1) * LANES))
            high_refs[g][place] = high
            low_refs[g][place] = low

    def first_part(g, start):
        lanes = slice(start * LANES, (start + 2) * LANES)
        both = jnp.dot(stage_ref[...], high_refs[g][:, lanes], preferred_element_type=F32)
        rest = jnp.dot(stage_ref[:size, :], low_refs[g][:, lanes], preferred_element_type=F32)
        section = both[:size] + (both[size:] + rest)
        turn_real, turn_imag = turn_ref[0], turn_ref[1]
        for u in range(GROUP):
            pair, place = divmod(u, beside)
            for m in range(start, start + 2):
                at = slice((m - start) * LANES, (m - start + 1) * LANES)
                real = section[u * WIDE : u * WIDE + AVG, at]
                imag = section[u * WIDE + AVG : (u + 1) * WIDE, at]
                for ri, value in enumerate((real * turn_real - imag * turn_imag, real * turn_imag + imag * turn_real)):
                    where = slice((2 * place + ri) * LANES, (2 * place + ri + 1) * LANES)
                    for part, kept in enumerate(halves(value)):
                        row = (2 * pair + part) * WIDTH + m * AVG
                        turned_refs[g][row : row + AVG, where] = kept

    def last_part(g, pair):
        rows = slice(2 * pair * WIDTH, 2 * (pair + 1) * WIDTH)
        product = jnp.dot(turned_refs[g][rows, :], last_ref[...], preferred_element_type=F32)
        found = product[:WIDTH, :columns] + (product[:WIDTH, columns:] + product[WIDTH:, :columns])
        found = found.T
        for place in range(beside):
            stream = g * GROUP + pair * beside + place
            factor = gain_ref[(first_stream + outer * ROWS + inner * STEP + stream) // 2]
            factor = factor * (1.0 / (64.0 * math.sqrt(NCHAN)))
            at = pl.multiple_of((inner * STEP + stream) * outs, outs)
            mine = found[place * outs : (place + 1) * outs] * factor
            for half in range(WIDTH // LANES):
                held_ref[half, pl.ds(at, outs), :] = mine[:, half * LANES : (half + 1) * LANES]

    for g in range(groups + 2):
        filters = [(g, u, r) for u in range(GROUP) for r in range(0, WIDE, 16)] if g < groups else []
        firsts = [(g - 1, start) for start in range(0, SPECTRA, 2)] if 1 <= g <= groups else []
        lasts = [(g - 2, pair) for pair in range(GROUP // beside)] if g >= 2 else []
        while filters or firsts or lasts:
            for work, jobs, most in ((first_part, firsts, 1), (filter_rows, filters, 2), (last_part, lasts, 1), (filter_rows, filters, 2)):
                for job in jobs[:most]:
                    work(*job)
                del jobs[:most]

    @pl.when(inner == ROWS // STEP - 1)
    def _():
        me = lax.axis_index("ingest") if partners else 0
        each = outs // len(out_refs)
        for k, out_ref in enumerate(out_refs):
            target = jnp.bitwise_xor(me, k) * each if partners else 0
            for q in range(each):
                for half in range(WIDTH // LANES):
                    rows = held_ref[half, pl.ds(target + q, ROWS, stride=outs), :]
                    out_ref[q, :, half * LANES : (half + 1) * LANES] = rows.astype(BF16)


def spectra(voltages, taps, station_gain, consts, outs, start, stop, partners=0):
    stage, turn, last = consts
    groups = STEP // GROUP
    inner = ROWS // STEP
    pieces = max(partners, 1)
    frame_spec = [
        pl.BlockSpec((STEP, 1, WIDE, LANES), functools.partial(lambda j, a, b: (start // STEP + a * inner + b, j, 0, 0), j))
        for j in range(FRAMES)
    ]
    whole = lambda shape: pl.BlockSpec(shape, lambda a, b: (0,) * len(shape))
    return pl.pallas_call(
        functools.partial(spectra_kernel, start, partners, outs),
        out_shape=[jax.ShapeDtypeStruct((outs // pieces, stop - start, WIDTH), BF16)] * pieces,
        grid=((stop - start) // ROWS, inner),
        in_specs=[pl.BlockSpec(memory_space=pltpu.SMEM)]
        + frame_spec
        + [whole(taps.shape), whole(stage.shape), whole(turn.shape), whole(last.shape)],
        out_specs=[pl.BlockSpec((outs // pieces, ROWS, WIDTH), lambda a, b: (0, a, 0))] * pieces,
        scratch_shapes=[
            pltpu.VMEM((TAPS, WIDE, LANES), F32),
            pltpu.VMEM((WIDTH // LANES, ROWS * outs, LANES), F32),
        ]
        + [pltpu.VMEM((GROUP * WIDE, SPECTRA * LANES), BF16)] * (2 * groups)
        + [pltpu.VMEM((2 * GROUP * WIDTH * 2 * LANES // last.shape[0], last.shape[0]), BF16)] * groups,
        compiler_params=pltpu.CompilerParams(vmem_limit_bytes=VMEM_LIMIT),
        cost_estimate=pl.CostEstimate(
            flops=(stop - start) * SPECTRA * 12_000_000,
            bytes_accessed=(stop - start) * FRAMES * WIDE * LANES * 4,
            transcendentals=0,
        ),
        name="spectra",
    )(station_gain, *([voltages] * FRAMES), taps, stage, turn, last)


def squares(values):
    values = values.astype(F32)
    values = jnp.sum((values * values).reshape(-1, 8, values.shape[-1]), axis=0)
    return sum(values[:, lane : lane + LANES] for lane in range(0, values.shape[-1], LANES))


def arrange_kernel(pick_ref, part_ref, out_ref, power_ref):
    rows = 2 * STATIONS
    data = jnp.concatenate([part_ref[:, ri].reshape(-1, WIDTH) for ri in range(2)], axis=1)
    power_ref[0] = squares(data)
    for r in range(0, rows, 2 * LANES):
        own = slice(r, r + 2 * LANES)
        out_ref[0, own, :] = jnp.dot(pick_ref[own, :], data, preferred_element_type=F32).astype(BF16)


def arrange(pick, part):
    devices, _, own, width = part.shape
    rows = 2 * STATIONS
    return pl.pallas_call(
        arrange_kernel,
        out_shape=(
            jax.ShapeDtypeStruct((OUT_DEV, rows, 2 * width), BF16),
            jax.ShapeDtypeStruct((OUT_DEV, 8, LANES), F32),
        ),
        grid=(OUT_DEV,),
        in_specs=[
            pl.BlockSpec(pick.shape, lambda o: (0, 0)),
            pl.BlockSpec((devices, 2, own, width), lambda o: (0, o, 0, 0)),
        ],
        out_specs=(
            pl.BlockSpec((1, rows, 2 * width), lambda o: (o, 0, 0)),
            pl.BlockSpec((1, 8, LANES), lambda o: (o, 0, 0)),
        ),
        compiler_params=pltpu.CompilerParams(vmem_limit_bytes=40 * 2**20),
        cost_estimate=pl.CostEstimate(flops=1_100_000_000, bytes_accessed=4_000_000, transcendentals=0),
        name="arrange",
    )(pick, part)


def tiles_kernel(late, early_ref, power_ref, *refs):
    (pick_refs, part_refs), refs = (refs[: min(late, 1)], refs[min(late, 1) :][:late]), refs[-3:]
    out_ref, left_ref, right_ref = refs
    rows = 2 * STATIONS
    side = 2 * BLOCK
    blocks = STATIONS // BLOCK
    total = power_ref[0]
    if late:
        data = [jnp.concatenate([part_ref[ri] for part_ref in part_refs], axis=0) for ri in range(2)]
        data = jnp.concatenate(data, axis=1)
        total = total + squares(data)
    power = jnp.sum(total) / (STATIONS * 2 * SPECTRA * AVG)
    scale = 1.0 / jnp.full((1, LANES), SPECTRA * AVG * power, F32)
    for r in range(0, rows, 2 * side):
        own = slice(r, r + 2 * side)
        found = early_ref[0, own, :]
        if late:
            found = (jnp.dot(pick_refs[0][own, :], data, preferred_element_type=F32) + found.astype(F32)).astype(BF16)
        right_ref[own, :] = found
        for p in range(2):
            mine = found[p * side : (p + 1) * side]
            at = 2 * r + p * 2 * side
            left_ref[at : at + side, :] = mine
            left_ref[at + side : at + 2 * side, :WIDTH] = mine[:, WIDTH:]
            left_ref[at + side : at + 2 * side, WIDTH:] = -mine[:, :WIDTH]
    for c in range(0, blocks, 2):
        right = right_ref[c * side : (c + 2) * side, :]
        for b in range(c, blocks):
            left = left_ref[b * 2 * side : (b + 1) * 2 * side, :]
            product = lax.dot_general(left, right, NT, preferred_element_type=F32)
            for p in range(2):
                if c + p <= b:
                    tile = b * (b + 1) // 2 + c + p
                    scaled = (product[:, p * side : (p + 1) * side] * scale).astype(BF16)
                    out_ref[0, tile, 0] = scaled[:side]
                    out_ref[0, tile, 1] = scaled[side:]


def tiles(early, power, picks, parts):
    blocks = STATIONS // BLOCK
    pairs = blocks * (blocks + 1) // 2
    side = 2 * BLOCK
    rows = 2 * STATIONS
    return pl.pallas_call(
        functools.partial(tiles_kernel, len(parts)),
        out_shape=jax.ShapeDtypeStruct((OUT_DEV, pairs, 2, side, side), BF16),
        grid=(OUT_DEV,),
        in_specs=[
            pl.BlockSpec((1, rows, 2 * WIDTH), lambda o: (o, 0, 0)),
            pl.BlockSpec((1, 8, LANES), lambda o: (o, 0, 0)),
        ]
        + [pl.BlockSpec(pick.shape, lambda o: (0, 0)) for pick in picks]
        + [pl.BlockSpec((2,) + part.shape[1:], lambda o: (o, 0, 0)) for part in parts],
        out_specs=pl.BlockSpec((1, pairs, 2, side, side), lambda o: (o, 0, 0, 0, 0)),
        scratch_shapes=[
            pltpu.VMEM((2 * rows, 2 * WIDTH), BF16),
            pltpu.VMEM((rows, 2 * WIDTH), BF16),
        ],
        compiler_params=pltpu.CompilerParams(vmem_limit_bytes=40 * 2**20),
        cost_estimate=pl.CostEstimate(flops=4_500_000_000, bytes_accessed=9_000_000, transcendentals=0),
        name="tiles",
    )(early, power, *picks, *parts)


def body(voltages, taps, station_gain, station_order):
    devices = lax.axis_size("ingest")
    streams = 2 * voltages.shape[0]
    blocks = NCHAN // LANES
    outs = 2 * OUT_DEV * devices
    consts = tables(OUT_DEV * devices)
    samples = voltages.reshape(streams, 2, FRAMES * blocks, LANES).transpose(0, 2, 1, 3)
    samples = samples.reshape(streams, FRAMES, 2 * blocks, LANES)
    coeffs = taps.reshape(TAPS, blocks, LANES).transpose(1, 0, 2).reshape(TAPS * blocks, LANES)
    cut = streams - streams // (2 * ROWS) * ROWS
    wanted = (2 * station_order[:, None] + jnp.arange(2, dtype=jnp.int32)).reshape(-1, 1)

    def pick(start, stop, first):
        place = np.arange(devices * (stop - start), dtype=np.int32)
        source = jnp.bitwise_xor(place // (stop - start), first) * streams + start + place % (stop - start)
        return (wanted == source).astype(BF16)

    packed = spectra(samples, coeffs, station_gain, consts, outs, 0, cut)[0]
    packed = packed.reshape(devices, 2 * OUT_DEV, cut, WIDTH)
    packed, station_gain = lax.optimization_barrier((packed, station_gain))
    early = lax.all_to_all(packed, "ingest", split_axis=0, concat_axis=0, tiled=True)
    picks, late = [], []
    if cut < streams:
        sent = spectra(samples, coeffs, station_gain, consts, outs, cut, streams, devices)
        late = [sent[0]]
        for k in range(1, devices):
            ready = sent[k]
            if k > WINDOW:
                ready, late[k - WINDOW] = lax.optimization_barrier((ready, late[k - WINDOW]))
            late.append(lax.ppermute(ready, "ingest", [(i, i ^ k) for i in range(devices)]))
        picks = [pick(cut, streams, lax.axis_index("ingest"))]
    rows, power = arrange(pick(0, cut, 0), early)
    return tiles(rows, power, picks, late)


def solution(mesh):
    return jax.shard_map(
        body,
        mesh=mesh,
        in_specs=(P(("band", "ingest"), None, None, None), P(), P("ingest"), P()),
        out_specs=P(("band", "ingest"), None, None, None, None),
        check_vma=False,
    )
```

time: 90 us -> 79.3 us (0.88)
  the two profiles are of different devices: /device:TPU:0 before, /device:TPU:11 now
where the time goes in v5:
time: 79.3 us; the launch traced here: 79 us
  Pallas kernels  38.2 us (48%)
  starting transfers between devices  27.4 us (35%)
  waiting for transfers between devices  9.34 us (12%)
  local copies, waits for them, and re-layouts  3.33 us (4%)
    pallas_call x2, Pallas kernels, spectra(): pl.pallas_call(functools.partial(spectra_kernel, start, partners, outs),...  30.2 us
    ppermute x15, starting transfers between devices, body(): lax.ppermute(ready, 'ingest', [(i, i ^ k) for i in range(devices)])  20.8 us
    ppermute x15, waiting for transfers between devices, body(): lax.ppermute(ready, 'ingest', [(i, i ^ k) for i in range(devices)])  9.33 us
    all_to_all x1, starting transfers between devices, body(): lax.all_to_all(packed, 'ingest', split_axis=0, concat_axis=0, tiled=True)  6.62 us
    pallas_call x1, Pallas kernels, tiles(): pl.pallas_call(functools.partial(tiles_kernel, len(parts)), out_shape=jax...  6.47 us
    unnamed x30, local copies, waits for them, and re-layouts  3.16 us
  transfers between devices with their start and end apart: 16, of which 4 were waited for; matrix products, arithmetic and copies ran while one was open for 1% of the time, Pallas kernels for 21%

profile of v5, /device:TPU:11, one launch (start us, length us, event | category | flops | bytes accessed | tf_op | source)
XLA Modules:
  0.0 79.0 jit_solution(17419453194344695789)
XLA Ops:
  0.0 14.9 %spectra.2 = bf16[64,32,256]{2,1,0:T(8,128)(2,1)} custom-call(f32[32]{0:T(128)} %gain_ref.2, s32[64,11,64,128]{3,2,1,0:T(8,128)} %bitcast.11, s32[64,11,64,128]{3,2,1,0:T(8,128)} %bitcast.12, s32[64,11,64,128]{3,2,1,0:T(8,128)} %bitcast.13, s32[64,11,64,128]{3,2,1,0:T(8,128)} %bitcast.14, s32[64,11,64,128]{3,2,1,0:T(8,128)} %bitcast.15, ...), custom_call_target="tpu_custom_call" | custom-call | flops 3072000000 | bytes 11534336 | tf_op jit(solution)/shard_map/spectra/pallas_call | solution.py:163
  14.9 6.6 %all-to-all-start = ((bf16[16,4,32,256]{3,2,1,0:T(8,128)(2,1)}), bf16[16,4,32,256]{3,2,1,0:T(8,128)(2,1)S(1)}, u32[]{:S(2)}, u32[]{:S(2)}) async-start(bf16[16,4,32,256]{3,2,1,0:T(8,128)(2,1)} %bitcast.33), calls=%async_computation | async-start | bytes 2097152 | tf_op jit(solution)/shard_map/all_to_all | solution.py:310
  21.6 15.3 %spectra.3 = (bf16[4,32,256]{2,1,0:T(8,128)(2,1)}, bf16[4,32,256]{2,1,0:T(8,128)(2,1)}, bf16[4,32,256]{2,1,0:T(8,128)(2,1)}, bf16[4,32,256]{2,1,0:T(8,128)(2,1)}...) custom-call(f32[32]{0:T(128)} %gain_ref.2, ...), custom_call_target="tpu_custom_call" | custom-call | flops 3072000000 | bytes 11534336 | tf_op jit(solution)/shard_map/spectra/pallas_call | solution.py:163
  37.3 1.2 %collective-permute-start.1 = (bf16[4,32,256]{2,1,0:T(8,128)(2,1)}, bf16[4,32,256]{2,1,0:T(8,128)(2,1)S(1)}, u32[]{:S(2)}, u32[]{:S(2)}) collective-permute-start(bf16[4,32,256]{2,1,0:T(8,128)(2,1)} %get-tuple-element.54), channel_id=1, source_target_pairs={{0,2},{1,3},{2,0},{3,1},{4,6},{5,7},{6,4},{7,5},{8,10},{9,11},{10,... | collective-permute-start | bytes 196616 | tf_op jit(solution)/shard_map/ppermute | solution.py:319
  39.1 1.6 %collective-permute-start.4 = (bf16[4,32,256]{2,1,0:T(8,128)(2,1)}, bf16[4,32,256]{2,1,0:T(8,128)(2,1)S(1)}, u32[]{:S(2)}, u32[]{:S(2)}) collective-permute-start(bf16[4,32,256]{2,1,0:T(8,128)(2,1)} %get-tuple-element.63), channel_id=1, source_target_pairs={{0,5},{1,4},{2,7},{3,6},{4,1},{5,0},{6,3},{7,2},{8,13},{9,12},{10,... | collective-permute-start | bytes 196616 | tf_op jit(solution)/shard_map/ppermute | solution.py:319
  41.1 1.2 %collective-permute-start.5 = (bf16[4,32,256]{2,1,0:T(8,128)(2,1)}, bf16[4,32,256]{2,1,0:T(8,128)(2,1)S(1)}, u32[]{:S(2)}, u32[]{:S(2)}) collective-permute-start(bf16[4,32,256]{2,1,0:T(8,128)(2,1)} %get-tuple-element.66), channel_id=1, source_target_pairs={{0,6},{1,7},{2,4},{3,5},{4,2},{5,3},{6,0},{7,1},{8,14},{9,15},{10,... | collective-permute-start | bytes 196616 | tf_op jit(solution)/shard_map/ppermute | solution.py:319
  42.4 1.5 %collective-permute-start.6 = (bf16[4,32,256]{2,1,0:T(8,128)(2,1)}, bf16[4,32,256]{2,1,0:T(8,128)(2,1)S(1)}, u32[]{:S(2)}, u32[]{:S(2)}) collective-permute-start(bf16[4,32,256]{2,1,0:T(8,128)(2,1)} %get-tuple-element.69), channel_id=1, source_target_pairs={{0,7},{1,6},{2,5},{3,4},{4,3},{5,2},{6,1},{7,0},{8,15},{9,14},{10,... | collective-permute-start | bytes 196616 | tf_op jit(solution)/shard_map/ppermute | solution.py:319
  43.9 3.6 %collective-permute-start.7 = (bf16[4,32,256]{2,1,0:T(8,128)(2,1)}, bf16[4,32,256]{2,1,0:T(8,128)(2,1)S(1)}, u32[]{:S(2)}, u32[]{:S(2)}) collective-permute-start(bf16[4,32,256]{2,1,0:T(8,128)(2,1)} %get-tuple-element.72), channel_id=1, source_target_pairs={{0,8},{1,9},{2,10},{3,11},{4,12},{5,13},{6,14},{7,15},{8,0},{9,1},... | collective-permute-start | bytes 196616 | tf_op jit(solution)/shard_map/ppermute | solution.py:319
  47.5 1.5 %collective-permute-start.8 = (bf16[4,32,256]{2,1,0:T(8,128)(2,1)}, bf16[4,32,256]{2,1,0:T(8,128)(2,1)S(1)}, u32[]{:S(2)}, u32[]{:S(2)}) collective-permute-start(bf16[4,32,256]{2,1,0:T(8,128)(2,1)} %get-tuple-element.75), channel_id=1, source_target_pairs={{0,9},{1,8},{2,11},{3,10},{4,13},{5,12},{6,15},{7,14},{8,1},{9,0},... | collective-permute-start | bytes 196616 | tf_op jit(solution)/shard_map/ppermute | solution.py:319
  49.0 1.0 %collective-permute-start.9 = (bf16[4,32,256]{2,1,0:T(8,128)(2,1)}, bf16[4,32,256]{2,1,0:T(8,128)(2,1)S(1)}, u32[]{:S(2)}, u32[]{:S(2)}) collective-permute-start(bf16[4,32,256]{2,1,0:T(8,128)(2,1)} %get-tuple-element.78), channel_id=1, source_target_pairs={{0,10},{1,11},{2,8},{3,9},{4,14},{5,15},{6,12},{7,13},{8,2},{9,3},... | collective-permute-start | bytes 196616 | tf_op jit(solution)/shard_map/ppermute | solution.py:319
  51.1 2.3 %collective-permute-start.10 = (bf16[4,32,256]{2,1,0:T(8,128)(2,1)}, bf16[4,32,256]{2,1,0:T(8,128)(2,1)}, u32[]{:S(2)}, u32[]{:S(2)}) collective-permute-start(bf16[4,32,256]{2,1,0:T(8,128)(2,1)} %get-tuple-element.80), channel_id=1, source_target_pairs={{0,11},{1,10},{2,9},{3,8},{4,15},{5,14},{6,13},{7,12},{8,3},{9,2},... | collective-permute-start | bytes 196616 | tf_op jit(solution)/shard_map/ppermute | solution.py:319
  53.4 0.6 copy-done.3
  54.0 0.6 copy-done.5
  54.6 2.0 %collective-permute-start.12 = (bf16[4,32,256]{2,1,0:T(8,128)(2,1)}, bf16[4,32,256]{2,1,0:T(8,128)(2,1)}, u32[]{:S(2)}, u32[]{:S(2)}) collective-permute-start(bf16[4,32,256]{2,1,0:T(8,128)(2,1)} %get-tuple-element.82), channel_id=1, source_target_pairs={{0,13},{1,12},{2,15},{3,14},{4,9},{5,8},{6,11},{7,10},{8,5},{9,4},... | collective-permute-start | bytes 196616 | tf_op jit(solution)/shard_map/ppermute | solution.py:319
  56.6 0.6 copy-done.7
  57.3 2.7 %collective-permute-start.13 = (bf16[4,32,256]{2,1,0:T(8,128)(2,1)}, bf16[4,32,256]{2,1,0:T(8,128)(2,1)}, u32[]{:S(2)}, u32[]{:S(2)}) collective-permute-start(bf16[4,32,256]{2,1,0:T(8,128)(2,1)} %get-tuple-element.83), channel_id=1, source_target_pairs={{0,14},{1,15},{2,12},{3,13},{4,10},{5,11},{6,8},{7,9},{8,6},{9,7},... | collective-permute-start | bytes 196616 | tf_op jit(solution)/shard_map/ppermute | solution.py:319
  60.0 0.6 copy-done.9
  60.6 1.0 %collective-permute-start.14 = (bf16[4,32,256]{2,1,0:T(8,128)(2,1)}, bf16[4,32,256]{2,1,0:T(8,128)(2,1)}, u32[]{:S(2)}, u32[]{:S(2)}) collective-permute-start(bf16[4,32,256]{2,1,0:T(8,128)(2,1)} %get-tuple-element.84), channel_id=1, source_target_pairs={{0,15},{1,14},{2,13},{3,12},{4,11},{5,10},{6,9},{7,8},{8,7},{9,6},... | collective-permute-start | bytes 196616 | tf_op jit(solution)/shard_map/ppermute | solution.py:319
  61.7 1.6 %arrange.1 = (bf16[2,1024,512]{2,1,0:T(8,128)(2,1)S(1)}, f32[2,8,128]{2,1,0:T(8,128)S(1)}) custom-call(bf16[1024,512]{1,0:T(8,128)(2,1)S(1)} %get-tuple-element.86.pick_ref, bf16[16,4,32,256]{3,2,1,0:T(8,128)(2,1)S(1)} %all-to-all-done.part_ref), custom_call_target="tpu_custom_call" | custom-call | flops 1100000000 | bytes 4000000 | tf_op jit(solution)/shard_map/arrange/pallas_call | solution.py:205
  63.3 2.5 %collective-permute-done.11.refs_13_ = bf16[4,32,256]{2,1,0:T(8,128)(2,1)} collective-permute-done((bf16[4,32,256]{2,1,0:T(8,128)(2,1)}, bf16[4,32,256]{2,1,0:T(8,128)(2,1)}, u32[]{:S(2)}, u32[]{:S(2)}) %collective-permute-start.11) | collective-permute-done | bytes 65568 | tf_op jit(solution)/shard_map/ppermute | solution.py:319
  65.8 0.9 %collective-permute-done.12.refs_14_ = bf16[4,32,256]{2,1,0:T(8,128)(2,1)} collective-permute-done((bf16[4,32,256]{2,1,0:T(8,128)(2,1)}, bf16[4,32,256]{2,1,0:T(8,128)(2,1)}, u32[]{:S(2)}, u32[]{:S(2)}) %collective-permute-start.12) | collective-permute-done | bytes 65568 | tf_op jit(solution)/shard_map/ppermute | solution.py:319
  66.7 4.4 %collective-permute-done.13.refs_15_ = bf16[4,32,256]{2,1,0:T(8,128)(2,1)} collective-permute-done((bf16[4,32,256]{2,1,0:T(8,128)(2,1)}, bf16[4,32,256]{2,1,0:T(8,128)(2,1)}, u32[]{:S(2)}, u32[]{:S(2)}) %collective-permute-start.13) | collective-permute-done | bytes 65568 | tf_op jit(solution)/shard_map/ppermute | solution.py:319
  71.1 1.4 %collective-permute-done.14.refs_16_ = bf16[4,32,256]{2,1,0:T(8,128)(2,1)} collective-permute-done((bf16[4,32,256]{2,1,0:T(8,128)(2,1)}, bf16[4,32,256]{2,1,0:T(8,128)(2,1)}, u32[]{:S(2)}, u32[]{:S(2)}) %collective-permute-start.14) | collective-permute-done | bytes 65568 | tf_op jit(solution)/shard_map/ppermute | solution.py:319
  72.6 6.5 %tiles.1 = bf16[2,36,2,128,128]{4,3,2,1,0:T(8,128)(2,1)} custom-call(bf16[2,1024,512]{2,1,0:T(8,128)(2,1)S(1)} %get-tuple-element.46.early_ref, f32[2,8,128]{2,1,0:T(8,128)S(1)} %get-tuple-element.47.power_ref, bf16[1024,512]{1,0:T(8,128)(2,1)S(1)} %get-tuple-element.85.refs_0_, bf16[4,32,256]{2,1,0:T(8,128)(2,1)S(1)} %copy-done, ...), custom_call_target="tpu_custom_call" | custom-call | flops 4499999744 | bytes 9000000 | tf_op jit(solution)/shard_map/tiles/pallas_call | solution.py:269
  (47 shorter events, 2.5 us)
Async XLA Ops:
  14.9 46.8 %all-to-all-start = ((bf16[16,4,32,256]{3,2,1,0:T(8,128)(2,1)}), bf16[16,4,32,256]{3,2,1,0:T(8,128)(2,1)S(1)}, u32[]{:S(2)}, u32[]{:S(2)}) async-start(bf16[16,4,32,256]{3,2,1,0:T(8,128)(2,1)} %bitcast.33), calls=%async_computation | async-start | bytes 2097152 | tf_op jit(solution)/shard_map/all_to_all | solution.py:310
  21.5 19.3 %copy-start.11 = (s32[512]{0:T(512)S(1)}, s32[512]{0:T(512)}, u32[]{:S(2)}) copy-start(s32[512]{0:T(512)} %param.14) | copy-start | bytes 6148
  21.5 19.4 %copy-start.12 = (s32[512]{0:T(512)S(1)}, s32[512]{0:T(512)}, u32[]{:S(2)}) copy-start(s32[512]{0:T(512)} %constant.24.clone) | copy-start | bytes 6148
  21.5 19.4 %copy-start.13 = (s32[512]{0:T(512)S(1)}, s32[512]{0:T(512)}, u32[]{:S(2)}) copy-start(s32[512]{0:T(512)} %constant.23.clone) | copy-start | bytes 6148
  21.5 28.5 %copy-start.14 = (s32[512]{0:T(512)S(1)}, s32[512]{0:T(512)}, u32[]{:S(2)}) copy-start(s32[512]{0:T(512)} %constant.26) | copy-start | bytes 6148
  36.9 4.3 %collective-permute-start = (bf16[4,32,256]{2,1,0:T(8,128)(2,1)}, bf16[4,32,256]{2,1,0:T(8,128)(2,1)S(1)}, u32[]{:S(2)}, u32[]{:S(2)}) collective-permute-start(bf16[4,32,256]{2,1,0:T(8,128)(2,1)} %get-tuple-element.51), channel_id=1, source_target_pairs={{0,1},{1,0},{2,3},{3,2},{4,5},{5,4},{6,7},{7,6},{8,9},{9,8},{10,11... | collective-permute-start | bytes 196616 | tf_op jit(solution)/shard_map/ppermute | solution.py:319
  37.3 5.1 %collective-permute-start.1 = (bf16[4,32,256]{2,1,0:T(8,128)(2,1)}, bf16[4,32,256]{2,1,0:T(8,128)(2,1)S(1)}, u32[]{:S(2)}, u32[]{:S(2)}) collective-permute-start(bf16[4,32,256]{2,1,0:T(8,128)(2,1)} %get-tuple-element.54), channel_id=1, source_target_pairs={{0,2},{1,3},{2,0},{3,1},{4,6},{5,7},{6,4},{7,5},{8,10},{9,11},{10,... | collective-permute-start | bytes 196616 | tf_op jit(solution)/shard_map/ppermute | solution.py:319
  38.5 5.4 %collective-permute-start.2 = (bf16[4,32,256]{2,1,0:T(8,128)(2,1)}, bf16[4,32,256]{2,1,0:T(8,128)(2,1)S(1)}, u32[]{:S(2)}, u32[]{:S(2)}) collective-permute-start(bf16[4,32,256]{2,1,0:T(8,128)(2,1)} %get-tuple-element.57), channel_id=1, source_target_pairs={{0,3},{1,2},{2,1},{3,0},{4,7},{5,6},{6,5},{7,4},{8,11},{9,10},{10,... | collective-permute-start | bytes 196616 | tf_op jit(solution)/shard_map/ppermute | solution.py:319
  39.1 8.5 %collective-permute-start.3 = (bf16[4,32,256]{2,1,0:T(8,128)(2,1)}, bf16[4,32,256]{2,1,0:T(8,128)(2,1)S(1)}, u32[]{:S(2)}, u32[]{:S(2)}) collective-permute-start(bf16[4,32,256]{2,1,0:T(8,128)(2,1)} %get-tuple-element.60), channel_id=1, source_target_pairs={{0,4},{1,5},{2,6},{3,7},{4,0},{5,1},{6,2},{7,3},{8,12},{9,13},{10,... | collective-permute-start | bytes 196616 | tf_op jit(solution)/shard_map/ppermute | solution.py:319
  39.1 9.9 %collective-permute-start.4 = (bf16[4,32,256]{2,1,0:T(8,128)(2,1)}, bf16[4,32,256]{2,1,0:T(8,128)(2,1)S(1)}, u32[]{:S(2)}, u32[]{:S(2)}) collective-permute-start(bf16[4,32,256]{2,1,0:T(8,128)(2,1)} %get-tuple-element.63), channel_id=1, source_target_pairs={{0,5},{1,4},{2,7},{3,6},{4,1},{5,0},{6,3},{7,2},{8,13},{9,12},{10,... | collective-permute-start | bytes 196616 | tf_op jit(solution)/shard_map/ppermute | solution.py:319
  41.1 9.3 %collective-permute-start.5 = (bf16[4,32,256]{2,1,0:T(8,128)(2,1)}, bf16[4,32,256]{2,1,0:T(8,128)(2,1)S(1)}, u32[]{:S(2)}, u32[]{:S(2)}) collective-permute-start(bf16[4,32,256]{2,1,0:T(8,128)(2,1)} %get-tuple-element.66), channel_id=1, source_target_pairs={{0,6},{1,7},{2,4},{3,5},{4,2},{5,3},{6,0},{7,1},{8,14},{9,15},{10,... | collective-permute-start | bytes 196616 | tf_op jit(solution)/shard_map/ppermute | solution.py:319
  42.4 10.9 %collective-permute-start.6 = (bf16[4,32,256]{2,1,0:T(8,128)(2,1)}, bf16[4,32,256]{2,1,0:T(8,128)(2,1)S(1)}, u32[]{:S(2)}, u32[]{:S(2)}) collective-permute-start(bf16[4,32,256]{2,1,0:T(8,128)(2,1)} %get-tuple-element.69), channel_id=1, source_target_pairs={{0,7},{1,6},{2,5},{3,4},{4,3},{5,2},{6,1},{7,0},{8,15},{9,14},{10,... | collective-permute-start | bytes 196616 | tf_op jit(solution)/shard_map/ppermute | solution.py:319
  43.9 10.1 %collective-permute-start.7 = (bf16[4,32,256]{2,1,0:T(8,128)(2,1)}, bf16[4,32,256]{2,1,0:T(8,128)(2,1)S(1)}, u32[]{:S(2)}, u32[]{:S(2)}) collective-permute-start(bf16[4,32,256]{2,1,0:T(8,128)(2,1)} %get-tuple-element.72), channel_id=1, source_target_pairs={{0,8},{1,9},{2,10},{3,11},{4,12},{5,13},{6,14},{7,15},{8,0},{9,1},... | collective-permute-start | bytes 196616 | tf_op jit(solution)/shard_map/ppermute | solution.py:319
  47.5 9.1 %collective-permute-start.8 = (bf16[4,32,256]{2,1,0:T(8,128)(2,1)}, bf16[4,32,256]{2,1,0:T(8,128)(2,1)S(1)}, u32[]{:S(2)}, u32[]{:S(2)}) collective-permute-start(bf16[4,32,256]{2,1,0:T(8,128)(2,1)} %get-tuple-element.75), channel_id=1, source_target_pairs={{0,9},{1,8},{2,11},{3,10},{4,13},{5,12},{6,15},{7,14},{8,1},{9,0},... | collective-permute-start | bytes 196616 | tf_op jit(solution)/shard_map/ppermute | solution.py:319
  49.0 11.0 %collective-permute-start.9 = (bf16[4,32,256]{2,1,0:T(8,128)(2,1)}, bf16[4,32,256]{2,1,0:T(8,128)(2,1)S(1)}, u32[]{:S(2)}, u32[]{:S(2)}) collective-permute-start(bf16[4,32,256]{2,1,0:T(8,128)(2,1)} %get-tuple-element.78), channel_id=1, source_target_pairs={{0,10},{1,11},{2,8},{3,9},{4,14},{5,15},{6,12},{7,13},{8,2},{9,3},... | collective-permute-start | bytes 196616 | tf_op jit(solution)/shard_map/ppermute | solution.py:319
  50.4 22.1 %copy-start = (bf16[4,32,256]{2,1,0:T(8,128)(2,1)S(1)}, bf16[4,32,256]{2,1,0:T(8,128)(2,1)}, u32[]{:S(2)}) copy-start(bf16[4,32,256]{2,1,0:T(8,128)(2,1)} %get-tuple-element.49.refs_1_) | copy-start | bytes 196612
  51.1 12.2 %collective-permute-start.10 = (bf16[4,32,256]{2,1,0:T(8,128)(2,1)}, bf16[4,32,256]{2,1,0:T(8,128)(2,1)}, u32[]{:S(2)}, u32[]{:S(2)}) collective-permute-start(bf16[4,32,256]{2,1,0:T(8,128)(2,1)} %get-tuple-element.80), channel_id=1, source_target_pairs={{0,11},{1,10},{2,9},{3,8},{4,15},{5,14},{6,13},{7,12},{8,3},{9,2},... | collective-permute-start | bytes 196616 | tf_op jit(solution)/shard_map/ppermute | solution.py:319
  54.0 11.8 %collective-permute-start.11 = (bf16[4,32,256]{2,1,0:T(8,128)(2,1)}, bf16[4,32,256]{2,1,0:T(8,128)(2,1)}, u32[]{:S(2)}, u32[]{:S(2)}) collective-permute-start(bf16[4,32,256]{2,1,0:T(8,128)(2,1)} %get-tuple-element.81), channel_id=1, source_target_pairs={{0,12},{1,13},{2,14},{3,15},{4,8},{5,9},{6,10},{7,11},{8,4},{9,5},... | collective-permute-start | bytes 196616 | tf_op jit(solution)/shard_map/ppermute | solution.py:319
  54.6 12.1 %collective-permute-start.12 = (bf16[4,32,256]{2,1,0:T(8,128)(2,1)}, bf16[4,32,256]{2,1,0:T(8,128)(2,1)}, u32[]{:S(2)}, u32[]{:S(2)}) collective-permute-start(bf16[4,32,256]{2,1,0:T(8,128)(2,1)} %get-tuple-element.82), channel_id=1, source_target_pairs={{0,13},{1,12},{2,15},{3,14},{4,9},{5,8},{6,11},{7,10},{8,5},{9,4},... | collective-permute-start | bytes 196616 | tf_op jit(solution)/shard_map/ppermute | solution.py:319
  57.3 13.9 %collective-permute-start.13 = (bf16[4,32,256]{2,1,0:T(8,128)(2,1)}, bf16[4,32,256]{2,1,0:T(8,128)(2,1)}, u32[]{:S(2)}, u32[]{:S(2)}) collective-permute-start(bf16[4,32,256]{2,1,0:T(8,128)(2,1)} %get-tuple-element.83), channel_id=1, source_target_pairs={{0,14},{1,15},{2,12},{3,13},{4,10},{5,11},{6,8},{7,9},{8,6},{9,7},... | collective-permute-start | bytes 196616 | tf_op jit(solution)/shard_map/ppermute | solution.py:319
  60.6 11.9 %collective-permute-start.14 = (bf16[4,32,256]{2,1,0:T(8,128)(2,1)}, bf16[4,32,256]{2,1,0:T(8,128)(2,1)}, u32[]{:S(2)}, u32[]{:S(2)}) collective-permute-start(bf16[4,32,256]{2,1,0:T(8,128)(2,1)} %get-tuple-element.84), channel_id=1, source_target_pairs={{0,15},{1,14},{2,13},{3,12},{4,11},{5,10},{6,9},{7,8},{8,7},{9,6},... | collective-permute-start | bytes 196616 | tf_op jit(solution)/shard_map/ppermute | solution.py:319
  61.7 10.9 %copy-start.6 = (bf16[4,32,256]{2,1,0:T(8,128)(2,1)S(1)}, bf16[4,32,256]{2,1,0:T(8,128)(2,1)}, u32[]{:S(2)}) copy-start(bf16[4,32,256]{2,1,0:T(8,128)(2,1)} %copy-done.5) | copy-start | bytes 196612
  61.7 10.9 %copy-start.8 = (bf16[4,32,256]{2,1,0:T(8,128)(2,1)S(1)}, bf16[4,32,256]{2,1,0:T(8,128)(2,1)}, u32[]{:S(2)}) copy-start(bf16[4,32,256]{2,1,0:T(8,128)(2,1)} %copy-done.7) | copy-start | bytes 196612
  61.7 10.9 %copy-start.10 = (bf16[4,32,256]{2,1,0:T(8,128)(2,1)S(1)}, bf16[4,32,256]{2,1,0:T(8,128)(2,1)}, u32[]{:S(2)}) copy-start(bf16[4,32,256]{2,1,0:T(8,128)(2,1)} %copy-done.9) | copy-start | bytes 196612
  (7 other events, 24.9 us)

commit v6 on v5

--- a/solution.py
+++ b/solution.py
@@ -21,7 +21,7 @@
 LANES = 128
 WIDE = 2 * AVG
 WIDTH = SPECTRA * AVG
-GROUP = 4
+GROUP = 2
 STEP = 8
 ROWS = 16
 WINDOW = 5
@@ -44,7 +44,8 @@
     stage = np.zeros((2, AVG, blocks, 2))
     stage[0, :, :, 0], stage[0, :, :, 1] = cos, sin
     stage[1, :, :, 0], stage[1, :, :, 1] = -sin, cos
-    stage = np.kron(np.eye(GROUP), stage.reshape(2 * AVG, 2 * blocks))
+    stage = np.stack(split(stage), axis=1).reshape(4 * AVG, 2 * blocks)
+    stage = np.concatenate([np.kron(np.eye(GROUP), stage.astype(np.float32))] * 2, axis=1).astype(ml_dtypes.bfloat16)
     angle = 2.0 * math.pi * np.outer(np.arange(AVG), np.arange(LANES)) / NCHAN
     turn = np.stack([np.cos(angle), -np.sin(angle)]).astype(np.float32)
     first = (NCHAN - all_out * AVG) // 2
@@ -56,7 +57,8 @@
     last[1, :, :, 0], last[1, :, :, 1] = sin, cos
     beside = max(1, LANES // (2 * all_out))
     last = np.kron(np.eye(beside), last.reshape(2 * LANES, 2 * all_out))
-    return np.concatenate(split(stage)), turn, np.concatenate(split(last), axis=1)
+    last = np.concatenate(split(last), axis=1)
+    return stage, turn, np.concatenate([last, last])
 
 
 def halves(values):
@@ -70,10 +72,10 @@
     out_refs, refs = refs[: max(partners, 1)], refs[max(partners, 1) :]
     (coeff_ref, held_ref), refs = refs[:2], refs[2:]
     groups = STEP // GROUP
-    high_refs, low_refs, turned_refs = [refs[i * groups : (i + 1) * groups] for i in range(3)]
+    halves_refs, turned_refs = refs[:groups], refs[groups:]
     outer, inner = pl.program_id(0), pl.program_id(1)
     size = GROUP * WIDE
-    beside = last_ref.shape[0] // (2 * LANES)
+    beside = last_ref.shape[0] // (4 * LANES)
     columns = beside * outs
 
     @pl.when((outer == 0) & (inner == 0))
@@ -91,34 +93,30 @@
             value = coeffs[0] * samples[m]
             for j in range(1, TAPS):
                 value = value + coeffs[j] * samples[m + j]
-            high, low = halves(value)
-            place = (slice(u * WIDE + r, u * WIDE + r + 16), slice(m * LANES, (m + 1) * LANES))
-            high_refs[g][place] = high
-            low_refs[g][place] = low
+            for part, kept in enumerate(halves(value)):
+                row = part * size + u * WIDE + r
+                halves_refs[g][row : row + 16, m * LANES : (m + 1) * LANES] = kept
 
     def first_part(g, start):
         lanes = slice(start * LANES, (start + 2) * LANES)
-        both = jnp.dot(stage_ref[...], high_refs[g][:, lanes], preferred_element_type=F32)
-        rest = jnp.dot(stage_ref[:size, :], low_refs[g][:, lanes], preferred_element_type=F32)
-        section = both[:size] + (both[size:] + rest)
+        section = jnp.dot(stage_ref[...], halves_refs[g][:, lanes], preferred_element_type=F32)
         turn_real, turn_imag = turn_ref[0], turn_ref[1]
         for u in range(GROUP):
             pair, place = divmod(u, beside)
             for m in range(start, start + 2):
                 at = slice((m - start) * LANES, (m - start + 1) * LANES)
-                real = section[u * WIDE : u * WIDE + AVG, at]
-                imag = section[u * WIDE + AVG : (u + 1) * WIDE, at]
+                blocks = [section[(4 * u + i) * AVG : (4 * u + i + 1) * AVG, at] for i in range(4)]
+                real, imag = blocks[0] + blocks[1], blocks[2] + blocks[3]
+                row = pair * WIDTH + m * AVG
                 for ri, value in enumerate((real * turn_real - imag * turn_imag, real * turn_imag + imag * turn_real)):
-                    where = slice((2 * place + ri) * LANES, (2 * place + ri + 1) * LANES)
                     for part, kept in enumerate(halves(value)):
-                        row = (2 * pair + part) * WIDTH + m * AVG
-                        turned_refs[g][row : row + AVG, where] = kept
+                        lane = ((part * beside + place) * 2 + ri) * LANES
+                        turned_refs[g][row : row + AVG, lane : lane + LANES] = kept
 
     def last_part(g, pair):
-        rows = slice(2 * pair * WIDTH, 2 * (pair + 1) * WIDTH)
+        rows = slice(pair * WIDTH, (pair + 1) * WIDTH)
         product = jnp.dot(turned_refs[g][rows, :], last_ref[...], preferred_element_type=F32)
-        found = product[:WIDTH, :columns] + (product[:WIDTH, columns:] + product[WIDTH:, :columns])
-        found = found.T
+        found = (product[:, :columns] + product[:, columns:]).T
         for place in range(beside):
             stream = g * GROUP + pair * beside + place
             factor = gain_ref[(first_stream + outer * ROWS + inner * STEP + stream) // 2]
@@ -172,8 +170,8 @@
             pltpu.VMEM((TAPS, WIDE, LANES), F32),
             pltpu.VMEM((WIDTH // LANES, ROWS * outs, LANES), F32),
         ]
-        + [pltpu.VMEM((GROUP * WIDE, SPECTRA * LANES), BF16)] * (2 * groups)
-        + [pltpu.VMEM((2 * GROUP * WIDTH * 2 * LANES // last.shape[0], last.shape[0]), BF16)] * groups,
+        + [pltpu.VMEM((2 * GROUP * WIDE, SPECTRA * LANES), BF16)] * groups
+        + [pltpu.VMEM((4 * GROUP * WIDTH * LANES // last.shape[0], last.shape[0]), BF16)] * groups,
         compiler_params=pltpu.CompilerParams(vmem_limit_bytes=VMEM_LIMIT),
         cost_estimate=pl.CostEstimate(
             flops=(stop - start) * SPECTRA * 12_000_000,
@@ -296,7 +294,7 @@
     samples = voltages.reshape(streams, 2, FRAMES * blocks, LANES).transpose(0, 2, 1, 3)
     samples = samples.reshape(streams, FRAMES, 2 * blocks, LANES)
     coeffs = taps.reshape(TAPS, blocks, LANES).transpose(1, 0, 2).reshape(TAPS * blocks, LANES)
-    cut = streams - streams // (2 * ROWS) * ROWS
+    cut = min(streams, ROWS)
     wanted = (2 * station_order[:, None] + jnp.arange(2, dtype=jnp.int32)).reshape(-1, 1)
 
     def pick(start, stop, first):

time: 79.3 us -> 89.7 us (1.13)
  waiting for transfers between devices: 9.34 us -> 23.1 us
  starting transfers between devices: 27.4 us -> 25.3 us
  local copies, waits for them, and re-layouts: 3.33 us -> 1.48 us
    ppermute x15, waiting for transfers between devices: 9.33 us -> 23.1 us  [body(): lax.ppermute(ready, 'ingest', [(i, i ^ k) for i in range(devices)])]
    ppermute x15, starting transfers between devices: 20.8 us -> 18.7 us  [body(): lax.ppermute(ready, 'ingest', [(i, i ^ k) for i in range(devices)])]
    unnamed x30 -> x18, local copies, waits for them, and re-layouts: 3.16 us -> 1.31 us
  transfers between devices with their start and end apart: 16 -> 16, of which waited for: 4 -> 7; matrix products, arithmetic and copies ran while one was open for 1% -> 1% of each run, Pallas kernels for 21% -> 25%
where the time goes in v6:
time: 89.7 us; the launch traced here: 88.6 us
  Pallas kernels  37.9 us (42%)
  starting transfers between devices  25.3 us (28%)
  waiting for transfers between devices  23.1 us (26%)
  local copies, waits for them, and re-layouts  1.48 us (2%)
    pallas_call x2, Pallas kernels, spectra(): pl.pallas_call(functools.partial(spectra_kernel, start, partners, outs),...  29.9 us
    ppermute x15, waiting for transfers between devices, body(): lax.ppermute(ready, 'ingest', [(i, i ^ k) for i in range(devices)])  23.1 us
    ppermute x15, starting transfers between devices, body(): lax.ppermute(ready, 'ingest', [(i, i ^ k) for i in range(devices)])  18.7 us
    pallas_call x1, Pallas kernels, tiles(): pl.pallas_call(functools.partial(tiles_kernel, len(parts)), out_shape=jax...  7.08 us
    all_to_all x1, starting transfers between devices, body(): lax.all_to_all(packed, 'ingest', split_axis=0, concat_axis=0, tiled=True)  6.63 us
  transfers between devices with their start and end apart: 16, of which 7 were waited for; matrix products, arithmetic and copies ran while one was open for 1% of the time, Pallas kernels for 25%

profile of v6, /device:TPU:11, one launch (start us, length us, event | category | flops | bytes accessed | tf_op | source)
XLA Modules:
  0.0 88.6 jit_solution(15204394517697121363)
XLA Ops:
  0.0 8.6 %spectra.2 = bf16[64,16,256]{2,1,0:T(8,128)(2,1)} custom-call(f32[32]{0:T(128)} %gain_ref.2, s32[64,11,64,128]{3,2,1,0:T(8,128)} %bitcast.11, s32[64,11,64,128]{3,2,1,0:T(8,128)} %bitcast.12, s32[64,11,64,128]{3,2,1,0:T(8,128)} %bitcast.13, s32[64,11,64,128]{3,2,1,0:T(8,128)} %bitcast.14, s32[64,11,64,128]{3,2,1,0:T(8,128)} %bitcast.15, ...), custom_call_target="tpu_custom_call" | custom-call | flops 1536000000 | bytes 5767168 | tf_op jit(solution)/shard_map/spectra/pallas_call | solution.py:161
  8.6 6.6 %all-to-all-start = ((bf16[16,4,16,256]{3,2,1,0:T(8,128)(2,1)}), bf16[16,4,16,256]{3,2,1,0:T(8,128)(2,1)S(1)}, u32[]{:S(2)}, u32[]{:S(2)}) async-start(bf16[16,4,16,256]{3,2,1,0:T(8,128)(2,1)} %bitcast.33), calls=%async_computation | async-start | bytes 1048576 | tf_op jit(solution)/shard_map/all_to_all | solution.py:308
  15.3 21.3 %spectra.3 = (bf16[4,48,256]{2,1,0:T(8,128)(2,1)}, bf16[4,48,256]{2,1,0:T(8,128)(2,1)}, bf16[4,48,256]{2,1,0:T(8,128)(2,1)}, bf16[4,48,256]{2,1,0:T(8,128)(2,1)}...) custom-call(f32[32]{0:T(128)} %gain_ref.2, ...), custom_call_target="tpu_custom_call" | custom-call | flops 4608000000 | bytes 17301504 | tf_op jit(solution)/shard_map/spectra/pallas_call | solution.py:161
  36.6 0.4 collective-permute-start
  37.0 1.2 %collective-permute-start.1 = (bf16[4,48,256]{2,1,0:T(8,128)(2,1)}, bf16[4,48,256]{2,1,0:T(8,128)(2,1)S(1)}, u32[]{:S(2)}, u32[]{:S(2)}) collective-permute-start(bf16[4,48,256]{2,1,0:T(8,128)(2,1)} %get-tuple-element.54), channel_id=1, source_target_pairs={{0,2},{1,3},{2,0},{3,1},{4,6},{5,7},{6,4},{7,5},{8,10},{9,11},{10,... | collective-permute-start | bytes 294920 | tf_op jit(solution)/shard_map/ppermute | solution.py:317
  38.2 0.6 collective-permute-start.2
  38.8 1.6 %collective-permute-start.4 = (bf16[4,48,256]{2,1,0:T(8,128)(2,1)}, bf16[4,48,256]{2,1,0:T(8,128)(2,1)S(1)}, u32[]{:S(2)}, u32[]{:S(2)}) collective-permute-start(bf16[4,48,256]{2,1,0:T(8,128)(2,1)} %get-tuple-element.63), channel_id=1, source_target_pairs={{0,5},{1,4},{2,7},{3,6},{4,1},{5,0},{6,3},{7,2},{8,13},{9,12},{10,... | collective-permute-start | bytes 294920 | tf_op jit(solution)/shard_map/ppermute | solution.py:317
  41.2 1.2 %collective-permute-start.5 = (bf16[4,48,256]{2,1,0:T(8,128)(2,1)}, bf16[4,48,256]{2,1,0:T(8,128)(2,1)S(1)}, u32[]{:S(2)}, u32[]{:S(2)}) collective-permute-start(bf16[4,48,256]{2,1,0:T(8,128)(2,1)} %get-tuple-element.66), channel_id=1, source_target_pairs={{0,6},{1,7},{2,4},{3,5},{4,2},{5,3},{6,0},{7,1},{8,14},{9,15},{10,... | collective-permute-start | bytes 294920 | tf_op jit(solution)/shard_map/ppermute | solution.py:317
  42.4 1.6 %collective-permute-start.6 = (bf16[4,48,256]{2,1,0:T(8,128)(2,1)}, bf16[4,48,256]{2,1,0:T(8,128)(2,1)S(1)}, u32[]{:S(2)}, u32[]{:S(2)}) collective-permute-start(bf16[4,48,256]{2,1,0:T(8,128)(2,1)} %get-tuple-element.69), channel_id=1, source_target_pairs={{0,7},{1,6},{2,5},{3,4},{4,3},{5,2},{6,1},{7,0},{8,15},{9,14},{10,... | collective-permute-start | bytes 294920 | tf_op jit(solution)/shard_map/ppermute | solution.py:317
  44.1 2.1 %collective-permute-start.7 = (bf16[4,48,256]{2,1,0:T(8,128)(2,1)}, bf16[4,48,256]{2,1,0:T(8,128)(2,1)S(1)}, u32[]{:S(2)}, u32[]{:S(2)}) collective-permute-start(bf16[4,48,256]{2,1,0:T(8,128)(2,1)} %get-tuple-element.72), channel_id=1, source_target_pairs={{0,8},{1,9},{2,10},{3,11},{4,12},{5,13},{6,14},{7,15},{8,0},{9,1},... | collective-permute-start | bytes 294920 | tf_op jit(solution)/shard_map/ppermute | solution.py:317
  46.2 0.4 collective-permute-start.8
  46.6 2.9 %collective-permute-start.9 = (bf16[4,48,256]{2,1,0:T(8,128)(2,1)}, bf16[4,48,256]{2,1,0:T(8,128)(2,1)S(1)}, u32[]{:S(2)}, u32[]{:S(2)}) collective-permute-start(bf16[4,48,256]{2,1,0:T(8,128)(2,1)} %get-tuple-element.78), channel_id=1, source_target_pairs={{0,10},{1,11},{2,8},{3,9},{4,14},{5,15},{6,12},{7,13},{8,2},{9,3},... | collective-permute-start | bytes 294920 | tf_op jit(solution)/shard_map/ppermute | solution.py:317
  49.8 4.2 %collective-permute-start.10 = (bf16[4,48,256]{2,1,0:T(8,128)(2,1)}, bf16[4,48,256]{2,1,0:T(8,128)(2,1)}, u32[]{:S(2)}, u32[]{:S(2)}) collective-permute-start(bf16[4,48,256]{2,1,0:T(8,128)(2,1)} %get-tuple-element.80), channel_id=1, source_target_pairs={{0,11},{1,10},{2,9},{3,8},{4,15},{5,14},{6,13},{7,12},{8,3},{9,2},... | collective-permute-start | bytes 294920 | tf_op jit(solution)/shard_map/ppermute | solution.py:317
  54.3 8.4 %collective-permute-done.8.refs_10_ = bf16[4,48,256]{2,1,0:T(8,128)(2,1)S(1)} collective-permute-done((bf16[4,48,256]{2,1,0:T(8,128)(2,1)}, bf16[4,48,256]{2,1,0:T(8,128)(2,1)S(1)}, u32[]{:S(2)}, u32[]{:S(2)}) %collective-permute-start.8) | collective-permute-done | bytes 98336 | tf_op jit(solution)/shard_map/ppermute | solution.py:317
  62.6 0.6 copy-done.1
  63.3 1.5 %collective-permute-done.9.refs_11_ = bf16[4,48,256]{2,1,0:T(8,128)(2,1)S(1)} collective-permute-done((bf16[4,48,256]{2,1,0:T(8,128)(2,1)}, bf16[4,48,256]{2,1,0:T(8,128)(2,1)S(1)}, u32[]{:S(2)}, u32[]{:S(2)}) %collective-permute-start.9) | collective-permute-done | bytes 98336 | tf_op jit(solution)/shard_map/ppermute | solution.py:317
  64.7 0.6 copy-done.3
  65.4 2.0 %collective-permute-start.14 = (bf16[4,48,256]{2,1,0:T(8,128)(2,1)}, bf16[4,48,256]{2,1,0:T(8,128)(2,1)}, u32[]{:S(2)}, u32[]{:S(2)}) collective-permute-start(bf16[4,48,256]{2,1,0:T(8,128)(2,1)} %get-tuple-element.84), channel_id=1, source_target_pairs={{0,15},{1,14},{2,13},{3,12},{4,11},{5,10},{6,9},{7,8},{8,7},{9,6},... | collective-permute-start | bytes 294920 | tf_op jit(solution)/shard_map/ppermute | solution.py:317
  67.3 0.9 %arrange.1 = (bf16[2,1024,512]{2,1,0:T(8,128)(2,1)S(1)}, f32[2,8,128]{2,1,0:T(8,128)S(1)}) custom-call(bf16[1024,256]{1,0:T(8,128)(2,1)S(1)} %compare_convert_fusion.1.pick_ref, bf16[16,4,16,256]{3,2,1,0:T(8,128)(2,1)S(1)} %all-to-all-done.part_ref), custom_call_target="tpu_custom_call" | custom-call | flops 1100000000 | bytes 4000000 | tf_op jit(solution)/shard_map/arrange/pallas_call | solution.py:203
  68.3 3.7 %collective-permute-done.11.refs_13_ = bf16[4,48,256]{2,1,0:T(8,128)(2,1)} collective-permute-done((bf16[4,48,256]{2,1,0:T(8,128)(2,1)}, bf16[4,48,256]{2,1,0:T(8,128)(2,1)}, u32[]{:S(2)}, u32[]{:S(2)}) %collective-permute-start.11) | collective-permute-done | bytes 98336 | tf_op jit(solution)/shard_map/ppermute | solution.py:317
  72.0 6.1 %collective-permute-done.12.refs_14_ = bf16[4,48,256]{2,1,0:T(8,128)(2,1)} collective-permute-done((bf16[4,48,256]{2,1,0:T(8,128)(2,1)}, bf16[4,48,256]{2,1,0:T(8,128)(2,1)}, u32[]{:S(2)}, u32[]{:S(2)}) %collective-permute-start.12) | collective-permute-done | bytes 98336 | tf_op jit(solution)/shard_map/ppermute | solution.py:317
  78.1 1.2 %collective-permute-done.13.refs_15_ = bf16[4,48,256]{2,1,0:T(8,128)(2,1)} collective-permute-done((bf16[4,48,256]{2,1,0:T(8,128)(2,1)}, bf16[4,48,256]{2,1,0:T(8,128)(2,1)}, u32[]{:S(2)}, u32[]{:S(2)}) %collective-permute-start.13) | collective-permute-done | bytes 98336 | tf_op jit(solution)/shard_map/ppermute | solution.py:317
  79.3 2.3 %collective-permute-done.14.refs_16_ = bf16[4,48,256]{2,1,0:T(8,128)(2,1)} collective-permute-done((bf16[4,48,256]{2,1,0:T(8,128)(2,1)}, bf16[4,48,256]{2,1,0:T(8,128)(2,1)}, u32[]{:S(2)}, u32[]{:S(2)}) %collective-permute-start.14) | collective-permute-done | bytes 98336 | tf_op jit(solution)/shard_map/ppermute | solution.py:317
  81.5 7.1 %tiles.1 = bf16[2,36,2,128,128]{4,3,2,1,0:T(8,128)(2,1)} custom-call(bf16[2,1024,512]{2,1,0:T(8,128)(2,1)S(1)} %get-tuple-element.46.early_ref, f32[2,8,128]{2,1,0:T(8,128)S(1)} %get-tuple-element.47.power_ref, bf16[1024,768]{1,0:T(8,128)(2,1)S(1)} %compare_convert_fusion.refs_0_, bf16[4,48,256]{2,1,0:T(8,128)(2,1)S(1)} %copy-done, ...), custom_call_target="tpu_custom_call" | custom-call | flops 4499999744 | bytes 9000000 | tf_op jit(solution)/shard_map/tiles/pallas_call | solution.py:267
  (36 shorter events, 1.3 us)
Async XLA Ops:
  8.6 58.7 %all-to-all-start = ((bf16[16,4,16,256]{3,2,1,0:T(8,128)(2,1)}), bf16[16,4,16,256]{3,2,1,0:T(8,128)(2,1)S(1)}, u32[]{:S(2)}, u32[]{:S(2)}) async-start(bf16[16,4,16,256]{3,2,1,0:T(8,128)(2,1)} %bitcast.33), calls=%async_computation | async-start | bytes 1048576 | tf_op jit(solution)/shard_map/all_to_all | solution.py:308
  15.2 25.3 %copy-start.7 = (s32[512]{0:T(512)S(1)}, s32[512]{0:T(512)}, u32[]{:S(2)}) copy-start(s32[512]{0:T(512)} %param.14) | copy-start | bytes 6148
  15.2 25.6 %copy-start.5 = (s32[768]{0:T(1024)S(1)}, s32[768]{0:T(1024)}, u32[]{:S(2)}) copy-start(s32[768]{0:T(1024)} %constant.29.clone) | copy-start | bytes 9220
  15.2 25.6 %copy-start.6 = (s32[768]{0:T(1024)S(1)}, s32[768]{0:T(1024)}, u32[]{:S(2)}) copy-start(s32[768]{0:T(1024)} %constant.28.clone) | copy-start | bytes 9220
  15.3 34.3 %copy-start.8 = (s32[256]{0:T(256)S(1)}, s32[256]{0:T(256)}, u32[]{:S(2)}) copy-start(s32[256]{0:T(256)} %constant.33) | copy-start | bytes 3076
  36.6 4.6 %collective-permute-start = (bf16[4,48,256]{2,1,0:T(8,128)(2,1)}, bf16[4,48,256]{2,1,0:T(8,128)(2,1)S(1)}, u32[]{:S(2)}, u32[]{:S(2)}) collective-permute-start(bf16[4,48,256]{2,1,0:T(8,128)(2,1)} %get-tuple-element.51), channel_id=1, source_target_pairs={{0,1},{1,0},{2,3},{3,2},{4,5},{5,4},{6,7},{7,6},{8,9},{9,8},{10,11... | collective-permute-start | bytes 294920 | tf_op jit(solution)/shard_map/ppermute | solution.py:317
  37.0 5.4 %collective-permute-start.1 = (bf16[4,48,256]{2,1,0:T(8,128)(2,1)}, bf16[4,48,256]{2,1,0:T(8,128)(2,1)S(1)}, u32[]{:S(2)}, u32[]{:S(2)}) collective-permute-start(bf16[4,48,256]{2,1,0:T(8,128)(2,1)} %get-tuple-element.54), channel_id=1, source_target_pairs={{0,2},{1,3},{2,0},{3,1},{4,6},{5,7},{6,4},{7,5},{8,10},{9,11},{10,... | collective-permute-start | bytes 294920 | tf_op jit(solution)/shard_map/ppermute | solution.py:317
  38.2 6.0 %collective-permute-start.2 = (bf16[4,48,256]{2,1,0:T(8,128)(2,1)}, bf16[4,48,256]{2,1,0:T(8,128)(2,1)S(1)}, u32[]{:S(2)}, u32[]{:S(2)}) collective-permute-start(bf16[4,48,256]{2,1,0:T(8,128)(2,1)} %get-tuple-element.57), channel_id=1, source_target_pairs={{0,3},{1,2},{2,1},{3,0},{4,7},{5,6},{6,5},{7,4},{8,11},{9,10},{10,... | collective-permute-start | bytes 294920 | tf_op jit(solution)/shard_map/ppermute | solution.py:317
  38.8 7.4 %collective-permute-start.3 = (bf16[4,48,256]{2,1,0:T(8,128)(2,1)}, bf16[4,48,256]{2,1,0:T(8,128)(2,1)S(1)}, u32[]{:S(2)}, u32[]{:S(2)}) collective-permute-start(bf16[4,48,256]{2,1,0:T(8,128)(2,1)} %get-tuple-element.60), channel_id=1, source_target_pairs={{0,4},{1,5},{2,6},{3,7},{4,0},{5,1},{6,2},{7,3},{8,12},{9,13},{10,... | collective-permute-start | bytes 294920 | tf_op jit(solution)/shard_map/ppermute | solution.py:317
  38.8 7.8 %collective-permute-start.4 = (bf16[4,48,256]{2,1,0:T(8,128)(2,1)}, bf16[4,48,256]{2,1,0:T(8,128)(2,1)S(1)}, u32[]{:S(2)}, u32[]{:S(2)}) collective-permute-start(bf16[4,48,256]{2,1,0:T(8,128)(2,1)} %get-tuple-element.63), channel_id=1, source_target_pairs={{0,5},{1,4},{2,7},{3,6},{4,1},{5,0},{6,3},{7,2},{8,13},{9,12},{10,... | collective-permute-start | bytes 294920 | tf_op jit(solution)/shard_map/ppermute | solution.py:317
  40.8 40.7 %copy-start = (bf16[4,48,256]{2,1,0:T(8,128)(2,1)S(1)}, bf16[4,48,256]{2,1,0:T(8,128)(2,1)}, u32[]{:S(2)}) copy-start(bf16[4,48,256]{2,1,0:T(8,128)(2,1)} %get-tuple-element.49.refs_1_) | copy-start | bytes 294916
  41.2 8.6 %collective-permute-start.5 = (bf16[4,48,256]{2,1,0:T(8,128)(2,1)}, bf16[4,48,256]{2,1,0:T(8,128)(2,1)S(1)}, u32[]{:S(2)}, u32[]{:S(2)}) collective-permute-start(bf16[4,48,256]{2,1,0:T(8,128)(2,1)} %get-tuple-element.66), channel_id=1, source_target_pairs={{0,6},{1,7},{2,4},{3,5},{4,2},{5,3},{6,0},{7,1},{8,14},{9,15},{10,... | collective-permute-start | bytes 294920 | tf_op jit(solution)/shard_map/ppermute | solution.py:317
  42.4 11.6 %collective-permute-start.6 = (bf16[4,48,256]{2,1,0:T(8,128)(2,1)}, bf16[4,48,256]{2,1,0:T(8,128)(2,1)S(1)}, u32[]{:S(2)}, u32[]{:S(2)}) collective-permute-start(bf16[4,48,256]{2,1,0:T(8,128)(2,1)} %get-tuple-element.69), channel_id=1, source_target_pairs={{0,7},{1,6},{2,5},{3,4},{4,3},{5,2},{6,1},{7,0},{8,15},{9,14},{10,... | collective-permute-start | bytes 294920 | tf_op jit(solution)/shard_map/ppermute | solution.py:317
  44.1 9.9 %collective-permute-start.7 = (bf16[4,48,256]{2,1,0:T(8,128)(2,1)}, bf16[4,48,256]{2,1,0:T(8,128)(2,1)S(1)}, u32[]{:S(2)}, u32[]{:S(2)}) collective-permute-start(bf16[4,48,256]{2,1,0:T(8,128)(2,1)} %get-tuple-element.72), channel_id=1, source_target_pairs={{0,8},{1,9},{2,10},{3,11},{4,12},{5,13},{6,14},{7,15},{8,0},{9,1},... | collective-permute-start | bytes 294920 | tf_op jit(solution)/shard_map/ppermute | solution.py:317
  46.2 16.4 %collective-permute-start.8 = (bf16[4,48,256]{2,1,0:T(8,128)(2,1)}, bf16[4,48,256]{2,1,0:T(8,128)(2,1)S(1)}, u32[]{:S(2)}, u32[]{:S(2)}) collective-permute-start(bf16[4,48,256]{2,1,0:T(8,128)(2,1)} %get-tuple-element.75), channel_id=1, source_target_pairs={{0,9},{1,8},{2,11},{3,10},{4,13},{5,12},{6,15},{7,14},{8,1},{9,0},... | collective-permute-start | bytes 294920 | tf_op jit(solution)/shard_map/ppermute | solution.py:317
  46.6 18.1 %collective-permute-start.9 = (bf16[4,48,256]{2,1,0:T(8,128)(2,1)}, bf16[4,48,256]{2,1,0:T(8,128)(2,1)S(1)}, u32[]{:S(2)}, u32[]{:S(2)}) collective-permute-start(bf16[4,48,256]{2,1,0:T(8,128)(2,1)} %get-tuple-element.78), channel_id=1, source_target_pairs={{0,10},{1,11},{2,8},{3,9},{4,14},{5,15},{6,12},{7,13},{8,2},{9,3},... | collective-permute-start | bytes 294920 | tf_op jit(solution)/shard_map/ppermute | solution.py:317
  49.8 18.6 %collective-permute-start.10 = (bf16[4,48,256]{2,1,0:T(8,128)(2,1)}, bf16[4,48,256]{2,1,0:T(8,128)(2,1)}, u32[]{:S(2)}, u32[]{:S(2)}) collective-permute-start(bf16[4,48,256]{2,1,0:T(8,128)(2,1)} %get-tuple-element.80), channel_id=1, source_target_pairs={{0,11},{1,10},{2,9},{3,8},{4,15},{5,14},{6,13},{7,12},{8,3},{9,2},... | collective-permute-start | bytes 294920 | tf_op jit(solution)/shard_map/ppermute | solution.py:317
  54.0 18.0 %collective-permute-start.11 = (bf16[4,48,256]{2,1,0:T(8,128)(2,1)}, bf16[4,48,256]{2,1,0:T(8,128)(2,1)}, u32[]{:S(2)}, u32[]{:S(2)}) collective-permute-start(bf16[4,48,256]{2,1,0:T(8,128)(2,1)} %get-tuple-element.81), channel_id=1, source_target_pairs={{0,12},{1,13},{2,14},{3,15},{4,8},{5,9},{6,10},{7,11},{8,4},{9,5},... | collective-permute-start | bytes 294920 | tf_op jit(solution)/shard_map/ppermute | solution.py:317
  54.0 24.1 %collective-permute-start.12 = (bf16[4,48,256]{2,1,0:T(8,128)(2,1)}, bf16[4,48,256]{2,1,0:T(8,128)(2,1)}, u32[]{:S(2)}, u32[]{:S(2)}) collective-permute-start(bf16[4,48,256]{2,1,0:T(8,128)(2,1)} %get-tuple-element.82), channel_id=1, source_target_pairs={{0,13},{1,12},{2,15},{3,14},{4,9},{5,8},{6,11},{7,10},{8,5},{9,4},... | collective-permute-start | bytes 294920 | tf_op jit(solution)/shard_map/ppermute | solution.py:317
  62.6 0.6 copy-start.1
  63.3 16.0 %collective-permute-start.13 = (bf16[4,48,256]{2,1,0:T(8,128)(2,1)}, bf16[4,48,256]{2,1,0:T(8,128)(2,1)}, u32[]{:S(2)}, u32[]{:S(2)}) collective-permute-start(bf16[4,48,256]{2,1,0:T(8,128)(2,1)} %get-tuple-element.83), channel_id=1, source_target_pairs={{0,14},{1,15},{2,12},{3,13},{4,10},{5,11},{6,8},{7,9},{8,6},{9,7},... | collective-permute-start | bytes 294920 | tf_op jit(solution)/shard_map/ppermute | solution.py:317
  65.4 16.1 %collective-permute-start.14 = (bf16[4,48,256]{2,1,0:T(8,128)(2,1)}, bf16[4,48,256]{2,1,0:T(8,128)(2,1)}, u32[]{:S(2)}, u32[]{:S(2)}) collective-permute-start(bf16[4,48,256]{2,1,0:T(8,128)(2,1)} %get-tuple-element.84), channel_id=1, source_target_pairs={{0,15},{1,14},{2,13},{3,12},{4,11},{5,10},{6,9},{7,8},{8,7},{9,6},... | collective-permute-start | bytes 294920 | tf_op jit(solution)/shard_map/ppermute | solution.py:317
  67.3 14.2 %copy-start.2 = (bf16[4,48,256]{2,1,0:T(8,128)(2,1)S(1)}, bf16[4,48,256]{2,1,0:T(8,128)(2,1)}, u32[]{:S(2)}) copy-start(bf16[4,48,256]{2,1,0:T(8,128)(2,1)} %copy-done.1) | copy-start | bytes 294916
  67.3 14.2 %copy-start.4 = (bf16[4,48,256]{2,1,0:T(8,128)(2,1)S(1)}, bf16[4,48,256]{2,1,0:T(8,128)(2,1)}, u32[]{:S(2)}) copy-start(bf16[4,48,256]{2,1,0:T(8,128)(2,1)} %copy-done.3) | copy-start | bytes 294916
  (1 other events, 0.6 us)

commit v7 on v6

--- a/solution.py
+++ b/solution.py
@@ -97,9 +97,11 @@
                 row = part * size + u * WIDE + r
                 halves_refs[g][row : row + 16, m * LANES : (m + 1) * LANES] = kept
 
-    def first_part(g, start):
+    def first_product(g, start):
         lanes = slice(start * LANES, (start + 2) * LANES)
-        section = jnp.dot(stage_ref[...], halves_refs[g][:, lanes], preferred_element_type=F32)
+        return jnp.dot(stage_ref[...], halves_refs[g][:, lanes], preferred_element_type=F32)
+
+    def first_rest(g, start, section):
         turn_real, turn_imag = turn_ref[0], turn_ref[1]
         for u in range(GROUP):
             pair, place = divmod(u, beside)
@@ -113,9 +115,11 @@
                         lane = ((part * beside + place) * 2 + ri) * LANES
                         turned_refs[g][row : row + AVG, lane : lane + LANES] = kept
 
-    def last_part(g, pair):
+    def last_product(g, pair):
         rows = slice(pair * WIDTH, (pair + 1) * WIDTH)
-        product = jnp.dot(turned_refs[g][rows, :], last_ref[...], preferred_element_type=F32)
+        return jnp.dot(turned_refs[g][rows, :], last_ref[...], preferred_element_type=F32)
+
+    def last_rest(g, pair, product):
         found = (product[:, :columns] + product[:, columns:]).T
         for place in range(beside):
             stream = g * GROUP + pair * beside + place
@@ -126,15 +130,25 @@
             for half in range(WIDTH // LANES):
                 held_ref[half, pl.ds(at, outs), :] = mine[:, half * LANES : (half + 1) * LANES]
 
-    for g in range(groups + 2):
+    waiting = []
+    for g in range(groups + 3):
         filters = [(g, u, r) for u in range(GROUP) for r in range(0, WIDE, 16)] if g < groups else []
-        firsts = [(g - 1, start) for start in range(0, SPECTRA, 2)] if 1 <= g <= groups else []
-        lasts = [(g - 2, pair) for pair in range(GROUP // beside)] if g >= 2 else []
-        while filters or firsts or lasts:
-            for work, jobs, most in ((first_part, firsts, 1), (filter_rows, filters, 2), (last_part, lasts, 1), (filter_rows, filters, 2)):
-                for job in jobs[:most]:
-                    work(*job)
-                del jobs[:most]
+        units = [(first_product, first_rest, g - 1, start) for start in range(0, SPECTRA, 2)] if 1 <= g <= groups else []
+        if 3 <= g:
+            units += [(last_product, last_rest, g - 3, pair) for pair in range(GROUP // beside)]
+        while filters or units:
+            if units:
+                product, rest, *job = units.pop(0)
+                waiting.append((rest, job, product(*job)))
+            for job in filters[:2]:
+                filter_rows(*job)
+            del filters[:2]
+            if len(waiting) > 1 or not units:
+                for rest, job, result in waiting[:1]:
+                    rest(*job, result)
+                del waiting[:1]
+    for rest, job, result in waiting:
+        rest(*job, result)
 
     @pl.when(inner == ROWS // STEP - 1)
     def _():
@@ -285,6 +299,15 @@
     )(early, power, *picks, *parts)
 
 
+def sending_order(devices):
+    far, near = list(range(devices // 2, devices)), list(range(1, devices // 2))
+    order, near = near[:4], near[4:]
+    while far or near:
+        order += far[:1] + near[:1]
+        far, near = far[1:], near[1:]
+    return order
+
+
 def body(voltages, taps, station_gain, station_order):
     devices = lax.axis_size("ingest")
     streams = 2 * voltages.shape[0]
@@ -294,7 +317,7 @@
     samples = voltages.reshape(streams, 2, FRAMES * blocks, LANES).transpose(0, 2, 1, 3)
     samples = samples.reshape(streams, FRAMES, 2 * blocks, LANES)
     coeffs = taps.reshape(TAPS, blocks, LANES).transpose(1, 0, 2).reshape(TAPS * blocks, LANES)
-    cut = min(streams, ROWS)
+    cut = streams - streams // (2 * ROWS) * ROWS
     wanted = (2 * station_order[:, None] + jnp.arange(2, dtype=jnp.int32)).reshape(-1, 1)
 
     def pick(start, stop, first):
@@ -309,12 +332,15 @@
     picks, late = [], []
     if cut < streams:
         sent = spectra(samples, coeffs, station_gain, consts, outs, cut, streams, devices)
-        late = [sent[0]]
-        for k in range(1, devices):
+        received = {0: sent[0]}
+        order = sending_order(devices)
+        for place, k in enumerate(order):
             ready = sent[k]
-            if k > WINDOW:
-                ready, late[k - WINDOW] = lax.optimization_barrier((ready, late[k - WINDOW]))
-            late.append(lax.ppermute(ready, "ingest", [(i, i ^ k) for i in range(devices)]))
+            if place >= WINDOW:
+                past = order[place - WINDOW]
+                ready, received[past] = lax.optimization_barrier((ready, received[past]))
+            received[k] = lax.ppermute(ready, "ingest", [(i, i ^ k) for i in range(devices)])
+        late = [received[k] for k in range(devices)]
         picks = [pick(cut, streams, lax.axis_index("ingest"))]
     rows, power = arrange(pick(0, cut, 0), early)
     return tiles(rows, power, picks, late)

time: 89.7 us -> 79.5 us (0.89)
  the two profiles are of different devices: /device:TPU:11 before, /device:TPU:1 now
where the time goes in v7:
time: 79.5 us; the launch traced here: 79.3 us
  Pallas kernels  37.5 us (47%)
  starting transfers between devices  30 us (38%)
  waiting for transfers between devices  7.59 us (10%)
  local copies, waits for them, and re-layouts  3.33 us (4%)
    pallas_call x2, Pallas kernels, spectra(): pl.pallas_call(functools.partial(spectra_kernel, start, partners, outs),...  29.5 us
    ppermute x15, starting transfers between devices, body(): lax.ppermute(ready, 'ingest', [(i, i ^ k) for i in range(devices)])  22.7 us
    ppermute x15, waiting for transfers between devices, body(): lax.ppermute(ready, 'ingest', [(i, i ^ k) for i in range(devices)])  7.58 us
    all_to_all x1, starting transfers between devices, body(): lax.all_to_all(packed, 'ingest', split_axis=0, concat_axis=0, tiled=True)  7.36 us
    pallas_call x1, Pallas kernels, tiles(): pl.pallas_call(functools.partial(tiles_kernel, len(parts)), out_shape=jax...  6.47 us
    unnamed x30, local copies, waits for them, and re-layouts  3.16 us
  transfers between devices with their start and end apart: 16, of which 4 were waited for; matrix products, arithmetic and copies ran while one was open for 1% of the time, Pallas kernels for 21%

profile of v7, /device:TPU:1, one launch (start us, length us, event | category | flops | bytes accessed | tf_op | source)
XLA Modules:
  0.0 79.3 jit_solution(115906292065360491)
XLA Ops:
  0.0 14.5 %spectra.2 = bf16[64,32,256]{2,1,0:T(8,128)(2,1)} custom-call(f32[32]{0:T(128)} %gain_ref.2, s32[64,11,64,128]{3,2,1,0:T(8,128)} %bitcast.11, s32[64,11,64,128]{3,2,1,0:T(8,128)} %bitcast.12, s32[64,11,64,128]{3,2,1,0:T(8,128)} %bitcast.13, s32[64,11,64,128]{3,2,1,0:T(8,128)} %bitcast.14, s32[64,11,64,128]{3,2,1,0:T(8,128)} %bitcast.15, ...), custom_call_target="tpu_custom_call" | custom-call | flops 3072000000 | bytes 11534336 | tf_op jit(solution)/shard_map/spectra/pallas_call | solution.py:175
  14.5 7.4 %all-to-all-start = ((bf16[16,4,32,256]{3,2,1,0:T(8,128)(2,1)}), bf16[16,4,32,256]{3,2,1,0:T(8,128)(2,1)S(1)}, u32[]{:S(2)}, u32[]{:S(2)}) async-start(bf16[16,4,32,256]{3,2,1,0:T(8,128)(2,1)} %bitcast.33), calls=%async_computation | async-start | bytes 2097152 | tf_op jit(solution)/shard_map/all_to_all | solution.py:331
  21.9 15.0 %spectra.3 = (bf16[4,32,256]{2,1,0:T(8,128)(2,1)}, bf16[4,32,256]{2,1,0:T(8,128)(2,1)}, bf16[4,32,256]{2,1,0:T(8,128)(2,1)}, bf16[4,32,256]{2,1,0:T(8,128)(2,1)}...) custom-call(f32[32]{0:T(128)} %gain_ref.2, ...), custom_call_target="tpu_custom_call" | custom-call | flops 3072000000 | bytes 11534336 | tf_op jit(solution)/shard_map/spectra/pallas_call | solution.py:175
  37.1 1.6 %collective-permute-start.1 = (bf16[4,32,256]{2,1,0:T(8,128)(2,1)}, bf16[4,32,256]{2,1,0:T(8,128)(2,1)S(1)}, u32[]{:S(2)}, u32[]{:S(2)}) collective-permute-start(bf16[4,32,256]{2,1,0:T(8,128)(2,1)} %get-tuple-element.54), channel_id=1, source_target_pairs={{0,2},{1,3},{2,0},{3,1},{4,6},{5,7},{6,4},{7,5},{8,10},{9,11},{10,... | collective-permute-start | bytes 196616 | tf_op jit(solution)/shard_map/ppermute | solution.py:342
  39.1 1.4 %collective-permute-start.3 = (bf16[4,32,256]{2,1,0:T(8,128)(2,1)}, bf16[4,32,256]{2,1,0:T(8,128)(2,1)S(1)}, u32[]{:S(2)}, u32[]{:S(2)}) collective-permute-start(bf16[4,32,256]{2,1,0:T(8,128)(2,1)} %get-tuple-element.60), channel_id=1, source_target_pairs={{0,4},{1,5},{2,6},{3,7},{4,0},{5,1},{6,2},{7,3},{8,12},{9,13},{10,... | collective-permute-start | bytes 196616 | tf_op jit(solution)/shard_map/ppermute | solution.py:342
  40.5 2.1 %collective-permute-start.6 = (bf16[4,32,256]{2,1,0:T(8,128)(2,1)}, bf16[4,32,256]{2,1,0:T(8,128)(2,1)S(1)}, u32[]{:S(2)}, u32[]{:S(2)}) collective-permute-start(bf16[4,32,256]{2,1,0:T(8,128)(2,1)} %get-tuple-element.70), channel_id=1, source_target_pairs={{0,8},{1,9},{2,10},{3,11},{4,12},{5,13},{6,14},{7,15},{8,0},{9,1},... | collective-permute-start | bytes 196616 | tf_op jit(solution)/shard_map/ppermute | solution.py:342
  43.0 0.8 %collective-permute-start.4 = (bf16[4,32,256]{2,1,0:T(8,128)(2,1)}, bf16[4,32,256]{2,1,0:T(8,128)(2,1)S(1)}, u32[]{:S(2)}, u32[]{:S(2)}) collective-permute-start(bf16[4,32,256]{2,1,0:T(8,128)(2,1)} %get-tuple-element.63), channel_id=1, source_target_pairs={{0,5},{1,4},{2,7},{3,6},{4,1},{5,0},{6,3},{7,2},{8,13},{9,12},{10,... | collective-permute-start | bytes 196616 | tf_op jit(solution)/shard_map/ppermute | solution.py:342
  43.8 2.1 %collective-permute-start.8 = (bf16[4,32,256]{2,1,0:T(8,128)(2,1)}, bf16[4,32,256]{2,1,0:T(8,128)(2,1)S(1)}, u32[]{:S(2)}, u32[]{:S(2)}) collective-permute-start(bf16[4,32,256]{2,1,0:T(8,128)(2,1)} %get-tuple-element.75), channel_id=1, source_target_pairs={{0,9},{1,8},{2,11},{3,10},{4,13},{5,12},{6,15},{7,14},{8,1},{9,0},... | collective-permute-start | bytes 196616 | tf_op jit(solution)/shard_map/ppermute | solution.py:342
  46.0 1.0 %collective-permute-start.5 = (bf16[4,32,256]{2,1,0:T(8,128)(2,1)}, bf16[4,32,256]{2,1,0:T(8,128)(2,1)S(1)}, u32[]{:S(2)}, u32[]{:S(2)}) collective-permute-start(bf16[4,32,256]{2,1,0:T(8,128)(2,1)} %get-tuple-element.66), channel_id=1, source_target_pairs={{0,6},{1,7},{2,4},{3,5},{4,2},{5,3},{6,0},{7,1},{8,14},{9,15},{10,... | collective-permute-start | bytes 196616 | tf_op jit(solution)/shard_map/ppermute | solution.py:342
  47.0 1.8 %collective-permute-start.9 = (bf16[4,32,256]{2,1,0:T(8,128)(2,1)}, bf16[4,32,256]{2,1,0:T(8,128)(2,1)S(1)}, u32[]{:S(2)}, u32[]{:S(2)}) collective-permute-start(bf16[4,32,256]{2,1,0:T(8,128)(2,1)} %get-tuple-element.78), channel_id=1, source_target_pairs={{0,10},{1,11},{2,8},{3,9},{4,14},{5,15},{6,12},{7,13},{8,2},{9,3},... | collective-permute-start | bytes 196616 | tf_op jit(solution)/shard_map/ppermute | solution.py:342
  48.8 3.2 %collective-permute-done.6.refs_9_ = bf16[4,32,256]{2,1,0:T(8,128)(2,1)S(1)} collective-permute-done((bf16[4,32,256]{2,1,0:T(8,128)(2,1)}, bf16[4,32,256]{2,1,0:T(8,128)(2,1)S(1)}, u32[]{:S(2)}, u32[]{:S(2)}) %collective-permute-start.6) | collective-permute-done | bytes 65568 | tf_op jit(solution)/shard_map/ppermute | solution.py:342
  53.6 2.0 %collective-permute-start.10 = (bf16[4,32,256]{2,1,0:T(8,128)(2,1)}, bf16[4,32,256]{2,1,0:T(8,128)(2,1)}, u32[]{:S(2)}, u32[]{:S(2)}) collective-permute-start(bf16[4,32,256]{2,1,0:T(8,128)(2,1)} %get-tuple-element.80), channel_id=1, source_target_pairs={{0,11},{1,10},{2,9},{3,8},{4,15},{5,14},{6,13},{7,12},{8,3},{9,2},... | collective-permute-start | bytes 196616 | tf_op jit(solution)/shard_map/ppermute | solution.py:342
  55.6 0.6 copy-done.3
  56.2 2.1 %collective-permute-start.11 = (bf16[4,32,256]{2,1,0:T(8,128)(2,1)}, bf16[4,32,256]{2,1,0:T(8,128)(2,1)}, u32[]{:S(2)}, u32[]{:S(2)}) collective-permute-start(bf16[4,32,256]{2,1,0:T(8,128)(2,1)} %get-tuple-element.81), channel_id=1, source_target_pairs={{0,12},{1,13},{2,14},{3,15},{4,8},{5,9},{6,10},{7,11},{8,4},{9,5},... | collective-permute-start | bytes 196616 | tf_op jit(solution)/shard_map/ppermute | solution.py:342
  58.4 0.6 copy-done.5
  59.0 4.1 %collective-permute-start.12 = (bf16[4,32,256]{2,1,0:T(8,128)(2,1)}, bf16[4,32,256]{2,1,0:T(8,128)(2,1)}, u32[]{:S(2)}, u32[]{:S(2)}) collective-permute-start(bf16[4,32,256]{2,1,0:T(8,128)(2,1)} %get-tuple-element.82), channel_id=1, source_target_pairs={{0,13},{1,12},{2,15},{3,14},{4,9},{5,8},{6,11},{7,10},{8,5},{9,4},... | collective-permute-start | bytes 196616 | tf_op jit(solution)/shard_map/ppermute | solution.py:342
  63.1 0.6 copy-done.7
  63.7 1.6 %collective-permute-start.13 = (bf16[4,32,256]{2,1,0:T(8,128)(2,1)}, bf16[4,32,256]{2,1,0:T(8,128)(2,1)}, u32[]{:S(2)}, u32[]{:S(2)}) collective-permute-start(bf16[4,32,256]{2,1,0:T(8,128)(2,1)} %get-tuple-element.83), channel_id=1, source_target_pairs={{0,14},{1,15},{2,12},{3,13},{4,10},{5,11},{6,8},{7,9},{8,6},{9,7},... | collective-permute-start | bytes 196616 | tf_op jit(solution)/shard_map/ppermute | solution.py:342
  65.3 0.6 copy-done.9
  65.9 0.8 %collective-permute-start.14 = (bf16[4,32,256]{2,1,0:T(8,128)(2,1)}, bf16[4,32,256]{2,1,0:T(8,128)(2,1)}, u32[]{:S(2)}, u32[]{:S(2)}) collective-permute-start(bf16[4,32,256]{2,1,0:T(8,128)(2,1)} %get-tuple-element.84), channel_id=1, source_target_pairs={{0,15},{1,14},{2,13},{3,12},{4,11},{5,10},{6,9},{7,8},{8,7},{9,6},... | collective-permute-start | bytes 196616 | tf_op jit(solution)/shard_map/ppermute | solution.py:342
  66.8 1.6 %arrange.1 = (bf16[2,1024,512]{2,1,0:T(8,128)(2,1)S(1)}, f32[2,8,128]{2,1,0:T(8,128)S(1)}) custom-call(bf16[1024,512]{1,0:T(8,128)(2,1)S(1)} %get-tuple-element.86.pick_ref, bf16[16,4,32,256]{3,2,1,0:T(8,128)(2,1)S(1)} %all-to-all-done.part_ref), custom_call_target="tpu_custom_call" | custom-call | flops 1100000000 | bytes 4000000 | tf_op jit(solution)/shard_map/arrange/pallas_call | solution.py:217
  68.4 1.5 %collective-permute-done.13.refs_15_ = bf16[4,32,256]{2,1,0:T(8,128)(2,1)} collective-permute-done((bf16[4,32,256]{2,1,0:T(8,128)(2,1)}, bf16[4,32,256]{2,1,0:T(8,128)(2,1)}, u32[]{:S(2)}, u32[]{:S(2)}) %collective-permute-start.13) | collective-permute-done | bytes 65568 | tf_op jit(solution)/shard_map/ppermute | solution.py:342
  69.9 2.8 %collective-permute-done.14.refs_16_ = bf16[4,32,256]{2,1,0:T(8,128)(2,1)} collective-permute-done((bf16[4,32,256]{2,1,0:T(8,128)(2,1)}, bf16[4,32,256]{2,1,0:T(8,128)(2,1)}, u32[]{:S(2)}, u32[]{:S(2)}) %collective-permute-start.14) | collective-permute-done | bytes 65568 | tf_op jit(solution)/shard_map/ppermute | solution.py:342
  72.8 6.5 %tiles.1 = bf16[2,36,2,128,128]{4,3,2,1,0:T(8,128)(2,1)} custom-call(bf16[2,1024,512]{2,1,0:T(8,128)(2,1)S(1)} %get-tuple-element.46.early_ref, f32[2,8,128]{2,1,0:T(8,128)S(1)} %get-tuple-element.47.power_ref, bf16[1024,512]{1,0:T(8,128)(2,1)S(1)} %get-tuple-element.85.refs_0_, bf16[4,32,256]{2,1,0:T(8,128)(2,1)S(1)} %copy-done, ...), custom_call_target="tpu_custom_call" | custom-call | flops 4499999744 | bytes 9000000 | tf_op jit(solution)/shard_map/tiles/pallas_call | solution.py:281
  (47 shorter events, 2.6 us)
Async XLA Ops:
  14.5 52.2 %all-to-all-start = ((bf16[16,4,32,256]{3,2,1,0:T(8,128)(2,1)}), bf16[16,4,32,256]{3,2,1,0:T(8,128)(2,1)S(1)}, u32[]{:S(2)}, u32[]{:S(2)}) async-start(bf16[16,4,32,256]{3,2,1,0:T(8,128)(2,1)} %bitcast.33), calls=%async_computation | async-start | bytes 2097152 | tf_op jit(solution)/shard_map/all_to_all | solution.py:331
  21.9 20.7 %copy-start.11 = (s32[512]{0:T(512)S(1)}, s32[512]{0:T(512)}, u32[]{:S(2)}) copy-start(s32[512]{0:T(512)} %param.14) | copy-start | bytes 6148
  21.9 20.9 %copy-start.12 = (s32[512]{0:T(512)S(1)}, s32[512]{0:T(512)}, u32[]{:S(2)}) copy-start(s32[512]{0:T(512)} %constant.24.clone) | copy-start | bytes 6148
  21.9 20.9 %copy-start.13 = (s32[512]{0:T(512)S(1)}, s32[512]{0:T(512)}, u32[]{:S(2)}) copy-start(s32[512]{0:T(512)} %constant.23.clone) | copy-start | bytes 6148
  21.9 30.6 %copy-start.14 = (s32[512]{0:T(512)S(1)}, s32[512]{0:T(512)}, u32[]{:S(2)}) copy-start(s32[512]{0:T(512)} %constant.26) | copy-start | bytes 6148
  36.9 6.1 %collective-permute-start = (bf16[4,32,256]{2,1,0:T(8,128)(2,1)}, bf16[4,32,256]{2,1,0:T(8,128)(2,1)S(1)}, u32[]{:S(2)}, u32[]{:S(2)}) collective-permute-start(bf16[4,32,256]{2,1,0:T(8,128)(2,1)} %get-tuple-element.51), channel_id=1, source_target_pairs={{0,1},{1,0},{2,3},{3,2},{4,5},{5,4},{6,7},{7,6},{8,9},{9,8},{10,11... | collective-permute-start | bytes 196616 | tf_op jit(solution)/shard_map/ppermute | solution.py:342
  37.1 6.7 %collective-permute-start.1 = (bf16[4,32,256]{2,1,0:T(8,128)(2,1)}, bf16[4,32,256]{2,1,0:T(8,128)(2,1)S(1)}, u32[]{:S(2)}, u32[]{:S(2)}) collective-permute-start(bf16[4,32,256]{2,1,0:T(8,128)(2,1)} %get-tuple-element.54), channel_id=1, source_target_pairs={{0,2},{1,3},{2,0},{3,1},{4,6},{5,7},{6,4},{7,5},{8,10},{9,11},{10,... | collective-permute-start | bytes 196616 | tf_op jit(solution)/shard_map/ppermute | solution.py:342
  38.7 7.3 %collective-permute-start.2 = (bf16[4,32,256]{2,1,0:T(8,128)(2,1)}, bf16[4,32,256]{2,1,0:T(8,128)(2,1)S(1)}, u32[]{:S(2)}, u32[]{:S(2)}) collective-permute-start(bf16[4,32,256]{2,1,0:T(8,128)(2,1)} %get-tuple-element.57), channel_id=1, source_target_pairs={{0,3},{1,2},{2,1},{3,0},{4,7},{5,6},{6,5},{7,4},{8,11},{9,10},{10,... | collective-permute-start | bytes 196616 | tf_op jit(solution)/shard_map/ppermute | solution.py:342
  39.1 7.9 %collective-permute-start.3 = (bf16[4,32,256]{2,1,0:T(8,128)(2,1)}, bf16[4,32,256]{2,1,0:T(8,128)(2,1)S(1)}, u32[]{:S(2)}, u32[]{:S(2)}) collective-permute-start(bf16[4,32,256]{2,1,0:T(8,128)(2,1)} %get-tuple-element.60), channel_id=1, source_target_pairs={{0,4},{1,5},{2,6},{3,7},{4,0},{5,1},{6,2},{7,3},{8,12},{9,13},{10,... | collective-permute-start | bytes 196616 | tf_op jit(solution)/shard_map/ppermute | solution.py:342
  40.5 11.4 %collective-permute-start.6 = (bf16[4,32,256]{2,1,0:T(8,128)(2,1)}, bf16[4,32,256]{2,1,0:T(8,128)(2,1)S(1)}, u32[]{:S(2)}, u32[]{:S(2)}) collective-permute-start(bf16[4,32,256]{2,1,0:T(8,128)(2,1)} %get-tuple-element.70), channel_id=1, source_target_pairs={{0,8},{1,9},{2,10},{3,11},{4,12},{5,13},{6,14},{7,15},{8,0},{9,1},... | collective-permute-start | bytes 196616 | tf_op jit(solution)/shard_map/ppermute | solution.py:342
  43.0 10.0 %collective-permute-start.4 = (bf16[4,32,256]{2,1,0:T(8,128)(2,1)}, bf16[4,32,256]{2,1,0:T(8,128)(2,1)S(1)}, u32[]{:S(2)}, u32[]{:S(2)}) collective-permute-start(bf16[4,32,256]{2,1,0:T(8,128)(2,1)} %get-tuple-element.63), channel_id=1, source_target_pairs={{0,5},{1,4},{2,7},{3,6},{4,1},{5,0},{6,3},{7,2},{8,13},{9,12},{10,... | collective-permute-start | bytes 196616 | tf_op jit(solution)/shard_map/ppermute | solution.py:342
  43.8 11.8 %collective-permute-start.8 = (bf16[4,32,256]{2,1,0:T(8,128)(2,1)}, bf16[4,32,256]{2,1,0:T(8,128)(2,1)S(1)}, u32[]{:S(2)}, u32[]{:S(2)}) collective-permute-start(bf16[4,32,256]{2,1,0:T(8,128)(2,1)} %get-tuple-element.75), channel_id=1, source_target_pairs={{0,9},{1,8},{2,11},{3,10},{4,13},{5,12},{6,15},{7,14},{8,1},{9,0},... | collective-permute-start | bytes 196616 | tf_op jit(solution)/shard_map/ppermute | solution.py:342
  46.0 12.4 %collective-permute-start.5 = (bf16[4,32,256]{2,1,0:T(8,128)(2,1)}, bf16[4,32,256]{2,1,0:T(8,128)(2,1)S(1)}, u32[]{:S(2)}, u32[]{:S(2)}) collective-permute-start(bf16[4,32,256]{2,1,0:T(8,128)(2,1)} %get-tuple-element.66), channel_id=1, source_target_pairs={{0,6},{1,7},{2,4},{3,5},{4,2},{5,3},{6,0},{7,1},{8,14},{9,15},{10,... | collective-permute-start | bytes 196616 | tf_op jit(solution)/shard_map/ppermute | solution.py:342
  47.0 16.0 %collective-permute-start.9 = (bf16[4,32,256]{2,1,0:T(8,128)(2,1)}, bf16[4,32,256]{2,1,0:T(8,128)(2,1)S(1)}, u32[]{:S(2)}, u32[]{:S(2)}) collective-permute-start(bf16[4,32,256]{2,1,0:T(8,128)(2,1)} %get-tuple-element.78), channel_id=1, source_target_pairs={{0,10},{1,11},{2,8},{3,9},{4,14},{5,15},{6,12},{7,13},{8,2},{9,3},... | collective-permute-start | bytes 196616 | tf_op jit(solution)/shard_map/ppermute | solution.py:342
  51.9 13.4 %collective-permute-start.7 = (bf16[4,32,256]{2,1,0:T(8,128)(2,1)}, bf16[4,32,256]{2,1,0:T(8,128)(2,1)S(1)}, u32[]{:S(2)}, u32[]{:S(2)}) collective-permute-start(bf16[4,32,256]{2,1,0:T(8,128)(2,1)} %get-tuple-element.71), channel_id=1, source_target_pairs={{0,7},{1,6},{2,5},{3,4},{4,3},{5,2},{6,1},{7,0},{8,15},{9,14},{10,... | collective-permute-start | bytes 196616 | tf_op jit(solution)/shard_map/ppermute | solution.py:342
  52.9 19.8 %copy-start = (bf16[4,32,256]{2,1,0:T(8,128)(2,1)S(1)}, bf16[4,32,256]{2,1,0:T(8,128)(2,1)}, u32[]{:S(2)}) copy-start(bf16[4,32,256]{2,1,0:T(8,128)(2,1)} %get-tuple-element.49.refs_1_) | copy-start | bytes 196612
  53.6 14.8 %collective-permute-start.10 = (bf16[4,32,256]{2,1,0:T(8,128)(2,1)}, bf16[4,32,256]{2,1,0:T(8,128)(2,1)}, u32[]{:S(2)}, u32[]{:S(2)}) collective-permute-start(bf16[4,32,256]{2,1,0:T(8,128)(2,1)} %get-tuple-element.80), channel_id=1, source_target_pairs={{0,11},{1,10},{2,9},{3,8},{4,15},{5,14},{6,13},{7,12},{8,3},{9,2},... | collective-permute-start | bytes 196616 | tf_op jit(solution)/shard_map/ppermute | solution.py:342
  56.2 12.2 %collective-permute-start.11 = (bf16[4,32,256]{2,1,0:T(8,128)(2,1)}, bf16[4,32,256]{2,1,0:T(8,128)(2,1)}, u32[]{:S(2)}, u32[]{:S(2)}) collective-permute-start(bf16[4,32,256]{2,1,0:T(8,128)(2,1)} %get-tuple-element.81), channel_id=1, source_target_pairs={{0,12},{1,13},{2,14},{3,15},{4,8},{5,9},{6,10},{7,11},{8,4},{9,5},... | collective-permute-start | bytes 196616 | tf_op jit(solution)/shard_map/ppermute | solution.py:342
  59.0 9.4 %collective-permute-start.12 = (bf16[4,32,256]{2,1,0:T(8,128)(2,1)}, bf16[4,32,256]{2,1,0:T(8,128)(2,1)}, u32[]{:S(2)}, u32[]{:S(2)}) collective-permute-start(bf16[4,32,256]{2,1,0:T(8,128)(2,1)} %get-tuple-element.82), channel_id=1, source_target_pairs={{0,13},{1,12},{2,15},{3,14},{4,9},{5,8},{6,11},{7,10},{8,5},{9,4},... | collective-permute-start | bytes 196616 | tf_op jit(solution)/shard_map/ppermute | solution.py:342
  63.7 6.2 %collective-permute-start.13 = (bf16[4,32,256]{2,1,0:T(8,128)(2,1)}, bf16[4,32,256]{2,1,0:T(8,128)(2,1)}, u32[]{:S(2)}, u32[]{:S(2)}) collective-permute-start(bf16[4,32,256]{2,1,0:T(8,128)(2,1)} %get-tuple-element.83), channel_id=1, source_target_pairs={{0,14},{1,15},{2,12},{3,13},{4,10},{5,11},{6,8},{7,9},{8,6},{9,7},... | collective-permute-start | bytes 196616 | tf_op jit(solution)/shard_map/ppermute | solution.py:342
  65.9 6.8 %collective-permute-start.14 = (bf16[4,32,256]{2,1,0:T(8,128)(2,1)}, bf16[4,32,256]{2,1,0:T(8,128)(2,1)}, u32[]{:S(2)}, u32[]{:S(2)}) collective-permute-start(bf16[4,32,256]{2,1,0:T(8,128)(2,1)} %get-tuple-element.84), channel_id=1, source_target_pairs={{0,15},{1,14},{2,13},{3,12},{4,11},{5,10},{6,9},{7,8},{8,7},{9,6},... | collective-permute-start | bytes 196616 | tf_op jit(solution)/shard_map/ppermute | solution.py:342
  66.8 6.0 %copy-start.6 = (bf16[4,32,256]{2,1,0:T(8,128)(2,1)S(1)}, bf16[4,32,256]{2,1,0:T(8,128)(2,1)}, u32[]{:S(2)}) copy-start(bf16[4,32,256]{2,1,0:T(8,128)(2,1)} %copy-done.5) | copy-start | bytes 196612
  66.8 6.0 %copy-start.8 = (bf16[4,32,256]{2,1,0:T(8,128)(2,1)S(1)}, bf16[4,32,256]{2,1,0:T(8,128)(2,1)}, u32[]{:S(2)}) copy-start(bf16[4,32,256]{2,1,0:T(8,128)(2,1)} %copy-done.7) | copy-start | bytes 196612
  66.8 6.0 %copy-start.10 = (bf16[4,32,256]{2,1,0:T(8,128)(2,1)S(1)}, bf16[4,32,256]{2,1,0:T(8,128)(2,1)}, u32[]{:S(2)}) copy-start(bf16[4,32,256]{2,1,0:T(8,128)(2,1)} %copy-done.9) | copy-start | bytes 196612
  (7 other events, 15.1 us)

commit v8 on v7

--- a/solution.py
+++ b/solution.py
@@ -62,8 +62,9 @@
 
 
 def halves(values):
-    high = values.astype(BF16)
-    return high, (values - high.astype(F32)).astype(BF16)
+    scaled = values * 65537.0
+    high = scaled - (scaled - values)
+    return high.astype(BF16), (values - high).astype(BF16)
 
 
 def spectra_kernel(first_stream, partners, outs, gain_ref, *refs):
@@ -88,14 +89,17 @@
     def filter_rows(g, u, r):
         rows = slice(r, r + 16)
         coeffs = [coeff_ref[j, rows, :] for j in range(TAPS)]
-        samples = [ref[g * GROUP + u, 0, rows, :].astype(F32) for ref in frames]
-        for m in range(SPECTRA):
-            value = coeffs[0] * samples[m]
-            for j in range(1, TAPS):
-                value = value + coeffs[j] * samples[m + j]
-            for part, kept in enumerate(halves(value)):
-                row = part * size + u * WIDE + r
-                halves_refs[g][row : row + 16, m * LANES : (m + 1) * LANES] = kept
+        sums = {}
+        for f, ref in enumerate(frames):
+            sample = ref[g * GROUP + u, 0, rows, :].astype(F32)
+            for m in range(max(f - TAPS + 1, 0), min(f + 1, SPECTRA)):
+                term = coeffs[f - m] * sample
+                sums[m] = sums[m] + term if m in sums else term
+            if f >= TAPS - 1:
+                m = f - TAPS + 1
+                for part, kept in enumerate(halves(sums.pop(m))):
+                    row = part * size + u * WIDE + r
+                    halves_refs[g][row : row + 16, m * LANES : (m + 1) * LANES] = kept
 
     def first_product(g, start):
         lanes = slice(start * LANES, (start + 2) * LANES)

time: 79.5 us -> 80.2 us (level)
  Pallas kernels: 37.5 us -> 39 us
    pallas_call x2, Pallas kernels: 29.5 us -> 31 us  [spectra(): pl.pallas_call(functools.partial(spectra_kernel, start, partners, outs),...]
  transfers between devices with their start and end apart: 16 -> 16, of which waited for: 4 -> 4; matrix products, arithmetic and copies ran while one was open for 1% -> 1% of each run, Pallas kernels for 21% -> 22%
where the time goes in v8:
time: 80.2 us; the launch traced here: 79.9 us
  Pallas kernels  39 us (49%)
  starting transfers between devices  29.6 us (37%)
  waiting for transfers between devices  7.2 us (9%)
  local copies, waits for them, and re-layouts  3.33 us (4%)
    pallas_call x2, Pallas kernels, spectra(): pl.pallas_call(functools.partial(spectra_kernel, start, partners, outs),...  31 us
    ppermute x15, starting transfers between devices, body(): lax.ppermute(ready, 'ingest', [(i, i ^ k) for i in range(devices)])  22.3 us
    all_to_all x1, starting transfers between devices, body(): lax.all_to_all(packed, 'ingest', split_axis=0, concat_axis=0, tiled=True)  7.36 us
    ppermute x15, waiting for transfers between devices, body(): lax.ppermute(ready, 'ingest', [(i, i ^ k) for i in range(devices)])  7.2 us
    pallas_call x1, Pallas kernels, tiles(): pl.pallas_call(functools.partial(tiles_kernel, len(parts)), out_shape=jax...  6.47 us
    unnamed x30, local copies, waits for them, and re-layouts  3.16 us
  transfers between devices with their start and end apart: 16, of which 4 were waited for; matrix products, arithmetic and copies ran while one was open for 1% of the time, Pallas kernels for 22%

profile of v8, /device:TPU:1, one launch (start us, length us, event | category | flops | bytes accessed | tf_op | source)
XLA Modules:
  0.0 79.9 jit_solution(9942800827004041481)
XLA Ops:
  0.0 15.3 %spectra.2 = bf16[64,32,256]{2,1,0:T(8,128)(2,1)} custom-call(f32[32]{0:T(128)} %gain_ref.2, s32[64,11,64,128]{3,2,1,0:T(8,128)} %bitcast.11, s32[64,11,64,128]{3,2,1,0:T(8,128)} %bitcast.12, s32[64,11,64,128]{3,2,1,0:T(8,128)} %bitcast.13, s32[64,11,64,128]{3,2,1,0:T(8,128)} %bitcast.14, s32[64,11,64,128]{3,2,1,0:T(8,128)} %bitcast.15, ...), custom_call_target="tpu_custom_call" | custom-call | flops 3072000000 | bytes 11534336 | tf_op jit(solution)/shard_map/spectra/pallas_call | solution.py:179
  15.3 7.4 %all-to-all-start = ((bf16[16,4,32,256]{3,2,1,0:T(8,128)(2,1)}), bf16[16,4,32,256]{3,2,1,0:T(8,128)(2,1)S(1)}, u32[]{:S(2)}, u32[]{:S(2)}) async-start(bf16[16,4,32,256]{3,2,1,0:T(8,128)(2,1)} %bitcast.33), calls=%async_computation | async-start | bytes 2097152 | tf_op jit(solution)/shard_map/all_to_all | solution.py:335
  22.7 15.7 %spectra.3 = (bf16[4,32,256]{2,1,0:T(8,128)(2,1)}, bf16[4,32,256]{2,1,0:T(8,128)(2,1)}, bf16[4,32,256]{2,1,0:T(8,128)(2,1)}, bf16[4,32,256]{2,1,0:T(8,128)(2,1)}...) custom-call(f32[32]{0:T(128)} %gain_ref.2, ...), custom_call_target="tpu_custom_call" | custom-call | flops 3072000000 | bytes 11534336 | tf_op jit(solution)/shard_map/spectra/pallas_call | solution.py:179
  38.6 1.6 %collective-permute-start.1 = (bf16[4,32,256]{2,1,0:T(8,128)(2,1)}, bf16[4,32,256]{2,1,0:T(8,128)(2,1)S(1)}, u32[]{:S(2)}, u32[]{:S(2)}) collective-permute-start(bf16[4,32,256]{2,1,0:T(8,128)(2,1)} %get-tuple-element.54), channel_id=1, source_target_pairs={{0,2},{1,3},{2,0},{3,1},{4,6},{5,7},{6,4},{7,5},{8,10},{9,11},{10,... | collective-permute-start | bytes 196616 | tf_op jit(solution)/shard_map/ppermute | solution.py:346
  40.6 1.4 %collective-permute-start.3 = (bf16[4,32,256]{2,1,0:T(8,128)(2,1)}, bf16[4,32,256]{2,1,0:T(8,128)(2,1)S(1)}, u32[]{:S(2)}, u32[]{:S(2)}) collective-permute-start(bf16[4,32,256]{2,1,0:T(8,128)(2,1)} %get-tuple-element.60), channel_id=1, source_target_pairs={{0,4},{1,5},{2,6},{3,7},{4,0},{5,1},{6,2},{7,3},{8,12},{9,13},{10,... | collective-permute-start | bytes 196616 | tf_op jit(solution)/shard_map/ppermute | solution.py:346
  42.0 2.1 %collective-permute-start.6 = (bf16[4,32,256]{2,1,0:T(8,128)(2,1)}, bf16[4,32,256]{2,1,0:T(8,128)(2,1)S(1)}, u32[]{:S(2)}, u32[]{:S(2)}) collective-permute-start(bf16[4,32,256]{2,1,0:T(8,128)(2,1)} %get-tuple-element.70), channel_id=1, source_target_pairs={{0,8},{1,9},{2,10},{3,11},{4,12},{5,13},{6,14},{7,15},{8,0},{9,1},... | collective-permute-start | bytes 196616 | tf_op jit(solution)/shard_map/ppermute | solution.py:346
  44.4 0.9 %collective-permute-start.4 = (bf16[4,32,256]{2,1,0:T(8,128)(2,1)}, bf16[4,32,256]{2,1,0:T(8,128)(2,1)S(1)}, u32[]{:S(2)}, u32[]{:S(2)}) collective-permute-start(bf16[4,32,256]{2,1,0:T(8,128)(2,1)} %get-tuple-element.63), channel_id=1, source_target_pairs={{0,5},{1,4},{2,7},{3,6},{4,1},{5,0},{6,3},{7,2},{8,13},{9,12},{10,... | collective-permute-start | bytes 196616 | tf_op jit(solution)/shard_map/ppermute | solution.py:346
  45.3 1.5 %collective-permute-start.8 = (bf16[4,32,256]{2,1,0:T(8,128)(2,1)}, bf16[4,32,256]{2,1,0:T(8,128)(2,1)S(1)}, u32[]{:S(2)}, u32[]{:S(2)}) collective-permute-start(bf16[4,32,256]{2,1,0:T(8,128)(2,1)} %get-tuple-element.75), channel_id=1, source_target_pairs={{0,9},{1,8},{2,11},{3,10},{4,13},{5,12},{6,15},{7,14},{8,1},{9,0},... | collective-permute-start | bytes 196616 | tf_op jit(solution)/shard_map/ppermute | solution.py:346
  47.3 1.1 %collective-permute-start.5 = (bf16[4,32,256]{2,1,0:T(8,128)(2,1)}, bf16[4,32,256]{2,1,0:T(8,128)(2,1)S(1)}, u32[]{:S(2)}, u32[]{:S(2)}) collective-permute-start(bf16[4,32,256]{2,1,0:T(8,128)(2,1)} %get-tuple-element.66), channel_id=1, source_target_pairs={{0,6},{1,7},{2,4},{3,5},{4,2},{5,3},{6,0},{7,1},{8,14},{9,15},{10,... | collective-permute-start | bytes 196616 | tf_op jit(solution)/shard_map/ppermute | solution.py:346
  48.4 2.0 %collective-permute-start.9 = (bf16[4,32,256]{2,1,0:T(8,128)(2,1)}, bf16[4,32,256]{2,1,0:T(8,128)(2,1)S(1)}, u32[]{:S(2)}, u32[]{:S(2)}) collective-permute-start(bf16[4,32,256]{2,1,0:T(8,128)(2,1)} %get-tuple-element.78), channel_id=1, source_target_pairs={{0,10},{1,11},{2,8},{3,9},{4,14},{5,15},{6,12},{7,13},{8,2},{9,3},... | collective-permute-start | bytes 196616 | tf_op jit(solution)/shard_map/ppermute | solution.py:346
  50.4 2.3 %collective-permute-done.6.refs_9_ = bf16[4,32,256]{2,1,0:T(8,128)(2,1)S(1)} collective-permute-done((bf16[4,32,256]{2,1,0:T(8,128)(2,1)}, bf16[4,32,256]{2,1,0:T(8,128)(2,1)S(1)}, u32[]{:S(2)}, u32[]{:S(2)}) %collective-permute-start.6) | collective-permute-done | bytes 65568 | tf_op jit(solution)/shard_map/ppermute | solution.py:346
  54.1 2.2 %collective-permute-start.10 = (bf16[4,32,256]{2,1,0:T(8,128)(2,1)}, bf16[4,32,256]{2,1,0:T(8,128)(2,1)}, u32[]{:S(2)}, u32[]{:S(2)}) collective-permute-start(bf16[4,32,256]{2,1,0:T(8,128)(2,1)} %get-tuple-element.80), channel_id=1, source_target_pairs={{0,11},{1,10},{2,9},{3,8},{4,15},{5,14},{6,13},{7,12},{8,3},{9,2},... | collective-permute-start | bytes 196616 | tf_op jit(solution)/shard_map/ppermute | solution.py:346
  56.4 0.6 copy-done.3
  57.0 2.1 %collective-permute-start.11 = (bf16[4,32,256]{2,1,0:T(8,128)(2,1)}, bf16[4,32,256]{2,1,0:T(8,128)(2,1)}, u32[]{:S(2)}, u32[]{:S(2)}) collective-permute-start(bf16[4,32,256]{2,1,0:T(8,128)(2,1)} %get-tuple-element.81), channel_id=1, source_target_pairs={{0,12},{1,13},{2,14},{3,15},{4,8},{5,9},{6,10},{7,11},{8,4},{9,5},... | collective-permute-start | bytes 196616 | tf_op jit(solution)/shard_map/ppermute | solution.py:346
  59.1 0.6 copy-done.5
  59.7 2.8 %collective-permute-start.12 = (bf16[4,32,256]{2,1,0:T(8,128)(2,1)}, bf16[4,32,256]{2,1,0:T(8,128)(2,1)}, u32[]{:S(2)}, u32[]{:S(2)}) collective-permute-start(bf16[4,32,256]{2,1,0:T(8,128)(2,1)} %get-tuple-element.82), channel_id=1, source_target_pairs={{0,13},{1,12},{2,15},{3,14},{4,9},{5,8},{6,11},{7,10},{8,5},{9,4},... | collective-permute-start | bytes 196616 | tf_op jit(solution)/shard_map/ppermute | solution.py:346
  62.5 0.6 copy-done.7
  63.1 2.9 %collective-permute-start.13 = (bf16[4,32,256]{2,1,0:T(8,128)(2,1)}, bf16[4,32,256]{2,1,0:T(8,128)(2,1)}, u32[]{:S(2)}, u32[]{:S(2)}) collective-permute-start(bf16[4,32,256]{2,1,0:T(8,128)(2,1)} %get-tuple-element.83), channel_id=1, source_target_pairs={{0,14},{1,15},{2,12},{3,13},{4,10},{5,11},{6,8},{7,9},{8,6},{9,7},... | collective-permute-start | bytes 196616 | tf_op jit(solution)/shard_map/ppermute | solution.py:346
  66.1 0.6 copy-done.9
  66.7 0.7 collective-permute-start.14
  67.5 1.6 %arrange.1 = (bf16[2,1024,512]{2,1,0:T(8,128)(2,1)S(1)}, f32[2,8,128]{2,1,0:T(8,128)S(1)}) custom-call(bf16[1024,512]{1,0:T(8,128)(2,1)S(1)} %get-tuple-element.86.pick_ref, bf16[16,4,32,256]{3,2,1,0:T(8,128)(2,1)S(1)} %all-to-all-done.part_ref), custom_call_target="tpu_custom_call" | custom-call | flops 1100000000 | bytes 4000000 | tf_op jit(solution)/shard_map/arrange/pallas_call | solution.py:221
  69.1 0.8 %collective-permute-done.13.refs_15_ = bf16[4,32,256]{2,1,0:T(8,128)(2,1)} collective-permute-done((bf16[4,32,256]{2,1,0:T(8,128)(2,1)}, bf16[4,32,256]{2,1,0:T(8,128)(2,1)}, u32[]{:S(2)}, u32[]{:S(2)}) %collective-permute-start.13) | collective-permute-done | bytes 65568 | tf_op jit(solution)/shard_map/ppermute | solution.py:346
  69.9 3.5 %collective-permute-done.14.refs_16_ = bf16[4,32,256]{2,1,0:T(8,128)(2,1)} collective-permute-done((bf16[4,32,256]{2,1,0:T(8,128)(2,1)}, bf16[4,32,256]{2,1,0:T(8,128)(2,1)}, u32[]{:S(2)}, u32[]{:S(2)}) %collective-permute-start.14) | collective-permute-done | bytes 65568 | tf_op jit(solution)/shard_map/ppermute | solution.py:346
  73.4 6.5 %tiles.1 = bf16[2,36,2,128,128]{4,3,2,1,0:T(8,128)(2,1)} custom-call(bf16[2,1024,512]{2,1,0:T(8,128)(2,1)S(1)} %get-tuple-element.46.early_ref, f32[2,8,128]{2,1,0:T(8,128)S(1)} %get-tuple-element.47.power_ref, bf16[1024,512]{1,0:T(8,128)(2,1)S(1)} %get-tuple-element.85.refs_0_, bf16[4,32,256]{2,1,0:T(8,128)(2,1)S(1)} %copy-done, ...), custom_call_target="tpu_custom_call" | custom-call | flops 4499999744 | bytes 9000000 | tf_op jit(solution)/shard_map/tiles/pallas_call | solution.py:285
  (47 shorter events, 2.9 us)
Async XLA Ops:
  15.3 52.1 %all-to-all-start = ((bf16[16,4,32,256]{3,2,1,0:T(8,128)(2,1)}), bf16[16,4,32,256]{3,2,1,0:T(8,128)(2,1)S(1)}, u32[]{:S(2)}, u32[]{:S(2)}) async-start(bf16[16,4,32,256]{3,2,1,0:T(8,128)(2,1)} %bitcast.33), calls=%async_computation | async-start | bytes 2097152 | tf_op jit(solution)/shard_map/all_to_all | solution.py:335
  22.6 21.4 %copy-start.11 = (s32[512]{0:T(512)S(1)}, s32[512]{0:T(512)}, u32[]{:S(2)}) copy-start(s32[512]{0:T(512)} %param.14) | copy-start | bytes 6148
  22.6 21.6 %copy-start.12 = (s32[512]{0:T(512)S(1)}, s32[512]{0:T(512)}, u32[]{:S(2)}) copy-start(s32[512]{0:T(512)} %constant.24.clone) | copy-start | bytes 6148
  22.7 21.6 %copy-start.13 = (s32[512]{0:T(512)S(1)}, s32[512]{0:T(512)}, u32[]{:S(2)}) copy-start(s32[512]{0:T(512)} %constant.23.clone) | copy-start | bytes 6148
  22.7 30.4 %copy-start.14 = (s32[512]{0:T(512)S(1)}, s32[512]{0:T(512)}, u32[]{:S(2)}) copy-start(s32[512]{0:T(512)} %constant.26) | copy-start | bytes 6148
  38.4 6.0 %collective-permute-start = (bf16[4,32,256]{2,1,0:T(8,128)(2,1)}, bf16[4,32,256]{2,1,0:T(8,128)(2,1)S(1)}, u32[]{:S(2)}, u32[]{:S(2)}) collective-permute-start(bf16[4,32,256]{2,1,0:T(8,128)(2,1)} %get-tuple-element.51), channel_id=1, source_target_pairs={{0,1},{1,0},{2,3},{3,2},{4,5},{5,4},{6,7},{7,6},{8,9},{9,8},{10,11... | collective-permute-start | bytes 196616 | tf_op jit(solution)/shard_map/ppermute | solution.py:346
  38.6 6.7 %collective-permute-start.1 = (bf16[4,32,256]{2,1,0:T(8,128)(2,1)}, bf16[4,32,256]{2,1,0:T(8,128)(2,1)S(1)}, u32[]{:S(2)}, u32[]{:S(2)}) collective-permute-start(bf16[4,32,256]{2,1,0:T(8,128)(2,1)} %get-tuple-element.54), channel_id=1, source_target_pairs={{0,2},{1,3},{2,0},{3,1},{4,6},{5,7},{6,4},{7,5},{8,10},{9,11},{10,... | collective-permute-start | bytes 196616 | tf_op jit(solution)/shard_map/ppermute | solution.py:346
  40.2 7.1 %collective-permute-start.2 = (bf16[4,32,256]{2,1,0:T(8,128)(2,1)}, bf16[4,32,256]{2,1,0:T(8,128)(2,1)S(1)}, u32[]{:S(2)}, u32[]{:S(2)}) collective-permute-start(bf16[4,32,256]{2,1,0:T(8,128)(2,1)} %get-tuple-element.57), channel_id=1, source_target_pairs={{0,3},{1,2},{2,1},{3,0},{4,7},{5,6},{6,5},{7,4},{8,11},{9,10},{10,... | collective-permute-start | bytes 196616 | tf_op jit(solution)/shard_map/ppermute | solution.py:346
  40.6 7.8 %collective-permute-start.3 = (bf16[4,32,256]{2,1,0:T(8,128)(2,1)}, bf16[4,32,256]{2,1,0:T(8,128)(2,1)S(1)}, u32[]{:S(2)}, u32[]{:S(2)}) collective-permute-start(bf16[4,32,256]{2,1,0:T(8,128)(2,1)} %get-tuple-element.60), channel_id=1, source_target_pairs={{0,4},{1,5},{2,6},{3,7},{4,0},{5,1},{6,2},{7,3},{8,12},{9,13},{10,... | collective-permute-start | bytes 196616 | tf_op jit(solution)/shard_map/ppermute | solution.py:346
  42.0 10.7 %collective-permute-start.6 = (bf16[4,32,256]{2,1,0:T(8,128)(2,1)}, bf16[4,32,256]{2,1,0:T(8,128)(2,1)S(1)}, u32[]{:S(2)}, u32[]{:S(2)}) collective-permute-start(bf16[4,32,256]{2,1,0:T(8,128)(2,1)} %get-tuple-element.70), channel_id=1, source_target_pairs={{0,8},{1,9},{2,10},{3,11},{4,12},{5,13},{6,14},{7,15},{8,0},{9,1},... | collective-permute-start | bytes 196616 | tf_op jit(solution)/shard_map/ppermute | solution.py:346
  44.4 9.1 %collective-permute-start.4 = (bf16[4,32,256]{2,1,0:T(8,128)(2,1)}, bf16[4,32,256]{2,1,0:T(8,128)(2,1)S(1)}, u32[]{:S(2)}, u32[]{:S(2)}) collective-permute-start(bf16[4,32,256]{2,1,0:T(8,128)(2,1)} %get-tuple-element.63), channel_id=1, source_target_pairs={{0,5},{1,4},{2,7},{3,6},{4,1},{5,0},{6,3},{7,2},{8,13},{9,12},{10,... | collective-permute-start | bytes 196616 | tf_op jit(solution)/shard_map/ppermute | solution.py:346
  45.3 11.1 %collective-permute-start.8 = (bf16[4,32,256]{2,1,0:T(8,128)(2,1)}, bf16[4,32,256]{2,1,0:T(8,128)(2,1)S(1)}, u32[]{:S(2)}, u32[]{:S(2)}) collective-permute-start(bf16[4,32,256]{2,1,0:T(8,128)(2,1)} %get-tuple-element.75), channel_id=1, source_target_pairs={{0,9},{1,8},{2,11},{3,10},{4,13},{5,12},{6,15},{7,14},{8,1},{9,0},... | collective-permute-start | bytes 196616 | tf_op jit(solution)/shard_map/ppermute | solution.py:346
  47.3 11.8 %collective-permute-start.5 = (bf16[4,32,256]{2,1,0:T(8,128)(2,1)}, bf16[4,32,256]{2,1,0:T(8,128)(2,1)S(1)}, u32[]{:S(2)}, u32[]{:S(2)}) collective-permute-start(bf16[4,32,256]{2,1,0:T(8,128)(2,1)} %get-tuple-element.66), channel_id=1, source_target_pairs={{0,6},{1,7},{2,4},{3,5},{4,2},{5,3},{6,0},{7,1},{8,14},{9,15},{10,... | collective-permute-start | bytes 196616 | tf_op jit(solution)/shard_map/ppermute | solution.py:346
  48.4 14.1 %collective-permute-start.9 = (bf16[4,32,256]{2,1,0:T(8,128)(2,1)}, bf16[4,32,256]{2,1,0:T(8,128)(2,1)S(1)}, u32[]{:S(2)}, u32[]{:S(2)}) collective-permute-start(bf16[4,32,256]{2,1,0:T(8,128)(2,1)} %get-tuple-element.78), channel_id=1, source_target_pairs={{0,10},{1,11},{2,8},{3,9},{4,14},{5,15},{6,12},{7,13},{8,2},{9,3},... | collective-permute-start | bytes 196616 | tf_op jit(solution)/shard_map/ppermute | solution.py:346
  52.7 13.4 %collective-permute-start.7 = (bf16[4,32,256]{2,1,0:T(8,128)(2,1)}, bf16[4,32,256]{2,1,0:T(8,128)(2,1)S(1)}, u32[]{:S(2)}, u32[]{:S(2)}) collective-permute-start(bf16[4,32,256]{2,1,0:T(8,128)(2,1)} %get-tuple-element.71), channel_id=1, source_target_pairs={{0,7},{1,6},{2,5},{3,4},{4,3},{5,2},{6,1},{7,0},{8,15},{9,14},{10,... | collective-permute-start | bytes 196616 | tf_op jit(solution)/shard_map/ppermute | solution.py:346
  53.5 19.9 %copy-start = (bf16[4,32,256]{2,1,0:T(8,128)(2,1)S(1)}, bf16[4,32,256]{2,1,0:T(8,128)(2,1)}, u32[]{:S(2)}) copy-start(bf16[4,32,256]{2,1,0:T(8,128)(2,1)} %get-tuple-element.49.refs_1_) | copy-start | bytes 196612
  54.1 14.9 %collective-permute-start.10 = (bf16[4,32,256]{2,1,0:T(8,128)(2,1)}, bf16[4,32,256]{2,1,0:T(8,128)(2,1)}, u32[]{:S(2)}, u32[]{:S(2)}) collective-permute-start(bf16[4,32,256]{2,1,0:T(8,128)(2,1)} %get-tuple-element.80), channel_id=1, source_target_pairs={{0,11},{1,10},{2,9},{3,8},{4,15},{5,14},{6,13},{7,12},{8,3},{9,2},... | collective-permute-start | bytes 196616 | tf_op jit(solution)/shard_map/ppermute | solution.py:346
  57.0 12.0 %collective-permute-start.11 = (bf16[4,32,256]{2,1,0:T(8,128)(2,1)}, bf16[4,32,256]{2,1,0:T(8,128)(2,1)}, u32[]{:S(2)}, u32[]{:S(2)}) collective-permute-start(bf16[4,32,256]{2,1,0:T(8,128)(2,1)} %get-tuple-element.81), channel_id=1, source_target_pairs={{0,12},{1,13},{2,14},{3,15},{4,8},{5,9},{6,10},{7,11},{8,4},{9,5},... | collective-permute-start | bytes 196616 | tf_op jit(solution)/shard_map/ppermute | solution.py:346
  59.7 9.3 %collective-permute-start.12 = (bf16[4,32,256]{2,1,0:T(8,128)(2,1)}, bf16[4,32,256]{2,1,0:T(8,128)(2,1)}, u32[]{:S(2)}, u32[]{:S(2)}) collective-permute-start(bf16[4,32,256]{2,1,0:T(8,128)(2,1)} %get-tuple-element.82), channel_id=1, source_target_pairs={{0,13},{1,12},{2,15},{3,14},{4,9},{5,8},{6,11},{7,10},{8,5},{9,4},... | collective-permute-start | bytes 196616 | tf_op jit(solution)/shard_map/ppermute | solution.py:346
  63.1 6.7 %collective-permute-start.13 = (bf16[4,32,256]{2,1,0:T(8,128)(2,1)}, bf16[4,32,256]{2,1,0:T(8,128)(2,1)}, u32[]{:S(2)}, u32[]{:S(2)}) collective-permute-start(bf16[4,32,256]{2,1,0:T(8,128)(2,1)} %get-tuple-element.83), channel_id=1, source_target_pairs={{0,14},{1,15},{2,12},{3,13},{4,10},{5,11},{6,8},{7,9},{8,6},{9,7},... | collective-permute-start | bytes 196616 | tf_op jit(solution)/shard_map/ppermute | solution.py:346
  66.7 6.7 %collective-permute-start.14 = (bf16[4,32,256]{2,1,0:T(8,128)(2,1)}, bf16[4,32,256]{2,1,0:T(8,128)(2,1)}, u32[]{:S(2)}, u32[]{:S(2)}) collective-permute-start(bf16[4,32,256]{2,1,0:T(8,128)(2,1)} %get-tuple-element.84), channel_id=1, source_target_pairs={{0,15},{1,14},{2,13},{3,12},{4,11},{5,10},{6,9},{7,8},{8,7},{9,6},... | collective-permute-start | bytes 196616 | tf_op jit(solution)/shard_map/ppermute | solution.py:346
  67.4 6.0 %copy-start.6 = (bf16[4,32,256]{2,1,0:T(8,128)(2,1)S(1)}, bf16[4,32,256]{2,1,0:T(8,128)(2,1)}, u32[]{:S(2)}) copy-start(bf16[4,32,256]{2,1,0:T(8,128)(2,1)} %copy-done.5) | copy-start | bytes 196612
  67.4 6.0 %copy-start.8 = (bf16[4,32,256]{2,1,0:T(8,128)(2,1)S(1)}, bf16[4,32,256]{2,1,0:T(8,128)(2,1)}, u32[]{:S(2)}) copy-start(bf16[4,32,256]{2,1,0:T(8,128)(2,1)} %copy-done.7) | copy-start | bytes 196612
  67.4 6.0 %copy-start.10 = (bf16[4,32,256]{2,1,0:T(8,128)(2,1)S(1)}, bf16[4,32,256]{2,1,0:T(8,128)(2,1)}, u32[]{:S(2)}) copy-start(bf16[4,32,256]{2,1,0:T(8,128)(2,1)} %copy-done.9) | copy-start | bytes 196612
  (7 other events, 15.1 us)

commit v9 on v7

--- a/solution.py
+++ b/solution.py
@@ -58,12 +58,13 @@
     beside = max(1, LANES // (2 * all_out))
     last = np.kron(np.eye(beside), last.reshape(2 * LANES, 2 * all_out))
     last = np.concatenate(split(last), axis=1)
-    return stage, turn, np.concatenate([last, last])
+    return stage.astype(np.float32), turn, np.concatenate([last, last]).astype(np.float32)
 
 
 def halves(values):
-    high = values.astype(BF16)
-    return high, (values - high.astype(F32)).astype(BF16)
+    scaled = values * 65537.0
+    high = scaled - (scaled - values)
+    return high, values - high
 
 
 def spectra_kernel(first_stream, partners, outs, gain_ref, *refs):
@@ -184,8 +185,8 @@
             pltpu.VMEM((TAPS, WIDE, LANES), F32),
             pltpu.VMEM((WIDTH // LANES, ROWS * outs, LANES), F32),
         ]
-        + [pltpu.VMEM((2 * GROUP * WIDE, SPECTRA * LANES), BF16)] * groups
-        + [pltpu.VMEM((4 * GROUP * WIDTH * LANES // last.shape[0], last.shape[0]), BF16)] * groups,
+        + [pltpu.VMEM((2 * GROUP * WIDE, SPECTRA * LANES), F32)] * groups
+        + [pltpu.VMEM((4 * GROUP * WIDTH * LANES // last.shape[0], last.shape[0]), F32)] * groups,
         compiler_params=pltpu.CompilerParams(vmem_limit_bytes=VMEM_LIMIT),
         cost_estimate=pl.CostEstimate(
             flops=(stop - start) * SPECTRA * 12_000_000,
@@ -317,7 +318,7 @@
     samples = voltages.reshape(streams, 2, FRAMES * blocks, LANES).transpose(0, 2, 1, 3)
     samples = samples.reshape(streams, FRAMES, 2 * blocks, LANES)
     coeffs = taps.reshape(TAPS, blocks, LANES).transpose(1, 0, 2).reshape(TAPS * blocks, LANES)
-    cut = streams - streams // (2 * ROWS) * ROWS
+    cut = max(streams - ROWS, ROWS)
     wanted = (2 * station_order[:, None] + jnp.arange(2, dtype=jnp.int32)).reshape(-1, 1)
 
     def pick(start, stop, first):

time: 79.5 us -> 89 us (1.12)
  waiting for transfers between devices: 7.59 us -> 19.2 us
  starting transfers between devices: 30 us -> 34 us
  Pallas kernels: 37.5 us -> 33.7 us
  local copies, waits for them, and re-layouts: 3.33 us -> 0.2 us
  other arithmetic: 0.55 us -> 1.47 us
    ppermute x15, waiting for transfers between devices: 7.58 us -> 19.2 us  [body(): lax.ppermute(ready, 'ingest', [(i, i ^ k) for i in range(devices)])]
    ppermute x15, starting transfers between devices: 22.7 us -> 26.7 us  [body(): lax.ppermute(ready, 'ingest', [(i, i ^ k) for i in range(devices)])]
    pallas_call x2, Pallas kernels: 29.5 us -> 25.7 us  [spectra(): pl.pallas_call(functools.partial(spectra_kernel, start, partners, outs),...]
    unnamed x30 -> x14, local copies, waits for them, and re-layouts: 3.16 us -> 0.04 us
    convert_element_type x1 -> x2, other arithmetic: 0.4 us -> 1.33 us  [pick(): return (wanted == source).astype(BF16)]
  transfers between devices with their start and end apart: 16 -> 16, of which waited for: 4 -> 4; matrix products, arithmetic and copies ran while one was open for 1% -> 2% of each run, Pallas kernels for 21% -> 11%
where the time goes in v9:
time: 89 us; the launch traced here: 88.7 us
  starting transfers between devices  34 us (38%)
  Pallas kernels  33.7 us (38%)
  waiting for transfers between devices  19.2 us (22%)
  other arithmetic  1.47 us (2%)
    ppermute x15, starting transfers between devices, body(): lax.ppermute(ready, 'ingest', [(i, i ^ k) for i in range(devices)])  26.7 us
    pallas_call x2, Pallas kernels, spectra(): pl.pallas_call(functools.partial(spectra_kernel, start, partners, outs),...  25.7 us
    ppermute x15, waiting for transfers between devices, body(): lax.ppermute(ready, 'ingest', [(i, i ^ k) for i in range(devices)])  19.2 us
    all_to_all x1, starting transfers between devices, body(): lax.all_to_all(packed, 'ingest', split_axis=0, concat_axis=0, tiled=True)  7.38 us
    pallas_call x1, Pallas kernels, tiles(): pl.pallas_call(functools.partial(tiles_kernel, len(parts)), out_shape=jax...  5.87 us
    pallas_call x1, Pallas kernels, arrange(): pl.pallas_call(arrange_kernel, out_shape=(jax.ShapeDtypeStruct((OUT_DEV,...  2.14 us
  transfers between devices with their start and end apart: 16, of which 4 were waited for; matrix products, arithmetic and copies ran while one was open for 2% of the time, Pallas kernels for 11%

profile of v9, /device:TPU:1, one launch (start us, length us, event | category | flops | bytes accessed | tf_op | source)
XLA Modules:
  0.0 88.7 jit_solution(8323594680826480994)
XLA Ops:
  0.0 17.7 %spectra.2 = bf16[64,48,256]{2,1,0:T(8,128)(2,1)} custom-call(f32[32]{0:T(128)} %gain_ref.2, s32[64,11,64,128]{3,2,1,0:T(8,128)} %bitcast.11, s32[64,11,64,128]{3,2,1,0:T(8,128)} %bitcast.12, s32[64,11,64,128]{3,2,1,0:T(8,128)} %bitcast.13, s32[64,11,64,128]{3,2,1,0:T(8,128)} %bitcast.14, s32[64,11,64,128]{3,2,1,0:T(8,128)} %bitcast.15, ...), custom_call_target="tpu_custom_call" | custom-call | flops 4608000000 | bytes 17301504 | tf_op jit(solution)/shard_map/spectra/pallas_call | solution.py:176
  17.7 7.4 %all-to-all-start = ((bf16[16,4,48,256]{3,2,1,0:T(8,128)(2,1)}), bf16[16,4,48,256]{3,2,1,0:T(8,128)(2,1)S(1)}, u32[]{:S(2)}, u32[]{:S(2)}) async-start(bf16[16,4,48,256]{3,2,1,0:T(8,128)(2,1)} %bitcast.33), calls=%async_computation | async-start | bytes 3145728 | tf_op jit(solution)/shard_map/all_to_all | solution.py:332
  25.1 7.9 %spectra.3 = (bf16[4,16,256]{2,1,0:T(8,128)(2,1)}, bf16[4,16,256]{2,1,0:T(8,128)(2,1)}, bf16[4,16,256]{2,1,0:T(8,128)(2,1)}, bf16[4,16,256]{2,1,0:T(8,128)(2,1)}...) custom-call(f32[32]{0:T(128)} %gain_ref.2, ...), custom_call_target="tpu_custom_call" | custom-call | flops 1536000000 | bytes 5767168 | tf_op jit(solution)/shard_map/spectra/pallas_call | solution.py:176
  33.3 1.6 %collective-permute-start.1 = (bf16[4,16,256]{2,1,0:T(8,128)(2,1)}, bf16[4,16,256]{2,1,0:T(8,128)(2,1)S(1)}, u32[]{:S(2)}, u32[]{:S(2)}) collective-permute-start(bf16[4,16,256]{2,1,0:T(8,128)(2,1)} %get-tuple-element.54), channel_id=1, source_target_pairs={{0,2},{1,3},{2,0},{3,1},{4,6},{5,7},{6,4},{7,5},{8,10},{9,11},{10,... | collective-permute-start | bytes 98312 | tf_op jit(solution)/shard_map/ppermute | solution.py:343
  34.9 0.4 collective-permute-start.2
  35.3 1.4 %collective-permute-start.3 = (bf16[4,16,256]{2,1,0:T(8,128)(2,1)}, bf16[4,16,256]{2,1,0:T(8,128)(2,1)S(1)}, u32[]{:S(2)}, u32[]{:S(2)}) collective-permute-start(bf16[4,16,256]{2,1,0:T(8,128)(2,1)} %get-tuple-element.60), channel_id=1, source_target_pairs={{0,4},{1,5},{2,6},{3,7},{4,0},{5,1},{6,2},{7,3},{8,12},{9,13},{10,... | collective-permute-start | bytes 98312 | tf_op jit(solution)/shard_map/ppermute | solution.py:343
  36.7 2.1 %collective-permute-start.6 = (bf16[4,16,256]{2,1,0:T(8,128)(2,1)}, bf16[4,16,256]{2,1,0:T(8,128)(2,1)S(1)}, u32[]{:S(2)}, u32[]{:S(2)}) collective-permute-start(bf16[4,16,256]{2,1,0:T(8,128)(2,1)} %get-tuple-element.70), channel_id=1, source_target_pairs={{0,8},{1,9},{2,10},{3,11},{4,12},{5,13},{6,14},{7,15},{8,0},{9,1},... | collective-permute-start | bytes 98312 | tf_op jit(solution)/shard_map/ppermute | solution.py:343
  39.1 0.3 compare_convert_fusion.pick_ref
  39.5 0.9 collective-permute-start.4
  40.6 4.0 %collective-permute-start.5 = (bf16[4,16,256]{2,1,0:T(8,128)(2,1)}, bf16[4,16,256]{2,1,0:T(8,128)(2,1)S(1)}, u32[]{:S(2)}, u32[]{:S(2)}) collective-permute-start(bf16[4,16,256]{2,1,0:T(8,128)(2,1)} %get-tuple-element.66), channel_id=1, source_target_pairs={{0,6},{1,7},{2,4},{3,5},{4,2},{5,3},{6,0},{7,1},{8,14},{9,15},{10,... | collective-permute-start | bytes 98312 | tf_op jit(solution)/shard_map/ppermute | solution.py:343
  44.6 7.3 %collective-permute-done.3.refs_5_ = bf16[4,16,256]{2,1,0:T(8,128)(2,1)S(1)} collective-permute-done((bf16[4,16,256]{2,1,0:T(8,128)(2,1)}, bf16[4,16,256]{2,1,0:T(8,128)(2,1)S(1)}, u32[]{:S(2)}, u32[]{:S(2)}) %collective-permute-start.3) | collective-permute-done | bytes 32800 | tf_op jit(solution)/shard_map/ppermute | solution.py:343
  51.9 4.8 %collective-permute-start.9 = (bf16[4,16,256]{2,1,0:T(8,128)(2,1)}, bf16[4,16,256]{2,1,0:T(8,128)(2,1)S(1)}, u32[]{:S(2)}, u32[]{:S(2)}) collective-permute-start(bf16[4,16,256]{2,1,0:T(8,128)(2,1)} %get-tuple-element.78), channel_id=1, source_target_pairs={{0,10},{1,11},{2,8},{3,9},{4,14},{5,15},{6,12},{7,13},{8,2},{9,3},... | collective-permute-start | bytes 98312 | tf_op jit(solution)/shard_map/ppermute | solution.py:343
  56.7 8.0 %collective-permute-done.6.refs_9_ = bf16[4,16,256]{2,1,0:T(8,128)(2,1)S(1)} collective-permute-done((bf16[4,16,256]{2,1,0:T(8,128)(2,1)}, bf16[4,16,256]{2,1,0:T(8,128)(2,1)S(1)}, u32[]{:S(2)}, u32[]{:S(2)}) %collective-permute-start.6) | collective-permute-done | bytes 32800 | tf_op jit(solution)/shard_map/ppermute | solution.py:343
  64.7 0.8 collective-permute-start.7
  65.5 1.0 %compare_convert_fusion.1.refs_0_ = bf16[1024,256]{1,0:T(8,128)(2,1)} fusion(s32[256]{0:T(256)S(1)} %add_add_fusion, s32[1024]{0:T(1024)S(1)} %add.35), kind=kLoop, calls=%fused_computation.1 | loop fusion | flops 524288 | bytes 529408 | tf_op jit(solution)/shard_map/convert_element_type | solution.py:327
  66.5 1.8 %collective-permute-start.10 = (bf16[4,16,256]{2,1,0:T(8,128)(2,1)}, bf16[4,16,256]{2,1,0:T(8,128)(2,1)S(1)}, u32[]{:S(2)}, u32[]{:S(2)}) collective-permute-start(bf16[4,16,256]{2,1,0:T(8,128)(2,1)} %get-tuple-element.80), channel_id=1, source_target_pairs={{0,11},{1,10},{2,9},{3,8},{4,15},{5,14},{6,13},{7,12},{8,3},{9,2},... | collective-permute-start | bytes 98312 | tf_op jit(solution)/shard_map/ppermute | solution.py:343
  68.4 2.1 %collective-permute-start.11 = (bf16[4,16,256]{2,1,0:T(8,128)(2,1)}, bf16[4,16,256]{2,1,0:T(8,128)(2,1)}, u32[]{:S(2)}, u32[]{:S(2)}) collective-permute-start(bf16[4,16,256]{2,1,0:T(8,128)(2,1)} %get-tuple-element.81), channel_id=1, source_target_pairs={{0,12},{1,13},{2,14},{3,15},{4,8},{5,9},{6,10},{7,11},{8,4},{9,5},... | collective-permute-start | bytes 98312 | tf_op jit(solution)/shard_map/ppermute | solution.py:343
  70.4 3.0 %collective-permute-start.12 = (bf16[4,16,256]{2,1,0:T(8,128)(2,1)}, bf16[4,16,256]{2,1,0:T(8,128)(2,1)}, u32[]{:S(2)}, u32[]{:S(2)}) collective-permute-start(bf16[4,16,256]{2,1,0:T(8,128)(2,1)} %get-tuple-element.82), channel_id=1, source_target_pairs={{0,13},{1,12},{2,15},{3,14},{4,9},{5,8},{6,11},{7,10},{8,5},{9,4},... | collective-permute-start | bytes 98312 | tf_op jit(solution)/shard_map/ppermute | solution.py:343
  73.4 3.1 %collective-permute-start.13 = (bf16[4,16,256]{2,1,0:T(8,128)(2,1)}, bf16[4,16,256]{2,1,0:T(8,128)(2,1)}, u32[]{:S(2)}, u32[]{:S(2)}) collective-permute-start(bf16[4,16,256]{2,1,0:T(8,128)(2,1)} %get-tuple-element.83), channel_id=1, source_target_pairs={{0,14},{1,15},{2,12},{3,13},{4,10},{5,11},{6,8},{7,9},{8,6},{9,7},... | collective-permute-start | bytes 98312 | tf_op jit(solution)/shard_map/ppermute | solution.py:343
  76.5 0.3 collective-permute-start.14
  76.8 2.1 %arrange.1 = (bf16[2,1024,512]{2,1,0:T(8,128)(2,1)S(1)}, f32[2,8,128]{2,1,0:T(8,128)S(1)}) custom-call(bf16[1024,768]{1,0:T(8,128)(2,1)S(1)} %compare_convert_fusion.pick_ref, bf16[16,4,48,256]{3,2,1,0:T(8,128)(2,1)S(1)} %all-to-all-done.part_ref), custom_call_target="tpu_custom_call" | custom-call | flops 1100000000 | bytes 4000000 | tf_op jit(solution)/shard_map/arrange/pallas_call | solution.py:218
  78.9 0.3 collective-permute-done.13.refs_15_
  79.2 3.6 %collective-permute-done.14.refs_16_ = bf16[4,16,256]{2,1,0:T(8,128)(2,1)} collective-permute-done((bf16[4,16,256]{2,1,0:T(8,128)(2,1)}, bf16[4,16,256]{2,1,0:T(8,128)(2,1)}, u32[]{:S(2)}, u32[]{:S(2)}) %collective-permute-start.14) | collective-permute-done | bytes 32800 | tf_op jit(solution)/shard_map/ppermute | solution.py:343
  82.9 5.9 %tiles.1 = bf16[2,36,2,128,128]{4,3,2,1,0:T(8,128)(2,1)} custom-call(bf16[2,1024,512]{2,1,0:T(8,128)(2,1)S(1)} %get-tuple-element.46.early_ref, f32[2,8,128]{2,1,0:T(8,128)S(1)} %get-tuple-element.47.power_ref, bf16[1024,256]{1,0:T(8,128)(2,1)S(1)} %copy-done, bf16[4,16,256]{2,1,0:T(8,128)(2,1)S(1)} %copy-done.1, ...), custom_call_target="tpu_custom_call" | custom-call | flops 4499999744 | bytes 9000000 | tf_op jit(solution)/shard_map/tiles/pallas_call | solution.py:282
  (32 shorter events, 0.8 us)
Async XLA Ops:
  17.7 59.0 %all-to-all-start = ((bf16[16,4,48,256]{3,2,1,0:T(8,128)(2,1)}), bf16[16,4,48,256]{3,2,1,0:T(8,128)(2,1)S(1)}, u32[]{:S(2)}, u32[]{:S(2)}) async-start(bf16[16,4,48,256]{3,2,1,0:T(8,128)(2,1)} %bitcast.33), calls=%async_computation | async-start | bytes 3145728 | tf_op jit(solution)/shard_map/all_to_all | solution.py:332
  25.1 13.7 %copy-start.3 = (s32[512]{0:T(512)S(1)}, s32[512]{0:T(512)}, u32[]{:S(2)}) copy-start(s32[512]{0:T(512)} %param.14) | copy-start | bytes 6148
  25.1 14.0 %copy-start.2 = (s32[768]{0:T(1024)S(1)}, s32[768]{0:T(1024)}, u32[]{:S(2)}) copy-start(s32[768]{0:T(1024)} %constant.33) | copy-start | bytes 9220
  33.1 6.4 %copy-start.4 = (s32[256]{0:T(256)S(1)}, s32[256]{0:T(256)}, u32[]{:S(2)}) copy-start(s32[256]{0:T(256)} %constant.29.clone) | copy-start | bytes 3076
  33.1 6.4 %copy-start.5 = (s32[256]{0:T(256)S(1)}, s32[256]{0:T(256)}, u32[]{:S(2)}) copy-start(s32[256]{0:T(256)} %constant.28.clone) | copy-start | bytes 3076
  33.1 6.4 %copy-start.6 = (bf16[4,16,256]{2,1,0:T(8,128)(2,1)S(1)}, bf16[4,16,256]{2,1,0:T(8,128)(2,1)}, u32[]{:S(2)}) copy-start(bf16[4,16,256]{2,1,0:T(8,128)(2,1)} %get-tuple-element.63) | copy-start | bytes 98308
  33.1 6.4 %collective-permute-start = (bf16[4,16,256]{2,1,0:T(8,128)(2,1)}, bf16[4,16,256]{2,1,0:T(8,128)(2,1)S(1)}, u32[]{:S(2)}, u32[]{:S(2)}) collective-permute-start(bf16[4,16,256]{2,1,0:T(8,128)(2,1)} %get-tuple-element.51), channel_id=1, source_target_pairs={{0,1},{1,0},{2,3},{3,2},{4,5},{5,4},{6,7},{7,6},{8,9},{9,8},{10,11... | collective-permute-start | bytes 98312 | tf_op jit(solution)/shard_map/ppermute | solution.py:343
  33.3 7.1 %collective-permute-start.1 = (bf16[4,16,256]{2,1,0:T(8,128)(2,1)}, bf16[4,16,256]{2,1,0:T(8,128)(2,1)S(1)}, u32[]{:S(2)}, u32[]{:S(2)}) collective-permute-start(bf16[4,16,256]{2,1,0:T(8,128)(2,1)} %get-tuple-element.54), channel_id=1, source_target_pairs={{0,2},{1,3},{2,0},{3,1},{4,6},{5,7},{6,4},{7,5},{8,10},{9,11},{10,... | collective-permute-start | bytes 98312 | tf_op jit(solution)/shard_map/ppermute | solution.py:343
  34.9 5.7 %collective-permute-start.2 = (bf16[4,16,256]{2,1,0:T(8,128)(2,1)}, bf16[4,16,256]{2,1,0:T(8,128)(2,1)S(1)}, u32[]{:S(2)}, u32[]{:S(2)}) collective-permute-start(bf16[4,16,256]{2,1,0:T(8,128)(2,1)} %get-tuple-element.57), channel_id=1, source_target_pairs={{0,3},{1,2},{2,1},{3,0},{4,7},{5,6},{6,5},{7,4},{8,11},{9,10},{10,... | collective-permute-start | bytes 98312 | tf_op jit(solution)/shard_map/ppermute | solution.py:343
  35.3 16.6 %collective-permute-start.3 = (bf16[4,16,256]{2,1,0:T(8,128)(2,1)}, bf16[4,16,256]{2,1,0:T(8,128)(2,1)S(1)}, u32[]{:S(2)}, u32[]{:S(2)}) collective-permute-start(bf16[4,16,256]{2,1,0:T(8,128)(2,1)} %get-tuple-element.60), channel_id=1, source_target_pairs={{0,4},{1,5},{2,6},{3,7},{4,0},{5,1},{6,2},{7,3},{8,12},{9,13},{10,... | collective-permute-start | bytes 98312 | tf_op jit(solution)/shard_map/ppermute | solution.py:343
  36.7 28.0 %collective-permute-start.6 = (bf16[4,16,256]{2,1,0:T(8,128)(2,1)}, bf16[4,16,256]{2,1,0:T(8,128)(2,1)S(1)}, u32[]{:S(2)}, u32[]{:S(2)}) collective-permute-start(bf16[4,16,256]{2,1,0:T(8,128)(2,1)} %get-tuple-element.70), channel_id=1, source_target_pairs={{0,8},{1,9},{2,10},{3,11},{4,12},{5,13},{6,14},{7,15},{8,0},{9,1},... | collective-permute-start | bytes 98312 | tf_op jit(solution)/shard_map/ppermute | solution.py:343
  39.5 27.1 %collective-permute-start.4 = (bf16[4,16,256]{2,1,0:T(8,128)(2,1)S(1)}, bf16[4,16,256]{2,1,0:T(8,128)(2,1)S(1)}, u32[]{:S(2)}, u32[]{:S(2)}) collective-permute-start(bf16[4,16,256]{2,1,0:T(8,128)(2,1)S(1)} %copy-done.6), channel_id=1, source_target_pairs={{0,5},{1,4},{2,7},{3,6},{4,1},{5,0},{6,3},{7,2},{8,13},{9,12},{10,... | collective-permute-start | bytes 98312 | tf_op jit(solution)/shard_map/ppermute | solution.py:343
  40.4 28.0 %collective-permute-start.8 = (bf16[4,16,256]{2,1,0:T(8,128)(2,1)}, bf16[4,16,256]{2,1,0:T(8,128)(2,1)S(1)}, u32[]{:S(2)}, u32[]{:S(2)}) collective-permute-start(bf16[4,16,256]{2,1,0:T(8,128)(2,1)} %get-tuple-element.75), channel_id=1, source_target_pairs={{0,9},{1,8},{2,11},{3,10},{4,13},{5,12},{6,15},{7,14},{8,1},{9,0},... | collective-permute-start | bytes 98312 | tf_op jit(solution)/shard_map/ppermute | solution.py:343
  40.6 29.9 %collective-permute-start.5 = (bf16[4,16,256]{2,1,0:T(8,128)(2,1)}, bf16[4,16,256]{2,1,0:T(8,128)(2,1)S(1)}, u32[]{:S(2)}, u32[]{:S(2)}) collective-permute-start(bf16[4,16,256]{2,1,0:T(8,128)(2,1)} %get-tuple-element.66), channel_id=1, source_target_pairs={{0,6},{1,7},{2,4},{3,5},{4,2},{5,3},{6,0},{7,1},{8,14},{9,15},{10,... | collective-permute-start | bytes 98312 | tf_op jit(solution)/shard_map/ppermute | solution.py:343
  51.9 21.5 %collective-permute-start.9 = (bf16[4,16,256]{2,1,0:T(8,128)(2,1)}, bf16[4,16,256]{2,1,0:T(8,128)(2,1)S(1)}, u32[]{:S(2)}, u32[]{:S(2)}) collective-permute-start(bf16[4,16,256]{2,1,0:T(8,128)(2,1)} %get-tuple-element.78), channel_id=1, source_target_pairs={{0,10},{1,11},{2,8},{3,9},{4,14},{5,15},{6,12},{7,13},{8,2},{9,3},... | collective-permute-start | bytes 98312 | tf_op jit(solution)/shard_map/ppermute | solution.py:343
  64.7 11.8 %collective-permute-start.7 = (bf16[4,16,256]{2,1,0:T(8,128)(2,1)}, bf16[4,16,256]{2,1,0:T(8,128)(2,1)S(1)}, u32[]{:S(2)}, u32[]{:S(2)}) collective-permute-start(bf16[4,16,256]{2,1,0:T(8,128)(2,1)} %get-tuple-element.71), channel_id=1, source_target_pairs={{0,7},{1,6},{2,5},{3,4},{4,3},{5,2},{6,1},{7,0},{8,15},{9,14},{10,... | collective-permute-start | bytes 98312 | tf_op jit(solution)/shard_map/ppermute | solution.py:343
  66.5 16.3 %copy-start.1 = (bf16[4,16,256]{2,1,0:T(8,128)(2,1)S(1)}, bf16[4,16,256]{2,1,0:T(8,128)(2,1)}, u32[]{:S(2)}) copy-start(bf16[4,16,256]{2,1,0:T(8,128)(2,1)} %get-tuple-element.49.refs_1_) | copy-start | bytes 98308
  66.5 12.4 %collective-permute-start.10 = (bf16[4,16,256]{2,1,0:T(8,128)(2,1)}, bf16[4,16,256]{2,1,0:T(8,128)(2,1)S(1)}, u32[]{:S(2)}, u32[]{:S(2)}) collective-permute-start(bf16[4,16,256]{2,1,0:T(8,128)(2,1)} %get-tuple-element.80), channel_id=1, source_target_pairs={{0,11},{1,10},{2,9},{3,8},{4,15},{5,14},{6,13},{7,12},{8,3},{9,2},... | collective-permute-start | bytes 98312 | tf_op jit(solution)/shard_map/ppermute | solution.py:343
  68.4 10.6 %collective-permute-start.11 = (bf16[4,16,256]{2,1,0:T(8,128)(2,1)}, bf16[4,16,256]{2,1,0:T(8,128)(2,1)}, u32[]{:S(2)}, u32[]{:S(2)}) collective-permute-start(bf16[4,16,256]{2,1,0:T(8,128)(2,1)} %get-tuple-element.81), channel_id=1, source_target_pairs={{0,12},{1,13},{2,14},{3,15},{4,8},{5,9},{6,10},{7,11},{8,4},{9,5},... | collective-permute-start | bytes 98312 | tf_op jit(solution)/shard_map/ppermute | solution.py:343
  70.4 8.5 %collective-permute-start.12 = (bf16[4,16,256]{2,1,0:T(8,128)(2,1)}, bf16[4,16,256]{2,1,0:T(8,128)(2,1)}, u32[]{:S(2)}, u32[]{:S(2)}) collective-permute-start(bf16[4,16,256]{2,1,0:T(8,128)(2,1)} %get-tuple-element.82), channel_id=1, source_target_pairs={{0,13},{1,12},{2,15},{3,14},{4,9},{5,8},{6,11},{7,10},{8,5},{9,4},... | collective-permute-start | bytes 98312 | tf_op jit(solution)/shard_map/ppermute | solution.py:343
  73.4 5.8 %collective-permute-start.13 = (bf16[4,16,256]{2,1,0:T(8,128)(2,1)}, bf16[4,16,256]{2,1,0:T(8,128)(2,1)}, u32[]{:S(2)}, u32[]{:S(2)}) collective-permute-start(bf16[4,16,256]{2,1,0:T(8,128)(2,1)} %get-tuple-element.83), channel_id=1, source_target_pairs={{0,14},{1,15},{2,12},{3,13},{4,10},{5,11},{6,8},{7,9},{8,6},{9,7},... | collective-permute-start | bytes 98312 | tf_op jit(solution)/shard_map/ppermute | solution.py:343
  76.5 6.4 %collective-permute-start.14 = (bf16[4,16,256]{2,1,0:T(8,128)(2,1)}, bf16[4,16,256]{2,1,0:T(8,128)(2,1)}, u32[]{:S(2)}, u32[]{:S(2)}) collective-permute-start(bf16[4,16,256]{2,1,0:T(8,128)(2,1)} %get-tuple-element.84), channel_id=1, source_target_pairs={{0,15},{1,14},{2,13},{3,12},{4,11},{5,10},{6,9},{7,8},{8,7},{9,6},... | collective-permute-start | bytes 98312 | tf_op jit(solution)/shard_map/ppermute | solution.py:343
  76.8 6.1 %copy-start = (bf16[1024,256]{1,0:T(8,128)(2,1)S(1)}, bf16[1024,256]{1,0:T(8,128)(2,1)}, u32[]{:S(2)}) copy-start(bf16[1024,256]{1,0:T(8,128)(2,1)} %compare_convert_fusion.1.refs_0_) | copy-start | bytes 1572868

commit v10 on v9

--- a/solution.py
+++ b/solution.py
@@ -300,15 +300,6 @@
     )(early, power, *picks, *parts)
 
 
-def sending_order(devices):
-    far, near = list(range(devices // 2, devices)), list(range(1, devices // 2))
-    order, near = near[:4], near[4:]
-    while far or near:
-        order += far[:1] + near[:1]
-        far, near = far[1:], near[1:]
-    return order
-
-
 def body(voltages, taps, station_gain, station_order):
     devices = lax.axis_size("ingest")
     streams = 2 * voltages.shape[0]
@@ -318,7 +309,7 @@
     samples = voltages.reshape(streams, 2, FRAMES * blocks, LANES).transpose(0, 2, 1, 3)
     samples = samples.reshape(streams, FRAMES, 2 * blocks, LANES)
     coeffs = taps.reshape(TAPS, blocks, LANES).transpose(1, 0, 2).reshape(TAPS * blocks, LANES)
-    cut = max(streams - ROWS, ROWS)
+    cut = streams - streams // (2 * ROWS) * ROWS
     wanted = (2 * station_order[:, None] + jnp.arange(2, dtype=jnp.int32)).reshape(-1, 1)
 
     def pick(start, stop, first):
@@ -334,12 +325,10 @@
     if cut < streams:
         sent = spectra(samples, coeffs, station_gain, consts, outs, cut, streams, devices)
         received = {0: sent[0]}
-        order = sending_order(devices)
-        for place, k in enumerate(order):
+        for k in range(1, devices):
             ready = sent[k]
-            if place >= WINDOW:
-                past = order[place - WINDOW]
-                ready, received[past] = lax.optimization_barrier((ready, received[past]))
+            if k > WINDOW:
+                ready, received[k - WINDOW] = lax.optimization_barrier((ready, received[k - WINDOW]))
             received[k] = lax.ppermute(ready, "ingest", [(i, i ^ k) for i in range(devices)])
         late = [received[k] for k in range(devices)]
         picks = [pick(cut, streams, lax.axis_index("ingest"))]

time: 89 us -> 75.4 us (0.85)
  the two profiles are of different devices: /device:TPU:1 before, /device:TPU:11 now
where the time goes in v10:
time: 75.4 us; the launch traced here: 75.2 us
  Pallas kernels  34 us (45%)
  starting transfers between devices  26.7 us (35%)
  waiting for transfers between devices  10.4 us (14%)
  local copies, waits for them, and re-layouts  3.33 us (4%)
    pallas_call x2, Pallas kernels, spectra(): pl.pallas_call(functools.partial(spectra_kernel, start, partners, outs),...  26 us
    ppermute x15, starting transfers between devices, body(): lax.ppermute(ready, 'ingest', [(i, i ^ k) for i in range(devices)])  20.1 us
    ppermute x15, waiting for transfers between devices, body(): lax.ppermute(ready, 'ingest', [(i, i ^ k) for i in range(devices)])  10.4 us
    all_to_all x1, starting transfers between devices, body(): lax.all_to_all(packed, 'ingest', split_axis=0, concat_axis=0, tiled=True)  6.62 us
    pallas_call x1, Pallas kernels, tiles(): pl.pallas_call(functools.partial(tiles_kernel, len(parts)), out_shape=jax...  6.47 us
    unnamed x30, local copies, waits for them, and re-layouts  3.16 us
    pallas_call x1, Pallas kernels, arrange(): pl.pallas_call(arrange_kernel, out_shape=(jax.ShapeDtypeStruct((OUT_DEV,...  1.57 us
  transfers between devices with their start and end apart: 16, of which 6 were waited for; matrix products, arithmetic and copies ran while one was open for 1% of the time, Pallas kernels for 20%

profile of v10, /device:TPU:11, one launch (start us, length us, event | category | flops | bytes accessed | tf_op | source)
XLA Modules:
  0.0 75.2 jit_solution(9104920114190922638)
XLA Ops:
  0.0 12.8 %spectra.2 = bf16[64,32,256]{2,1,0:T(8,128)(2,1)} custom-call(f32[32]{0:T(128)} %gain_ref.2, s32[64,11,64,128]{3,2,1,0:T(8,128)} %bitcast.11, s32[64,11,64,128]{3,2,1,0:T(8,128)} %bitcast.12, s32[64,11,64,128]{3,2,1,0:T(8,128)} %bitcast.13, s32[64,11,64,128]{3,2,1,0:T(8,128)} %bitcast.14, s32[64,11,64,128]{3,2,1,0:T(8,128)} %bitcast.15, ...), custom_call_target="tpu_custom_call" | custom-call | flops 3072000000 | bytes 11534336 | tf_op jit(solution)/shard_map/spectra/pallas_call | solution.py:176
  12.8 6.6 %all-to-all-start = ((bf16[16,4,32,256]{3,2,1,0:T(8,128)(2,1)}), bf16[16,4,32,256]{3,2,1,0:T(8,128)(2,1)S(1)}, u32[]{:S(2)}, u32[]{:S(2)}) async-start(bf16[16,4,32,256]{3,2,1,0:T(8,128)(2,1)} %bitcast.33), calls=%async_computation | async-start | bytes 2097152 | tf_op jit(solution)/shard_map/all_to_all | solution.py:323
  19.5 13.2 %spectra.3 = (bf16[4,32,256]{2,1,0:T(8,128)(2,1)}, bf16[4,32,256]{2,1,0:T(8,128)(2,1)}, bf16[4,32,256]{2,1,0:T(8,128)(2,1)}, bf16[4,32,256]{2,1,0:T(8,128)(2,1)}...) custom-call(f32[32]{0:T(128)} %gain_ref.2, ...), custom_call_target="tpu_custom_call" | custom-call | flops 3072000000 | bytes 11534336 | tf_op jit(solution)/shard_map/spectra/pallas_call | solution.py:176
  33.1 1.2 %collective-permute-start.1 = (bf16[4,32,256]{2,1,0:T(8,128)(2,1)}, bf16[4,32,256]{2,1,0:T(8,128)(2,1)S(1)}, u32[]{:S(2)}, u32[]{:S(2)}) collective-permute-start(bf16[4,32,256]{2,1,0:T(8,128)(2,1)} %get-tuple-element.54), channel_id=1, source_target_pairs={{0,2},{1,3},{2,0},{3,1},{4,6},{5,7},{6,4},{7,5},{8,10},{9,11},{10,... | collective-permute-start | bytes 196616 | tf_op jit(solution)/shard_map/ppermute | solution.py:332
  35.0 1.6 %collective-permute-start.4 = (bf16[4,32,256]{2,1,0:T(8,128)(2,1)}, bf16[4,32,256]{2,1,0:T(8,128)(2,1)S(1)}, u32[]{:S(2)}, u32[]{:S(2)}) collective-permute-start(bf16[4,32,256]{2,1,0:T(8,128)(2,1)} %get-tuple-element.63), channel_id=1, source_target_pairs={{0,5},{1,4},{2,7},{3,6},{4,1},{5,0},{6,3},{7,2},{8,13},{9,12},{10,... | collective-permute-start | bytes 196616 | tf_op jit(solution)/shard_map/ppermute | solution.py:332
  37.0 1.2 %collective-permute-start.5 = (bf16[4,32,256]{2,1,0:T(8,128)(2,1)}, bf16[4,32,256]{2,1,0:T(8,128)(2,1)S(1)}, u32[]{:S(2)}, u32[]{:S(2)}) collective-permute-start(bf16[4,32,256]{2,1,0:T(8,128)(2,1)} %get-tuple-element.66), channel_id=1, source_target_pairs={{0,6},{1,7},{2,4},{3,5},{4,2},{5,3},{6,0},{7,1},{8,14},{9,15},{10,... | collective-permute-start | bytes 196616 | tf_op jit(solution)/shard_map/ppermute | solution.py:332
  38.4 1.3 %collective-permute-start.6 = (bf16[4,32,256]{2,1,0:T(8,128)(2,1)}, bf16[4,32,256]{2,1,0:T(8,128)(2,1)S(1)}, u32[]{:S(2)}, u32[]{:S(2)}) collective-permute-start(bf16[4,32,256]{2,1,0:T(8,128)(2,1)} %get-tuple-element.69), channel_id=1, source_target_pairs={{0,7},{1,6},{2,5},{3,4},{4,3},{5,2},{6,1},{7,0},{8,15},{9,14},{10,... | collective-permute-start | bytes 196616 | tf_op jit(solution)/shard_map/ppermute | solution.py:332
  39.7 0.8 %collective-permute-done.2.refs_4_ = bf16[4,32,256]{2,1,0:T(8,128)(2,1)S(1)} collective-permute-done((bf16[4,32,256]{2,1,0:T(8,128)(2,1)}, bf16[4,32,256]{2,1,0:T(8,128)(2,1)S(1)}, u32[]{:S(2)}, u32[]{:S(2)}) %collective-permute-start.2) | collective-permute-done | bytes 65568 | tf_op jit(solution)/shard_map/ppermute | solution.py:332
  40.5 2.9 %collective-permute-start.7 = (bf16[4,32,256]{2,1,0:T(8,128)(2,1)}, bf16[4,32,256]{2,1,0:T(8,128)(2,1)S(1)}, u32[]{:S(2)}, u32[]{:S(2)}) collective-permute-start(bf16[4,32,256]{2,1,0:T(8,128)(2,1)} %get-tuple-element.72), channel_id=1, source_target_pairs={{0,8},{1,9},{2,10},{3,11},{4,12},{5,13},{6,14},{7,15},{8,0},{9,1},... | collective-permute-start | bytes 196616 | tf_op jit(solution)/shard_map/ppermute | solution.py:332
  43.3 1.3 %collective-permute-start.8 = (bf16[4,32,256]{2,1,0:T(8,128)(2,1)}, bf16[4,32,256]{2,1,0:T(8,128)(2,1)S(1)}, u32[]{:S(2)}, u32[]{:S(2)}) collective-permute-start(bf16[4,32,256]{2,1,0:T(8,128)(2,1)} %get-tuple-element.75), channel_id=1, source_target_pairs={{0,9},{1,8},{2,11},{3,10},{4,13},{5,12},{6,15},{7,14},{8,1},{9,0},... | collective-permute-start | bytes 196616 | tf_op jit(solution)/shard_map/ppermute | solution.py:332
  44.7 1.9 %collective-permute-start.9 = (bf16[4,32,256]{2,1,0:T(8,128)(2,1)}, bf16[4,32,256]{2,1,0:T(8,128)(2,1)S(1)}, u32[]{:S(2)}, u32[]{:S(2)}) collective-permute-start(bf16[4,32,256]{2,1,0:T(8,128)(2,1)} %get-tuple-element.78), channel_id=1, source_target_pairs={{0,10},{1,11},{2,8},{3,9},{4,14},{5,15},{6,12},{7,13},{8,2},{9,3},... | collective-permute-start | bytes 196616 | tf_op jit(solution)/shard_map/ppermute | solution.py:332
  47.6 3.1 %collective-permute-start.10 = (bf16[4,32,256]{2,1,0:T(8,128)(2,1)}, bf16[4,32,256]{2,1,0:T(8,128)(2,1)}, u32[]{:S(2)}, u32[]{:S(2)}) collective-permute-start(bf16[4,32,256]{2,1,0:T(8,128)(2,1)} %get-tuple-element.80), channel_id=1, source_target_pairs={{0,11},{1,10},{2,9},{3,8},{4,15},{5,14},{6,13},{7,12},{8,3},{9,2},... | collective-permute-start | bytes 196616 | tf_op jit(solution)/shard_map/ppermute | solution.py:332
  50.7 0.6 copy-done.3
  51.4 0.6 copy-done.5
  52.0 1.5 %collective-permute-start.12 = (bf16[4,32,256]{2,1,0:T(8,128)(2,1)}, bf16[4,32,256]{2,1,0:T(8,128)(2,1)}, u32[]{:S(2)}, u32[]{:S(2)}) collective-permute-start(bf16[4,32,256]{2,1,0:T(8,128)(2,1)} %get-tuple-element.82), channel_id=1, source_target_pairs={{0,13},{1,12},{2,15},{3,14},{4,9},{5,8},{6,11},{7,10},{8,5},{9,4},... | collective-permute-start | bytes 196616 | tf_op jit(solution)/shard_map/ppermute | solution.py:332
  53.5 0.6 copy-done.7
  54.1 1.0 %collective-permute-start.13 = (bf16[4,32,256]{2,1,0:T(8,128)(2,1)}, bf16[4,32,256]{2,1,0:T(8,128)(2,1)}, u32[]{:S(2)}, u32[]{:S(2)}) collective-permute-start(bf16[4,32,256]{2,1,0:T(8,128)(2,1)} %get-tuple-element.83), channel_id=1, source_target_pairs={{0,14},{1,15},{2,12},{3,13},{4,10},{5,11},{6,8},{7,9},{8,6},{9,7},... | collective-permute-start | bytes 196616 | tf_op jit(solution)/shard_map/ppermute | solution.py:332
  55.7 1.9 %collective-permute-start.14 = (bf16[4,32,256]{2,1,0:T(8,128)(2,1)}, bf16[4,32,256]{2,1,0:T(8,128)(2,1)}, u32[]{:S(2)}, u32[]{:S(2)}) collective-permute-start(bf16[4,32,256]{2,1,0:T(8,128)(2,1)} %get-tuple-element.84), channel_id=1, source_target_pairs={{0,15},{1,14},{2,13},{3,12},{4,11},{5,10},{6,9},{7,8},{8,7},{9,6},... | collective-permute-start | bytes 196616 | tf_op jit(solution)/shard_map/ppermute | solution.py:332
  57.7 1.6 %arrange.1 = (bf16[2,1024,512]{2,1,0:T(8,128)(2,1)S(1)}, f32[2,8,128]{2,1,0:T(8,128)S(1)}) custom-call(bf16[1024,512]{1,0:T(8,128)(2,1)S(1)} %get-tuple-element.86.pick_ref, bf16[16,4,32,256]{3,2,1,0:T(8,128)(2,1)S(1)} %all-to-all-done.part_ref), custom_call_target="tpu_custom_call" | custom-call | flops 1100000000 | bytes 4000000 | tf_op jit(solution)/shard_map/arrange/pallas_call | solution.py:218
  59.3 2.9 %collective-permute-done.11.refs_13_ = bf16[4,32,256]{2,1,0:T(8,128)(2,1)} collective-permute-done((bf16[4,32,256]{2,1,0:T(8,128)(2,1)}, bf16[4,32,256]{2,1,0:T(8,128)(2,1)}, u32[]{:S(2)}, u32[]{:S(2)}) %collective-permute-start.11) | collective-permute-done | bytes 65568 | tf_op jit(solution)/shard_map/ppermute | solution.py:332
  62.1 2.8 %collective-permute-done.12.refs_14_ = bf16[4,32,256]{2,1,0:T(8,128)(2,1)} collective-permute-done((bf16[4,32,256]{2,1,0:T(8,128)(2,1)}, bf16[4,32,256]{2,1,0:T(8,128)(2,1)}, u32[]{:S(2)}, u32[]{:S(2)}) %collective-permute-start.12) | collective-permute-done | bytes 65568 | tf_op jit(solution)/shard_map/ppermute | solution.py:332
  64.9 2.3 %collective-permute-done.13.refs_15_ = bf16[4,32,256]{2,1,0:T(8,128)(2,1)} collective-permute-done((bf16[4,32,256]{2,1,0:T(8,128)(2,1)}, bf16[4,32,256]{2,1,0:T(8,128)(2,1)}, u32[]{:S(2)}, u32[]{:S(2)}) %collective-permute-start.13) | collective-permute-done | bytes 65568 | tf_op jit(solution)/shard_map/ppermute | solution.py:332
  67.2 1.4 %collective-permute-done.14.refs_16_ = bf16[4,32,256]{2,1,0:T(8,128)(2,1)} collective-permute-done((bf16[4,32,256]{2,1,0:T(8,128)(2,1)}, bf16[4,32,256]{2,1,0:T(8,128)(2,1)}, u32[]{:S(2)}, u32[]{:S(2)}) %collective-permute-start.14) | collective-permute-done | bytes 65568 | tf_op jit(solution)/shard_map/ppermute | solution.py:332
  68.7 6.5 %tiles.1 = bf16[2,36,2,128,128]{4,3,2,1,0:T(8,128)(2,1)} custom-call(bf16[2,1024,512]{2,1,0:T(8,128)(2,1)S(1)} %get-tuple-element.46.early_ref, f32[2,8,128]{2,1,0:T(8,128)S(1)} %get-tuple-element.47.power_ref, bf16[1024,512]{1,0:T(8,128)(2,1)S(1)} %get-tuple-element.85.refs_0_, bf16[4,32,256]{2,1,0:T(8,128)(2,1)S(1)} %copy-done, ...), custom_call_target="tpu_custom_call" | custom-call | flops 4499999744 | bytes 9000000 | tf_op jit(solution)/shard_map/tiles/pallas_call | solution.py:282
  (47 shorter events, 3.3 us)
Async XLA Ops:
  12.8 44.8 %all-to-all-start = ((bf16[16,4,32,256]{3,2,1,0:T(8,128)(2,1)}), bf16[16,4,32,256]{3,2,1,0:T(8,128)(2,1)S(1)}, u32[]{:S(2)}, u32[]{:S(2)}) async-start(bf16[16,4,32,256]{3,2,1,0:T(8,128)(2,1)} %bitcast.33), calls=%async_computation | async-start | bytes 2097152 | tf_op jit(solution)/shard_map/all_to_all | solution.py:323
  19.4 17.2 %copy-start.11 = (s32[512]{0:T(512)S(1)}, s32[512]{0:T(512)}, u32[]{:S(2)}) copy-start(s32[512]{0:T(512)} %param.14) | copy-start | bytes 6148
  19.4 17.3 %copy-start.12 = (s32[512]{0:T(512)S(1)}, s32[512]{0:T(512)}, u32[]{:S(2)}) copy-start(s32[512]{0:T(512)} %constant.24.clone) | copy-start | bytes 6148
  19.4 17.3 %copy-start.13 = (s32[512]{0:T(512)S(1)}, s32[512]{0:T(512)}, u32[]{:S(2)}) copy-start(s32[512]{0:T(512)} %constant.23.clone) | copy-start | bytes 6148
  19.5 27.1 %copy-start.14 = (s32[512]{0:T(512)S(1)}, s32[512]{0:T(512)}, u32[]{:S(2)}) copy-start(s32[512]{0:T(512)} %constant.26) | copy-start | bytes 6148
  32.7 4.3 %collective-permute-start = (bf16[4,32,256]{2,1,0:T(8,128)(2,1)}, bf16[4,32,256]{2,1,0:T(8,128)(2,1)S(1)}, u32[]{:S(2)}, u32[]{:S(2)}) collective-permute-start(bf16[4,32,256]{2,1,0:T(8,128)(2,1)} %get-tuple-element.51), channel_id=1, source_target_pairs={{0,1},{1,0},{2,3},{3,2},{4,5},{5,4},{6,7},{7,6},{8,9},{9,8},{10,11... | collective-permute-start | bytes 196616 | tf_op jit(solution)/shard_map/ppermute | solution.py:332
  33.1 5.3 %collective-permute-start.1 = (bf16[4,32,256]{2,1,0:T(8,128)(2,1)}, bf16[4,32,256]{2,1,0:T(8,128)(2,1)S(1)}, u32[]{:S(2)}, u32[]{:S(2)}) collective-permute-start(bf16[4,32,256]{2,1,0:T(8,128)(2,1)} %get-tuple-element.54), channel_id=1, source_target_pairs={{0,2},{1,3},{2,0},{3,1},{4,6},{5,7},{6,4},{7,5},{8,10},{9,11},{10,... | collective-permute-start | bytes 196616 | tf_op jit(solution)/shard_map/ppermute | solution.py:332
  34.3 6.2 %collective-permute-start.2 = (bf16[4,32,256]{2,1,0:T(8,128)(2,1)}, bf16[4,32,256]{2,1,0:T(8,128)(2,1)S(1)}, u32[]{:S(2)}, u32[]{:S(2)}) collective-permute-start(bf16[4,32,256]{2,1,0:T(8,128)(2,1)} %get-tuple-element.57), channel_id=1, source_target_pairs={{0,3},{1,2},{2,1},{3,0},{4,7},{5,6},{6,5},{7,4},{8,11},{9,10},{10,... | collective-permute-start | bytes 196616 | tf_op jit(solution)/shard_map/ppermute | solution.py:332
  34.9 8.5 %collective-permute-start.3 = (bf16[4,32,256]{2,1,0:T(8,128)(2,1)}, bf16[4,32,256]{2,1,0:T(8,128)(2,1)S(1)}, u32[]{:S(2)}, u32[]{:S(2)}) collective-permute-start(bf16[4,32,256]{2,1,0:T(8,128)(2,1)} %get-tuple-element.60), channel_id=1, source_target_pairs={{0,4},{1,5},{2,6},{3,7},{4,0},{5,1},{6,2},{7,3},{8,12},{9,13},{10,... | collective-permute-start | bytes 196616 | tf_op jit(solution)/shard_map/ppermute | solution.py:332
  35.0 9.7 %collective-permute-start.4 = (bf16[4,32,256]{2,1,0:T(8,128)(2,1)}, bf16[4,32,256]{2,1,0:T(8,128)(2,1)S(1)}, u32[]{:S(2)}, u32[]{:S(2)}) collective-permute-start(bf16[4,32,256]{2,1,0:T(8,128)(2,1)} %get-tuple-element.63), channel_id=1, source_target_pairs={{0,5},{1,4},{2,7},{3,6},{4,1},{5,0},{6,3},{7,2},{8,13},{9,12},{10,... | collective-permute-start | bytes 196616 | tf_op jit(solution)/shard_map/ppermute | solution.py:332
  37.0 10.0 %collective-permute-start.5 = (bf16[4,32,256]{2,1,0:T(8,128)(2,1)}, bf16[4,32,256]{2,1,0:T(8,128)(2,1)S(1)}, u32[]{:S(2)}, u32[]{:S(2)}) collective-permute-start(bf16[4,32,256]{2,1,0:T(8,128)(2,1)} %get-tuple-element.66), channel_id=1, source_target_pairs={{0,6},{1,7},{2,4},{3,5},{4,2},{5,3},{6,0},{7,1},{8,14},{9,15},{10,... | collective-permute-start | bytes 196616 | tf_op jit(solution)/shard_map/ppermute | solution.py:332
  38.4 12.3 %collective-permute-start.6 = (bf16[4,32,256]{2,1,0:T(8,128)(2,1)}, bf16[4,32,256]{2,1,0:T(8,128)(2,1)S(1)}, u32[]{:S(2)}, u32[]{:S(2)}) collective-permute-start(bf16[4,32,256]{2,1,0:T(8,128)(2,1)} %get-tuple-element.69), channel_id=1, source_target_pairs={{0,7},{1,6},{2,5},{3,4},{4,3},{5,2},{6,1},{7,0},{8,15},{9,14},{10,... | collective-permute-start | bytes 196616 | tf_op jit(solution)/shard_map/ppermute | solution.py:332
  40.5 10.9 %collective-permute-start.7 = (bf16[4,32,256]{2,1,0:T(8,128)(2,1)}, bf16[4,32,256]{2,1,0:T(8,128)(2,1)S(1)}, u32[]{:S(2)}, u32[]{:S(2)}) collective-permute-start(bf16[4,32,256]{2,1,0:T(8,128)(2,1)} %get-tuple-element.72), channel_id=1, source_target_pairs={{0,8},{1,9},{2,10},{3,11},{4,12},{5,13},{6,14},{7,15},{8,0},{9,1},... | collective-permute-start | bytes 196616 | tf_op jit(solution)/shard_map/ppermute | solution.py:332
  43.3 10.2 %collective-permute-start.8 = (bf16[4,32,256]{2,1,0:T(8,128)(2,1)}, bf16[4,32,256]{2,1,0:T(8,128)(2,1)S(1)}, u32[]{:S(2)}, u32[]{:S(2)}) collective-permute-start(bf16[4,32,256]{2,1,0:T(8,128)(2,1)} %get-tuple-element.75), channel_id=1, source_target_pairs={{0,9},{1,8},{2,11},{3,10},{4,13},{5,12},{6,15},{7,14},{8,1},{9,0},... | collective-permute-start | bytes 196616 | tf_op jit(solution)/shard_map/ppermute | solution.py:332
  44.7 10.4 %collective-permute-start.9 = (bf16[4,32,256]{2,1,0:T(8,128)(2,1)}, bf16[4,32,256]{2,1,0:T(8,128)(2,1)S(1)}, u32[]{:S(2)}, u32[]{:S(2)}) collective-permute-start(bf16[4,32,256]{2,1,0:T(8,128)(2,1)} %get-tuple-element.78), channel_id=1, source_target_pairs={{0,10},{1,11},{2,8},{3,9},{4,14},{5,15},{6,12},{7,13},{8,2},{9,3},... | collective-permute-start | bytes 196616 | tf_op jit(solution)/shard_map/ppermute | solution.py:332
  47.0 21.7 %copy-start = (bf16[4,32,256]{2,1,0:T(8,128)(2,1)S(1)}, bf16[4,32,256]{2,1,0:T(8,128)(2,1)}, u32[]{:S(2)}) copy-start(bf16[4,32,256]{2,1,0:T(8,128)(2,1)} %get-tuple-element.49.refs_1_) | copy-start | bytes 196612
  47.6 11.6 %collective-permute-start.10 = (bf16[4,32,256]{2,1,0:T(8,128)(2,1)}, bf16[4,32,256]{2,1,0:T(8,128)(2,1)}, u32[]{:S(2)}, u32[]{:S(2)}) collective-permute-start(bf16[4,32,256]{2,1,0:T(8,128)(2,1)} %get-tuple-element.80), channel_id=1, source_target_pairs={{0,11},{1,10},{2,9},{3,8},{4,15},{5,14},{6,13},{7,12},{8,3},{9,2},... | collective-permute-start | bytes 196616 | tf_op jit(solution)/shard_map/ppermute | solution.py:332
  51.4 10.8 %collective-permute-start.11 = (bf16[4,32,256]{2,1,0:T(8,128)(2,1)}, bf16[4,32,256]{2,1,0:T(8,128)(2,1)}, u32[]{:S(2)}, u32[]{:S(2)}) collective-permute-start(bf16[4,32,256]{2,1,0:T(8,128)(2,1)} %get-tuple-element.81), channel_id=1, source_target_pairs={{0,12},{1,13},{2,14},{3,15},{4,8},{5,9},{6,10},{7,11},{8,4},{9,5},... | collective-permute-start | bytes 196616 | tf_op jit(solution)/shard_map/ppermute | solution.py:332
  52.0 12.9 %collective-permute-start.12 = (bf16[4,32,256]{2,1,0:T(8,128)(2,1)}, bf16[4,32,256]{2,1,0:T(8,128)(2,1)}, u32[]{:S(2)}, u32[]{:S(2)}) collective-permute-start(bf16[4,32,256]{2,1,0:T(8,128)(2,1)} %get-tuple-element.82), channel_id=1, source_target_pairs={{0,13},{1,12},{2,15},{3,14},{4,9},{5,8},{6,11},{7,10},{8,5},{9,4},... | collective-permute-start | bytes 196616 | tf_op jit(solution)/shard_map/ppermute | solution.py:332
  54.1 13.1 %collective-permute-start.13 = (bf16[4,32,256]{2,1,0:T(8,128)(2,1)}, bf16[4,32,256]{2,1,0:T(8,128)(2,1)}, u32[]{:S(2)}, u32[]{:S(2)}) collective-permute-start(bf16[4,32,256]{2,1,0:T(8,128)(2,1)} %get-tuple-element.83), channel_id=1, source_target_pairs={{0,14},{1,15},{2,12},{3,13},{4,10},{5,11},{6,8},{7,9},{8,6},{9,7},... | collective-permute-start | bytes 196616 | tf_op jit(solution)/shard_map/ppermute | solution.py:332
  55.7 12.9 %collective-permute-start.14 = (bf16[4,32,256]{2,1,0:T(8,128)(2,1)}, bf16[4,32,256]{2,1,0:T(8,128)(2,1)}, u32[]{:S(2)}, u32[]{:S(2)}) collective-permute-start(bf16[4,32,256]{2,1,0:T(8,128)(2,1)} %get-tuple-element.84), channel_id=1, source_target_pairs={{0,15},{1,14},{2,13},{3,12},{4,11},{5,10},{6,9},{7,8},{8,7},{9,6},... | collective-permute-start | bytes 196616 | tf_op jit(solution)/shard_map/ppermute | solution.py:332
  57.7 11.0 %copy-start.6 = (bf16[4,32,256]{2,1,0:T(8,128)(2,1)S(1)}, bf16[4,32,256]{2,1,0:T(8,128)(2,1)}, u32[]{:S(2)}) copy-start(bf16[4,32,256]{2,1,0:T(8,128)(2,1)} %copy-done.5) | copy-start | bytes 196612
  57.7 11.0 %copy-start.8 = (bf16[4,32,256]{2,1,0:T(8,128)(2,1)S(1)}, bf16[4,32,256]{2,1,0:T(8,128)(2,1)}, u32[]{:S(2)}) copy-start(bf16[4,32,256]{2,1,0:T(8,128)(2,1)} %copy-done.7) | copy-start | bytes 196612
  57.7 11.0 %copy-start.10 = (bf16[4,32,256]{2,1,0:T(8,128)(2,1)S(1)}, bf16[4,32,256]{2,1,0:T(8,128)(2,1)}, u32[]{:S(2)}) copy-start(bf16[4,32,256]{2,1,0:T(8,128)(2,1)} %copy-done.9) | copy-start | bytes 196612
  (7 other events, 25.1 us)

commit v11 on v9

--- a/solution.py
+++ b/solution.py
@@ -302,7 +302,7 @@
 
 def sending_order(devices):
     far, near = list(range(devices // 2, devices)), list(range(1, devices // 2))
-    order, near = near[:4], near[4:]
+    order = []
     while far or near:
         order += far[:1] + near[:1]
         far, near = far[1:], near[1:]
@@ -318,7 +318,7 @@
     samples = voltages.reshape(streams, 2, FRAMES * blocks, LANES).transpose(0, 2, 1, 3)
     samples = samples.reshape(streams, FRAMES, 2 * blocks, LANES)
     coeffs = taps.reshape(TAPS, blocks, LANES).transpose(1, 0, 2).reshape(TAPS * blocks, LANES)
-    cut = max(streams - ROWS, ROWS)
+    cut = min(streams, ROWS)
     wanted = (2 * station_order[:, None] + jnp.arange(2, dtype=jnp.int32)).reshape(-1, 1)
 
     def pick(start, stop, first):

time: 89 us -> 83.5 us (0.938)
  the two profiles are of different devices: /device:TPU:1 before, /device:TPU:11 now
where the time goes in v11:
time: 83.5 us; the launch traced here: 83.2 us
  Pallas kernels  34.3 us (41%)
  starting transfers between devices  28 us (34%)
  waiting for transfers between devices  18.6 us (22%)
  local copies, waits for them, and re-layouts  1.48 us (2%)
    pallas_call x2, Pallas kernels, spectra(): pl.pallas_call(functools.partial(spectra_kernel, start, partners, outs),...  26.2 us
    ppermute x15, starting transfers between devices, body(): lax.ppermute(ready, 'ingest', [(i, i ^ k) for i in range(devices)])  21.4 us
    ppermute x15, waiting for transfers between devices, body(): lax.ppermute(ready, 'ingest', [(i, i ^ k) for i in range(devices)])  18.6 us
    pallas_call x1, Pallas kernels, tiles(): pl.pallas_call(functools.partial(tiles_kernel, len(parts)), out_shape=jax...  7.08 us
    all_to_all x1, starting transfers between devices, body(): lax.all_to_all(packed, 'ingest', split_axis=0, concat_axis=0, tiled=True)  6.64 us
  transfers between devices with their start and end apart: 16, of which 4 were waited for; matrix products, arithmetic and copies ran while one was open for 1% of the time, Pallas kernels for 23%

profile of v11, /device:TPU:11, one launch (start us, length us, event | category | flops | bytes accessed | tf_op | source)
XLA Modules:
  0.0 83.2 jit_solution(18203528654810297406)
XLA Ops:
  0.0 7.8 %spectra.2 = bf16[64,16,256]{2,1,0:T(8,128)(2,1)} custom-call(f32[32]{0:T(128)} %gain_ref.2, s32[64,11,64,128]{3,2,1,0:T(8,128)} %bitcast.11, s32[64,11,64,128]{3,2,1,0:T(8,128)} %bitcast.12, s32[64,11,64,128]{3,2,1,0:T(8,128)} %bitcast.13, s32[64,11,64,128]{3,2,1,0:T(8,128)} %bitcast.14, s32[64,11,64,128]{3,2,1,0:T(8,128)} %bitcast.15, ...), custom_call_target="tpu_custom_call" | custom-call | flops 1536000000 | bytes 5767168 | tf_op jit(solution)/shard_map/spectra/pallas_call | solution.py:176
  7.8 6.6 %all-to-all-start = ((bf16[16,4,16,256]{3,2,1,0:T(8,128)(2,1)}), bf16[16,4,16,256]{3,2,1,0:T(8,128)(2,1)S(1)}, u32[]{:S(2)}, u32[]{:S(2)}) async-start(bf16[16,4,16,256]{3,2,1,0:T(8,128)(2,1)} %bitcast.33), calls=%async_computation | async-start | bytes 1048576 | tf_op jit(solution)/shard_map/all_to_all | solution.py:332
  14.5 18.4 %spectra.3 = (bf16[4,48,256]{2,1,0:T(8,128)(2,1)}, bf16[4,48,256]{2,1,0:T(8,128)(2,1)}, bf16[4,48,256]{2,1,0:T(8,128)(2,1)}, bf16[4,48,256]{2,1,0:T(8,128)(2,1)}...) custom-call(f32[32]{0:T(128)} %gain_ref.2, ...), custom_call_target="tpu_custom_call" | custom-call | flops 4608000000 | bytes 17301504 | tf_op jit(solution)/shard_map/spectra/pallas_call | solution.py:176
  33.3 1.2 %collective-permute-start.1 = (bf16[4,48,256]{2,1,0:T(8,128)(2,1)}, bf16[4,48,256]{2,1,0:T(8,128)(2,1)S(1)}, u32[]{:S(2)}, u32[]{:S(2)}) collective-permute-start(bf16[4,48,256]{2,1,0:T(8,128)(2,1)} %get-tuple-element.54), channel_id=1, source_target_pairs={{0,2},{1,3},{2,0},{3,1},{4,6},{5,7},{6,4},{7,5},{8,10},{9,11},{10,... | collective-permute-start | bytes 294920 | tf_op jit(solution)/shard_map/ppermute | solution.py:343
  34.5 2.1 %collective-permute-start.2 = (bf16[4,48,256]{2,1,0:T(8,128)(2,1)}, bf16[4,48,256]{2,1,0:T(8,128)(2,1)S(1)}, u32[]{:S(2)}, u32[]{:S(2)}) collective-permute-start(bf16[4,48,256]{2,1,0:T(8,128)(2,1)} %get-tuple-element.58), channel_id=1, source_target_pairs={{0,8},{1,9},{2,10},{3,11},{4,12},{5,13},{6,14},{7,15},{8,0},{9,1},... | collective-permute-start | bytes 294920 | tf_op jit(solution)/shard_map/ppermute | solution.py:343
  36.7 0.8 collective-permute-start.4
  37.5 2.1 %collective-permute-start.6 = (bf16[4,48,256]{2,1,0:T(8,128)(2,1)}, bf16[4,48,256]{2,1,0:T(8,128)(2,1)S(1)}, u32[]{:S(2)}, u32[]{:S(2)}) collective-permute-start(bf16[4,48,256]{2,1,0:T(8,128)(2,1)} %get-tuple-element.68), channel_id=1, source_target_pairs={{0,10},{1,11},{2,8},{3,9},{4,14},{5,15},{6,12},{7,13},{8,2},{9,3},... | collective-permute-start | bytes 294920 | tf_op jit(solution)/shard_map/ppermute | solution.py:343
  40.3 1.2 %collective-permute-start.8 = (bf16[4,48,256]{2,1,0:T(8,128)(2,1)}, bf16[4,48,256]{2,1,0:T(8,128)(2,1)S(1)}, u32[]{:S(2)}, u32[]{:S(2)}) collective-permute-start(bf16[4,48,256]{2,1,0:T(8,128)(2,1)} %get-tuple-element.72), channel_id=1, source_target_pairs={{0,11},{1,10},{2,9},{3,8},{4,15},{5,14},{6,13},{7,12},{8,3},{9,2},... | collective-permute-start | bytes 294920 | tf_op jit(solution)/shard_map/ppermute | solution.py:343
  41.5 1.1 %collective-permute-start.10 = (bf16[4,48,256]{2,1,0:T(8,128)(2,1)}, bf16[4,48,256]{2,1,0:T(8,128)(2,1)S(1)}, u32[]{:S(2)}, u32[]{:S(2)}) collective-permute-start(bf16[4,48,256]{2,1,0:T(8,128)(2,1)} %get-tuple-element.75), channel_id=1, source_target_pairs={{0,12},{1,13},{2,14},{3,15},{4,8},{5,9},{6,10},{7,11},{8,4},{9,5},... | collective-permute-start | bytes 294920 | tf_op jit(solution)/shard_map/ppermute | solution.py:343
  42.7 7.3 %collective-permute-done.2.refs_9_ = bf16[4,48,256]{2,1,0:T(8,128)(2,1)S(1)} collective-permute-done((bf16[4,48,256]{2,1,0:T(8,128)(2,1)}, bf16[4,48,256]{2,1,0:T(8,128)(2,1)S(1)}, u32[]{:S(2)}, u32[]{:S(2)}) %collective-permute-start.2) | collective-permute-done | bytes 98336 | tf_op jit(solution)/shard_map/ppermute | solution.py:343
  50.0 0.7 collective-permute-start.3
  50.7 1.4 %collective-permute-done.4.refs_10_ = bf16[4,48,256]{2,1,0:T(8,128)(2,1)S(1)} collective-permute-done((bf16[4,48,256]{2,1,0:T(8,128)(2,1)}, bf16[4,48,256]{2,1,0:T(8,128)(2,1)S(1)}, u32[]{:S(2)}, u32[]{:S(2)}) %collective-permute-start.4) | collective-permute-done | bytes 98336 | tf_op jit(solution)/shard_map/ppermute | solution.py:343
  52.1 2.2 %collective-permute-start.5 = (bf16[4,48,256]{2,1,0:T(8,128)(2,1)}, bf16[4,48,256]{2,1,0:T(8,128)(2,1)S(1)}, u32[]{:S(2)}, u32[]{:S(2)}) collective-permute-start(bf16[4,48,256]{2,1,0:T(8,128)(2,1)} %get-tuple-element.64), channel_id=1, source_target_pairs={{0,4},{1,5},{2,6},{3,7},{4,0},{5,1},{6,2},{7,3},{8,12},{9,13},{10,... | collective-permute-start | bytes 294920 | tf_op jit(solution)/shard_map/ppermute | solution.py:343
  54.3 2.2 %collective-permute-start.7 = (bf16[4,48,256]{2,1,0:T(8,128)(2,1)}, bf16[4,48,256]{2,1,0:T(8,128)(2,1)S(1)}, u32[]{:S(2)}, u32[]{:S(2)}) collective-permute-start(bf16[4,48,256]{2,1,0:T(8,128)(2,1)} %get-tuple-element.69), channel_id=1, source_target_pairs={{0,5},{1,4},{2,7},{3,6},{4,1},{5,0},{6,3},{7,2},{8,13},{9,12},{10,... | collective-permute-start | bytes 294920 | tf_op jit(solution)/shard_map/ppermute | solution.py:343
  56.7 2.4 %collective-permute-start.9 = (bf16[4,48,256]{2,1,0:T(8,128)(2,1)}, bf16[4,48,256]{2,1,0:T(8,128)(2,1)}, u32[]{:S(2)}, u32[]{:S(2)}) collective-permute-start(bf16[4,48,256]{2,1,0:T(8,128)(2,1)} %get-tuple-element.73), channel_id=1, source_target_pairs={{0,6},{1,7},{2,4},{3,5},{4,2},{5,3},{6,0},{7,1},{8,14},{9,15},{10,... | collective-permute-start | bytes 294920 | tf_op jit(solution)/shard_map/ppermute | solution.py:343
  59.4 1.9 %collective-permute-start.12 = (bf16[4,48,256]{2,1,0:T(8,128)(2,1)}, bf16[4,48,256]{2,1,0:T(8,128)(2,1)}, u32[]{:S(2)}, u32[]{:S(2)}) collective-permute-start(bf16[4,48,256]{2,1,0:T(8,128)(2,1)} %get-tuple-element.82), channel_id=1, source_target_pairs={{0,13},{1,12},{2,15},{3,14},{4,9},{5,8},{6,11},{7,10},{8,5},{9,4},... | collective-permute-start | bytes 294920 | tf_op jit(solution)/shard_map/ppermute | solution.py:343
  61.3 0.6 copy-done.1
  62.0 0.7 collective-permute-start.13
  62.7 0.6 copy-done.3
  63.3 1.9 %collective-permute-start.14 = (bf16[4,48,256]{2,1,0:T(8,128)(2,1)}, bf16[4,48,256]{2,1,0:T(8,128)(2,1)}, u32[]{:S(2)}, u32[]{:S(2)}) collective-permute-start(bf16[4,48,256]{2,1,0:T(8,128)(2,1)} %get-tuple-element.84), channel_id=1, source_target_pairs={{0,15},{1,14},{2,13},{3,12},{4,11},{5,10},{6,9},{7,8},{8,7},{9,6},... | collective-permute-start | bytes 294920 | tf_op jit(solution)/shard_map/ppermute | solution.py:343
  65.2 0.9 %arrange.1 = (bf16[2,1024,512]{2,1,0:T(8,128)(2,1)S(1)}, f32[2,8,128]{2,1,0:T(8,128)S(1)}) custom-call(bf16[1024,256]{1,0:T(8,128)(2,1)S(1)} %compare_convert_fusion.1.pick_ref, bf16[16,4,16,256]{3,2,1,0:T(8,128)(2,1)S(1)} %all-to-all-done.part_ref), custom_call_target="tpu_custom_call" | custom-call | flops 1100000000 | bytes 4000000 | tf_op jit(solution)/shard_map/arrange/pallas_call | solution.py:218
  66.2 7.6 %collective-permute-done.13.refs_15_ = bf16[4,48,256]{2,1,0:T(8,128)(2,1)} collective-permute-done((bf16[4,48,256]{2,1,0:T(8,128)(2,1)}, bf16[4,48,256]{2,1,0:T(8,128)(2,1)}, u32[]{:S(2)}, u32[]{:S(2)}) %collective-permute-start.13) | collective-permute-done | bytes 98336 | tf_op jit(solution)/shard_map/ppermute | solution.py:343
  73.8 2.3 %collective-permute-done.14.refs_16_ = bf16[4,48,256]{2,1,0:T(8,128)(2,1)} collective-permute-done((bf16[4,48,256]{2,1,0:T(8,128)(2,1)}, bf16[4,48,256]{2,1,0:T(8,128)(2,1)}, u32[]{:S(2)}, u32[]{:S(2)}) %collective-permute-start.14) | collective-permute-done | bytes 98336 | tf_op jit(solution)/shard_map/ppermute | solution.py:343
  76.1 7.1 %tiles.1 = bf16[2,36,2,128,128]{4,3,2,1,0:T(8,128)(2,1)} custom-call(bf16[2,1024,512]{2,1,0:T(8,128)(2,1)S(1)} %get-tuple-element.46.early_ref, f32[2,8,128]{2,1,0:T(8,128)S(1)} %get-tuple-element.47.power_ref, bf16[1024,768]{1,0:T(8,128)(2,1)S(1)} %compare_convert_fusion.refs_0_, bf16[4,48,256]{2,1,0:T(8,128)(2,1)S(1)} %copy-done, ...), custom_call_target="tpu_custom_call" | custom-call | flops 4499999744 | bytes 9000000 | tf_op jit(solution)/shard_map/tiles/pallas_call | solution.py:282
  (36 shorter events, 1.7 us)
Async XLA Ops:
  7.8 57.4 %all-to-all-start = ((bf16[16,4,16,256]{3,2,1,0:T(8,128)(2,1)}), bf16[16,4,16,256]{3,2,1,0:T(8,128)(2,1)S(1)}, u32[]{:S(2)}, u32[]{:S(2)}) async-start(bf16[16,4,16,256]{3,2,1,0:T(8,128)(2,1)} %bitcast.33), calls=%async_computation | async-start | bytes 1048576 | tf_op jit(solution)/shard_map/all_to_all | solution.py:332
  14.4 25.2 %copy-start.7 = (s32[512]{0:T(512)S(1)}, s32[512]{0:T(512)}, u32[]{:S(2)}) copy-start(s32[512]{0:T(512)} %param.14) | copy-start | bytes 6148
  14.4 25.5 %copy-start.5 = (s32[768]{0:T(1024)S(1)}, s32[768]{0:T(1024)}, u32[]{:S(2)}) copy-start(s32[768]{0:T(1024)} %constant.29.clone) | copy-start | bytes 9220
  14.5 25.5 %copy-start.6 = (s32[768]{0:T(1024)S(1)}, s32[768]{0:T(1024)}, u32[]{:S(2)}) copy-start(s32[768]{0:T(1024)} %constant.28.clone) | copy-start | bytes 9220
  14.5 42.0 %copy-start.8 = (s32[256]{0:T(256)S(1)}, s32[256]{0:T(256)}, u32[]{:S(2)}) copy-start(s32[256]{0:T(256)} %constant.33) | copy-start | bytes 3076
  32.9 7.4 %collective-permute-start = (bf16[4,48,256]{2,1,0:T(8,128)(2,1)}, bf16[4,48,256]{2,1,0:T(8,128)(2,1)S(1)}, u32[]{:S(2)}, u32[]{:S(2)}) collective-permute-start(bf16[4,48,256]{2,1,0:T(8,128)(2,1)} %get-tuple-element.51), channel_id=1, source_target_pairs={{0,1},{1,0},{2,3},{3,2},{4,5},{5,4},{6,7},{7,6},{8,9},{9,8},{10,11... | collective-permute-start | bytes 294920 | tf_op jit(solution)/shard_map/ppermute | solution.py:343
  33.3 8.2 %collective-permute-start.1 = (bf16[4,48,256]{2,1,0:T(8,128)(2,1)}, bf16[4,48,256]{2,1,0:T(8,128)(2,1)S(1)}, u32[]{:S(2)}, u32[]{:S(2)}) collective-permute-start(bf16[4,48,256]{2,1,0:T(8,128)(2,1)} %get-tuple-element.54), channel_id=1, source_target_pairs={{0,2},{1,3},{2,0},{3,1},{4,6},{5,7},{6,4},{7,5},{8,10},{9,11},{10,... | collective-permute-start | bytes 294920 | tf_op jit(solution)/shard_map/ppermute | solution.py:343
  34.5 15.5 %collective-permute-start.2 = (bf16[4,48,256]{2,1,0:T(8,128)(2,1)}, bf16[4,48,256]{2,1,0:T(8,128)(2,1)S(1)}, u32[]{:S(2)}, u32[]{:S(2)}) collective-permute-start(bf16[4,48,256]{2,1,0:T(8,128)(2,1)} %get-tuple-element.58), channel_id=1, source_target_pairs={{0,8},{1,9},{2,10},{3,11},{4,12},{5,13},{6,14},{7,15},{8,0},{9,1},... | collective-permute-start | bytes 294920 | tf_op jit(solution)/shard_map/ppermute | solution.py:343
  36.7 15.4 %collective-permute-start.4 = (bf16[4,48,256]{2,1,0:T(8,128)(2,1)}, bf16[4,48,256]{2,1,0:T(8,128)(2,1)S(1)}, u32[]{:S(2)}, u32[]{:S(2)}) collective-permute-start(bf16[4,48,256]{2,1,0:T(8,128)(2,1)} %get-tuple-element.63), channel_id=1, source_target_pairs={{0,9},{1,8},{2,11},{3,10},{4,13},{5,12},{6,15},{7,14},{8,1},{9,0},... | collective-permute-start | bytes 294920 | tf_op jit(solution)/shard_map/ppermute | solution.py:343
  37.5 16.8 %collective-permute-start.6 = (bf16[4,48,256]{2,1,0:T(8,128)(2,1)}, bf16[4,48,256]{2,1,0:T(8,128)(2,1)S(1)}, u32[]{:S(2)}, u32[]{:S(2)}) collective-permute-start(bf16[4,48,256]{2,1,0:T(8,128)(2,1)} %get-tuple-element.68), channel_id=1, source_target_pairs={{0,10},{1,11},{2,8},{3,9},{4,14},{5,15},{6,12},{7,13},{8,2},{9,3},... | collective-permute-start | bytes 294920 | tf_op jit(solution)/shard_map/ppermute | solution.py:343
  39.9 36.2 %copy-start = (bf16[4,48,256]{2,1,0:T(8,128)(2,1)S(1)}, bf16[4,48,256]{2,1,0:T(8,128)(2,1)}, u32[]{:S(2)}) copy-start(bf16[4,48,256]{2,1,0:T(8,128)(2,1)} %get-tuple-element.49.refs_1_) | copy-start | bytes 294916
  40.3 16.4 %collective-permute-start.8 = (bf16[4,48,256]{2,1,0:T(8,128)(2,1)}, bf16[4,48,256]{2,1,0:T(8,128)(2,1)S(1)}, u32[]{:S(2)}, u32[]{:S(2)}) collective-permute-start(bf16[4,48,256]{2,1,0:T(8,128)(2,1)} %get-tuple-element.72), channel_id=1, source_target_pairs={{0,11},{1,10},{2,9},{3,8},{4,15},{5,14},{6,13},{7,12},{8,3},{9,2},... | collective-permute-start | bytes 294920 | tf_op jit(solution)/shard_map/ppermute | solution.py:343
  41.5 17.6 %collective-permute-start.10 = (bf16[4,48,256]{2,1,0:T(8,128)(2,1)}, bf16[4,48,256]{2,1,0:T(8,128)(2,1)S(1)}, u32[]{:S(2)}, u32[]{:S(2)}) collective-permute-start(bf16[4,48,256]{2,1,0:T(8,128)(2,1)} %get-tuple-element.75), channel_id=1, source_target_pairs={{0,12},{1,13},{2,14},{3,15},{4,8},{5,9},{6,10},{7,11},{8,4},{9,5},... | collective-permute-start | bytes 294920 | tf_op jit(solution)/shard_map/ppermute | solution.py:343
  50.0 9.5 %collective-permute-start.3 = (bf16[4,48,256]{2,1,0:T(8,128)(2,1)}, bf16[4,48,256]{2,1,0:T(8,128)(2,1)S(1)}, u32[]{:S(2)}, u32[]{:S(2)}) collective-permute-start(bf16[4,48,256]{2,1,0:T(8,128)(2,1)} %get-tuple-element.59), channel_id=1, source_target_pairs={{0,3},{1,2},{2,1},{3,0},{4,7},{5,6},{6,5},{7,4},{8,11},{9,10},{10,... | collective-permute-start | bytes 294920 | tf_op jit(solution)/shard_map/ppermute | solution.py:343
  52.1 9.2 %collective-permute-start.5 = (bf16[4,48,256]{2,1,0:T(8,128)(2,1)}, bf16[4,48,256]{2,1,0:T(8,128)(2,1)S(1)}, u32[]{:S(2)}, u32[]{:S(2)}) collective-permute-start(bf16[4,48,256]{2,1,0:T(8,128)(2,1)} %get-tuple-element.64), channel_id=1, source_target_pairs={{0,4},{1,5},{2,6},{3,7},{4,0},{5,1},{6,2},{7,3},{8,12},{9,13},{10,... | collective-permute-start | bytes 294920 | tf_op jit(solution)/shard_map/ppermute | solution.py:343
  54.3 8.4 %collective-permute-start.7 = (bf16[4,48,256]{2,1,0:T(8,128)(2,1)}, bf16[4,48,256]{2,1,0:T(8,128)(2,1)S(1)}, u32[]{:S(2)}, u32[]{:S(2)}) collective-permute-start(bf16[4,48,256]{2,1,0:T(8,128)(2,1)} %get-tuple-element.69), channel_id=1, source_target_pairs={{0,5},{1,4},{2,7},{3,6},{4,1},{5,0},{6,3},{7,2},{8,13},{9,12},{10,... | collective-permute-start | bytes 294920 | tf_op jit(solution)/shard_map/ppermute | solution.py:343
  56.7 9.5 %collective-permute-start.9 = (bf16[4,48,256]{2,1,0:T(8,128)(2,1)}, bf16[4,48,256]{2,1,0:T(8,128)(2,1)}, u32[]{:S(2)}, u32[]{:S(2)}) collective-permute-start(bf16[4,48,256]{2,1,0:T(8,128)(2,1)} %get-tuple-element.73), channel_id=1, source_target_pairs={{0,6},{1,7},{2,4},{3,5},{4,2},{5,3},{6,0},{7,1},{8,14},{9,15},{10,... | collective-permute-start | bytes 294920 | tf_op jit(solution)/shard_map/ppermute | solution.py:343
  59.1 7.1 %collective-permute-start.11 = (bf16[4,48,256]{2,1,0:T(8,128)(2,1)}, bf16[4,48,256]{2,1,0:T(8,128)(2,1)}, u32[]{:S(2)}, u32[]{:S(2)}) collective-permute-start(bf16[4,48,256]{2,1,0:T(8,128)(2,1)} %get-tuple-element.76), channel_id=1, source_target_pairs={{0,7},{1,6},{2,5},{3,4},{4,3},{5,2},{6,1},{7,0},{8,15},{9,14},{10,... | collective-permute-start | bytes 294920 | tf_op jit(solution)/shard_map/ppermute | solution.py:343
  59.4 6.7 %collective-permute-start.12 = (bf16[4,48,256]{2,1,0:T(8,128)(2,1)}, bf16[4,48,256]{2,1,0:T(8,128)(2,1)}, u32[]{:S(2)}, u32[]{:S(2)}) collective-permute-start(bf16[4,48,256]{2,1,0:T(8,128)(2,1)} %get-tuple-element.82), channel_id=1, source_target_pairs={{0,13},{1,12},{2,15},{3,14},{4,9},{5,8},{6,11},{7,10},{8,5},{9,4},... | collective-permute-start | bytes 294920 | tf_op jit(solution)/shard_map/ppermute | solution.py:343
  61.3 0.6 copy-start.1
  62.0 11.9 %collective-permute-start.13 = (bf16[4,48,256]{2,1,0:T(8,128)(2,1)}, bf16[4,48,256]{2,1,0:T(8,128)(2,1)}, u32[]{:S(2)}, u32[]{:S(2)}) collective-permute-start(bf16[4,48,256]{2,1,0:T(8,128)(2,1)} %get-tuple-element.83), channel_id=1, source_target_pairs={{0,14},{1,15},{2,12},{3,13},{4,10},{5,11},{6,8},{7,9},{8,6},{9,7},... | collective-permute-start | bytes 294920 | tf_op jit(solution)/shard_map/ppermute | solution.py:343
  63.3 12.8 %collective-permute-start.14 = (bf16[4,48,256]{2,1,0:T(8,128)(2,1)}, bf16[4,48,256]{2,1,0:T(8,128)(2,1)}, u32[]{:S(2)}, u32[]{:S(2)}) collective-permute-start(bf16[4,48,256]{2,1,0:T(8,128)(2,1)} %get-tuple-element.84), channel_id=1, source_target_pairs={{0,15},{1,14},{2,13},{3,12},{4,11},{5,10},{6,9},{7,8},{8,7},{9,6},... | collective-permute-start | bytes 294920 | tf_op jit(solution)/shard_map/ppermute | solution.py:343
  65.2 10.9 %copy-start.2 = (bf16[4,48,256]{2,1,0:T(8,128)(2,1)S(1)}, bf16[4,48,256]{2,1,0:T(8,128)(2,1)}, u32[]{:S(2)}) copy-start(bf16[4,48,256]{2,1,0:T(8,128)(2,1)} %copy-done.1) | copy-start | bytes 294916
  65.2 10.9 %copy-start.4 = (bf16[4,48,256]{2,1,0:T(8,128)(2,1)S(1)}, bf16[4,48,256]{2,1,0:T(8,128)(2,1)}, u32[]{:S(2)}) copy-start(bf16[4,48,256]{2,1,0:T(8,128)(2,1)} %copy-done.3) | copy-start | bytes 294916
  (1 other events, 0.6 us)

commit v12 on v10

--- a/solution.py
+++ b/solution.py
@@ -45,7 +45,7 @@
     stage[0, :, :, 0], stage[0, :, :, 1] = cos, sin
     stage[1, :, :, 0], stage[1, :, :, 1] = -sin, cos
     stage = np.stack(split(stage), axis=1).reshape(4 * AVG, 2 * blocks)
-    stage = np.concatenate([np.kron(np.eye(GROUP), stage.astype(np.float32))] * 2, axis=1).astype(ml_dtypes.bfloat16)
+    stage = np.kron(np.eye(GROUP), stage.astype(np.float32))
     angle = 2.0 * math.pi * np.outer(np.arange(AVG), np.arange(LANES)) / NCHAN
     turn = np.stack([np.cos(angle), -np.sin(angle)]).astype(np.float32)
     first = (NCHAN - all_out * AVG) // 2
@@ -58,7 +58,7 @@
     beside = max(1, LANES // (2 * all_out))
     last = np.kron(np.eye(beside), last.reshape(2 * LANES, 2 * all_out))
     last = np.concatenate(split(last), axis=1)
-    return stage.astype(np.float32), turn, np.concatenate([last, last]).astype(np.float32)
+    return stage.astype(np.float32), turn, last.astype(np.float32)
 
 
 def halves(values):
@@ -76,7 +76,7 @@
     halves_refs, turned_refs = refs[:groups], refs[groups:]
     outer, inner = pl.program_id(0), pl.program_id(1)
     size = GROUP * WIDE
-    beside = last_ref.shape[0] // (4 * LANES)
+    beside = last_ref.shape[0] // (2 * LANES)
     columns = beside * outs
 
     @pl.when((outer == 0) & (inner == 0))
@@ -100,7 +100,8 @@
 
     def first_product(g, start):
         lanes = slice(start * LANES, (start + 2) * LANES)
-        return jnp.dot(stage_ref[...], halves_refs[g][:, lanes], preferred_element_type=F32)
+        table = stage_ref[...]
+        return jnp.dot(jnp.concatenate([table, table], axis=1), halves_refs[g][:, lanes], preferred_element_type=F32)
 
     def first_rest(g, start, section):
         turn_real, turn_imag = turn_ref[0], turn_ref[1]
@@ -118,7 +119,8 @@
 
     def last_product(g, pair):
         rows = slice(pair * WIDTH, (pair + 1) * WIDTH)
-        return jnp.dot(turned_refs[g][rows, :], last_ref[...], preferred_element_type=F32)
+        table = last_ref[...]
+        return jnp.dot(turned_refs[g][rows, :], jnp.concatenate([table, table]), preferred_element_type=F32)
 
     def last_rest(g, pair, product):
         found = (product[:, :columns] + product[:, columns:]).T
@@ -186,7 +188,7 @@
             pltpu.VMEM((WIDTH // LANES, ROWS * outs, LANES), F32),
         ]
         + [pltpu.VMEM((2 * GROUP * WIDE, SPECTRA * LANES), F32)] * groups
-        + [pltpu.VMEM((4 * GROUP * WIDTH * LANES // last.shape[0], last.shape[0]), F32)] * groups,
+        + [pltpu.VMEM((2 * GROUP * WIDTH * LANES // last.shape[0], 2 * last.shape[0]), F32)] * groups,
         compiler_params=pltpu.CompilerParams(vmem_limit_bytes=VMEM_LIMIT),
         cost_estimate=pl.CostEstimate(
             flops=(stop - start) * SPECTRA * 12_000_000,
@@ -237,14 +239,33 @@
 
 
 def tiles_kernel(late, early_ref, power_ref, *refs):
-    (pick_refs, part_refs), refs = (refs[: min(late, 1)], refs[min(late, 1) :][:late]), refs[-3:]
-    out_ref, left_ref, right_ref = refs
+    pick_refs, part_refs, refs = refs[: min(late, 1)], refs[min(late, 1) :][:late], refs[min(late, 1) + late :]
+    out_ref, left_ref, right_ref, *refs = refs
     rows = 2 * STATIONS
     side = 2 * BLOCK
     blocks = STATIONS // BLOCK
     total = power_ref[0]
     if late:
-        data = [jnp.concatenate([part_ref[ri] for part_ref in part_refs], axis=0) for ri in range(2)]
+        late_ref, sems = refs
+        item = pl.program_id(0)
+
+        def copy(o, k):
+            return pltpu.make_async_copy(part_refs[k].at[pl.ds(2 * o, 2)], late_ref.at[o, k], sems.at[o, k])
+
+        @pl.when(item == 0)
+        def _():
+            for o in range(OUT_DEV):
+                for k in range(late):
+                    copy(o, k).start()
+
+        for o in range(OUT_DEV):
+
+            @pl.when(item == o)
+            def _():
+                for k in range(late):
+                    copy(o, k).wait()
+
+        data = [late_ref[item, :, ri].reshape(-1, WIDTH) for ri in range(2)]
         data = jnp.concatenate(data, axis=1)
         total = total + squares(data)
     power = jnp.sum(total) / (STATIONS * 2 * SPECTRA * AVG)
@@ -288,12 +309,14 @@
             pl.BlockSpec((1, 8, LANES), lambda o: (o, 0, 0)),
         ]
         + [pl.BlockSpec(pick.shape, lambda o: (0, 0)) for pick in picks]
-        + [pl.BlockSpec((2,) + part.shape[1:], lambda o: (o, 0, 0)) for part in parts],
+        + [pl.BlockSpec(memory_space=pltpu.HBM)] * len(parts),
         out_specs=pl.BlockSpec((1, pairs, 2, side, side), lambda o: (o, 0, 0, 0, 0)),
         scratch_shapes=[
             pltpu.VMEM((2 * rows, 2 * WIDTH), BF16),
             pltpu.VMEM((rows, 2 * WIDTH), BF16),
-        ],
+        ]
+        + [pltpu.VMEM((OUT_DEV, len(parts), 2) + part.shape[1:], BF16) for part in parts[:1]]
+        + [pltpu.SemaphoreType.DMA((OUT_DEV, len(parts))) for _ in parts[:1]],
         compiler_params=pltpu.CompilerParams(vmem_limit_bytes=40 * 2**20),
         cost_estimate=pl.CostEstimate(flops=4_500_000_000, bytes_accessed=9_000_000, transcendentals=0),
         name="tiles",

time: 75.4 us -> 75.9 us (level)
    pallas_call x1, Pallas kernels: 6.47 us -> 7.26 us  [tiles(): pl.pallas_call(functools.partial(tiles_kernel, len(parts)), out_shape=jax...]
  transfers between devices with their start and end apart: 16 -> 16, of which waited for: 6 -> 5; matrix products, arithmetic and copies ran while one was open for 1% -> 1% of each run, Pallas kernels for 20% -> 19%
where the time goes in v12:
time: 75.9 us; the launch traced here: 75.6 us
  Pallas kernels  34.3 us (45%)
  starting transfers between devices  27.2 us (36%)
  waiting for transfers between devices  10 us (13%)
  local copies, waits for them, and re-layouts  3.33 us (4%)
    pallas_call x2, Pallas kernels, spectra(): pl.pallas_call(functools.partial(spectra_kernel, start, partners, outs),...  25.5 us
    ppermute x15, starting transfers between devices, body(): lax.ppermute(ready, 'ingest', [(i, i ^ k) for i in range(devices)])  20.6 us
    ppermute x15, waiting for transfers between devices, body(): lax.ppermute(ready, 'ingest', [(i, i ^ k) for i in range(devices)])  10 us
    pallas_call x1, Pallas kernels, tiles(): pl.pallas_call(functools.partial(tiles_kernel, len(parts)), out_shape=jax...  7.26 us
    all_to_all x1, starting transfers between devices, body(): lax.all_to_all(packed, 'ingest', split_axis=0, concat_axis=0, tiled=True)  6.63 us
    unnamed x30, local copies, waits for them, and re-layouts  3.16 us
    pallas_call x1, Pallas kernels, arrange(): pl.pallas_call(arrange_kernel, out_shape=(jax.ShapeDtypeStruct((OUT_DEV,...  1.56 us
  transfers between devices with their start and end apart: 16, of which 5 were waited for; matrix products, arithmetic and copies ran while one was open for 1% of the time, Pallas kernels for 19%

profile of v12, /device:TPU:11, one launch (start us, length us, event | category | flops | bytes accessed | tf_op | source)
XLA Modules:
  0.0 75.6 jit_solution(14573517255247946523)
XLA Ops:
  0.0 12.5 %spectra.2 = bf16[64,32,256]{2,1,0:T(8,128)(2,1)} custom-call(f32[32]{0:T(128)} %gain_ref.2, s32[64,11,64,128]{3,2,1,0:T(8,128)} %bitcast.11, s32[64,11,64,128]{3,2,1,0:T(8,128)} %bitcast.12, s32[64,11,64,128]{3,2,1,0:T(8,128)} %bitcast.13, s32[64,11,64,128]{3,2,1,0:T(8,128)} %bitcast.14, s32[64,11,64,128]{3,2,1,0:T(8,128)} %bitcast.15, ...), custom_call_target="tpu_custom_call" | custom-call | flops 3072000000 | bytes 11534336 | tf_op jit(solution)/shard_map/spectra/pallas_call | solution.py:178
  12.5 6.6 %all-to-all-start = ((bf16[16,4,32,256]{3,2,1,0:T(8,128)(2,1)}), bf16[16,4,32,256]{3,2,1,0:T(8,128)(2,1)S(1)}, u32[]{:S(2)}, u32[]{:S(2)}) async-start(bf16[16,4,32,256]{3,2,1,0:T(8,128)(2,1)} %bitcast.33), calls=%async_computation | async-start | bytes 2097152 | tf_op jit(solution)/shard_map/all_to_all | solution.py:346
  19.2 12.9 %spectra.3 = (bf16[4,32,256]{2,1,0:T(8,128)(2,1)}, bf16[4,32,256]{2,1,0:T(8,128)(2,1)}, bf16[4,32,256]{2,1,0:T(8,128)(2,1)}, bf16[4,32,256]{2,1,0:T(8,128)(2,1)}...) custom-call(f32[32]{0:T(128)} %gain_ref.2, ...), custom_call_target="tpu_custom_call" | custom-call | flops 3072000000 | bytes 11534336 | tf_op jit(solution)/shard_map/spectra/pallas_call | solution.py:178
  32.6 1.2 %collective-permute-start.1 = (bf16[4,32,256]{2,1,0:T(8,128)(2,1)}, bf16[4,32,256]{2,1,0:T(8,128)(2,1)S(1)}, u32[]{:S(2)}, u32[]{:S(2)}) collective-permute-start(bf16[4,32,256]{2,1,0:T(8,128)(2,1)} %get-tuple-element.54), channel_id=1, source_target_pairs={{0,2},{1,3},{2,0},{3,1},{4,6},{5,7},{6,4},{7,5},{8,10},{9,11},{10,... | collective-permute-start | bytes 196616 | tf_op jit(solution)/shard_map/ppermute | solution.py:355
  34.4 1.6 %collective-permute-start.4 = (bf16[4,32,256]{2,1,0:T(8,128)(2,1)}, bf16[4,32,256]{2,1,0:T(8,128)(2,1)S(1)}, u32[]{:S(2)}, u32[]{:S(2)}) collective-permute-start(bf16[4,32,256]{2,1,0:T(8,128)(2,1)} %get-tuple-element.63), channel_id=1, source_target_pairs={{0,5},{1,4},{2,7},{3,6},{4,1},{5,0},{6,3},{7,2},{8,13},{9,12},{10,... | collective-permute-start | bytes 196616 | tf_op jit(solution)/shard_map/ppermute | solution.py:355
  36.4 1.3 %collective-permute-start.5 = (bf16[4,32,256]{2,1,0:T(8,128)(2,1)}, bf16[4,32,256]{2,1,0:T(8,128)(2,1)S(1)}, u32[]{:S(2)}, u32[]{:S(2)}) collective-permute-start(bf16[4,32,256]{2,1,0:T(8,128)(2,1)} %get-tuple-element.66), channel_id=1, source_target_pairs={{0,6},{1,7},{2,4},{3,5},{4,2},{5,3},{6,0},{7,1},{8,14},{9,15},{10,... | collective-permute-start | bytes 196616 | tf_op jit(solution)/shard_map/ppermute | solution.py:355
  37.7 1.5 %collective-permute-start.6 = (bf16[4,32,256]{2,1,0:T(8,128)(2,1)}, bf16[4,32,256]{2,1,0:T(8,128)(2,1)S(1)}, u32[]{:S(2)}, u32[]{:S(2)}) collective-permute-start(bf16[4,32,256]{2,1,0:T(8,128)(2,1)} %get-tuple-element.69), channel_id=1, source_target_pairs={{0,7},{1,6},{2,5},{3,4},{4,3},{5,2},{6,1},{7,0},{8,15},{9,14},{10,... | collective-permute-start | bytes 196616 | tf_op jit(solution)/shard_map/ppermute | solution.py:355
  39.2 1.0 %collective-permute-done.2.refs_4_ = bf16[4,32,256]{2,1,0:T(8,128)(2,1)S(1)} collective-permute-done((bf16[4,32,256]{2,1,0:T(8,128)(2,1)}, bf16[4,32,256]{2,1,0:T(8,128)(2,1)S(1)}, u32[]{:S(2)}, u32[]{:S(2)}) %collective-permute-start.2) | collective-permute-done | bytes 65568 | tf_op jit(solution)/shard_map/ppermute | solution.py:355
  40.1 1.4 %collective-permute-start.7 = (bf16[4,32,256]{2,1,0:T(8,128)(2,1)}, bf16[4,32,256]{2,1,0:T(8,128)(2,1)S(1)}, u32[]{:S(2)}, u32[]{:S(2)}) collective-permute-start(bf16[4,32,256]{2,1,0:T(8,128)(2,1)} %get-tuple-element.72), channel_id=1, source_target_pairs={{0,8},{1,9},{2,10},{3,11},{4,12},{5,13},{6,14},{7,15},{8,0},{9,1},... | collective-permute-start | bytes 196616 | tf_op jit(solution)/shard_map/ppermute | solution.py:355
  41.5 2.8 %collective-permute-start.8 = (bf16[4,32,256]{2,1,0:T(8,128)(2,1)}, bf16[4,32,256]{2,1,0:T(8,128)(2,1)S(1)}, u32[]{:S(2)}, u32[]{:S(2)}) collective-permute-start(bf16[4,32,256]{2,1,0:T(8,128)(2,1)} %get-tuple-element.75), channel_id=1, source_target_pairs={{0,9},{1,8},{2,11},{3,10},{4,13},{5,12},{6,15},{7,14},{8,1},{9,0},... | collective-permute-start | bytes 196616 | tf_op jit(solution)/shard_map/ppermute | solution.py:355
  44.3 1.8 %collective-permute-start.9 = (bf16[4,32,256]{2,1,0:T(8,128)(2,1)}, bf16[4,32,256]{2,1,0:T(8,128)(2,1)S(1)}, u32[]{:S(2)}, u32[]{:S(2)}) collective-permute-start(bf16[4,32,256]{2,1,0:T(8,128)(2,1)} %get-tuple-element.78), channel_id=1, source_target_pairs={{0,10},{1,11},{2,8},{3,9},{4,14},{5,15},{6,12},{7,13},{8,2},{9,3},... | collective-permute-start | bytes 196616 | tf_op jit(solution)/shard_map/ppermute | solution.py:355
  47.1 3.6 %collective-permute-start.10 = (bf16[4,32,256]{2,1,0:T(8,128)(2,1)}, bf16[4,32,256]{2,1,0:T(8,128)(2,1)}, u32[]{:S(2)}, u32[]{:S(2)}) collective-permute-start(bf16[4,32,256]{2,1,0:T(8,128)(2,1)} %get-tuple-element.80), channel_id=1, source_target_pairs={{0,11},{1,10},{2,9},{3,8},{4,15},{5,14},{6,13},{7,12},{8,3},{9,2},... | collective-permute-start | bytes 196616 | tf_op jit(solution)/shard_map/ppermute | solution.py:355
  50.7 0.6 copy-done.3
  51.4 0.6 copy-done.5
  52.0 1.6 %collective-permute-start.12 = (bf16[4,32,256]{2,1,0:T(8,128)(2,1)}, bf16[4,32,256]{2,1,0:T(8,128)(2,1)}, u32[]{:S(2)}, u32[]{:S(2)}) collective-permute-start(bf16[4,32,256]{2,1,0:T(8,128)(2,1)} %get-tuple-element.82), channel_id=1, source_target_pairs={{0,13},{1,12},{2,15},{3,14},{4,9},{5,8},{6,11},{7,10},{8,5},{9,4},... | collective-permute-start | bytes 196616 | tf_op jit(solution)/shard_map/ppermute | solution.py:355
  53.6 0.6 copy-done.7
  54.3 0.6 copy-done.9
  54.9 2.8 %collective-permute-start.14 = (bf16[4,32,256]{2,1,0:T(8,128)(2,1)}, bf16[4,32,256]{2,1,0:T(8,128)(2,1)}, u32[]{:S(2)}, u32[]{:S(2)}) collective-permute-start(bf16[4,32,256]{2,1,0:T(8,128)(2,1)} %get-tuple-element.84), channel_id=1, source_target_pairs={{0,15},{1,14},{2,13},{3,12},{4,11},{5,10},{6,9},{7,8},{8,7},{9,6},... | collective-permute-start | bytes 196616 | tf_op jit(solution)/shard_map/ppermute | solution.py:355
  57.7 1.6 %arrange.1 = (bf16[2,1024,512]{2,1,0:T(8,128)(2,1)S(1)}, f32[2,8,128]{2,1,0:T(8,128)S(1)}) custom-call(bf16[1024,512]{1,0:T(8,128)(2,1)S(1)} %get-tuple-element.86.pick_ref, bf16[16,4,32,256]{3,2,1,0:T(8,128)(2,1)S(1)} %all-to-all-done.part_ref), custom_call_target="tpu_custom_call" | custom-call | flops 1100000000 | bytes 4000000 | tf_op jit(solution)/shard_map/arrange/pallas_call | solution.py:220
  59.3 2.5 %collective-permute-done.11.refs_13_ = bf16[4,32,256]{2,1,0:T(8,128)(2,1)} collective-permute-done((bf16[4,32,256]{2,1,0:T(8,128)(2,1)}, bf16[4,32,256]{2,1,0:T(8,128)(2,1)}, u32[]{:S(2)}, u32[]{:S(2)}) %collective-permute-start.11) | collective-permute-done | bytes 65568 | tf_op jit(solution)/shard_map/ppermute | solution.py:355
  61.8 1.4 %collective-permute-done.12.refs_14_ = bf16[4,32,256]{2,1,0:T(8,128)(2,1)} collective-permute-done((bf16[4,32,256]{2,1,0:T(8,128)(2,1)}, bf16[4,32,256]{2,1,0:T(8,128)(2,1)}, u32[]{:S(2)}, u32[]{:S(2)}) %collective-permute-start.12) | collective-permute-done | bytes 65568 | tf_op jit(solution)/shard_map/ppermute | solution.py:355
  63.2 3.7 %collective-permute-done.13.refs_15_ = bf16[4,32,256]{2,1,0:T(8,128)(2,1)} collective-permute-done((bf16[4,32,256]{2,1,0:T(8,128)(2,1)}, bf16[4,32,256]{2,1,0:T(8,128)(2,1)}, u32[]{:S(2)}, u32[]{:S(2)}) %collective-permute-start.13) | collective-permute-done | bytes 65568 | tf_op jit(solution)/shard_map/ppermute | solution.py:355
  66.9 1.4 %collective-permute-done.14.refs_16_ = bf16[4,32,256]{2,1,0:T(8,128)(2,1)} collective-permute-done((bf16[4,32,256]{2,1,0:T(8,128)(2,1)}, bf16[4,32,256]{2,1,0:T(8,128)(2,1)}, u32[]{:S(2)}, u32[]{:S(2)}) %collective-permute-start.14) | collective-permute-done | bytes 65568 | tf_op jit(solution)/shard_map/ppermute | solution.py:355
  68.4 7.3 %tiles.1 = bf16[2,36,2,128,128]{4,3,2,1,0:T(8,128)(2,1)} custom-call(bf16[2,1024,512]{2,1,0:T(8,128)(2,1)S(1)} %get-tuple-element.46.early_ref, f32[2,8,128]{2,1,0:T(8,128)S(1)} %get-tuple-element.47.power_ref, bf16[1024,512]{1,0:T(8,128)(2,1)S(1)} %get-tuple-element.85.refs_0_, bf16[4,32,256]{2,1,0:T(8,128)(2,1)S(1)} %copy-done, ...), custom_call_target="tpu_custom_call" | custom-call | flops 4499999744 | bytes 9000000 | tf_op jit(solution)/shard_map/tiles/pallas_call | solution.py:303
  (47 shorter events, 2.5 us)
Async XLA Ops:
  12.5 45.1 %all-to-all-start = ((bf16[16,4,32,256]{3,2,1,0:T(8,128)(2,1)}), bf16[16,4,32,256]{3,2,1,0:T(8,128)(2,1)S(1)}, u32[]{:S(2)}, u32[]{:S(2)}) async-start(bf16[16,4,32,256]{3,2,1,0:T(8,128)(2,1)} %bitcast.33), calls=%async_computation | async-start | bytes 2097152 | tf_op jit(solution)/shard_map/all_to_all | solution.py:346
  19.2 16.9 %copy-start.11 = (s32[512]{0:T(512)S(1)}, s32[512]{0:T(512)}, u32[]{:S(2)}) copy-start(s32[512]{0:T(512)} %param.14) | copy-start | bytes 6148
  19.2 17.0 %copy-start.12 = (s32[512]{0:T(512)S(1)}, s32[512]{0:T(512)}, u32[]{:S(2)}) copy-start(s32[512]{0:T(512)} %constant.24.clone) | copy-start | bytes 6148
  19.2 17.0 %copy-start.13 = (s32[512]{0:T(512)S(1)}, s32[512]{0:T(512)}, u32[]{:S(2)}) copy-start(s32[512]{0:T(512)} %constant.23.clone) | copy-start | bytes 6148
  19.2 26.9 %copy-start.14 = (s32[512]{0:T(512)S(1)}, s32[512]{0:T(512)}, u32[]{:S(2)}) copy-start(s32[512]{0:T(512)} %constant.26) | copy-start | bytes 6148
  32.1 4.3 %collective-permute-start = (bf16[4,32,256]{2,1,0:T(8,128)(2,1)}, bf16[4,32,256]{2,1,0:T(8,128)(2,1)S(1)}, u32[]{:S(2)}, u32[]{:S(2)}) collective-permute-start(bf16[4,32,256]{2,1,0:T(8,128)(2,1)} %get-tuple-element.51), channel_id=1, source_target_pairs={{0,1},{1,0},{2,3},{3,2},{4,5},{5,4},{6,7},{7,6},{8,9},{9,8},{10,11... | collective-permute-start | bytes 196616 | tf_op jit(solution)/shard_map/ppermute | solution.py:355
  32.6 5.1 %collective-permute-start.1 = (bf16[4,32,256]{2,1,0:T(8,128)(2,1)}, bf16[4,32,256]{2,1,0:T(8,128)(2,1)S(1)}, u32[]{:S(2)}, u32[]{:S(2)}) collective-permute-start(bf16[4,32,256]{2,1,0:T(8,128)(2,1)} %get-tuple-element.54), channel_id=1, source_target_pairs={{0,2},{1,3},{2,0},{3,1},{4,6},{5,7},{6,4},{7,5},{8,10},{9,11},{10,... | collective-permute-start | bytes 196616 | tf_op jit(solution)/shard_map/ppermute | solution.py:355
  33.8 6.4 %collective-permute-start.2 = (bf16[4,32,256]{2,1,0:T(8,128)(2,1)}, bf16[4,32,256]{2,1,0:T(8,128)(2,1)S(1)}, u32[]{:S(2)}, u32[]{:S(2)}) collective-permute-start(bf16[4,32,256]{2,1,0:T(8,128)(2,1)} %get-tuple-element.57), channel_id=1, source_target_pairs={{0,3},{1,2},{2,1},{3,0},{4,7},{5,6},{6,5},{7,4},{8,11},{9,10},{10,... | collective-permute-start | bytes 196616 | tf_op jit(solution)/shard_map/ppermute | solution.py:355
  34.4 7.1 %collective-permute-start.3 = (bf16[4,32,256]{2,1,0:T(8,128)(2,1)}, bf16[4,32,256]{2,1,0:T(8,128)(2,1)S(1)}, u32[]{:S(2)}, u32[]{:S(2)}) collective-permute-start(bf16[4,32,256]{2,1,0:T(8,128)(2,1)} %get-tuple-element.60), channel_id=1, source_target_pairs={{0,4},{1,5},{2,6},{3,7},{4,0},{5,1},{6,2},{7,3},{8,12},{9,13},{10,... | collective-permute-start | bytes 196616 | tf_op jit(solution)/shard_map/ppermute | solution.py:355
  34.4 9.8 %collective-permute-start.4 = (bf16[4,32,256]{2,1,0:T(8,128)(2,1)}, bf16[4,32,256]{2,1,0:T(8,128)(2,1)S(1)}, u32[]{:S(2)}, u32[]{:S(2)}) collective-permute-start(bf16[4,32,256]{2,1,0:T(8,128)(2,1)} %get-tuple-element.63), channel_id=1, source_target_pairs={{0,5},{1,4},{2,7},{3,6},{4,1},{5,0},{6,3},{7,2},{8,13},{9,12},{10,... | collective-permute-start | bytes 196616 | tf_op jit(solution)/shard_map/ppermute | solution.py:355
  36.4 10.1 %collective-permute-start.5 = (bf16[4,32,256]{2,1,0:T(8,128)(2,1)}, bf16[4,32,256]{2,1,0:T(8,128)(2,1)S(1)}, u32[]{:S(2)}, u32[]{:S(2)}) collective-permute-start(bf16[4,32,256]{2,1,0:T(8,128)(2,1)} %get-tuple-element.66), channel_id=1, source_target_pairs={{0,6},{1,7},{2,4},{3,5},{4,2},{5,3},{6,0},{7,1},{8,14},{9,15},{10,... | collective-permute-start | bytes 196616 | tf_op jit(solution)/shard_map/ppermute | solution.py:355
  37.7 13.1 %collective-permute-start.6 = (bf16[4,32,256]{2,1,0:T(8,128)(2,1)}, bf16[4,32,256]{2,1,0:T(8,128)(2,1)S(1)}, u32[]{:S(2)}, u32[]{:S(2)}) collective-permute-start(bf16[4,32,256]{2,1,0:T(8,128)(2,1)} %get-tuple-element.69), channel_id=1, source_target_pairs={{0,7},{1,6},{2,5},{3,4},{4,3},{5,2},{6,1},{7,0},{8,15},{9,14},{10,... | collective-permute-start | bytes 196616 | tf_op jit(solution)/shard_map/ppermute | solution.py:355
  40.1 11.3 %collective-permute-start.7 = (bf16[4,32,256]{2,1,0:T(8,128)(2,1)}, bf16[4,32,256]{2,1,0:T(8,128)(2,1)S(1)}, u32[]{:S(2)}, u32[]{:S(2)}) collective-permute-start(bf16[4,32,256]{2,1,0:T(8,128)(2,1)} %get-tuple-element.72), channel_id=1, source_target_pairs={{0,8},{1,9},{2,10},{3,11},{4,12},{5,13},{6,14},{7,15},{8,0},{9,1},... | collective-permute-start | bytes 196616 | tf_op jit(solution)/shard_map/ppermute | solution.py:355
  41.5 12.1 %collective-permute-start.8 = (bf16[4,32,256]{2,1,0:T(8,128)(2,1)}, bf16[4,32,256]{2,1,0:T(8,128)(2,1)S(1)}, u32[]{:S(2)}, u32[]{:S(2)}) collective-permute-start(bf16[4,32,256]{2,1,0:T(8,128)(2,1)} %get-tuple-element.75), channel_id=1, source_target_pairs={{0,9},{1,8},{2,11},{3,10},{4,13},{5,12},{6,15},{7,14},{8,1},{9,0},... | collective-permute-start | bytes 196616 | tf_op jit(solution)/shard_map/ppermute | solution.py:355
  44.3 10.0 %collective-permute-start.9 = (bf16[4,32,256]{2,1,0:T(8,128)(2,1)}, bf16[4,32,256]{2,1,0:T(8,128)(2,1)S(1)}, u32[]{:S(2)}, u32[]{:S(2)}) collective-permute-start(bf16[4,32,256]{2,1,0:T(8,128)(2,1)} %get-tuple-element.78), channel_id=1, source_target_pairs={{0,10},{1,11},{2,8},{3,9},{4,14},{5,15},{6,12},{7,13},{8,2},{9,3},... | collective-permute-start | bytes 196616 | tf_op jit(solution)/shard_map/ppermute | solution.py:355
  46.5 21.9 %copy-start = (bf16[4,32,256]{2,1,0:T(8,128)(2,1)S(1)}, bf16[4,32,256]{2,1,0:T(8,128)(2,1)}, u32[]{:S(2)}) copy-start(bf16[4,32,256]{2,1,0:T(8,128)(2,1)} %get-tuple-element.49.refs_1_) | copy-start | bytes 196612
  47.1 12.2 %collective-permute-start.10 = (bf16[4,32,256]{2,1,0:T(8,128)(2,1)}, bf16[4,32,256]{2,1,0:T(8,128)(2,1)}, u32[]{:S(2)}, u32[]{:S(2)}) collective-permute-start(bf16[4,32,256]{2,1,0:T(8,128)(2,1)} %get-tuple-element.80), channel_id=1, source_target_pairs={{0,11},{1,10},{2,9},{3,8},{4,15},{5,14},{6,13},{7,12},{8,3},{9,2},... | collective-permute-start | bytes 196616 | tf_op jit(solution)/shard_map/ppermute | solution.py:355
  51.4 10.4 %collective-permute-start.11 = (bf16[4,32,256]{2,1,0:T(8,128)(2,1)}, bf16[4,32,256]{2,1,0:T(8,128)(2,1)}, u32[]{:S(2)}, u32[]{:S(2)}) collective-permute-start(bf16[4,32,256]{2,1,0:T(8,128)(2,1)} %get-tuple-element.81), channel_id=1, source_target_pairs={{0,12},{1,13},{2,14},{3,15},{4,8},{5,9},{6,10},{7,11},{8,4},{9,5},... | collective-permute-start | bytes 196616 | tf_op jit(solution)/shard_map/ppermute | solution.py:355
  52.0 11.2 %collective-permute-start.12 = (bf16[4,32,256]{2,1,0:T(8,128)(2,1)}, bf16[4,32,256]{2,1,0:T(8,128)(2,1)}, u32[]{:S(2)}, u32[]{:S(2)}) collective-permute-start(bf16[4,32,256]{2,1,0:T(8,128)(2,1)} %get-tuple-element.82), channel_id=1, source_target_pairs={{0,13},{1,12},{2,15},{3,14},{4,9},{5,8},{6,11},{7,10},{8,5},{9,4},... | collective-permute-start | bytes 196616 | tf_op jit(solution)/shard_map/ppermute | solution.py:355
  54.3 12.7 %collective-permute-start.13 = (bf16[4,32,256]{2,1,0:T(8,128)(2,1)}, bf16[4,32,256]{2,1,0:T(8,128)(2,1)}, u32[]{:S(2)}, u32[]{:S(2)}) collective-permute-start(bf16[4,32,256]{2,1,0:T(8,128)(2,1)} %get-tuple-element.83), channel_id=1, source_target_pairs={{0,14},{1,15},{2,12},{3,13},{4,10},{5,11},{6,8},{7,9},{8,6},{9,7},... | collective-permute-start | bytes 196616 | tf_op jit(solution)/shard_map/ppermute | solution.py:355
  54.9 13.4 %collective-permute-start.14 = (bf16[4,32,256]{2,1,0:T(8,128)(2,1)}, bf16[4,32,256]{2,1,0:T(8,128)(2,1)}, u32[]{:S(2)}, u32[]{:S(2)}) collective-permute-start(bf16[4,32,256]{2,1,0:T(8,128)(2,1)} %get-tuple-element.84), channel_id=1, source_target_pairs={{0,15},{1,14},{2,13},{3,12},{4,11},{5,10},{6,9},{7,8},{8,7},{9,6},... | collective-permute-start | bytes 196616 | tf_op jit(solution)/shard_map/ppermute | solution.py:355
  57.7 10.7 %copy-start.6 = (bf16[4,32,256]{2,1,0:T(8,128)(2,1)S(1)}, bf16[4,32,256]{2,1,0:T(8,128)(2,1)}, u32[]{:S(2)}) copy-start(bf16[4,32,256]{2,1,0:T(8,128)(2,1)} %copy-done.5) | copy-start | bytes 196612
  57.7 10.7 %copy-start.8 = (bf16[4,32,256]{2,1,0:T(8,128)(2,1)S(1)}, bf16[4,32,256]{2,1,0:T(8,128)(2,1)}, u32[]{:S(2)}) copy-start(bf16[4,32,256]{2,1,0:T(8,128)(2,1)} %copy-done.7) | copy-start | bytes 196612
  57.7 10.7 %copy-start.10 = (bf16[4,32,256]{2,1,0:T(8,128)(2,1)S(1)}, bf16[4,32,256]{2,1,0:T(8,128)(2,1)}, u32[]{:S(2)}) copy-start(bf16[4,32,256]{2,1,0:T(8,128)(2,1)} %copy-done.9) | copy-start | bytes 196612
  (7 other events, 24.5 us)

commit v13 on v10

--- a/solution.py
+++ b/solution.py
@@ -44,8 +44,7 @@
     stage = np.zeros((2, AVG, blocks, 2))
     stage[0, :, :, 0], stage[0, :, :, 1] = cos, sin
     stage[1, :, :, 0], stage[1, :, :, 1] = -sin, cos
-    stage = np.stack(split(stage), axis=1).reshape(4 * AVG, 2 * blocks)
-    stage = np.concatenate([np.kron(np.eye(GROUP), stage.astype(np.float32))] * 2, axis=1).astype(ml_dtypes.bfloat16)
+    stage = np.concatenate(split(np.kron(np.eye(GROUP), stage.reshape(2 * AVG, 2 * blocks))))
     angle = 2.0 * math.pi * np.outer(np.arange(AVG), np.arange(LANES)) / NCHAN
     turn = np.stack([np.cos(angle), -np.sin(angle)]).astype(np.float32)
     first = (NCHAN - all_out * AVG) // 2
@@ -58,7 +57,7 @@
     beside = max(1, LANES // (2 * all_out))
     last = np.kron(np.eye(beside), last.reshape(2 * LANES, 2 * all_out))
     last = np.concatenate(split(last), axis=1)
-    return stage.astype(np.float32), turn, np.concatenate([last, last]).astype(np.float32)
+    return stage.astype(np.float32), turn, last.astype(np.float32)
 
 
 def halves(values):
@@ -76,7 +75,7 @@
     halves_refs, turned_refs = refs[:groups], refs[groups:]
     outer, inner = pl.program_id(0), pl.program_id(1)
     size = GROUP * WIDE
-    beside = last_ref.shape[0] // (4 * LANES)
+    beside = last_ref.shape[0] // (2 * LANES)
     columns = beside * outs
 
     @pl.when((outer == 0) & (inner == 0))
@@ -100,7 +99,9 @@
 
     def first_product(g, start):
         lanes = slice(start * LANES, (start + 2) * LANES)
-        return jnp.dot(stage_ref[...], halves_refs[g][:, lanes], preferred_element_type=F32)
+        high, low = stage_ref[:size, :], stage_ref[size:, :]
+        data = jnp.concatenate([halves_refs[g][:, lanes], halves_refs[g][:size, lanes]])
+        return jnp.dot(jnp.concatenate([high, high, low], axis=1), data, preferred_element_type=F32)
 
     def first_rest(g, start, section):
         turn_real, turn_imag = turn_ref[0], turn_ref[1]
@@ -108,8 +109,7 @@
             pair, place = divmod(u, beside)
             for m in range(start, start + 2):
                 at = slice((m - start) * LANES, (m - start + 1) * LANES)
-                blocks = [section[(4 * u + i) * AVG : (4 * u + i + 1) * AVG, at] for i in range(4)]
-                real, imag = blocks[0] + blocks[1], blocks[2] + blocks[3]
+                real, imag = [section[(2 * u + i) * AVG : (2 * u + i + 1) * AVG, at] for i in range(2)]
                 row = pair * WIDTH + m * AVG
                 for ri, value in enumerate((real * turn_real - imag * turn_imag, real * turn_imag + imag * turn_real)):
                     for part, kept in enumerate(halves(value)):
@@ -118,7 +118,8 @@
 
     def last_product(g, pair):
         rows = slice(pair * WIDTH, (pair + 1) * WIDTH)
-        return jnp.dot(turned_refs[g][rows, :], last_ref[...], preferred_element_type=F32)
+        table = last_ref[...]
+        return jnp.dot(turned_refs[g][rows, :], jnp.concatenate([table, table]), preferred_element_type=F32)
 
     def last_rest(g, pair, product):
         found = (product[:, :columns] + product[:, columns:]).T
@@ -186,7 +187,7 @@
             pltpu.VMEM((WIDTH // LANES, ROWS * outs, LANES), F32),
         ]
         + [pltpu.VMEM((2 * GROUP * WIDE, SPECTRA * LANES), F32)] * groups
-        + [pltpu.VMEM((4 * GROUP * WIDTH * LANES // last.shape[0], last.shape[0]), F32)] * groups,
+        + [pltpu.VMEM((2 * GROUP * WIDTH * LANES // last.shape[0], 2 * last.shape[0]), F32)] * groups,
         compiler_params=pltpu.CompilerParams(vmem_limit_bytes=VMEM_LIMIT),
         cost_estimate=pl.CostEstimate(
             flops=(stop - start) * SPECTRA * 12_000_000,

time: 75.4 us -> 75.6 us (level)
  starting transfers between devices: 26.7 us -> 25.6 us
  waiting for transfers between devices: 10.4 us -> 11.3 us
    ppermute x15, starting transfers between devices: 20.1 us -> 19 us  [body(): lax.ppermute(ready, 'ingest', [(i, i ^ k) for i in range(devices)])]
    ppermute x15, waiting for transfers between devices: 10.4 us -> 11.3 us  [body(): lax.ppermute(ready, 'ingest', [(i, i ^ k) for i in range(devices)])]
  transfers between devices with their start and end apart: 16 -> 16, of which waited for: 6 -> 8; matrix products, arithmetic and copies ran while one was open for 1% -> 1% of each run, Pallas kernels for 20% -> 20%
where the time goes in v13:
time: 75.6 us; the launch traced here: 75.3 us
  Pallas kernels  34.3 us (45%)
  starting transfers between devices  25.6 us (34%)
  waiting for transfers between devices  11.3 us (15%)
  local copies, waits for them, and re-layouts  3.33 us (4%)
    pallas_call x2, Pallas kernels, spectra(): pl.pallas_call(functools.partial(spectra_kernel, start, partners, outs),...  26.3 us
    ppermute x15, starting transfers between devices, body(): lax.ppermute(ready, 'ingest', [(i, i ^ k) for i in range(devices)])  19 us
    ppermute x15, waiting for transfers between devices, body(): lax.ppermute(ready, 'ingest', [(i, i ^ k) for i in range(devices)])  11.3 us
    all_to_all x1, starting transfers between devices, body(): lax.all_to_all(packed, 'ingest', split_axis=0, concat_axis=0, tiled=True)  6.62 us
    pallas_call x1, Pallas kernels, tiles(): pl.pallas_call(functools.partial(tiles_kernel, len(parts)), out_shape=jax...  6.47 us
    unnamed x30, local copies, waits for them, and re-layouts  3.16 us
    pallas_call x1, Pallas kernels, arrange(): pl.pallas_call(arrange_kernel, out_shape=(jax.ShapeDtypeStruct((OUT_DEV,...  1.57 us
  transfers between devices with their start and end apart: 16, of which 8 were waited for; matrix products, arithmetic and copies ran while one was open for 1% of the time, Pallas kernels for 20%

profile of v13, /device:TPU:11, one launch (start us, length us, event | category | flops | bytes accessed | tf_op | source)
XLA Modules:
  0.0 75.3 jit_solution(16851290626862764351)
XLA Ops:
  0.0 12.9 %spectra.2 = bf16[64,32,256]{2,1,0:T(8,128)(2,1)} custom-call(f32[32]{0:T(128)} %gain_ref.2, s32[64,11,64,128]{3,2,1,0:T(8,128)} %bitcast.11, s32[64,11,64,128]{3,2,1,0:T(8,128)} %bitcast.12, s32[64,11,64,128]{3,2,1,0:T(8,128)} %bitcast.13, s32[64,11,64,128]{3,2,1,0:T(8,128)} %bitcast.14, s32[64,11,64,128]{3,2,1,0:T(8,128)} %bitcast.15, ...), custom_call_target="tpu_custom_call" | custom-call | flops 3072000000 | bytes 11534336 | tf_op jit(solution)/shard_map/spectra/pallas_call | solution.py:177
  12.9 6.6 %all-to-all-start = ((bf16[16,4,32,256]{3,2,1,0:T(8,128)(2,1)}), bf16[16,4,32,256]{3,2,1,0:T(8,128)(2,1)S(1)}, u32[]{:S(2)}, u32[]{:S(2)}) async-start(bf16[16,4,32,256]{3,2,1,0:T(8,128)(2,1)} %bitcast.33), calls=%async_computation | async-start | bytes 2097152 | tf_op jit(solution)/shard_map/all_to_all | solution.py:324
  19.6 13.3 %spectra.3 = (bf16[4,32,256]{2,1,0:T(8,128)(2,1)}, bf16[4,32,256]{2,1,0:T(8,128)(2,1)}, bf16[4,32,256]{2,1,0:T(8,128)(2,1)}, bf16[4,32,256]{2,1,0:T(8,128)(2,1)}...) custom-call(f32[32]{0:T(128)} %gain_ref.2, ...), custom_call_target="tpu_custom_call" | custom-call | flops 3072000000 | bytes 11534336 | tf_op jit(solution)/shard_map/spectra/pallas_call | solution.py:177
  33.4 1.2 %collective-permute-start.1 = (bf16[4,32,256]{2,1,0:T(8,128)(2,1)}, bf16[4,32,256]{2,1,0:T(8,128)(2,1)S(1)}, u32[]{:S(2)}, u32[]{:S(2)}) collective-permute-start(bf16[4,32,256]{2,1,0:T(8,128)(2,1)} %get-tuple-element.54), channel_id=1, source_target_pairs={{0,2},{1,3},{2,0},{3,1},{4,6},{5,7},{6,4},{7,5},{8,10},{9,11},{10,... | collective-permute-start | bytes 196616 | tf_op jit(solution)/shard_map/ppermute | solution.py:333
  35.2 1.6 %collective-permute-start.4 = (bf16[4,32,256]{2,1,0:T(8,128)(2,1)}, bf16[4,32,256]{2,1,0:T(8,128)(2,1)S(1)}, u32[]{:S(2)}, u32[]{:S(2)}) collective-permute-start(bf16[4,32,256]{2,1,0:T(8,128)(2,1)} %get-tuple-element.63), channel_id=1, source_target_pairs={{0,5},{1,4},{2,7},{3,6},{4,1},{5,0},{6,3},{7,2},{8,13},{9,12},{10,... | collective-permute-start | bytes 196616 | tf_op jit(solution)/shard_map/ppermute | solution.py:333
  37.2 1.3 %collective-permute-start.5 = (bf16[4,32,256]{2,1,0:T(8,128)(2,1)}, bf16[4,32,256]{2,1,0:T(8,128)(2,1)S(1)}, u32[]{:S(2)}, u32[]{:S(2)}) collective-permute-start(bf16[4,32,256]{2,1,0:T(8,128)(2,1)} %get-tuple-element.66), channel_id=1, source_target_pairs={{0,6},{1,7},{2,4},{3,5},{4,2},{5,3},{6,0},{7,1},{8,14},{9,15},{10,... | collective-permute-start | bytes 196616 | tf_op jit(solution)/shard_map/ppermute | solution.py:333
  38.7 1.2 %collective-permute-start.6 = (bf16[4,32,256]{2,1,0:T(8,128)(2,1)}, bf16[4,32,256]{2,1,0:T(8,128)(2,1)S(1)}, u32[]{:S(2)}, u32[]{:S(2)}) collective-permute-start(bf16[4,32,256]{2,1,0:T(8,128)(2,1)} %get-tuple-element.69), channel_id=1, source_target_pairs={{0,7},{1,6},{2,5},{3,4},{4,3},{5,2},{6,1},{7,0},{8,15},{9,14},{10,... | collective-permute-start | bytes 196616 | tf_op jit(solution)/shard_map/ppermute | solution.py:333
  40.0 0.6 collective-permute-done.2.refs_4_
  40.6 3.6 %collective-permute-start.7 = (bf16[4,32,256]{2,1,0:T(8,128)(2,1)}, bf16[4,32,256]{2,1,0:T(8,128)(2,1)S(1)}, u32[]{:S(2)}, u32[]{:S(2)}) collective-permute-start(bf16[4,32,256]{2,1,0:T(8,128)(2,1)} %get-tuple-element.72), channel_id=1, source_target_pairs={{0,8},{1,9},{2,10},{3,11},{4,12},{5,13},{6,14},{7,15},{8,0},{9,1},... | collective-permute-start | bytes 196616 | tf_op jit(solution)/shard_map/ppermute | solution.py:333
  44.2 0.7 collective-permute-start.8
  44.9 2.0 %collective-permute-start.9 = (bf16[4,32,256]{2,1,0:T(8,128)(2,1)}, bf16[4,32,256]{2,1,0:T(8,128)(2,1)S(1)}, u32[]{:S(2)}, u32[]{:S(2)}) collective-permute-start(bf16[4,32,256]{2,1,0:T(8,128)(2,1)} %get-tuple-element.78), channel_id=1, source_target_pairs={{0,10},{1,11},{2,8},{3,9},{4,14},{5,15},{6,12},{7,13},{8,2},{9,3},... | collective-permute-start | bytes 196616 | tf_op jit(solution)/shard_map/ppermute | solution.py:333
  47.9 2.5 %collective-permute-start.10 = (bf16[4,32,256]{2,1,0:T(8,128)(2,1)}, bf16[4,32,256]{2,1,0:T(8,128)(2,1)}, u32[]{:S(2)}, u32[]{:S(2)}) collective-permute-start(bf16[4,32,256]{2,1,0:T(8,128)(2,1)} %get-tuple-element.80), channel_id=1, source_target_pairs={{0,11},{1,10},{2,9},{3,8},{4,15},{5,14},{6,13},{7,12},{8,3},{9,2},... | collective-permute-start | bytes 196616 | tf_op jit(solution)/shard_map/ppermute | solution.py:333
  50.4 0.6 copy-done.3
  51.2 0.6 copy-done.5
  51.8 1.1 %collective-permute-start.12 = (bf16[4,32,256]{2,1,0:T(8,128)(2,1)}, bf16[4,32,256]{2,1,0:T(8,128)(2,1)}, u32[]{:S(2)}, u32[]{:S(2)}) collective-permute-start(bf16[4,32,256]{2,1,0:T(8,128)(2,1)} %get-tuple-element.82), channel_id=1, source_target_pairs={{0,13},{1,12},{2,15},{3,14},{4,9},{5,8},{6,11},{7,10},{8,5},{9,4},... | collective-permute-start | bytes 196616 | tf_op jit(solution)/shard_map/ppermute | solution.py:333
  53.3 0.6 copy-done.7
  53.9 1.6 %collective-permute-start.13 = (bf16[4,32,256]{2,1,0:T(8,128)(2,1)}, bf16[4,32,256]{2,1,0:T(8,128)(2,1)}, u32[]{:S(2)}, u32[]{:S(2)}) collective-permute-start(bf16[4,32,256]{2,1,0:T(8,128)(2,1)} %get-tuple-element.83), channel_id=1, source_target_pairs={{0,14},{1,15},{2,12},{3,13},{4,10},{5,11},{6,8},{7,9},{8,6},{9,7},... | collective-permute-start | bytes 196616 | tf_op jit(solution)/shard_map/ppermute | solution.py:333
  56.7 1.1 %collective-permute-start.14 = (bf16[4,32,256]{2,1,0:T(8,128)(2,1)}, bf16[4,32,256]{2,1,0:T(8,128)(2,1)}, u32[]{:S(2)}, u32[]{:S(2)}) collective-permute-start(bf16[4,32,256]{2,1,0:T(8,128)(2,1)} %get-tuple-element.84), channel_id=1, source_target_pairs={{0,15},{1,14},{2,13},{3,12},{4,11},{5,10},{6,9},{7,8},{8,7},{9,6},... | collective-permute-start | bytes 196616 | tf_op jit(solution)/shard_map/ppermute | solution.py:333
  57.8 1.6 %arrange.1 = (bf16[2,1024,512]{2,1,0:T(8,128)(2,1)S(1)}, f32[2,8,128]{2,1,0:T(8,128)S(1)}) custom-call(bf16[1024,512]{1,0:T(8,128)(2,1)S(1)} %get-tuple-element.86.pick_ref, bf16[16,4,32,256]{3,2,1,0:T(8,128)(2,1)S(1)} %all-to-all-done.part_ref), custom_call_target="tpu_custom_call" | custom-call | flops 1100000000 | bytes 4000000 | tf_op jit(solution)/shard_map/arrange/pallas_call | solution.py:219
  59.4 2.7 %collective-permute-done.11.refs_13_ = bf16[4,32,256]{2,1,0:T(8,128)(2,1)} collective-permute-done((bf16[4,32,256]{2,1,0:T(8,128)(2,1)}, bf16[4,32,256]{2,1,0:T(8,128)(2,1)}, u32[]{:S(2)}, u32[]{:S(2)}) %collective-permute-start.11) | collective-permute-done | bytes 65568 | tf_op jit(solution)/shard_map/ppermute | solution.py:333
  62.1 3.0 %collective-permute-done.12.refs_14_ = bf16[4,32,256]{2,1,0:T(8,128)(2,1)} collective-permute-done((bf16[4,32,256]{2,1,0:T(8,128)(2,1)}, bf16[4,32,256]{2,1,0:T(8,128)(2,1)}, u32[]{:S(2)}, u32[]{:S(2)}) %collective-permute-start.12) | collective-permute-done | bytes 65568 | tf_op jit(solution)/shard_map/ppermute | solution.py:333
  65.2 2.2 %collective-permute-done.13.refs_15_ = bf16[4,32,256]{2,1,0:T(8,128)(2,1)} collective-permute-done((bf16[4,32,256]{2,1,0:T(8,128)(2,1)}, bf16[4,32,256]{2,1,0:T(8,128)(2,1)}, u32[]{:S(2)}, u32[]{:S(2)}) %collective-permute-start.13) | collective-permute-done | bytes 65568 | tf_op jit(solution)/shard_map/ppermute | solution.py:333
  67.4 1.4 %collective-permute-done.14.refs_16_ = bf16[4,32,256]{2,1,0:T(8,128)(2,1)} collective-permute-done((bf16[4,32,256]{2,1,0:T(8,128)(2,1)}, bf16[4,32,256]{2,1,0:T(8,128)(2,1)}, u32[]{:S(2)}, u32[]{:S(2)}) %collective-permute-start.14) | collective-permute-done | bytes 65568 | tf_op jit(solution)/shard_map/ppermute | solution.py:333
  68.8 6.5 %tiles.1 = bf16[2,36,2,128,128]{4,3,2,1,0:T(8,128)(2,1)} custom-call(bf16[2,1024,512]{2,1,0:T(8,128)(2,1)S(1)} %get-tuple-element.46.early_ref, f32[2,8,128]{2,1,0:T(8,128)S(1)} %get-tuple-element.47.power_ref, bf16[1024,512]{1,0:T(8,128)(2,1)S(1)} %get-tuple-element.85.refs_0_, bf16[4,32,256]{2,1,0:T(8,128)(2,1)S(1)} %copy-done, ...), custom_call_target="tpu_custom_call" | custom-call | flops 4499999744 | bytes 9000000 | tf_op jit(solution)/shard_map/tiles/pallas_call | solution.py:283
  (47 shorter events, 4.5 us)
Async XLA Ops:
  12.9 44.9 %all-to-all-start = ((bf16[16,4,32,256]{3,2,1,0:T(8,128)(2,1)}), bf16[16,4,32,256]{3,2,1,0:T(8,128)(2,1)S(1)}, u32[]{:S(2)}, u32[]{:S(2)}) async-start(bf16[16,4,32,256]{3,2,1,0:T(8,128)(2,1)} %bitcast.33), calls=%async_computation | async-start | bytes 2097152 | tf_op jit(solution)/shard_map/all_to_all | solution.py:324
  19.5 17.3 %copy-start.11 = (s32[512]{0:T(512)S(1)}, s32[512]{0:T(512)}, u32[]{:S(2)}) copy-start(s32[512]{0:T(512)} %param.14) | copy-start | bytes 6148
  19.6 17.4 %copy-start.12 = (s32[512]{0:T(512)S(1)}, s32[512]{0:T(512)}, u32[]{:S(2)}) copy-start(s32[512]{0:T(512)} %constant.24.clone) | copy-start | bytes 6148
  19.6 17.4 %copy-start.13 = (s32[512]{0:T(512)S(1)}, s32[512]{0:T(512)}, u32[]{:S(2)}) copy-start(s32[512]{0:T(512)} %constant.23.clone) | copy-start | bytes 6148
  19.6 27.3 %copy-start.14 = (s32[512]{0:T(512)S(1)}, s32[512]{0:T(512)}, u32[]{:S(2)}) copy-start(s32[512]{0:T(512)} %constant.26) | copy-start | bytes 6148
  32.9 4.3 %collective-permute-start = (bf16[4,32,256]{2,1,0:T(8,128)(2,1)}, bf16[4,32,256]{2,1,0:T(8,128)(2,1)S(1)}, u32[]{:S(2)}, u32[]{:S(2)}) collective-permute-start(bf16[4,32,256]{2,1,0:T(8,128)(2,1)} %get-tuple-element.51), channel_id=1, source_target_pairs={{0,1},{1,0},{2,3},{3,2},{4,5},{5,4},{6,7},{7,6},{8,9},{9,8},{10,11... | collective-permute-start | bytes 196616 | tf_op jit(solution)/shard_map/ppermute | solution.py:333
  33.4 5.4 %collective-permute-start.1 = (bf16[4,32,256]{2,1,0:T(8,128)(2,1)}, bf16[4,32,256]{2,1,0:T(8,128)(2,1)S(1)}, u32[]{:S(2)}, u32[]{:S(2)}) collective-permute-start(bf16[4,32,256]{2,1,0:T(8,128)(2,1)} %get-tuple-element.54), channel_id=1, source_target_pairs={{0,2},{1,3},{2,0},{3,1},{4,6},{5,7},{6,4},{7,5},{8,10},{9,11},{10,... | collective-permute-start | bytes 196616 | tf_op jit(solution)/shard_map/ppermute | solution.py:333
  34.5 6.1 %collective-permute-start.2 = (bf16[4,32,256]{2,1,0:T(8,128)(2,1)}, bf16[4,32,256]{2,1,0:T(8,128)(2,1)S(1)}, u32[]{:S(2)}, u32[]{:S(2)}) collective-permute-start(bf16[4,32,256]{2,1,0:T(8,128)(2,1)} %get-tuple-element.57), channel_id=1, source_target_pairs={{0,3},{1,2},{2,1},{3,0},{4,7},{5,6},{6,5},{7,4},{8,11},{9,10},{10,... | collective-permute-start | bytes 196616 | tf_op jit(solution)/shard_map/ppermute | solution.py:333
  35.1 9.1 %collective-permute-start.3 = (bf16[4,32,256]{2,1,0:T(8,128)(2,1)}, bf16[4,32,256]{2,1,0:T(8,128)(2,1)S(1)}, u32[]{:S(2)}, u32[]{:S(2)}) collective-permute-start(bf16[4,32,256]{2,1,0:T(8,128)(2,1)} %get-tuple-element.60), channel_id=1, source_target_pairs={{0,4},{1,5},{2,6},{3,7},{4,0},{5,1},{6,2},{7,3},{8,12},{9,13},{10,... | collective-permute-start | bytes 196616 | tf_op jit(solution)/shard_map/ppermute | solution.py:333
  35.2 9.7 %collective-permute-start.4 = (bf16[4,32,256]{2,1,0:T(8,128)(2,1)}, bf16[4,32,256]{2,1,0:T(8,128)(2,1)S(1)}, u32[]{:S(2)}, u32[]{:S(2)}) collective-permute-start(bf16[4,32,256]{2,1,0:T(8,128)(2,1)} %get-tuple-element.63), channel_id=1, source_target_pairs={{0,5},{1,4},{2,7},{3,6},{4,1},{5,0},{6,3},{7,2},{8,13},{9,12},{10,... | collective-permute-start | bytes 196616 | tf_op jit(solution)/shard_map/ppermute | solution.py:333
  37.2 10.1 %collective-permute-start.5 = (bf16[4,32,256]{2,1,0:T(8,128)(2,1)}, bf16[4,32,256]{2,1,0:T(8,128)(2,1)S(1)}, u32[]{:S(2)}, u32[]{:S(2)}) collective-permute-start(bf16[4,32,256]{2,1,0:T(8,128)(2,1)} %get-tuple-element.66), channel_id=1, source_target_pairs={{0,6},{1,7},{2,4},{3,5},{4,2},{5,3},{6,0},{7,1},{8,14},{9,15},{10,... | collective-permute-start | bytes 196616 | tf_op jit(solution)/shard_map/ppermute | solution.py:333
  38.7 11.7 %collective-permute-start.6 = (bf16[4,32,256]{2,1,0:T(8,128)(2,1)}, bf16[4,32,256]{2,1,0:T(8,128)(2,1)S(1)}, u32[]{:S(2)}, u32[]{:S(2)}) collective-permute-start(bf16[4,32,256]{2,1,0:T(8,128)(2,1)} %get-tuple-element.69), channel_id=1, source_target_pairs={{0,7},{1,6},{2,5},{3,4},{4,3},{5,2},{6,1},{7,0},{8,15},{9,14},{10,... | collective-permute-start | bytes 196616 | tf_op jit(solution)/shard_map/ppermute | solution.py:333
  40.6 10.5 %collective-permute-start.7 = (bf16[4,32,256]{2,1,0:T(8,128)(2,1)}, bf16[4,32,256]{2,1,0:T(8,128)(2,1)S(1)}, u32[]{:S(2)}, u32[]{:S(2)}) collective-permute-start(bf16[4,32,256]{2,1,0:T(8,128)(2,1)} %get-tuple-element.72), channel_id=1, source_target_pairs={{0,8},{1,9},{2,10},{3,11},{4,12},{5,13},{6,14},{7,15},{8,0},{9,1},... | collective-permute-start | bytes 196616 | tf_op jit(solution)/shard_map/ppermute | solution.py:333
  44.2 9.1 %collective-permute-start.8 = (bf16[4,32,256]{2,1,0:T(8,128)(2,1)}, bf16[4,32,256]{2,1,0:T(8,128)(2,1)S(1)}, u32[]{:S(2)}, u32[]{:S(2)}) collective-permute-start(bf16[4,32,256]{2,1,0:T(8,128)(2,1)} %get-tuple-element.75), channel_id=1, source_target_pairs={{0,9},{1,8},{2,11},{3,10},{4,13},{5,12},{6,15},{7,14},{8,1},{9,0},... | collective-permute-start | bytes 196616 | tf_op jit(solution)/shard_map/ppermute | solution.py:333
  44.9 11.2 %collective-permute-start.9 = (bf16[4,32,256]{2,1,0:T(8,128)(2,1)}, bf16[4,32,256]{2,1,0:T(8,128)(2,1)S(1)}, u32[]{:S(2)}, u32[]{:S(2)}) collective-permute-start(bf16[4,32,256]{2,1,0:T(8,128)(2,1)} %get-tuple-element.78), channel_id=1, source_target_pairs={{0,10},{1,11},{2,8},{3,9},{4,14},{5,15},{6,12},{7,13},{8,2},{9,3},... | collective-permute-start | bytes 196616 | tf_op jit(solution)/shard_map/ppermute | solution.py:333
  47.2 21.5 %copy-start = (bf16[4,32,256]{2,1,0:T(8,128)(2,1)S(1)}, bf16[4,32,256]{2,1,0:T(8,128)(2,1)}, u32[]{:S(2)}) copy-start(bf16[4,32,256]{2,1,0:T(8,128)(2,1)} %get-tuple-element.49.refs_1_) | copy-start | bytes 196612
  47.9 11.5 %collective-permute-start.10 = (bf16[4,32,256]{2,1,0:T(8,128)(2,1)}, bf16[4,32,256]{2,1,0:T(8,128)(2,1)}, u32[]{:S(2)}, u32[]{:S(2)}) collective-permute-start(bf16[4,32,256]{2,1,0:T(8,128)(2,1)} %get-tuple-element.80), channel_id=1, source_target_pairs={{0,11},{1,10},{2,9},{3,8},{4,15},{5,14},{6,13},{7,12},{8,3},{9,2},... | collective-permute-start | bytes 196616 | tf_op jit(solution)/shard_map/ppermute | solution.py:333
  51.0 11.1 %collective-permute-start.11 = (bf16[4,32,256]{2,1,0:T(8,128)(2,1)}, bf16[4,32,256]{2,1,0:T(8,128)(2,1)}, u32[]{:S(2)}, u32[]{:S(2)}) collective-permute-start(bf16[4,32,256]{2,1,0:T(8,128)(2,1)} %get-tuple-element.81), channel_id=1, source_target_pairs={{0,12},{1,13},{2,14},{3,15},{4,8},{5,9},{6,10},{7,11},{8,4},{9,5},... | collective-permute-start | bytes 196616 | tf_op jit(solution)/shard_map/ppermute | solution.py:333
  51.8 13.4 %collective-permute-start.12 = (bf16[4,32,256]{2,1,0:T(8,128)(2,1)}, bf16[4,32,256]{2,1,0:T(8,128)(2,1)}, u32[]{:S(2)}, u32[]{:S(2)}) collective-permute-start(bf16[4,32,256]{2,1,0:T(8,128)(2,1)} %get-tuple-element.82), channel_id=1, source_target_pairs={{0,13},{1,12},{2,15},{3,14},{4,9},{5,8},{6,11},{7,10},{8,5},{9,4},... | collective-permute-start | bytes 196616 | tf_op jit(solution)/shard_map/ppermute | solution.py:333
  53.9 13.5 %collective-permute-start.13 = (bf16[4,32,256]{2,1,0:T(8,128)(2,1)}, bf16[4,32,256]{2,1,0:T(8,128)(2,1)}, u32[]{:S(2)}, u32[]{:S(2)}) collective-permute-start(bf16[4,32,256]{2,1,0:T(8,128)(2,1)} %get-tuple-element.83), channel_id=1, source_target_pairs={{0,14},{1,15},{2,12},{3,13},{4,10},{5,11},{6,8},{7,9},{8,6},{9,7},... | collective-permute-start | bytes 196616 | tf_op jit(solution)/shard_map/ppermute | solution.py:333
  56.7 12.1 %collective-permute-start.14 = (bf16[4,32,256]{2,1,0:T(8,128)(2,1)}, bf16[4,32,256]{2,1,0:T(8,128)(2,1)}, u32[]{:S(2)}, u32[]{:S(2)}) collective-permute-start(bf16[4,32,256]{2,1,0:T(8,128)(2,1)} %get-tuple-element.84), channel_id=1, source_target_pairs={{0,15},{1,14},{2,13},{3,12},{4,11},{5,10},{6,9},{7,8},{8,7},{9,6},... | collective-permute-start | bytes 196616 | tf_op jit(solution)/shard_map/ppermute | solution.py:333
  57.8 11.0 %copy-start.6 = (bf16[4,32,256]{2,1,0:T(8,128)(2,1)S(1)}, bf16[4,32,256]{2,1,0:T(8,128)(2,1)}, u32[]{:S(2)}) copy-start(bf16[4,32,256]{2,1,0:T(8,128)(2,1)} %copy-done.5) | copy-start | bytes 196612
  57.8 11.0 %copy-start.8 = (bf16[4,32,256]{2,1,0:T(8,128)(2,1)S(1)}, bf16[4,32,256]{2,1,0:T(8,128)(2,1)}, u32[]{:S(2)}) copy-start(bf16[4,32,256]{2,1,0:T(8,128)(2,1)} %copy-done.7) | copy-start | bytes 196612
  57.8 11.0 %copy-start.10 = (bf16[4,32,256]{2,1,0:T(8,128)(2,1)S(1)}, bf16[4,32,256]{2,1,0:T(8,128)(2,1)}, u32[]{:S(2)}) copy-start(bf16[4,32,256]{2,1,0:T(8,128)(2,1)} %copy-done.9) | copy-start | bytes 196612
  (7 other events, 25.1 us)

commit v14 on v13

--- a/solution.py
+++ b/solution.py
@@ -44,7 +44,8 @@
     stage = np.zeros((2, AVG, blocks, 2))
     stage[0, :, :, 0], stage[0, :, :, 1] = cos, sin
     stage[1, :, :, 0], stage[1, :, :, 1] = -sin, cos
-    stage = np.concatenate(split(np.kron(np.eye(GROUP), stage.reshape(2 * AVG, 2 * blocks))))
+    stage = np.stack(split(stage), axis=1).reshape(4 * AVG, 2 * blocks)
+    stage = np.kron(np.eye(GROUP), stage.astype(np.float32))
     angle = 2.0 * math.pi * np.outer(np.arange(AVG), np.arange(LANES)) / NCHAN
     turn = np.stack([np.cos(angle), -np.sin(angle)]).astype(np.float32)
     first = (NCHAN - all_out * AVG) // 2
@@ -99,9 +100,8 @@
 
     def first_product(g, start):
         lanes = slice(start * LANES, (start + 2) * LANES)
-        high, low = stage_ref[:size, :], stage_ref[size:, :]
-        data = jnp.concatenate([halves_refs[g][:, lanes], halves_refs[g][:size, lanes]])
-        return jnp.dot(jnp.concatenate([high, high, low], axis=1), data, preferred_element_type=F32)
+        table = stage_ref[...]
+        return jnp.dot(jnp.concatenate([table, table], axis=1), halves_refs[g][:, lanes], preferred_element_type=F32)
 
     def first_rest(g, start, section):
         turn_real, turn_imag = turn_ref[0], turn_ref[1]
@@ -109,35 +109,38 @@
             pair, place = divmod(u, beside)
             for m in range(start, start + 2):
                 at = slice((m - start) * LANES, (m - start + 1) * LANES)
-                real, imag = [section[(2 * u + i) * AVG : (2 * u + i + 1) * AVG, at] for i in range(2)]
+                blocks = [section[(4 * u + i) * AVG : (4 * u + i + 1) * AVG, at] for i in range(4)]
+                real, imag = blocks[0] + blocks[1], blocks[2] + blocks[3]
                 row = pair * WIDTH + m * AVG
                 for ri, value in enumerate((real * turn_real - imag * turn_imag, real * turn_imag + imag * turn_real)):
                     for part, kept in enumerate(halves(value)):
                         lane = ((part * beside + place) * 2 + ri) * LANES
                         turned_refs[g][row : row + AVG, lane : lane + LANES] = kept
 
-    def last_product(g, pair):
-        rows = slice(pair * WIDTH, (pair + 1) * WIDTH)
+    def last_product(g):
         table = last_ref[...]
-        return jnp.dot(turned_refs[g][rows, :], jnp.concatenate([table, table]), preferred_element_type=F32)
-
-    def last_rest(g, pair, product):
-        found = (product[:, :columns] + product[:, columns:]).T
-        for place in range(beside):
-            stream = g * GROUP + pair * beside + place
-            factor = gain_ref[(first_stream + outer * ROWS + inner * STEP + stream) // 2]
-            factor = factor * (1.0 / (64.0 * math.sqrt(NCHAN)))
-            at = pl.multiple_of((inner * STEP + stream) * outs, outs)
-            mine = found[place * outs : (place + 1) * outs] * factor
-            for half in range(WIDTH // LANES):
-                held_ref[half, pl.ds(at, outs), :] = mine[:, half * LANES : (half + 1) * LANES]
+        rows = jnp.concatenate([turned_refs[g][...], turned_refs[g + 1][...]])
+        return jnp.dot(rows, jnp.concatenate([table, table]), preferred_element_type=F32)
+
+    def last_rest(g, product):
+        for pair in range(2 * GROUP // beside):
+            mine = product[pair * WIDTH : (pair + 1) * WIDTH]
+            found = (mine[:, :columns] + mine[:, columns:]).T
+            for place in range(beside):
+                stream = g * GROUP + pair * beside + place
+                factor = gain_ref[(first_stream + outer * ROWS + inner * STEP + stream) // 2]
+                factor = factor * (1.0 / (64.0 * math.sqrt(NCHAN)))
+                at = pl.multiple_of((inner * STEP + stream) * outs, outs)
+                mine_out = found[place * outs : (place + 1) * outs] * factor
+                for half in range(WIDTH // LANES):
+                    held_ref[half, pl.ds(at, outs), :] = mine_out[:, half * LANES : (half + 1) * LANES]
 
     waiting = []
     for g in range(groups + 3):
         filters = [(g, u, r) for u in range(GROUP) for r in range(0, WIDE, 16)] if g < groups else []
         units = [(first_product, first_rest, g - 1, start) for start in range(0, SPECTRA, 2)] if 1 <= g <= groups else []
-        if 3 <= g:
-            units += [(last_product, last_rest, g - 3, pair) for pair in range(GROUP // beside)]
+        if 4 <= g and g % 2 == 0:
+            units.append((last_product, last_rest, g - 4))
         while filters or units:
             if units:
                 product, rest, *job = units.pop(0)

time: 75.6 us -> 75.3 us (level)
  starting transfers between devices: 25.6 us -> 26.8 us
  waiting for transfers between devices: 11.3 us -> 10.2 us
    ppermute x15, starting transfers between devices: 19 us -> 20.2 us  [body(): lax.ppermute(ready, 'ingest', [(i, i ^ k) for i in range(devices)])]
    ppermute x15, waiting for transfers between devices: 11.3 us -> 10.2 us  [body(): lax.ppermute(ready, 'ingest', [(i, i ^ k) for i in range(devices)])]
  transfers between devices with their start and end apart: 16 -> 16, of which waited for: 8 -> 6; matrix products, arithmetic and copies ran while one was open for 1% -> 1% of each run, Pallas kernels for 20% -> 20%
where the time goes in v14:
time: 75.3 us; the launch traced here: 75.1 us
  Pallas kernels  34 us (45%)
  starting transfers between devices  26.8 us (36%)
  waiting for transfers between devices  10.2 us (14%)
  local copies, waits for them, and re-layouts  3.33 us (4%)
    pallas_call x2, Pallas kernels, spectra(): pl.pallas_call(functools.partial(spectra_kernel, start, partners, outs),...  25.9 us
    ppermute x15, starting transfers between devices, body(): lax.ppermute(ready, 'ingest', [(i, i ^ k) for i in range(devices)])  20.2 us
    ppermute x15, waiting for transfers between devices, body(): lax.ppermute(ready, 'ingest', [(i, i ^ k) for i in range(devices)])  10.2 us
    all_to_all x1, starting transfers between devices, body(): lax.all_to_all(packed, 'ingest', split_axis=0, concat_axis=0, tiled=True)  6.62 us
    pallas_call x1, Pallas kernels, tiles(): pl.pallas_call(functools.partial(tiles_kernel, len(parts)), out_shape=jax...  6.47 us
    unnamed x30, local copies, waits for them, and re-layouts  3.16 us
    pallas_call x1, Pallas kernels, arrange(): pl.pallas_call(arrange_kernel, out_shape=(jax.ShapeDtypeStruct((OUT_DEV,...  1.56 us
  transfers between devices with their start and end apart: 16, of which 6 were waited for; matrix products, arithmetic and copies ran while one was open for 1% of the time, Pallas kernels for 20%

profile of v14, /device:TPU:11, one launch (start us, length us, event | category | flops | bytes accessed | tf_op | source)
XLA Modules:
  0.0 75.1 jit_solution(2211114010147784143)
XLA Ops:
  0.0 12.7 %spectra.2 = bf16[64,32,256]{2,1,0:T(8,128)(2,1)} custom-call(f32[32]{0:T(128)} %gain_ref.2, s32[64,11,64,128]{3,2,1,0:T(8,128)} %bitcast.11, s32[64,11,64,128]{3,2,1,0:T(8,128)} %bitcast.12, s32[64,11,64,128]{3,2,1,0:T(8,128)} %bitcast.13, s32[64,11,64,128]{3,2,1,0:T(8,128)} %bitcast.14, s32[64,11,64,128]{3,2,1,0:T(8,128)} %bitcast.15, ...), custom_call_target="tpu_custom_call" | custom-call | flops 3072000000 | bytes 11534336 | tf_op jit(solution)/shard_map/spectra/pallas_call | solution.py:180
  12.7 6.6 %all-to-all-start = ((bf16[16,4,32,256]{3,2,1,0:T(8,128)(2,1)}), bf16[16,4,32,256]{3,2,1,0:T(8,128)(2,1)S(1)}, u32[]{:S(2)}, u32[]{:S(2)}) async-start(bf16[16,4,32,256]{3,2,1,0:T(8,128)(2,1)} %bitcast.33), calls=%async_computation | async-start | bytes 2097152 | tf_op jit(solution)/shard_map/all_to_all | solution.py:327
  19.4 13.2 %spectra.3 = (bf16[4,32,256]{2,1,0:T(8,128)(2,1)}, bf16[4,32,256]{2,1,0:T(8,128)(2,1)}, bf16[4,32,256]{2,1,0:T(8,128)(2,1)}, bf16[4,32,256]{2,1,0:T(8,128)(2,1)}...) custom-call(f32[32]{0:T(128)} %gain_ref.2, ...), custom_call_target="tpu_custom_call" | custom-call | flops 3072000000 | bytes 11534336 | tf_op jit(solution)/shard_map/spectra/pallas_call | solution.py:180
  33.0 1.2 %collective-permute-start.1 = (bf16[4,32,256]{2,1,0:T(8,128)(2,1)}, bf16[4,32,256]{2,1,0:T(8,128)(2,1)S(1)}, u32[]{:S(2)}, u32[]{:S(2)}) collective-permute-start(bf16[4,32,256]{2,1,0:T(8,128)(2,1)} %get-tuple-element.54), channel_id=1, source_target_pairs={{0,2},{1,3},{2,0},{3,1},{4,6},{5,7},{6,4},{7,5},{8,10},{9,11},{10,... | collective-permute-start | bytes 196616 | tf_op jit(solution)/shard_map/ppermute | solution.py:336
  34.9 1.6 %collective-permute-start.4 = (bf16[4,32,256]{2,1,0:T(8,128)(2,1)}, bf16[4,32,256]{2,1,0:T(8,128)(2,1)S(1)}, u32[]{:S(2)}, u32[]{:S(2)}) collective-permute-start(bf16[4,32,256]{2,1,0:T(8,128)(2,1)} %get-tuple-element.63), channel_id=1, source_target_pairs={{0,5},{1,4},{2,7},{3,6},{4,1},{5,0},{6,3},{7,2},{8,13},{9,12},{10,... | collective-permute-start | bytes 196616 | tf_op jit(solution)/shard_map/ppermute | solution.py:336
  36.9 1.2 %collective-permute-start.5 = (bf16[4,32,256]{2,1,0:T(8,128)(2,1)}, bf16[4,32,256]{2,1,0:T(8,128)(2,1)S(1)}, u32[]{:S(2)}, u32[]{:S(2)}) collective-permute-start(bf16[4,32,256]{2,1,0:T(8,128)(2,1)} %get-tuple-element.66), channel_id=1, source_target_pairs={{0,6},{1,7},{2,4},{3,5},{4,2},{5,3},{6,0},{7,1},{8,14},{9,15},{10,... | collective-permute-start | bytes 196616 | tf_op jit(solution)/shard_map/ppermute | solution.py:336
  38.3 1.4 %collective-permute-start.6 = (bf16[4,32,256]{2,1,0:T(8,128)(2,1)}, bf16[4,32,256]{2,1,0:T(8,128)(2,1)S(1)}, u32[]{:S(2)}, u32[]{:S(2)}) collective-permute-start(bf16[4,32,256]{2,1,0:T(8,128)(2,1)} %get-tuple-element.69), channel_id=1, source_target_pairs={{0,7},{1,6},{2,5},{3,4},{4,3},{5,2},{6,1},{7,0},{8,15},{9,14},{10,... | collective-permute-start | bytes 196616 | tf_op jit(solution)/shard_map/ppermute | solution.py:336
  39.6 0.7 collective-permute-done.2.refs_4_
  40.4 2.9 %collective-permute-start.7 = (bf16[4,32,256]{2,1,0:T(8,128)(2,1)}, bf16[4,32,256]{2,1,0:T(8,128)(2,1)S(1)}, u32[]{:S(2)}, u32[]{:S(2)}) collective-permute-start(bf16[4,32,256]{2,1,0:T(8,128)(2,1)} %get-tuple-element.72), channel_id=1, source_target_pairs={{0,8},{1,9},{2,10},{3,11},{4,12},{5,13},{6,14},{7,15},{8,0},{9,1},... | collective-permute-start | bytes 196616 | tf_op jit(solution)/shard_map/ppermute | solution.py:336
  43.3 1.4 %collective-permute-start.8 = (bf16[4,32,256]{2,1,0:T(8,128)(2,1)}, bf16[4,32,256]{2,1,0:T(8,128)(2,1)S(1)}, u32[]{:S(2)}, u32[]{:S(2)}) collective-permute-start(bf16[4,32,256]{2,1,0:T(8,128)(2,1)} %get-tuple-element.75), channel_id=1, source_target_pairs={{0,9},{1,8},{2,11},{3,10},{4,13},{5,12},{6,15},{7,14},{8,1},{9,0},... | collective-permute-start | bytes 196616 | tf_op jit(solution)/shard_map/ppermute | solution.py:336
  44.6 1.9 %collective-permute-start.9 = (bf16[4,32,256]{2,1,0:T(8,128)(2,1)}, bf16[4,32,256]{2,1,0:T(8,128)(2,1)S(1)}, u32[]{:S(2)}, u32[]{:S(2)}) collective-permute-start(bf16[4,32,256]{2,1,0:T(8,128)(2,1)} %get-tuple-element.78), channel_id=1, source_target_pairs={{0,10},{1,11},{2,8},{3,9},{4,14},{5,15},{6,12},{7,13},{8,2},{9,3},... | collective-permute-start | bytes 196616 | tf_op jit(solution)/shard_map/ppermute | solution.py:336
  47.6 3.1 %collective-permute-start.10 = (bf16[4,32,256]{2,1,0:T(8,128)(2,1)}, bf16[4,32,256]{2,1,0:T(8,128)(2,1)}, u32[]{:S(2)}, u32[]{:S(2)}) collective-permute-start(bf16[4,32,256]{2,1,0:T(8,128)(2,1)} %get-tuple-element.80), channel_id=1, source_target_pairs={{0,11},{1,10},{2,9},{3,8},{4,15},{5,14},{6,13},{7,12},{8,3},{9,2},... | collective-permute-start | bytes 196616 | tf_op jit(solution)/shard_map/ppermute | solution.py:336
  50.7 0.6 copy-done.3
  51.3 0.6 copy-done.5
  52.0 1.5 %collective-permute-start.12 = (bf16[4,32,256]{2,1,0:T(8,128)(2,1)}, bf16[4,32,256]{2,1,0:T(8,128)(2,1)}, u32[]{:S(2)}, u32[]{:S(2)}) collective-permute-start(bf16[4,32,256]{2,1,0:T(8,128)(2,1)} %get-tuple-element.82), channel_id=1, source_target_pairs={{0,13},{1,12},{2,15},{3,14},{4,9},{5,8},{6,11},{7,10},{8,5},{9,4},... | collective-permute-start | bytes 196616 | tf_op jit(solution)/shard_map/ppermute | solution.py:336
  53.5 0.6 copy-done.7
  54.1 1.0 %collective-permute-start.13 = (bf16[4,32,256]{2,1,0:T(8,128)(2,1)}, bf16[4,32,256]{2,1,0:T(8,128)(2,1)}, u32[]{:S(2)}, u32[]{:S(2)}) collective-permute-start(bf16[4,32,256]{2,1,0:T(8,128)(2,1)} %get-tuple-element.83), channel_id=1, source_target_pairs={{0,14},{1,15},{2,12},{3,13},{4,10},{5,11},{6,8},{7,9},{8,6},{9,7},... | collective-permute-start | bytes 196616 | tf_op jit(solution)/shard_map/ppermute | solution.py:336
  55.7 1.9 %collective-permute-start.14 = (bf16[4,32,256]{2,1,0:T(8,128)(2,1)}, bf16[4,32,256]{2,1,0:T(8,128)(2,1)}, u32[]{:S(2)}, u32[]{:S(2)}) collective-permute-start(bf16[4,32,256]{2,1,0:T(8,128)(2,1)} %get-tuple-element.84), channel_id=1, source_target_pairs={{0,15},{1,14},{2,13},{3,12},{4,11},{5,10},{6,9},{7,8},{8,7},{9,6},... | collective-permute-start | bytes 196616 | tf_op jit(solution)/shard_map/ppermute | solution.py:336
  57.6 1.6 %arrange.1 = (bf16[2,1024,512]{2,1,0:T(8,128)(2,1)S(1)}, f32[2,8,128]{2,1,0:T(8,128)S(1)}) custom-call(bf16[1024,512]{1,0:T(8,128)(2,1)S(1)} %get-tuple-element.86.pick_ref, bf16[16,4,32,256]{3,2,1,0:T(8,128)(2,1)S(1)} %all-to-all-done.part_ref), custom_call_target="tpu_custom_call" | custom-call | flops 1100000000 | bytes 4000000 | tf_op jit(solution)/shard_map/arrange/pallas_call | solution.py:222
  59.2 2.9 %collective-permute-done.11.refs_13_ = bf16[4,32,256]{2,1,0:T(8,128)(2,1)} collective-permute-done((bf16[4,32,256]{2,1,0:T(8,128)(2,1)}, bf16[4,32,256]{2,1,0:T(8,128)(2,1)}, u32[]{:S(2)}, u32[]{:S(2)}) %collective-permute-start.11) | collective-permute-done | bytes 65568 | tf_op jit(solution)/shard_map/ppermute | solution.py:336
  62.1 2.8 %collective-permute-done.12.refs_14_ = bf16[4,32,256]{2,1,0:T(8,128)(2,1)} collective-permute-done((bf16[4,32,256]{2,1,0:T(8,128)(2,1)}, bf16[4,32,256]{2,1,0:T(8,128)(2,1)}, u32[]{:S(2)}, u32[]{:S(2)}) %collective-permute-start.12) | collective-permute-done | bytes 65568 | tf_op jit(solution)/shard_map/ppermute | solution.py:336
  64.9 2.2 %collective-permute-done.13.refs_15_ = bf16[4,32,256]{2,1,0:T(8,128)(2,1)} collective-permute-done((bf16[4,32,256]{2,1,0:T(8,128)(2,1)}, bf16[4,32,256]{2,1,0:T(8,128)(2,1)}, u32[]{:S(2)}, u32[]{:S(2)}) %collective-permute-start.13) | collective-permute-done | bytes 65568 | tf_op jit(solution)/shard_map/ppermute | solution.py:336
  67.1 1.4 %collective-permute-done.14.refs_16_ = bf16[4,32,256]{2,1,0:T(8,128)(2,1)} collective-permute-done((bf16[4,32,256]{2,1,0:T(8,128)(2,1)}, bf16[4,32,256]{2,1,0:T(8,128)(2,1)}, u32[]{:S(2)}, u32[]{:S(2)}) %collective-permute-start.14) | collective-permute-done | bytes 65568 | tf_op jit(solution)/shard_map/ppermute | solution.py:336
  68.6 6.5 %tiles.1 = bf16[2,36,2,128,128]{4,3,2,1,0:T(8,128)(2,1)} custom-call(bf16[2,1024,512]{2,1,0:T(8,128)(2,1)S(1)} %get-tuple-element.46.early_ref, f32[2,8,128]{2,1,0:T(8,128)S(1)} %get-tuple-element.47.power_ref, bf16[1024,512]{1,0:T(8,128)(2,1)S(1)} %get-tuple-element.85.refs_0_, bf16[4,32,256]{2,1,0:T(8,128)(2,1)S(1)} %copy-done, ...), custom_call_target="tpu_custom_call" | custom-call | flops 4499999744 | bytes 9000000 | tf_op jit(solution)/shard_map/tiles/pallas_call | solution.py:286
  (47 shorter events, 3.3 us)
Async XLA Ops:
  12.7 44.9 %all-to-all-start = ((bf16[16,4,32,256]{3,2,1,0:T(8,128)(2,1)}), bf16[16,4,32,256]{3,2,1,0:T(8,128)(2,1)S(1)}, u32[]{:S(2)}, u32[]{:S(2)}) async-start(bf16[16,4,32,256]{3,2,1,0:T(8,128)(2,1)} %bitcast.33), calls=%async_computation | async-start | bytes 2097152 | tf_op jit(solution)/shard_map/all_to_all | solution.py:327
  19.4 17.2 %copy-start.11 = (s32[512]{0:T(512)S(1)}, s32[512]{0:T(512)}, u32[]{:S(2)}) copy-start(s32[512]{0:T(512)} %param.14) | copy-start | bytes 6148
  19.4 17.3 %copy-start.12 = (s32[512]{0:T(512)S(1)}, s32[512]{0:T(512)}, u32[]{:S(2)}) copy-start(s32[512]{0:T(512)} %constant.24.clone) | copy-start | bytes 6148
  19.4 17.3 %copy-start.13 = (s32[512]{0:T(512)S(1)}, s32[512]{0:T(512)}, u32[]{:S(2)}) copy-start(s32[512]{0:T(512)} %constant.23.clone) | copy-start | bytes 6148
  19.4 27.1 %copy-start.14 = (s32[512]{0:T(512)S(1)}, s32[512]{0:T(512)}, u32[]{:S(2)}) copy-start(s32[512]{0:T(512)} %constant.26) | copy-start | bytes 6148
  32.6 4.3 %collective-permute-start = (bf16[4,32,256]{2,1,0:T(8,128)(2,1)}, bf16[4,32,256]{2,1,0:T(8,128)(2,1)S(1)}, u32[]{:S(2)}, u32[]{:S(2)}) collective-permute-start(bf16[4,32,256]{2,1,0:T(8,128)(2,1)} %get-tuple-element.51), channel_id=1, source_target_pairs={{0,1},{1,0},{2,3},{3,2},{4,5},{5,4},{6,7},{7,6},{8,9},{9,8},{10,11... | collective-permute-start | bytes 196616 | tf_op jit(solution)/shard_map/ppermute | solution.py:336
  33.0 5.2 %collective-permute-start.1 = (bf16[4,32,256]{2,1,0:T(8,128)(2,1)}, bf16[4,32,256]{2,1,0:T(8,128)(2,1)S(1)}, u32[]{:S(2)}, u32[]{:S(2)}) collective-permute-start(bf16[4,32,256]{2,1,0:T(8,128)(2,1)} %get-tuple-element.54), channel_id=1, source_target_pairs={{0,2},{1,3},{2,0},{3,1},{4,6},{5,7},{6,4},{7,5},{8,10},{9,11},{10,... | collective-permute-start | bytes 196616 | tf_op jit(solution)/shard_map/ppermute | solution.py:336
  34.2 6.2 %collective-permute-start.2 = (bf16[4,32,256]{2,1,0:T(8,128)(2,1)}, bf16[4,32,256]{2,1,0:T(8,128)(2,1)S(1)}, u32[]{:S(2)}, u32[]{:S(2)}) collective-permute-start(bf16[4,32,256]{2,1,0:T(8,128)(2,1)} %get-tuple-element.57), channel_id=1, source_target_pairs={{0,3},{1,2},{2,1},{3,0},{4,7},{5,6},{6,5},{7,4},{8,11},{9,10},{10,... | collective-permute-start | bytes 196616 | tf_op jit(solution)/shard_map/ppermute | solution.py:336
  34.8 8.4 %collective-permute-start.3 = (bf16[4,32,256]{2,1,0:T(8,128)(2,1)}, bf16[4,32,256]{2,1,0:T(8,128)(2,1)S(1)}, u32[]{:S(2)}, u32[]{:S(2)}) collective-permute-start(bf16[4,32,256]{2,1,0:T(8,128)(2,1)} %get-tuple-element.60), channel_id=1, source_target_pairs={{0,4},{1,5},{2,6},{3,7},{4,0},{5,1},{6,2},{7,3},{8,12},{9,13},{10,... | collective-permute-start | bytes 196616 | tf_op jit(solution)/shard_map/ppermute | solution.py:336
  34.9 9.7 %collective-permute-start.4 = (bf16[4,32,256]{2,1,0:T(8,128)(2,1)}, bf16[4,32,256]{2,1,0:T(8,128)(2,1)S(1)}, u32[]{:S(2)}, u32[]{:S(2)}) collective-permute-start(bf16[4,32,256]{2,1,0:T(8,128)(2,1)} %get-tuple-element.63), channel_id=1, source_target_pairs={{0,5},{1,4},{2,7},{3,6},{4,1},{5,0},{6,3},{7,2},{8,13},{9,12},{10,... | collective-permute-start | bytes 196616 | tf_op jit(solution)/shard_map/ppermute | solution.py:336
  36.9 10.1 %collective-permute-start.5 = (bf16[4,32,256]{2,1,0:T(8,128)(2,1)}, bf16[4,32,256]{2,1,0:T(8,128)(2,1)S(1)}, u32[]{:S(2)}, u32[]{:S(2)}) collective-permute-start(bf16[4,32,256]{2,1,0:T(8,128)(2,1)} %get-tuple-element.66), channel_id=1, source_target_pairs={{0,6},{1,7},{2,4},{3,5},{4,2},{5,3},{6,0},{7,1},{8,14},{9,15},{10,... | collective-permute-start | bytes 196616 | tf_op jit(solution)/shard_map/ppermute | solution.py:336
  38.3 12.4 %collective-permute-start.6 = (bf16[4,32,256]{2,1,0:T(8,128)(2,1)}, bf16[4,32,256]{2,1,0:T(8,128)(2,1)S(1)}, u32[]{:S(2)}, u32[]{:S(2)}) collective-permute-start(bf16[4,32,256]{2,1,0:T(8,128)(2,1)} %get-tuple-element.69), channel_id=1, source_target_pairs={{0,7},{1,6},{2,5},{3,4},{4,3},{5,2},{6,1},{7,0},{8,15},{9,14},{10,... | collective-permute-start | bytes 196616 | tf_op jit(solution)/shard_map/ppermute | solution.py:336
  40.4 10.9 %collective-permute-start.7 = (bf16[4,32,256]{2,1,0:T(8,128)(2,1)}, bf16[4,32,256]{2,1,0:T(8,128)(2,1)S(1)}, u32[]{:S(2)}, u32[]{:S(2)}) collective-permute-start(bf16[4,32,256]{2,1,0:T(8,128)(2,1)} %get-tuple-element.72), channel_id=1, source_target_pairs={{0,8},{1,9},{2,10},{3,11},{4,12},{5,13},{6,14},{7,15},{8,0},{9,1},... | collective-permute-start | bytes 196616 | tf_op jit(solution)/shard_map/ppermute | solution.py:336
  43.3 10.2 %collective-permute-start.8 = (bf16[4,32,256]{2,1,0:T(8,128)(2,1)}, bf16[4,32,256]{2,1,0:T(8,128)(2,1)S(1)}, u32[]{:S(2)}, u32[]{:S(2)}) collective-permute-start(bf16[4,32,256]{2,1,0:T(8,128)(2,1)} %get-tuple-element.75), channel_id=1, source_target_pairs={{0,9},{1,8},{2,11},{3,10},{4,13},{5,12},{6,15},{7,14},{8,1},{9,0},... | collective-permute-start | bytes 196616 | tf_op jit(solution)/shard_map/ppermute | solution.py:336
  44.6 10.5 %collective-permute-start.9 = (bf16[4,32,256]{2,1,0:T(8,128)(2,1)}, bf16[4,32,256]{2,1,0:T(8,128)(2,1)S(1)}, u32[]{:S(2)}, u32[]{:S(2)}) collective-permute-start(bf16[4,32,256]{2,1,0:T(8,128)(2,1)} %get-tuple-element.78), channel_id=1, source_target_pairs={{0,10},{1,11},{2,8},{3,9},{4,14},{5,15},{6,12},{7,13},{8,2},{9,3},... | collective-permute-start | bytes 196616 | tf_op jit(solution)/shard_map/ppermute | solution.py:336
  46.9 21.6 %copy-start = (bf16[4,32,256]{2,1,0:T(8,128)(2,1)S(1)}, bf16[4,32,256]{2,1,0:T(8,128)(2,1)}, u32[]{:S(2)}) copy-start(bf16[4,32,256]{2,1,0:T(8,128)(2,1)} %get-tuple-element.49.refs_1_) | copy-start | bytes 196612
  47.6 11.7 %collective-permute-start.10 = (bf16[4,32,256]{2,1,0:T(8,128)(2,1)}, bf16[4,32,256]{2,1,0:T(8,128)(2,1)}, u32[]{:S(2)}, u32[]{:S(2)}) collective-permute-start(bf16[4,32,256]{2,1,0:T(8,128)(2,1)} %get-tuple-element.80), channel_id=1, source_target_pairs={{0,11},{1,10},{2,9},{3,8},{4,15},{5,14},{6,13},{7,12},{8,3},{9,2},... | collective-permute-start | bytes 196616 | tf_op jit(solution)/shard_map/ppermute | solution.py:336
  51.3 10.8 %collective-permute-start.11 = (bf16[4,32,256]{2,1,0:T(8,128)(2,1)}, bf16[4,32,256]{2,1,0:T(8,128)(2,1)}, u32[]{:S(2)}, u32[]{:S(2)}) collective-permute-start(bf16[4,32,256]{2,1,0:T(8,128)(2,1)} %get-tuple-element.81), channel_id=1, source_target_pairs={{0,12},{1,13},{2,14},{3,15},{4,8},{5,9},{6,10},{7,11},{8,4},{9,5},... | collective-permute-start | bytes 196616 | tf_op jit(solution)/shard_map/ppermute | solution.py:336
  52.0 13.0 %collective-permute-start.12 = (bf16[4,32,256]{2,1,0:T(8,128)(2,1)}, bf16[4,32,256]{2,1,0:T(8,128)(2,1)}, u32[]{:S(2)}, u32[]{:S(2)}) collective-permute-start(bf16[4,32,256]{2,1,0:T(8,128)(2,1)} %get-tuple-element.82), channel_id=1, source_target_pairs={{0,13},{1,12},{2,15},{3,14},{4,9},{5,8},{6,11},{7,10},{8,5},{9,4},... | collective-permute-start | bytes 196616 | tf_op jit(solution)/shard_map/ppermute | solution.py:336
  54.1 13.0 %collective-permute-start.13 = (bf16[4,32,256]{2,1,0:T(8,128)(2,1)}, bf16[4,32,256]{2,1,0:T(8,128)(2,1)}, u32[]{:S(2)}, u32[]{:S(2)}) collective-permute-start(bf16[4,32,256]{2,1,0:T(8,128)(2,1)} %get-tuple-element.83), channel_id=1, source_target_pairs={{0,14},{1,15},{2,12},{3,13},{4,10},{5,11},{6,8},{7,9},{8,6},{9,7},... | collective-permute-start | bytes 196616 | tf_op jit(solution)/shard_map/ppermute | solution.py:336
  55.7 12.8 %collective-permute-start.14 = (bf16[4,32,256]{2,1,0:T(8,128)(2,1)}, bf16[4,32,256]{2,1,0:T(8,128)(2,1)}, u32[]{:S(2)}, u32[]{:S(2)}) collective-permute-start(bf16[4,32,256]{2,1,0:T(8,128)(2,1)} %get-tuple-element.84), channel_id=1, source_target_pairs={{0,15},{1,14},{2,13},{3,12},{4,11},{5,10},{6,9},{7,8},{8,7},{9,6},... | collective-permute-start | bytes 196616 | tf_op jit(solution)/shard_map/ppermute | solution.py:336
  57.6 10.9 %copy-start.6 = (bf16[4,32,256]{2,1,0:T(8,128)(2,1)S(1)}, bf16[4,32,256]{2,1,0:T(8,128)(2,1)}, u32[]{:S(2)}) copy-start(bf16[4,32,256]{2,1,0:T(8,128)(2,1)} %copy-done.5) | copy-start | bytes 196612
  57.6 10.9 %copy-start.8 = (bf16[4,32,256]{2,1,0:T(8,128)(2,1)S(1)}, bf16[4,32,256]{2,1,0:T(8,128)(2,1)}, u32[]{:S(2)}) copy-start(bf16[4,32,256]{2,1,0:T(8,128)(2,1)} %copy-done.7) | copy-start | bytes 196612
  57.6 10.9 %copy-start.10 = (bf16[4,32,256]{2,1,0:T(8,128)(2,1)S(1)}, bf16[4,32,256]{2,1,0:T(8,128)(2,1)}, u32[]{:S(2)}) copy-start(bf16[4,32,256]{2,1,0:T(8,128)(2,1)} %copy-done.9) | copy-start | bytes 196612
  (7 other events, 25.0 us)

commit v15 on v13

--- a/solution.py
+++ b/solution.py
@@ -44,7 +44,8 @@
     stage = np.zeros((2, AVG, blocks, 2))
     stage[0, :, :, 0], stage[0, :, :, 1] = cos, sin
     stage[1, :, :, 0], stage[1, :, :, 1] = -sin, cos
-    stage = np.concatenate(split(np.kron(np.eye(GROUP), stage.reshape(2 * AVG, 2 * blocks))))
+    stage = np.stack(split(stage), axis=1).reshape(4 * AVG, 2 * blocks)
+    stage = np.kron(np.eye(GROUP), stage.astype(np.float32))
     angle = 2.0 * math.pi * np.outer(np.arange(AVG), np.arange(LANES)) / NCHAN
     turn = np.stack([np.cos(angle), -np.sin(angle)]).astype(np.float32)
     first = (NCHAN - all_out * AVG) // 2
@@ -99,9 +100,8 @@
 
     def first_product(g, start):
         lanes = slice(start * LANES, (start + 2) * LANES)
-        high, low = stage_ref[:size, :], stage_ref[size:, :]
-        data = jnp.concatenate([halves_refs[g][:, lanes], halves_refs[g][:size, lanes]])
-        return jnp.dot(jnp.concatenate([high, high, low], axis=1), data, preferred_element_type=F32)
+        table = stage_ref[...]
+        return jnp.dot(jnp.concatenate([table, table], axis=1), halves_refs[g][:, lanes], preferred_element_type=F32)
 
     def first_rest(g, start, section):
         turn_real, turn_imag = turn_ref[0], turn_ref[1]
@@ -109,7 +109,8 @@
             pair, place = divmod(u, beside)
             for m in range(start, start + 2):
                 at = slice((m - start) * LANES, (m - start + 1) * LANES)
-                real, imag = [section[(2 * u + i) * AVG : (2 * u + i + 1) * AVG, at] for i in range(2)]
+                blocks = [section[(4 * u + i) * AVG : (4 * u + i + 1) * AVG, at] for i in range(4)]
+                real, imag = blocks[0] + blocks[1], blocks[2] + blocks[3]
                 row = pair * WIDTH + m * AVG
                 for ri, value in enumerate((real * turn_real - imag * turn_imag, real * turn_imag + imag * turn_real)):
                     for part, kept in enumerate(halves(value)):

time: 75.6 us -> 75.1 us (level)
  starting transfers between devices: 25.6 us -> 27.2 us
  waiting for transfers between devices: 11.3 us -> 10 us
  Pallas kernels: 34.3 us -> 33.5 us
    ppermute x15, starting transfers between devices: 19 us -> 20.6 us  [body(): lax.ppermute(ready, 'ingest', [(i, i ^ k) for i in range(devices)])]
    ppermute x15, waiting for transfers between devices: 11.3 us -> 10 us  [body(): lax.ppermute(ready, 'ingest', [(i, i ^ k) for i in range(devices)])]
    pallas_call x2, Pallas kernels: 26.3 us -> 25.5 us  [spectra(): pl.pallas_call(functools.partial(spectra_kernel, start, partners, outs),...]
  transfers between devices with their start and end apart: 16 -> 16, of which waited for: 8 -> 5; matrix products, arithmetic and copies ran while one was open for 1% -> 1% of each run, Pallas kernels for 20% -> 19%
where the time goes in v15:
time: 75.1 us; the launch traced here: 74.8 us
  Pallas kernels  33.5 us (45%)
  starting transfers between devices  27.2 us (36%)
  waiting for transfers between devices  10 us (13%)
  local copies, waits for them, and re-layouts  3.33 us (4%)
    pallas_call x2, Pallas kernels, spectra(): pl.pallas_call(functools.partial(spectra_kernel, start, partners, outs),...  25.5 us
    ppermute x15, starting transfers between devices, body(): lax.ppermute(ready, 'ingest', [(i, i ^ k) for i in range(devices)])  20.6 us
    ppermute x15, waiting for transfers between devices, body(): lax.ppermute(ready, 'ingest', [(i, i ^ k) for i in range(devices)])  10 us
    all_to_all x1, starting transfers between devices, body(): lax.all_to_all(packed, 'ingest', split_axis=0, concat_axis=0, tiled=True)  6.63 us
    pallas_call x1, Pallas kernels, tiles(): pl.pallas_call(functools.partial(tiles_kernel, len(parts)), out_shape=jax...  6.47 us
    unnamed x30, local copies, waits for them, and re-layouts  3.16 us
    pallas_call x1, Pallas kernels, arrange(): pl.pallas_call(arrange_kernel, out_shape=(jax.ShapeDtypeStruct((OUT_DEV,...  1.56 us
  transfers between devices with their start and end apart: 16, of which 5 were waited for; matrix products, arithmetic and copies ran while one was open for 1% of the time, Pallas kernels for 19%

profile of v15, /device:TPU:11, one launch (start us, length us, event | category | flops | bytes accessed | tf_op | source)
XLA Modules:
  0.0 74.8 jit_solution(10481917667222488197)
XLA Ops:
  0.0 12.5 %spectra.2 = bf16[64,32,256]{2,1,0:T(8,128)(2,1)} custom-call(f32[32]{0:T(128)} %gain_ref.2, s32[64,11,64,128]{3,2,1,0:T(8,128)} %bitcast.11, s32[64,11,64,128]{3,2,1,0:T(8,128)} %bitcast.12, s32[64,11,64,128]{3,2,1,0:T(8,128)} %bitcast.13, s32[64,11,64,128]{3,2,1,0:T(8,128)} %bitcast.14, s32[64,11,64,128]{3,2,1,0:T(8,128)} %bitcast.15, ...), custom_call_target="tpu_custom_call" | custom-call | flops 3072000000 | bytes 11534336 | tf_op jit(solution)/shard_map/spectra/pallas_call | solution.py:178
  12.5 6.6 %all-to-all-start = ((bf16[16,4,32,256]{3,2,1,0:T(8,128)(2,1)}), bf16[16,4,32,256]{3,2,1,0:T(8,128)(2,1)S(1)}, u32[]{:S(2)}, u32[]{:S(2)}) async-start(bf16[16,4,32,256]{3,2,1,0:T(8,128)(2,1)} %bitcast.33), calls=%async_computation | async-start | bytes 2097152 | tf_op jit(solution)/shard_map/all_to_all | solution.py:325
  19.2 12.9 %spectra.3 = (bf16[4,32,256]{2,1,0:T(8,128)(2,1)}, bf16[4,32,256]{2,1,0:T(8,128)(2,1)}, bf16[4,32,256]{2,1,0:T(8,128)(2,1)}, bf16[4,32,256]{2,1,0:T(8,128)(2,1)}...) custom-call(f32[32]{0:T(128)} %gain_ref.2, ...), custom_call_target="tpu_custom_call" | custom-call | flops 3072000000 | bytes 11534336 | tf_op jit(solution)/shard_map/spectra/pallas_call | solution.py:178
  32.6 1.2 %collective-permute-start.1 = (bf16[4,32,256]{2,1,0:T(8,128)(2,1)}, bf16[4,32,256]{2,1,0:T(8,128)(2,1)S(1)}, u32[]{:S(2)}, u32[]{:S(2)}) collective-permute-start(bf16[4,32,256]{2,1,0:T(8,128)(2,1)} %get-tuple-element.54), channel_id=1, source_target_pairs={{0,2},{1,3},{2,0},{3,1},{4,6},{5,7},{6,4},{7,5},{8,10},{9,11},{10,... | collective-permute-start | bytes 196616 | tf_op jit(solution)/shard_map/ppermute | solution.py:334
  34.4 1.6 %collective-permute-start.4 = (bf16[4,32,256]{2,1,0:T(8,128)(2,1)}, bf16[4,32,256]{2,1,0:T(8,128)(2,1)S(1)}, u32[]{:S(2)}, u32[]{:S(2)}) collective-permute-start(bf16[4,32,256]{2,1,0:T(8,128)(2,1)} %get-tuple-element.63), channel_id=1, source_target_pairs={{0,5},{1,4},{2,7},{3,6},{4,1},{5,0},{6,3},{7,2},{8,13},{9,12},{10,... | collective-permute-start | bytes 196616 | tf_op jit(solution)/shard_map/ppermute | solution.py:334
  36.4 1.3 %collective-permute-start.5 = (bf16[4,32,256]{2,1,0:T(8,128)(2,1)}, bf16[4,32,256]{2,1,0:T(8,128)(2,1)S(1)}, u32[]{:S(2)}, u32[]{:S(2)}) collective-permute-start(bf16[4,32,256]{2,1,0:T(8,128)(2,1)} %get-tuple-element.66), channel_id=1, source_target_pairs={{0,6},{1,7},{2,4},{3,5},{4,2},{5,3},{6,0},{7,1},{8,14},{9,15},{10,... | collective-permute-start | bytes 196616 | tf_op jit(solution)/shard_map/ppermute | solution.py:334
  37.7 1.5 %collective-permute-start.6 = (bf16[4,32,256]{2,1,0:T(8,128)(2,1)}, bf16[4,32,256]{2,1,0:T(8,128)(2,1)S(1)}, u32[]{:S(2)}, u32[]{:S(2)}) collective-permute-start(bf16[4,32,256]{2,1,0:T(8,128)(2,1)} %get-tuple-element.69), channel_id=1, source_target_pairs={{0,7},{1,6},{2,5},{3,4},{4,3},{5,2},{6,1},{7,0},{8,15},{9,14},{10,... | collective-permute-start | bytes 196616 | tf_op jit(solution)/shard_map/ppermute | solution.py:334
  39.2 1.0 %collective-permute-done.2.refs_4_ = bf16[4,32,256]{2,1,0:T(8,128)(2,1)S(1)} collective-permute-done((bf16[4,32,256]{2,1,0:T(8,128)(2,1)}, bf16[4,32,256]{2,1,0:T(8,128)(2,1)S(1)}, u32[]{:S(2)}, u32[]{:S(2)}) %collective-permute-start.2) | collective-permute-done | bytes 65568 | tf_op jit(solution)/shard_map/ppermute | solution.py:334
  40.1 1.4 %collective-permute-start.7 = (bf16[4,32,256]{2,1,0:T(8,128)(2,1)}, bf16[4,32,256]{2,1,0:T(8,128)(2,1)S(1)}, u32[]{:S(2)}, u32[]{:S(2)}) collective-permute-start(bf16[4,32,256]{2,1,0:T(8,128)(2,1)} %get-tuple-element.72), channel_id=1, source_target_pairs={{0,8},{1,9},{2,10},{3,11},{4,12},{5,13},{6,14},{7,15},{8,0},{9,1},... | collective-permute-start | bytes 196616 | tf_op jit(solution)/shard_map/ppermute | solution.py:334
  41.5 2.8 %collective-permute-start.8 = (bf16[4,32,256]{2,1,0:T(8,128)(2,1)}, bf16[4,32,256]{2,1,0:T(8,128)(2,1)S(1)}, u32[]{:S(2)}, u32[]{:S(2)}) collective-permute-start(bf16[4,32,256]{2,1,0:T(8,128)(2,1)} %get-tuple-element.75), channel_id=1, source_target_pairs={{0,9},{1,8},{2,11},{3,10},{4,13},{5,12},{6,15},{7,14},{8,1},{9,0},... | collective-permute-start | bytes 196616 | tf_op jit(solution)/shard_map/ppermute | solution.py:334
  44.3 1.8 %collective-permute-start.9 = (bf16[4,32,256]{2,1,0:T(8,128)(2,1)}, bf16[4,32,256]{2,1,0:T(8,128)(2,1)S(1)}, u32[]{:S(2)}, u32[]{:S(2)}) collective-permute-start(bf16[4,32,256]{2,1,0:T(8,128)(2,1)} %get-tuple-element.78), channel_id=1, source_target_pairs={{0,10},{1,11},{2,8},{3,9},{4,14},{5,15},{6,12},{7,13},{8,2},{9,3},... | collective-permute-start | bytes 196616 | tf_op jit(solution)/shard_map/ppermute | solution.py:334
  47.1 3.6 %collective-permute-start.10 = (bf16[4,32,256]{2,1,0:T(8,128)(2,1)}, bf16[4,32,256]{2,1,0:T(8,128)(2,1)}, u32[]{:S(2)}, u32[]{:S(2)}) collective-permute-start(bf16[4,32,256]{2,1,0:T(8,128)(2,1)} %get-tuple-element.80), channel_id=1, source_target_pairs={{0,11},{1,10},{2,9},{3,8},{4,15},{5,14},{6,13},{7,12},{8,3},{9,2},... | collective-permute-start | bytes 196616 | tf_op jit(solution)/shard_map/ppermute | solution.py:334
  50.7 0.6 copy-done.3
  51.4 0.6 copy-done.5
  52.0 1.6 %collective-permute-start.12 = (bf16[4,32,256]{2,1,0:T(8,128)(2,1)}, bf16[4,32,256]{2,1,0:T(8,128)(2,1)}, u32[]{:S(2)}, u32[]{:S(2)}) collective-permute-start(bf16[4,32,256]{2,1,0:T(8,128)(2,1)} %get-tuple-element.82), channel_id=1, source_target_pairs={{0,13},{1,12},{2,15},{3,14},{4,9},{5,8},{6,11},{7,10},{8,5},{9,4},... | collective-permute-start | bytes 196616 | tf_op jit(solution)/shard_map/ppermute | solution.py:334
  53.6 0.6 copy-done.7
  54.3 0.6 copy-done.9
  54.9 2.8 %collective-permute-start.14 = (bf16[4,32,256]{2,1,0:T(8,128)(2,1)}, bf16[4,32,256]{2,1,0:T(8,128)(2,1)}, u32[]{:S(2)}, u32[]{:S(2)}) collective-permute-start(bf16[4,32,256]{2,1,0:T(8,128)(2,1)} %get-tuple-element.84), channel_id=1, source_target_pairs={{0,15},{1,14},{2,13},{3,12},{4,11},{5,10},{6,9},{7,8},{8,7},{9,6},... | collective-permute-start | bytes 196616 | tf_op jit(solution)/shard_map/ppermute | solution.py:334
  57.7 1.6 %arrange.1 = (bf16[2,1024,512]{2,1,0:T(8,128)(2,1)S(1)}, f32[2,8,128]{2,1,0:T(8,128)S(1)}) custom-call(bf16[1024,512]{1,0:T(8,128)(2,1)S(1)} %get-tuple-element.86.pick_ref, bf16[16,4,32,256]{3,2,1,0:T(8,128)(2,1)S(1)} %all-to-all-done.part_ref), custom_call_target="tpu_custom_call" | custom-call | flops 1100000000 | bytes 4000000 | tf_op jit(solution)/shard_map/arrange/pallas_call | solution.py:220
  59.3 2.5 %collective-permute-done.11.refs_13_ = bf16[4,32,256]{2,1,0:T(8,128)(2,1)} collective-permute-done((bf16[4,32,256]{2,1,0:T(8,128)(2,1)}, bf16[4,32,256]{2,1,0:T(8,128)(2,1)}, u32[]{:S(2)}, u32[]{:S(2)}) %collective-permute-start.11) | collective-permute-done | bytes 65568 | tf_op jit(solution)/shard_map/ppermute | solution.py:334
  61.8 1.4 %collective-permute-done.12.refs_14_ = bf16[4,32,256]{2,1,0:T(8,128)(2,1)} collective-permute-done((bf16[4,32,256]{2,1,0:T(8,128)(2,1)}, bf16[4,32,256]{2,1,0:T(8,128)(2,1)}, u32[]{:S(2)}, u32[]{:S(2)}) %collective-permute-start.12) | collective-permute-done | bytes 65568 | tf_op jit(solution)/shard_map/ppermute | solution.py:334
  63.2 3.7 %collective-permute-done.13.refs_15_ = bf16[4,32,256]{2,1,0:T(8,128)(2,1)} collective-permute-done((bf16[4,32,256]{2,1,0:T(8,128)(2,1)}, bf16[4,32,256]{2,1,0:T(8,128)(2,1)}, u32[]{:S(2)}, u32[]{:S(2)}) %collective-permute-start.13) | collective-permute-done | bytes 65568 | tf_op jit(solution)/shard_map/ppermute | solution.py:334
  66.9 1.4 %collective-permute-done.14.refs_16_ = bf16[4,32,256]{2,1,0:T(8,128)(2,1)} collective-permute-done((bf16[4,32,256]{2,1,0:T(8,128)(2,1)}, bf16[4,32,256]{2,1,0:T(8,128)(2,1)}, u32[]{:S(2)}, u32[]{:S(2)}) %collective-permute-start.14) | collective-permute-done | bytes 65568 | tf_op jit(solution)/shard_map/ppermute | solution.py:334
  68.4 6.5 %tiles.1 = bf16[2,36,2,128,128]{4,3,2,1,0:T(8,128)(2,1)} custom-call(bf16[2,1024,512]{2,1,0:T(8,128)(2,1)S(1)} %get-tuple-element.46.early_ref, f32[2,8,128]{2,1,0:T(8,128)S(1)} %get-tuple-element.47.power_ref, bf16[1024,512]{1,0:T(8,128)(2,1)S(1)} %get-tuple-element.85.refs_0_, bf16[4,32,256]{2,1,0:T(8,128)(2,1)S(1)} %copy-done, ...), custom_call_target="tpu_custom_call" | custom-call | flops 4499999744 | bytes 9000000 | tf_op jit(solution)/shard_map/tiles/pallas_call | solution.py:284
  (47 shorter events, 2.5 us)
Async XLA Ops:
  12.5 45.1 %all-to-all-start = ((bf16[16,4,32,256]{3,2,1,0:T(8,128)(2,1)}), bf16[16,4,32,256]{3,2,1,0:T(8,128)(2,1)S(1)}, u32[]{:S(2)}, u32[]{:S(2)}) async-start(bf16[16,4,32,256]{3,2,1,0:T(8,128)(2,1)} %bitcast.33), calls=%async_computation | async-start | bytes 2097152 | tf_op jit(solution)/shard_map/all_to_all | solution.py:325
  19.2 16.9 %copy-start.11 = (s32[512]{0:T(512)S(1)}, s32[512]{0:T(512)}, u32[]{:S(2)}) copy-start(s32[512]{0:T(512)} %param.14) | copy-start | bytes 6148
  19.2 17.0 %copy-start.12 = (s32[512]{0:T(512)S(1)}, s32[512]{0:T(512)}, u32[]{:S(2)}) copy-start(s32[512]{0:T(512)} %constant.24.clone) | copy-start | bytes 6148
  19.2 17.0 %copy-start.13 = (s32[512]{0:T(512)S(1)}, s32[512]{0:T(512)}, u32[]{:S(2)}) copy-start(s32[512]{0:T(512)} %constant.23.clone) | copy-start | bytes 6148
  19.2 26.9 %copy-start.14 = (s32[512]{0:T(512)S(1)}, s32[512]{0:T(512)}, u32[]{:S(2)}) copy-start(s32[512]{0:T(512)} %constant.26) | copy-start | bytes 6148
  32.1 4.3 %collective-permute-start = (bf16[4,32,256]{2,1,0:T(8,128)(2,1)}, bf16[4,32,256]{2,1,0:T(8,128)(2,1)S(1)}, u32[]{:S(2)}, u32[]{:S(2)}) collective-permute-start(bf16[4,32,256]{2,1,0:T(8,128)(2,1)} %get-tuple-element.51), channel_id=1, source_target_pairs={{0,1},{1,0},{2,3},{3,2},{4,5},{5,4},{6,7},{7,6},{8,9},{9,8},{10,11... | collective-permute-start | bytes 196616 | tf_op jit(solution)/shard_map/ppermute | solution.py:334
  32.6 5.1 %collective-permute-start.1 = (bf16[4,32,256]{2,1,0:T(8,128)(2,1)}, bf16[4,32,256]{2,1,0:T(8,128)(2,1)S(1)}, u32[]{:S(2)}, u32[]{:S(2)}) collective-permute-start(bf16[4,32,256]{2,1,0:T(8,128)(2,1)} %get-tuple-element.54), channel_id=1, source_target_pairs={{0,2},{1,3},{2,0},{3,1},{4,6},{5,7},{6,4},{7,5},{8,10},{9,11},{10,... | collective-permute-start | bytes 196616 | tf_op jit(solution)/shard_map/ppermute | solution.py:334
  33.8 6.4 %collective-permute-start.2 = (bf16[4,32,256]{2,1,0:T(8,128)(2,1)}, bf16[4,32,256]{2,1,0:T(8,128)(2,1)S(1)}, u32[]{:S(2)}, u32[]{:S(2)}) collective-permute-start(bf16[4,32,256]{2,1,0:T(8,128)(2,1)} %get-tuple-element.57), channel_id=1, source_target_pairs={{0,3},{1,2},{2,1},{3,0},{4,7},{5,6},{6,5},{7,4},{8,11},{9,10},{10,... | collective-permute-start | bytes 196616 | tf_op jit(solution)/shard_map/ppermute | solution.py:334
  34.4 7.1 %collective-permute-start.3 = (bf16[4,32,256]{2,1,0:T(8,128)(2,1)}, bf16[4,32,256]{2,1,0:T(8,128)(2,1)S(1)}, u32[]{:S(2)}, u32[]{:S(2)}) collective-permute-start(bf16[4,32,256]{2,1,0:T(8,128)(2,1)} %get-tuple-element.60), channel_id=1, source_target_pairs={{0,4},{1,5},{2,6},{3,7},{4,0},{5,1},{6,2},{7,3},{8,12},{9,13},{10,... | collective-permute-start | bytes 196616 | tf_op jit(solution)/shard_map/ppermute | solution.py:334
  34.4 9.8 %collective-permute-start.4 = (bf16[4,32,256]{2,1,0:T(8,128)(2,1)}, bf16[4,32,256]{2,1,0:T(8,128)(2,1)S(1)}, u32[]{:S(2)}, u32[]{:S(2)}) collective-permute-start(bf16[4,32,256]{2,1,0:T(8,128)(2,1)} %get-tuple-element.63), channel_id=1, source_target_pairs={{0,5},{1,4},{2,7},{3,6},{4,1},{5,0},{6,3},{7,2},{8,13},{9,12},{10,... | collective-permute-start | bytes 196616 | tf_op jit(solution)/shard_map/ppermute | solution.py:334
  36.4 10.1 %collective-permute-start.5 = (bf16[4,32,256]{2,1,0:T(8,128)(2,1)}, bf16[4,32,256]{2,1,0:T(8,128)(2,1)S(1)}, u32[]{:S(2)}, u32[]{:S(2)}) collective-permute-start(bf16[4,32,256]{2,1,0:T(8,128)(2,1)} %get-tuple-element.66), channel_id=1, source_target_pairs={{0,6},{1,7},{2,4},{3,5},{4,2},{5,3},{6,0},{7,1},{8,14},{9,15},{10,... | collective-permute-start | bytes 196616 | tf_op jit(solution)/shard_map/ppermute | solution.py:334
  37.7 13.1 %collective-permute-start.6 = (bf16[4,32,256]{2,1,0:T(8,128)(2,1)}, bf16[4,32,256]{2,1,0:T(8,128)(2,1)S(1)}, u32[]{:S(2)}, u32[]{:S(2)}) collective-permute-start(bf16[4,32,256]{2,1,0:T(8,128)(2,1)} %get-tuple-element.69), channel_id=1, source_target_pairs={{0,7},{1,6},{2,5},{3,4},{4,3},{5,2},{6,1},{7,0},{8,15},{9,14},{10,... | collective-permute-start | bytes 196616 | tf_op jit(solution)/shard_map/ppermute | solution.py:334
  40.1 11.3 %collective-permute-start.7 = (bf16[4,32,256]{2,1,0:T(8,128)(2,1)}, bf16[4,32,256]{2,1,0:T(8,128)(2,1)S(1)}, u32[]{:S(2)}, u32[]{:S(2)}) collective-permute-start(bf16[4,32,256]{2,1,0:T(8,128)(2,1)} %get-tuple-element.72), channel_id=1, source_target_pairs={{0,8},{1,9},{2,10},{3,11},{4,12},{5,13},{6,14},{7,15},{8,0},{9,1},... | collective-permute-start | bytes 196616 | tf_op jit(solution)/shard_map/ppermute | solution.py:334
  41.5 12.1 %collective-permute-start.8 = (bf16[4,32,256]{2,1,0:T(8,128)(2,1)}, bf16[4,32,256]{2,1,0:T(8,128)(2,1)S(1)}, u32[]{:S(2)}, u32[]{:S(2)}) collective-permute-start(bf16[4,32,256]{2,1,0:T(8,128)(2,1)} %get-tuple-element.75), channel_id=1, source_target_pairs={{0,9},{1,8},{2,11},{3,10},{4,13},{5,12},{6,15},{7,14},{8,1},{9,0},... | collective-permute-start | bytes 196616 | tf_op jit(solution)/shard_map/ppermute | solution.py:334
  44.3 10.0 %collective-permute-start.9 = (bf16[4,32,256]{2,1,0:T(8,128)(2,1)}, bf16[4,32,256]{2,1,0:T(8,128)(2,1)S(1)}, u32[]{:S(2)}, u32[]{:S(2)}) collective-permute-start(bf16[4,32,256]{2,1,0:T(8,128)(2,1)} %get-tuple-element.78), channel_id=1, source_target_pairs={{0,10},{1,11},{2,8},{3,9},{4,14},{5,15},{6,12},{7,13},{8,2},{9,3},... | collective-permute-start | bytes 196616 | tf_op jit(solution)/shard_map/ppermute | solution.py:334
  46.5 21.9 %copy-start = (bf16[4,32,256]{2,1,0:T(8,128)(2,1)S(1)}, bf16[4,32,256]{2,1,0:T(8,128)(2,1)}, u32[]{:S(2)}) copy-start(bf16[4,32,256]{2,1,0:T(8,128)(2,1)} %get-tuple-element.49.refs_1_) | copy-start | bytes 196612
  47.1 12.2 %collective-permute-start.10 = (bf16[4,32,256]{2,1,0:T(8,128)(2,1)}, bf16[4,32,256]{2,1,0:T(8,128)(2,1)}, u32[]{:S(2)}, u32[]{:S(2)}) collective-permute-start(bf16[4,32,256]{2,1,0:T(8,128)(2,1)} %get-tuple-element.80), channel_id=1, source_target_pairs={{0,11},{1,10},{2,9},{3,8},{4,15},{5,14},{6,13},{7,12},{8,3},{9,2},... | collective-permute-start | bytes 196616 | tf_op jit(solution)/shard_map/ppermute | solution.py:334
  51.4 10.4 %collective-permute-start.11 = (bf16[4,32,256]{2,1,0:T(8,128)(2,1)}, bf16[4,32,256]{2,1,0:T(8,128)(2,1)}, u32[]{:S(2)}, u32[]{:S(2)}) collective-permute-start(bf16[4,32,256]{2,1,0:T(8,128)(2,1)} %get-tuple-element.81), channel_id=1, source_target_pairs={{0,12},{1,13},{2,14},{3,15},{4,8},{5,9},{6,10},{7,11},{8,4},{9,5},... | collective-permute-start | bytes 196616 | tf_op jit(solution)/shard_map/ppermute | solution.py:334
  52.0 11.2 %collective-permute-start.12 = (bf16[4,32,256]{2,1,0:T(8,128)(2,1)}, bf16[4,32,256]{2,1,0:T(8,128)(2,1)}, u32[]{:S(2)}, u32[]{:S(2)}) collective-permute-start(bf16[4,32,256]{2,1,0:T(8,128)(2,1)} %get-tuple-element.82), channel_id=1, source_target_pairs={{0,13},{1,12},{2,15},{3,14},{4,9},{5,8},{6,11},{7,10},{8,5},{9,4},... | collective-permute-start | bytes 196616 | tf_op jit(solution)/shard_map/ppermute | solution.py:334
  54.3 12.7 %collective-permute-start.13 = (bf16[4,32,256]{2,1,0:T(8,128)(2,1)}, bf16[4,32,256]{2,1,0:T(8,128)(2,1)}, u32[]{:S(2)}, u32[]{:S(2)}) collective-permute-start(bf16[4,32,256]{2,1,0:T(8,128)(2,1)} %get-tuple-element.83), channel_id=1, source_target_pairs={{0,14},{1,15},{2,12},{3,13},{4,10},{5,11},{6,8},{7,9},{8,6},{9,7},... | collective-permute-start | bytes 196616 | tf_op jit(solution)/shard_map/ppermute | solution.py:334
  54.9 13.4 %collective-permute-start.14 = (bf16[4,32,256]{2,1,0:T(8,128)(2,1)}, bf16[4,32,256]{2,1,0:T(8,128)(2,1)}, u32[]{:S(2)}, u32[]{:S(2)}) collective-permute-start(bf16[4,32,256]{2,1,0:T(8,128)(2,1)} %get-tuple-element.84), channel_id=1, source_target_pairs={{0,15},{1,14},{2,13},{3,12},{4,11},{5,10},{6,9},{7,8},{8,7},{9,6},... | collective-permute-start | bytes 196616 | tf_op jit(solution)/shard_map/ppermute | solution.py:334
  57.7 10.7 %copy-start.6 = (bf16[4,32,256]{2,1,0:T(8,128)(2,1)S(1)}, bf16[4,32,256]{2,1,0:T(8,128)(2,1)}, u32[]{:S(2)}) copy-start(bf16[4,32,256]{2,1,0:T(8,128)(2,1)} %copy-done.5) | copy-start | bytes 196612
  57.7 10.7 %copy-start.8 = (bf16[4,32,256]{2,1,0:T(8,128)(2,1)S(1)}, bf16[4,32,256]{2,1,0:T(8,128)(2,1)}, u32[]{:S(2)}) copy-start(bf16[4,32,256]{2,1,0:T(8,128)(2,1)} %copy-done.7) | copy-start | bytes 196612
  57.7 10.7 %copy-start.10 = (bf16[4,32,256]{2,1,0:T(8,128)(2,1)S(1)}, bf16[4,32,256]{2,1,0:T(8,128)(2,1)}, u32[]{:S(2)}) copy-start(bf16[4,32,256]{2,1,0:T(8,128)(2,1)} %copy-done.9) | copy-start | bytes 196612
  (7 other events, 24.5 us)
